TPU v7x, 32 devices: a whole 2x2x4 slice. The times are simulated.
32 devices in a mesh: wide: 8 (over y, x, core), narrow: 4 (over z).
Axes of the slice: x: 2, y: 2, z: 4, core: 2. Of those that a mesh axis runs over, the one named last changes fastest.
Arguments:
- vectors: float32 [32000, 8192], P('wide', 'narrow'), may hold values from -0.44860464 to 0.44860464
- reflectors: float32 [32000, 256], P('wide'), may hold values from -6 to 6
- triangle: float32 [256, 256], replicated, may hold values from -3.125e-05 to 7.8125e-05, as said below
- energies: float32 [32000], P('wide'), may hold values from -1 to 1
Outputs:
- updated: float32 [32000, 8192], P('wide', 'narrow')
- fock_block: float32 [8192, 512], P(('narrow', 'wide'))
Inputs may be any that keep to these rules, and one draw needn't show every extreme that they name: `triangle`: upper triangular, with diagonal entries between 1.5 / 32000 and 2.5 / 32000 and entries above the diagonal of magnitude at most 1 / 32000.
All inputs are finite; a program needn't handle non-finite values.
Results may differ from a plain program's by a relative error of at most 0.00007.
Values sent between devices are 32-bit elements; how exact they have to be, the bound alone decides.
No kernel may reach another device: no remote copies, remote signals or barrier semaphores. Data moves between devices by JAX's collectives and lax.ppermute only.
A program may use at most 128 MiB of HBM per device.

v0:
```python
import jax
import jax.numpy as jnp
from jax import lax
from jax.sharding import PartitionSpec as P

FB = 512
OFF = 256


def on_device(vectors, reflectors, triangle, energies):
    highest = lax.Precision.HIGHEST
    contract_rows = (((0,), (0,)), ((), ()))
    partial_proj = lax.dot_general(
        reflectors, vectors, contract_rows, precision=highest, preferred_element_type=jnp.float32
    )
    projected = lax.psum(partial_proj, "wide")
    coefficients = jnp.dot(
        triangle, projected, precision=highest, preferred_element_type=jnp.float32
    )
    updated = vectors - jnp.dot(
        reflectors, coefficients, precision=highest, preferred_element_type=jnp.float32
    )
    block_width = FB // lax.axis_size("narrow")
    scaled_rows = energies[:, None]
    raw_block = lax.all_gather(vectors[:, OFF : OFF + block_width], "narrow", axis=1, tiled=True)
    coef_block = lax.all_gather(
        coefficients[:, OFF : OFF + block_width], "narrow", axis=1, tiled=True
    )
    fock_input = raw_block - jnp.dot(
        reflectors, coef_block, precision=highest, preferred_element_type=jnp.float32
    )
    fock_part = lax.dot_general(
        updated,
        scaled_rows * fock_input,
        contract_rows,
        precision=highest,
        preferred_element_type=jnp.float32,
    )
    fock_block = lax.psum_scatter(fock_part, "wide", scatter_dimension=0, tiled=True)
    return (updated, fock_block)


def solution(mesh):
    return jax.shard_map(
        on_device,
        mesh=mesh,
        in_specs=(P("wide", "narrow"), P("wide", None), P(), P("wide")),
        out_specs=(P("wide", "narrow"), P(("narrow", "wide"), None)),
        check_vma=False,
    )
```

profile of v0, /device:TPU:0, one launch (start us, length us, event | category | flops | bytes accessed | tf_op | source)
XLA Modules:
  0.0 322.1 jit_solution(18332501188797184293)
XLA Ops:
  8.0 0.0 copy-start
  8.0 0.0 all-reduce.2.cloned.1.call-start
  8.1 33.7 %fusion.4 = f32[256,2048]{1,0:T(8,128)} fusion(f32[4000,256]{1,0:T(8,128)} %param.5, f32[4000,2048]{1,0:T(8,128)} %param.4), kind=kOutput, calls=%fused_computation.5 | convolution fusion | flops 25165824000 | bytes 38961152 | tf_op jit(solution)/shard_map/dot_general | solution.py:13
  41.8 0.0 all-reduce.2.cloned.1.call-update
  41.8 0.0 all-gather.2.cloned.1.call-start
  41.8 3.0 slice.6
  44.9 0.0 all-gather.2.cloned.1.call-update
  44.9 0.0 reduce-scatter.2.cloned.1.call-start
  44.9 61.1 %all-reduce.2.cloned.1.call-done = f32[256,2048]{1,0:T(8,128)} async-done(((f32[256,2048]{1,0:T(8,128)}), f32[256,2048]{1,0:T(8,128)}) %all-reduce.2.cloned.1.call-update) | async-done | bytes 2097168 | tf_op jit(solution)/shard_map/psum | solution.py:16
  106.1 0.0 copy-done
  106.1 0.0 copy-start.2
  106.1 5.3 %fusion.5 = f32[2048,256]{1,0:T(8,128)S(1)} fusion(f32[256,2048]{1,0:T(8,128)} %all-reduce.2.cloned.1.call-done, f32[256,256]{1,0:T(8,128)S(1)} %copy-done), kind=kOutput, calls=%fused_computation.6 | convolution fusion | flops 1610612736 | bytes 4456448 | tf_op jit(solution)/shard_map/dot_general | solution.py:17
  111.5 28.3 %all_gather.7 = f32[256,512]{0,1:T(8,128)S(1)} all-gather(f32[256,128]{0,1:T(8,128)S(1)} %slice.8), channel_id=1, replica_groups=mesh['wide'=8,'narrow'=4] {'narrow'}, dimensions={1}, use_global_device_ids=true | all-gather | bytes 655360 | tf_op jit(solution)/shard_map/all_gather | solution.py:26
  139.8 0.0 copy-done.2
  139.8 8.8 %fusion.6 = f32[512,4000]{0,1:T(8,128)} fusion(f32[256,512]{0,1:T(8,128)S(1)} %all_gather.7, f32[4000,256]{1,0:T(8,128)S(1)} %copy-done.2), kind=kOutput, calls=%fused_computation.7 | convolution fusion | flops 6291456000 | bytes 12812288 | tf_op jit(solution)/shard_map/dot_general | solution.py:29
  148.6 0.0 copy-start.3
  148.6 32.6 %bitcast_subtract_fusion = f32[4000,2048]{1,0:T(8,128)} fusion(f32[4000,2048]{1,0:T(8,128)} %param.4, f32[2048,256]{1,0:T(8,128)S(1)} %fusion.5, f32[4000,256]{1,0:T(8,128)S(1)} %copy-done.2), kind=kOutput, calls=%fused_computation | convolution fusion | flops 25174016000 | bytes 71729152 | tf_op jit(solution)/shard_map/dot_general | solution.py:20
  181.3 20.6 %all-gather.2.cloned.1.call-done = f32[4000,512]{1,0:T(8,128)} async-done(((f32[4000,128]{1,0:T(8,128)}), f32[4000,512]{1,0:T(8,128)}) %all-gather.2.cloned.1.call-update) | async-done | bytes 8192016 | tf_op jit(solution)/shard_map/all_gather | solution.py:25
  201.9 0.0 copy-done.3
  201.9 0.0 copy-start.1
  201.9 63.0 %fusion.1 = f32[2048,512]{1,0:T(8,128)} fusion(f32[4000,2048]{1,0:T(8,128)} %bitcast_subtract_fusion, f32[4000,512]{1,0:T(8,128)} %all-gather.2.cloned.1.call-done, f32[512,4000]{0,1:T(8,128)} %fusion.6, f32[4000]{0:T(1024)S(1)} %copy-done.3), kind=kOutput, calls=%fused_computation.3 | convolution fusion | flops 50335744000 | bytes 53362304 | tf_op jit(solution)/shard_map/dot_general | solution.py:32
  264.9 0.0 reduce-scatter.2.cloned.1.call-update
  264.9 49.7 %reduce-scatter.2.cloned.1.call-done = f32[256,512]{1,0:T(8,128)} async-done(((f32[2048,512]{1,0:T(8,128)}), f32[256,512]{1,0:T(8,128)}) %reduce-scatter.2.cloned.1.call-update) | async-done | bytes 524304 | tf_op jit(solution)/shard_map/reduce_scatter | solution.py:39
  314.6 0.0 copy-done.1
  (1 shorter events, 0.0 us)
Async XLA Ops:
  8.0 98.1 %copy-start = (f32[256,256]{1,0:T(8,128)S(1)}, f32[256,256]{1,0:T(8,128)}, u32[]{:S(2)}) copy-start(f32[256,256]{1,0:T(8,128)} %param.6) | copy-start | bytes 786436
  8.0 98.1 %all-reduce.2.cloned.1.call-start = ((), (), s32[]{:S(2)}) async-start(), calls=%async_computation.1 | async-start | bytes 4194304 | tf_op jit(solution)/shard_map/psum | solution.py:16
  41.8 160.1 %all-gather.2.cloned.1.call-start = ((), (), s32[]{:S(2)}) async-start(), calls=%async_computation.2 | async-start | bytes 10240000 | tf_op jit(solution)/shard_map/all_gather | solution.py:25
  44.9 269.7 %reduce-scatter.2.cloned.1.call-start = ((), (), s32[]{:S(2)}) async-start(), calls=%async_computation.3 | async-start | bytes 4718592 | tf_op jit(solution)/shard_map/reduce_scatter | solution.py:39
  106.1 33.7 %copy-start.2 = (f32[4000,256]{1,0:T(8,128)S(1)}, f32[4000,256]{1,0:T(8,128)}, u32[]{:S(2)}) copy-start(f32[4000,256]{1,0:T(8,128)} %param.5) | copy-start | bytes 12288004
  148.6 53.2 %copy-start.3 = (f32[4000]{0:T(1024)S(1)}, f32[4000]{0:T(1024)}, u32[]{:S(2)}) copy-start(f32[4000]{0:T(1024)} %param.7) | copy-start | bytes 48004
  201.9 112.8 %copy-start.1 = (f32[256,256]{1,0:T(8,128)S(1)}, f32[256,256]{1,0:T(8,128)}, u32[]{:S(2)}) copy-start(f32[256,256]{1,0:T(8,128)} %param.6) | copy-start | bytes 786436
Sparse Core Ops, SparseCore 0:
  41.9 64.1 all-reduce.1
  265.0 49.5 reduce-scatter.1
Sparse Core Ops, SparseCore 1:
  45.0 156.8 all-gather.1
where the time goes:
time: 322 us
  matrix products  144 us (45%)
  waiting for transfers between devices  131 us (41%)
  blocking collectives  28.3 us (9%)
  between operations  15.5 us (5%)
    dot_general x1, matrix products, on_device(): lax.dot_general(updated, scaled_rows * fock_input, contract_rows, precisi...  63 us
    psum x1, waiting for transfers between devices, on_device(): projected = lax.psum(partial_proj, 'wide')  61.1 us
    reduce_scatter x1, waiting for transfers between devices, on_device(): lax.psum_scatter(fock_part, 'wide', scatter_dimension=0, tiled=True)  49.7 us
    dot_general x1, matrix products, on_device(): lax.dot_general(reflectors, vectors, contract_rows, precision=highest, pr...  33.7 us
    dot_general x1, matrix products, on_device(): jnp.dot(reflectors, coefficients, precision=highest, preferred_element_ty...  32.6 us
    all_gather x1, blocking collectives, on_device(): lax.all_gather(coefficients[:, OFF:OFF + block_width], 'narrow', axis=1,...  28.3 us
    all_gather x1, waiting for transfers between devices, on_device(): lax.all_gather(vectors[:, OFF:OFF + block_width], 'narrow', axis=1, tiled...  20.6 us
    dot_general x1, matrix products, on_device(): jnp.dot(reflectors, coef_block, precision=highest, preferred_element_type...  8.83 us
  transfers between devices with their start and end apart: 3, of which 3 were waited for; matrix products, arithmetic and copies ran while one was open for 15% of the time, Pallas kernels for 0%

commit v1 on v0

v1 whole, which is shorter than its diff:
```python
import functools

import jax
import jax.numpy as jnp
from jax import lax
from jax.experimental import pallas as pl
from jax.experimental.pallas import tpu as pltpu
from jax.sharding import PartitionSpec as P

FB = 512
OFF = 256
CHUNKS = 1
VMEM = 56 * 1024 * 1024

F32 = jnp.float32
BF16 = jnp.bfloat16
LONG = pl.CostEstimate(flops=10**11, bytes_accessed=1024, transcendentals=0)
SHORT = pl.CostEstimate(flops=1024, bytes_accessed=1024, transcendentals=0)


def split(x):
    high = x.astype(BF16)
    return high, (x - high.astype(F32)).astype(BF16)


def mul(left, right):
    return jnp.dot(left, right, preferred_element_type=F32)


def three(left, right):
    (lh, ll), (rh, rl) = left, right
    return mul(lh, rh) + mul(ll, rh) + mul(lh, rl)


def stacked(both, high, right):
    rh, rl = right
    m = high.shape[0]
    top = mul(both, rh)
    return top[:m] + top[m:] + mul(high, rl)


def params():
    return pltpu.CompilerParams(
        dimension_semantics=("arbitrary",), vmem_limit_bytes=VMEM
    )


def width(columns, wide):
    return 256 if columns % 256 == 0 and 256 % (columns // wide) == 0 else columns // wide


def whole(shape):
    return pl.BlockSpec(shape, lambda j, *_: (0,) * len(shape), pipeline_mode=pl.Buffered(1))


ANY = pl.BlockSpec(memory_space=pl.ANY)


def gate_kernel(*refs):
    del refs


def gate(held, *others, cost=SHORT):
    count = len(held)
    return pl.pallas_call(
        gate_kernel,
        in_specs=[ANY] * (count + len(others)),
        out_specs=[ANY] * count,
        out_shape=[jax.ShapeDtypeStruct(x.shape, x.dtype) for x in held],
        input_output_aliases={k: k for k in range(count)},
        cost_estimate=cost,
        name="gate",
    )(*held, *others)


def place(value, index, even_ref, odd_ref):
    half = index // 2

    @pl.when(index % 2 == 0)
    def _():
        even_ref[half] = value

    @pl.when(index % 2 == 1)
    def _():
        odd_ref[half] = value


def take(index, even_ref, odd_ref):
    half = index // 2
    return jnp.where(index % 2 == 0, even_ref[half], odd_ref[half])


def own_kernel(block_width, v_ref, r_ref, out_ref):
    out_ref[...] = three(split(v_ref[:, :block_width].T), split(r_ref[...]))


def own_columns(vectors, reflectors, block_width):
    rows, nb = reflectors.shape
    taken = max(block_width, 128)
    return pl.pallas_call(
        functools.partial(own_kernel, block_width),
        grid=(1,),
        in_specs=[pl.BlockSpec((rows, taken), lambda j: (0, OFF // taken)), whole((rows, nb))],
        out_specs=whole((block_width, nb)),
        out_shape=jax.ShapeDtypeStruct((block_width, nb), F32),
        compiler_params=params(),
        cost_estimate=SHORT,
        name="own",
    )(vectors, reflectors)


def project_kernel(per, me_ref, v_ref, r_ref, after_ref, even_ref, odd_ref, token_ref, both_ref):
    j = pl.program_id(0)
    nb = r_ref.shape[1]

    @pl.when(j == 0)
    def _():
        high, low = split(r_ref[...].T)
        both_ref[:nb] = high
        both_ref[nb:] = low
        token_ref[...] = jnp.zeros_like(token_ref)

    value = stacked(both_ref[...], both_ref[:nb], split(v_ref[...]))
    step = v_ref.shape[1]
    for g in range(step // per):
        w = j * (step // per) + g
        place(value[:, g * per : (g + 1) * per], w ^ me_ref[0], even_ref, odd_ref)


def project(me, vectors, reflectors, after, wide):
    rows, columns = vectors.shape
    nb = reflectors.shape[1]
    per = columns // wide
    step = width(columns, wide)
    half = jax.ShapeDtypeStruct((wide // 2, nb, per), F32)
    return pl.pallas_call(
        functools.partial(project_kernel, per),
        grid_spec=pltpu.PrefetchScalarGridSpec(
            num_scalar_prefetch=1,
            grid=(columns // step,),
            in_specs=[pl.BlockSpec((rows, step), lambda j, *_: (0, j)), whole((rows, nb)), ANY],
            out_specs=[whole(half.shape), whole(half.shape), whole((8, 128))],
            scratch_shapes=[pltpu.VMEM((2 * nb, rows), BF16)],
        ),
        out_shape=[half, half, jax.ShapeDtypeStruct((8, 128), F32)],
        compiler_params=params(),
        cost_estimate=SHORT,
        name="project",
    )(me, vectors, reflectors, after)


def gather(choice, groups, block_ref):
    first = 0
    for group in groups:
        rows = group[0].shape[0]
        for k, ref in enumerate(group):

            @pl.when(choice == k)
            def _(ref=ref, first=first, rows=rows):
                pltpu.sync_copy(ref, block_ref.at[pl.ds(first, rows)])

        first += rows


def early_kernel(per, groups, me_ref, v_ref, r_ref, e_ref, after_ref, *refs):
    out_ref, small_ref, both_ref, *block = refs[-3 - bool(groups) :]
    j = pl.program_id(0)
    m = both_ref.shape[0] // 2

    @pl.when(j == 0)
    def _():
        if groups:
            gather(me_ref[1], regroup(refs, groups), block[0])
            x = block[0][...].T
        else:
            x = r_ref[...].T * e_ref[...]
        high, low = split(x)
        both_ref[:m] = high
        both_ref[m:] = low
        small_ref[...] = stacked(both_ref[...], both_ref[:m], split(r_ref[...]))

    value = stacked(both_ref[...], both_ref[:m], split(v_ref[...]))
    for g in range(v_ref.shape[1] // per):
        out_ref[g] = value[:, g * per : (g + 1) * per]


def regroup(refs, groups):
    refs = list(refs)
    return [[refs.pop(0) for _ in range(count)] for count in groups]


def early(me, vectors, reflectors, e_row, chosen, wide, after):
    rows, columns = vectors.shape
    nb = reflectors.shape[1]
    per = columns // wide
    step = width(columns, wide)
    flat = [x for group in chosen for x in group]
    m = flat[0].shape[1] if flat else nb
    scratch = [pltpu.VMEM((2 * m, rows), BF16)]
    if flat:
        scratch.append(pltpu.VMEM((rows, m), F32))
    return pl.pallas_call(
        functools.partial(early_kernel, per, [len(group) for group in chosen]),
        grid_spec=pltpu.PrefetchScalarGridSpec(
            num_scalar_prefetch=1,
            grid=(columns // step,),
            in_specs=[
                pl.BlockSpec((rows, step), lambda j, *_: (0, j)),
                whole((rows, nb)),
                whole((1, rows)),
                ANY,
            ]
            + [ANY] * len(flat),
            out_specs=[
                pl.BlockSpec((step // per, m, per), lambda j, *_: (j, 0, 0)),
                whole((m, nb)),
            ],
            scratch_shapes=scratch,
        ),
        out_shape=[
            jax.ShapeDtypeStruct((wide, m, per), F32),
            jax.ShapeDtypeStruct((m, nb), F32),
        ],
        compiler_params=params(),
        cost_estimate=SHORT,
        name="early",
    )(me, vectors, reflectors, e_row, after, *flat)


def finish_kernel(me_ref, even_ref, odd_ref, *refs):
    *refs, out_ref = refs
    w = pl.program_id(0)
    c = split(take(w ^ me_ref[0], even_ref, odd_ref))
    first = 0
    for a_ref, d_ref in zip(refs[::2], refs[1::2]):
        m = a_ref.shape[1]
        out_ref[0, first : first + m] = a_ref[0] - three(split(d_ref[...]), c)
        first += m


def finish(me, even, odd, *parts):
    wide, _, per = parts[0].shape
    m = sum(part.shape[1] for part in parts[::2])
    specs = []
    for a, d in zip(parts[::2], parts[1::2]):
        specs += [pl.BlockSpec((1, *a.shape[1:]), lambda w, *_: (w, 0, 0)), whole(d.shape)]
    return pl.pallas_call(
        finish_kernel,
        grid_spec=pltpu.PrefetchScalarGridSpec(
            num_scalar_prefetch=1,
            grid=(wide,),
            in_specs=[whole(even.shape), whole(odd.shape)] + specs,
            out_specs=pl.BlockSpec((1, m, per), lambda w, *_: (w, 0, 0)),
        ),
        out_shape=jax.ShapeDtypeStruct((wide, m, per), F32),
        compiler_params=params(),
        cost_estimate=SHORT,
        name="finish",
    )(me, even, odd, *parts)


def update_kernel(per, me_ref, v_ref, r_ref, even_ref, odd_ref, after_ref, out_ref, rh_ref, rl_ref):
    j = pl.program_id(0)

    @pl.when(j == 0)
    def _():
        rh_ref[...], rl_ref[...] = split(r_ref[...])

    count = v_ref.shape[1] // per
    blocks = [take((j * count + g) ^ me_ref[0], even_ref, odd_ref) for g in range(count)]
    c = blocks[0] if count == 1 else jnp.concatenate(blocks, axis=1)
    out_ref[...] = v_ref[...] - three((rh_ref[...], rl_ref[...]), split(c))


def update(me, vectors, reflectors, even, odd, after, wide):
    rows, columns = vectors.shape
    nb = reflectors.shape[1]
    per = columns // wide
    step = width(columns, wide)
    return pl.pallas_call(
        functools.partial(update_kernel, per),
        grid_spec=pltpu.PrefetchScalarGridSpec(
            num_scalar_prefetch=1,
            grid=(columns // step,),
            in_specs=[
                pl.BlockSpec((rows, step), lambda j, *_: (0, j)),
                whole((rows, nb)),
                whole(even.shape),
                whole(odd.shape),
                ANY,
            ],
            out_specs=pl.BlockSpec((rows, step), lambda j, *_: (0, j)),
            scratch_shapes=[pltpu.VMEM((rows, nb), BF16), pltpu.VMEM((rows, nb), BF16)],
        ),
        out_shape=jax.ShapeDtypeStruct(vectors.shape, F32),
        compiler_params=params(),
        cost_estimate=SHORT,
        name="update",
    )(me, vectors, reflectors, even, odd, after)


def late_kernel(per, relative, groups, *refs):
    me_ref, v_ref, r_ref, even_ref, odd_ref, before_ref, dbefore_ref, _, *refs = refs
    *outs, both_ref, small_ref, block_ref = refs[sum(groups) :]
    j = pl.program_id(0)
    m = block_ref.shape[1]

    @pl.when(j == 0)
    def _():
        gather(me_ref[1], regroup(refs, groups), block_ref)
        high, low = split(block_ref[...].T)
        both_ref[:m] = high
        both_ref[m:] = low
        small_ref[...] = dbefore_ref[...] + stacked(
            both_ref[...], both_ref[:m], split(r_ref[...])
        )

    value = stacked(both_ref[...], both_ref[:m], split(v_ref[...]))
    small = split(small_ref[...])
    count = v_ref.shape[1] // per
    for g in range(count):
        index = (j * count + g) ^ me_ref[0]
        c = split(take(index, even_ref, odd_ref))
        part = before_ref[g] + value[:, g * per : (g + 1) * per] - three(small, c)
        if relative:
            place(part, index, *outs)
        else:
            outs[0][g] = part


def late(me, vectors, reflectors, chosen, even, odd, before, dbefore, after, chunk, wide, relative):
    columns = vectors.shape[1]
    rows = sum(group[0].shape[0] for group in chosen)
    m = chosen[0][0].shape[1]
    flat = [x for group in chosen for x in group]
    nb = reflectors.shape[1]
    per = columns // wide
    step = width(columns, wide)
    count = step // per
    if relative:
        half = jax.ShapeDtypeStruct((wide // 2, m, per), F32)
        out_shape, out_specs = [half, half], [whole(half.shape)] * 2
    else:
        out_shape = [jax.ShapeDtypeStruct((wide, m, per), F32)]
        out_specs = [pl.BlockSpec((count, m, per), lambda j, *_: (j, 0, 0))]
    return pl.pallas_call(
        functools.partial(late_kernel, per, relative, [len(group) for group in chosen]),
        grid_spec=pltpu.PrefetchScalarGridSpec(
            num_scalar_prefetch=1,
            grid=(columns // step,),
            in_specs=[
                pl.BlockSpec((rows, step), lambda j, *_: (chunk, j)),
                pl.BlockSpec((rows, nb), lambda j, *_: (chunk, 0)),
                whole(even.shape),
                whole(odd.shape),
                pl.BlockSpec((count, m, per), lambda j, *_: (j, 0, 0)),
                whole((m, nb)),
                ANY,
            ]
            + [ANY] * len(flat),
            out_specs=out_specs,
            scratch_shapes=[
                pltpu.VMEM((2 * m, rows), BF16),
                pltpu.VMEM((m, nb), F32),
                pltpu.VMEM((rows, m), F32),
            ],
        ),
        out_shape=out_shape,
        compiler_params=params(),
        cost_estimate=SHORT,
        name="late",
    )(me, vectors, reflectors, even, odd, before, dbefore, after, *flat)


def last_kernel(block_width, n_early, groups, source_ref, y_ref, coef_ref, *refs):
    *refs, out_ref, scratch_ref = refs
    nb = coef_ref.shape[1]
    pieces = [y_ref[nb + s * block_width : nb + (s + 1) * block_width] for s in range(n_early)]
    pieces += [
        functools.reduce(jnp.add, [ref[...] for ref in group]) for group in regroup(refs, groups)
    ]
    for slot, piece in enumerate(pieces):
        first = pl.multiple_of(source_ref[slot] * block_width, block_width)
        scratch_ref[pl.ds(first, block_width), :] = piece
    taken = three(split(coef_ref[...]), split(y_ref[:nb]))
    out_ref[...] = (scratch_ref[...] - taken).T


def last(sources, ready, coef_block, terms, block_width, n_early):
    per = ready.shape[1]
    operands = [ready, coef_block] + [x for group in terms for x in group]
    return pl.pallas_call(
        functools.partial(last_kernel, block_width, n_early, [len(group) for group in terms]),
        grid_spec=pltpu.PrefetchScalarGridSpec(
            num_scalar_prefetch=1,
            grid=(1,),
            in_specs=[whole(x.shape) for x in operands],
            out_specs=whole((per, FB)),
            scratch_shapes=[pltpu.VMEM((FB, per), F32)],
        ),
        out_shape=jax.ShapeDtypeStruct((per, FB), F32),
        compiler_params=params(),
        cost_estimate=SHORT,
        name="last",
    )(sources, *operands)


def arrivals(n):
    order = []
    for z in range(n):
        found = [(hops, 0) for hops in range(1, n) if z + hops < n]
        found += [(hops, 1) for hops in range(1, n) if z - hops >= 0]
        order.append(sorted(found))
    return [[order[z][slot] for z in range(n)] for slot in range(n - 1)]


def exchange(blocks, n):
    came = {}
    held = [list(blocks), list(blocks)]
    for hops in range(1, n):
        pairs = [
            [(z, z - 1) for z in range(1, n - hops + 1)],
            [(z, z + 1) for z in range(hops - 1, n - 1)],
        ]
        held = [[lax.ppermute(x, "narrow", pairs[d]) for x in held[d]] for d in (0, 1)]
        if hops < n - 1:
            count = len(blocks)
            both = gate(held[0] + held[1], cost=LONG)
            held = [both[:count], both[count:]]
        for d in (0, 1):
            came[(hops, d)] = held[d]
    return came


def options(came, places, z):
    choices = sorted(set(places))
    which = jnp.int32(0)
    for p, place in enumerate(places):
        which = jnp.where(z == p, choices.index(place), which)
    return [[came[choice][c] for choice in choices] for c in range(CHUNKS)], which


def source(places, z):
    value = jnp.int32(0)
    for p, (hops, direction) in enumerate(places):
        value = jnp.where(z == p, p - hops if direction else p + hops, value)
    return value


def swap(x, wide, distance):
    return lax.ppermute(x, "wide", [(i, i ^ distance) for i in range(wide)])


def scatter_terms(even, odd, wide):
    other = swap(odd, wide, 1)
    sums = [even[h] + other[h] for h in range(wide // 2)]
    return [sums[0]] + [swap(sums[h], wide, 2 * h) for h in range(1, wide // 2)]


def on_device(vectors, reflectors, triangle, energies):
    n = lax.axis_size("narrow")
    wide = lax.axis_size("wide")
    z = lax.axis_index("narrow")
    me = lax.axis_index("wide").astype(jnp.int32).reshape(1)
    block_width = FB // n
    rows, columns = vectors.shape
    nb = reflectors.shape[1]
    step = rows // CHUNKS
    e_row = energies.reshape(1, rows)

    chunks = [
        energies[c * step : (c + 1) * step, None]
        * vectors[c * step : (c + 1) * step, OFF : OFF + block_width]
        for c in range(CHUNKS)
    ]
    came = exchange(chunks, n)
    table = arrivals(n)
    sources = jnp.stack([z.astype(jnp.int32)] + [source(places, z) for places in table])

    own = own_columns(vectors, reflectors, block_width)
    even, odd, token = project(me, vectors, reflectors, own, wide)

    part = lax.psum_scatter(own, "wide", scatter_dimension=0, tiled=True)
    share = lax.dot_general(
        part, triangle, (((1,), (1,)), ((), ())), precision=lax.Precision.HIGHEST
    )
    shares = lax.all_gather(share, "narrow", axis=0)
    coef_block = lax.all_gather(shares, "wide", axis=1).reshape(FB, nb)

    def with_choice(which):
        return jnp.stack([me[0], which.astype(jnp.int32)])

    none = with_choice(jnp.int32(0))
    y, dy = early(none, vectors, reflectors, e_row, [], wide, token)
    a, da = early(none, vectors, reflectors, e_row, [[chunk] for chunk in chunks], wide, dy)

    (odd,) = gate([odd], da, part, *came[(1, 0)], *came[(1, 1)])
    terms = scatter_terms(even, odd, wide)
    chosen, which = options(came, table[0], z)
    b, db = early(with_choice(which), vectors, reflectors, e_row, chosen, wide, da)
    terms[0] = gate(terms[:1], db)[0]
    projected = functools.reduce(jnp.add, terms)
    coefficients = jnp.dot(triangle, projected, precision=lax.Precision.HIGHEST)
    c_even = jnp.stack(
        [coefficients] + [swap(coefficients, wide, 2 * h) for h in range(1, wide // 2)]
    )
    c_odd = swap(c_even, wide, 1)

    (db,) = gate([db], cost=LONG)
    (db,) = gate([db], shares)
    first = finish(me, c_even, c_odd, y, dy, a, da, b, db)
    ready = lax.psum_scatter(first, "wide", scatter_dimension=0)

    zero = jnp.zeros((wide, block_width, columns // wide), F32)
    small_zero = jnp.zeros((block_width, nb), F32)
    mids, done = [], first
    for slot in range(1, n - 2):
        chosen, which = options(came, table[slot], z)
        halves = late(
            with_choice(which), vectors, reflectors, chosen, c_even, c_odd, zero, small_zero,
            done, 0, wide, True,
        )
        mids.append(scatter_terms(*halves, wide))
        done = halves[0]
    updated = update(me, vectors, reflectors, c_even, c_odd, done, wide)

    total = zero
    chosen, which = options(came, table[n - 2], z)
    for c in range(CHUNKS):
        out = late(
            with_choice(which), vectors, reflectors, chosen[c : c + 1], c_even, c_odd, total,
            small_zero, updated, c, wide, c == CHUNKS - 1,
        )
        total = out[0]
    tail = scatter_terms(*out, wide)
    fock_block = last(sources, ready, coef_block, mids + [tail], block_width, 2)
    return (updated, fock_block)


def solution(mesh):
    return jax.shard_map(
        on_device,
        mesh=mesh,
        in_specs=(P("wide", "narrow"), P("wide", None), P(), P("wide")),
        out_specs=(P("wide", "narrow"), P(("narrow", "wide"), None)),
        check_vma=False,
    )
```

time: 322 us -> 305 us (0.947); the launches traced: 322 us -> 300 us
  Pallas kernels: 0 us -> 177 us
  matrix products: 144 us -> 1.94 us
  waiting for transfers between devices: 131 us -> 34.4 us
  starting transfers between devices: 0.12 us -> 28 us
  other arithmetic: 0 us -> 10.2 us
    pallas_call x0 -> x16, Pallas kernels: none -> 177 us  [the longest x3 63.9 us: early(): pl.pallas_call(functools.partial(early_kernel, per, [len(group) for group...]
    dot_general x5 -> x2, matrix products: 144 us -> 1.94 us  [the longest x1 1.67 us: on_device(): coefficients = jnp.dot(triangle, projected, precision=lax.Precision.HIGHEST)]
    psum x1 -> x0, waiting for transfers between devices: 61.1 us -> none  [on_device(): projected = lax.psum(partial_proj, 'wide')]
    reduce_scatter x1 -> x2, waiting for transfers between devices: 49.7 us -> 0.02 us  [the longest x1 0.02 us: on_device(): ready = lax.psum_scatter(first, 'wide', scatter_dimension=0)]
    ppermute x0 -> x22, waiting for transfers between devices: none -> 34.3 us  [the longest x6 29.5 us: exchange(): lax.ppermute(x, 'narrow', pairs[d])]
    ppermute x0 -> x22, starting transfers between devices: none -> 27.8 us  [the longest x16 14.6 us: swap(): return lax.ppermute(x, 'wide', [(i, i ^ distance) for i in range(wide)])]
    all_gather x1 -> x0, waiting for transfers between devices: 20.6 us -> none  [on_device(): lax.all_gather(vectors[:, OFF:OFF + block_width], 'narrow', axis=1, tiled...]
    unnamed x8 -> x32, local copies, waits for them, and re-layouts: 0.02 us -> 4.33 us
  transfers between devices with their start and end apart: 3 -> 24, of which waited for: 3 -> 3; matrix products, arithmetic and copies ran while one was open for 15% -> 3% of each run, Pallas kernels for 0% -> 58%
where the time goes in v1:
time: 305 us; the launch traced here: 300 us
  Pallas kernels  177 us (58%)
  waiting for transfers between devices  34.4 us (11%)
  starting transfers between devices  28 us (9%)
  blocking collectives  27.5 us (9%)
  between operations  14.3 us (5%)
  other arithmetic  10.2 us (3%)
  local copies, waits for them, and re-layouts  6.06 us (2%)
    pallas_call x3, Pallas kernels, early(): pl.pallas_call(functools.partial(early_kernel, per, [len(group) for group...  63.9 us
    pallas_call x2, Pallas kernels, late(): pl.pallas_call(functools.partial(late_kernel, per, relative, [len(group)...  44 us
    pallas_call x1, Pallas kernels, update(): pl.pallas_call(functools.partial(update_kernel, per), grid_spec=pltpu.Pre...  30.9 us
    ppermute x6, waiting for transfers between devices, exchange(): lax.ppermute(x, 'narrow', pairs[d])  29.5 us
    pallas_call x1, Pallas kernels, project(): pl.pallas_call(functools.partial(project_kernel, per), grid_spec=pltpu.Pr...  21.9 us
    all_gather x1, blocking collectives, on_device(): shares = lax.all_gather(share, 'narrow', axis=0)  16 us
    ppermute x16, starting transfers between devices, swap(): return lax.ppermute(x, 'wide', [(i, i ^ distance) for i in range(wide)])  14.6 us
    ppermute x6, starting transfers between devices, exchange(): lax.ppermute(x, 'narrow', pairs[d])  13.2 us
  transfers between devices with their start and end apart: 24, of which 3 were waited for; matrix products, arithmetic and copies ran while one was open for 3% of the time, Pallas kernels for 58%

profile of v1, /device:TPU:0, one launch (start us, length us, event | category | flops | bytes accessed | tf_op | source)
XLA Modules:
  0.0 299.8 jit_solution(16294424964182650286)
XLA Ops:
  7.2 3.7 %slice_multiply_fusion.refs_0_ = f32[4000,128]{1,0:T(8,128)} fusion(f32[4000,2048]{1,0:T(8,128)} %refs_1_.3, f32[4000]{0:T(1024)} %param.7), kind=kLoop, calls=%fused_computation | loop fusion | flops 512000 | bytes 4112000 | tf_op jit(solution)/shard_map/mul | solution.py:472
  10.9 5.0 %collective-permute-start.1 = (f32[4000,128]{1,0:T(8,128)}, f32[4000,128]{1,0:T(8,128)S(1)}, u32[]{:S(2)}, u32[]{:S(2)}) collective-permute-start(f32[4000,128]{1,0:T(8,128)} %slice_multiply_fusion.refs_0_), channel_id=1, source_target_pairs={{0,1},{1,2},{2,3},{4,5},{5,6},{6,7},{8,9},{9,10},{10,11},{12,13},{... | collective-permute-start | bytes 6144008 | tf_op jit(solution)/shard_map/ppermute | solution.py:425
  16.0 1.3 collective-permute-start
  17.3 4.7 %own.1.after_ref = f32[128,256]{1,0:T(8,128)} custom-call(f32[4000,2048]{1,0:T(8,128)} %refs_1_.3, f32[4000,256]{1,0:T(8,128)} %refs_2_.3), custom_call_target="tpu_custom_call" | custom-call | flops 1024 | bytes 1024 | tf_op jit(solution)/shard_map/own/pallas_call | solution.py:100
  22.3 21.9 %project.1 = (f32[4,256,256]{2,1,0:T(8,128)}, f32[4,256,256]{2,1,0:T(8,128)}, f32[8,128]{1,0:T(8,128)}) custom-call(s32[1]{0:T(128)} %bitcast.me_ref, f32[4000,2048]{1,0:T(8,128)} %refs_1_.3, f32[4000,256]{1,0:T(8,128)} %refs_2_.3, f32[128,256]{1,0:T(8,128)} %own.1.after_ref), custom_call_target="tpu_custom_call" | custom-call | flops 1024 | bytes 1024 | tf_op jit(solution)/shard_map/project/pallas_call | solution.py:136
  44.1 0.6 pad_add_fusion.me_ref
  44.7 22.9 %early.3 = (f32[8,256,256]{2,1,0:T(8,128)}, f32[256,256]{1,0:T(8,128)}) custom-call(s32[2]{0:T(128)} %pad_add_fusion.me_ref, f32[4000,2048]{1,0:T(8,128)} %refs_1_.3, f32[4000,256]{1,0:T(8,128)} %refs_2_.3, f32[1,4000]{1,0:T(1,128)} %bitcast.53, f32[8,128]{1,0:T(8,128)} %get-tuple-element.21.after_ref), custom_call_target="tpu_custom_call" | custom-call | flops 1024 | bytes 1024 | tf_op jit(solution)/shard_map/early/pallas_call | solution.py:202
  67.6 20.5 %early.4 = (f32[8,128,256]{2,1,0:T(8,128)}, f32[128,256]{1,0:T(8,128)}) custom-call(s32[2]{0:T(128)} %pad_add_fusion.me_ref, f32[4000,2048]{1,0:T(8,128)} %refs_1_.3, f32[4000,256]{1,0:T(8,128)} %refs_2_.3, f32[1,4000]{1,0:T(1,128)} %bitcast.54, f32[256,256]{1,0:T(8,128)} %get-tuple-element.22.after_ref.refs_1_, f32[4000,128]{1,0:T(8,128)} %slice_multiply_fusion.refs_0_), custom_call_target="tpu_custom_call" | custom-call | flops 1024 | bytes 1024 | tf_op jit(solution)/shard_map/early/pallas_call | solution.py:202
  88.1 1.3 copy-done.3
  89.5 2.9 collective-permute-done.2
  92.3 0.8 fusion.2
  93.2 1.5 collective-permute-start.3
  94.7 1.5 collective-permute-start.5
  96.1 0.5 collective-permute-start.4
  96.6 0.6 pad_add_fusion.1.me_ref
  97.2 20.5 %early.5 = (f32[8,128,256]{2,1,0:T(8,128)}, f32[128,256]{1,0:T(8,128)}) custom-call(s32[2]{0:T(128)} %pad_add_fusion.1.me_ref, f32[4000,2048]{1,0:T(8,128)} %refs_1_.3, f32[4000,256]{1,0:T(8,128)} %refs_2_.3, f32[1,4000]{1,0:T(1,128)} %bitcast.55, f32[128,256]{1,0:T(8,128)} %get-tuple-element.23.refs_1_.after_ref.refs_3_, ...), custom_call_target="tpu_custom_call" | custom-call | flops 1024 | bytes 1024 | tf_op jit(solution)/shard_map/early/pallas_call | solution.py:202
  117.8 1.7 fusion.4
  119.5 1.6 collective-permute-start.7
  121.1 1.5 collective-permute-start.6
  122.6 0.5 collective-permute-start.8
  123.3 16.0 %all-gather = f32[64,256]{1,0:T(8,128)} all-gather(f32[16,256]{1,0:T(8,128)S(1)} %fusion.16), channel_id=2, replica_groups=mesh['wide'=8,'narrow'=4] {'narrow'}, dimensions={0}, use_global_device_ids=true | all-gather | bytes 81920 | tf_op jit(solution)/shard_map/all_gather | solution.py:487
  139.3 1.3 collective-permute-start.10
  140.6 2.1 collective-permute-start.11
  142.8 0.9 copy-done.2
  143.7 1.9 collective-permute-done.9.odd_ref.refs_4_
  145.6 8.6 %finish.1.refs_7_ = f32[8,512,256]{2,1,0:T(8,128)} custom-call(s32[1]{0:T(128)} %bitcast.me_ref, f32[4,256,256]{2,1,0:T(8,128)} %copy-done.2, f32[4,256,256]{2,1,0:T(8,128)} %collective-permute-done.9.odd_ref.refs_4_, f32[8,256,256]{2,1,0:T(8,128)} %get-tuple-element.27.refs_0_, f32[256,256]{1,0:T(8,128)} %get-tuple-element.22.after_ref.refs_1_, ...), custom_call_target="tpu_custom_call" | custom-call | flops 1024 | bytes 1024 | tf_op jit(solution)/shard_map/finish/pallas_call | solution.py:247
  154.3 29.5 %collective-permute-done.10.refs_0_ = f32[4000,128]{1,0:T(8,128)} collective-permute-done((f32[4000,128]{1,0:T(8,128)}, f32[4000,128]{1,0:T(8,128)}, u32[]{:S(2)}, u32[]{:S(2)}) %collective-permute-start.10) | collective-permute-done | bytes 2048032 | tf_op jit(solution)/shard_map/ppermute | solution.py:425
  183.8 1.5 collective-permute-start.16
  185.3 2.0 collective-permute-start.17
  187.3 0.6 pad_add_fusion.2.refs_0_
  187.9 0.7 broadcast_in_dim.8.refs_6_
  188.6 1.1 broadcast_in_dim.7.refs_5_
  189.6 22.2 %late.2 = (f32[4,128,256]{2,1,0:T(8,128)}, f32[4,128,256]{2,1,0:T(8,128)}) custom-call(s32[2]{0:T(128)} %pad_add_fusion.2.refs_0_, f32[4000,2048]{1,0:T(8,128)} %refs_1_.3, f32[4000,256]{1,0:T(8,128)} %refs_2_.3, f32[4,256,256]{2,1,0:T(8,128)} %copy-done.2, f32[4,256,256]{2,1,0:T(8,128)} %collective-permute-done.9.odd_ref.refs_4_, ...), custom_call_target="tpu_custom_call" | custom-call | flops 1024 | bytes 1024 | tf_op jit(solution)/shard_map/late/pallas_call | solution.py:346
  211.9 0.7 pad_add_fusion.4.refs_0_
  212.5 30.9 %update.1.refs_7_ = f32[4000,2048]{1,0:T(8,128)} custom-call(s32[1]{0:T(128)} %bitcast.me_ref, f32[4000,2048]{1,0:T(8,128)} %refs_1_.3, f32[4000,256]{1,0:T(8,128)} %refs_2_.3, f32[4,256,256]{2,1,0:T(8,128)} %copy-done.2, f32[4,256,256]{2,1,0:T(8,128)} %collective-permute-done.9.odd_ref.refs_4_, f32[4,128,256]{2,1,0:T(8,128)} %get-tuple-element.32.after_ref), custom_call_target="tpu_custom_call" | custom-call | flops 1024 | bytes 1024 | tf_op jit(solution)/shard_map/update/pallas_call | solution.py:280
  243.5 1.3 copy-done.6
  244.8 21.8 %late.3 = (f32[4,128,256]{2,1,0:T(8,128)}, f32[4,128,256]{2,1,0:T(8,128)}) custom-call(s32[2]{0:T(128)} %pad_add_fusion.4.refs_0_, f32[4000,2048]{1,0:T(8,128)} %refs_1_.3, f32[4000,256]{1,0:T(8,128)} %refs_2_.3, f32[4,256,256]{2,1,0:T(8,128)} %copy-done.2, f32[4,256,256]{2,1,0:T(8,128)} %collective-permute-done.9.odd_ref.refs_4_, ...), custom_call_target="tpu_custom_call" | custom-call | flops 1024 | bytes 1024 | tf_op jit(solution)/shard_map/late/pallas_call | solution.py:346
  266.5 0.5 collective-permute-start.18
  267.0 0.7 fusion.12
  267.8 2.4 collective-permute-start.15
  270.6 0.7 collective-permute-start.13
  271.3 1.9 fusion.8
  273.1 2.4 collective-permute-start.21
  275.9 0.7 collective-permute-start.19
  276.6 0.6 pad_add_fusion.3.source_ref
  277.3 11.5 %all-gather.1 = f32[4,128,256]{2,1,0:T(8,128)} all-gather(f32[4,16,256]{2,1,0:T(8,128)S(1)} %bitcast.51), channel_id=3, replica_groups=mesh['wide'=8,'narrow'=4] {'wide'}, dimensions={1}, use_global_device_ids=true | all-gather | bytes 589824 | tf_op jit(solution)/shard_map/all_gather | solution.py:488
  288.9 0.5 copy-done.10
  289.6 3.4 %last.1 = f32[256,512]{1,0:T(8,128)} custom-call(s32[4]{0:T(128)} %pad_add_fusion.3.source_ref, f32[512,256]{1,0:T(8,128)} %bitcast.52, f32[512,256]{1,0:T(8,128)} %bitcast.45, f32[128,256]{1,0:T(8,128)} %get-tuple-element.47.refs_0_, f32[128,256]{1,0:T(8,128)} %copy-done.11, f32[128,256]{1,0:T(8,128)} %copy-done.10, f32[128,256]{1,0:T(8,128)} %copy-done.9, ...), custom_call_target="tpu_custom_call" | custom-call | flops 1024 | bytes 1024 | tf_op jit(solution)/shard_map/last/pallas_call | solution.py:392
  (66 shorter events, 1.8 us)
Async XLA Ops:
  7.2 110.6 %copy-start = (f32[256,256]{1,0:T(8,128)S(1)}, f32[256,256]{1,0:T(8,128)}, u32[]{:S(2)}) copy-start(f32[256,256]{1,0:T(8,128)} %param.6) | copy-start | bytes 786436
  7.2 82.3 %reduce-scatter.3.cloned.1.call-start = ((), (), s32[]{:S(2)}) async-start(), calls=%async_computation.2 | async-start | bytes 147456 | tf_op jit(solution)/shard_map/reduce_scatter | solution.py:483
  10.9 77.2 %collective-permute-start.1 = (f32[4000,128]{1,0:T(8,128)}, f32[4000,128]{1,0:T(8,128)S(1)}, u32[]{:S(2)}, u32[]{:S(2)}) collective-permute-start(f32[4000,128]{1,0:T(8,128)} %slice_multiply_fusion.refs_0_), channel_id=1, source_target_pairs={{0,1},{1,2},{2,3},{4,5},{5,6},{6,7},{8,9},{9,10},{10,11},{12,13},{... | collective-permute-start | bytes 6144008 | tf_op jit(solution)/shard_map/ppermute | solution.py:425
  16.0 72.1 %collective-permute-start = (f32[4000,128]{1,0:T(8,128)}, f32[4000,128]{1,0:T(8,128)}, u32[]{:S(2)}, u32[]{:S(2)}) collective-permute-start(f32[4000,128]{1,0:T(8,128)} %slice_multiply_fusion.refs_0_), channel_id=1, source_target_pairs={{1,0},{2,1},{3,2},{5,4},{6,5},{7,6},{9,8},{10,9},{11,10},{13,12},{... | collective-permute-start | bytes 6144008 | tf_op jit(solution)/shard_map/ppermute | solution.py:425
  22.0 266.8 %reduce-scatter.5.cloned.1.call-start = ((), (), s32[]{:S(2)}) async-start(), calls=%async_computation.3 | async-start | bytes 4718592 | tf_op jit(solution)/shard_map/reduce_scatter | solution.py:512
  88.1 1.3 copy-start.3
  89.4 2.9 copy-start.7
  89.5 2.9 collective-permute-start.2
  93.2 24.6 %collective-permute-start.3 = (f32[256,256]{1,0:T(8,128)S(1)}, f32[256,256]{1,0:T(8,128)S(1)}, u32[]{:S(2)}, u32[]{:S(2)}) collective-permute-start(f32[256,256]{1,0:T(8,128)S(1)} %get-tuple-element.36), channel_id=1, source_target_pairs={{0,8},{4,12},{8,0},{12,4},{16,24},{20,28},{24,16},{28,20},{1,9},{5... | collective-permute-start | bytes 786440 | tf_op jit(solution)/shard_map/ppermute | solution.py:451
  94.7 23.1 %collective-permute-start.5 = (f32[256,256]{1,0:T(8,128)S(1)}, f32[256,256]{1,0:T(8,128)}, u32[]{:S(2)}, u32[]{:S(2)}) collective-permute-start(f32[256,256]{1,0:T(8,128)S(1)} %get-tuple-element.37), channel_id=1, source_target_pairs={{0,24},{4,28},{8,16},{12,20},{16,8},{20,12},{24,0},{28,4},{1,25},{... | collective-permute-start | bytes 786440 | tf_op jit(solution)/shard_map/ppermute | solution.py:451
  96.1 21.6 %collective-permute-start.4 = (f32[256,256]{1,0:T(8,128)S(1)}, f32[256,256]{1,0:T(8,128)}, u32[]{:S(2)}, u32[]{:S(2)}) collective-permute-start(f32[256,256]{1,0:T(8,128)S(1)} %get-tuple-element.38), channel_id=1, source_target_pairs={{0,16},{4,20},{8,24},{12,28},{16,0},{20,4},{24,8},{28,12},{1,17},{... | collective-permute-start | bytes 786440 | tf_op jit(solution)/shard_map/ppermute | solution.py:451
  117.7 5.3 %copy-start.15 = (f32[16,256]{1,0:T(8,128)S(1)}, f32[16,256]{1,0:T(8,128)}, u32[]{:S(2)}) copy-start(f32[16,256]{1,0:T(8,128)} %reduce-scatter.3.cloned.1.call-done.refs_2_) | copy-start | bytes 49156
  117.7 22.8 %copy-start.4 = (f32[4000,128]{1,0:T(8,128)S(1)}, f32[4000,128]{1,0:T(8,128)}, u32[]{:S(2)}) copy-start(f32[4000,128]{1,0:T(8,128)} %get-tuple-element.25.refs_4_.refs_1_.refs_8_) | copy-start | bytes 6144004
  119.5 23.2 %collective-permute-start.7 = (f32[256,256]{1,0:T(8,128)S(1)}, f32[256,256]{1,0:T(8,128)S(1)}, u32[]{:S(2)}, u32[]{:S(2)}) collective-permute-start(f32[256,256]{1,0:T(8,128)S(1)} %bitcast.46), channel_id=1, source_target_pairs={{0,16},{4,20},{8,24},{12,28},{16,0},{20,4},{24,8},{28,12},{1,17},{... | collective-permute-start | bytes 786440 | tf_op jit(solution)/shard_map/ppermute | solution.py:451
  121.1 21.6 %collective-permute-start.6 = (f32[256,256]{1,0:T(8,128)S(1)}, f32[256,256]{1,0:T(8,128)S(1)}, u32[]{:S(2)}, u32[]{:S(2)}) collective-permute-start(f32[256,256]{1,0:T(8,128)S(1)} %bitcast.47), channel_id=1, source_target_pairs={{0,8},{4,12},{8,0},{12,4},{16,24},{20,28},{24,16},{28,20},{1,9},{5... | collective-permute-start | bytes 786440 | tf_op jit(solution)/shard_map/ppermute | solution.py:451
  122.6 20.1 %collective-permute-start.8 = (f32[256,256]{1,0:T(8,128)S(1)}, f32[256,256]{1,0:T(8,128)S(1)}, u32[]{:S(2)}, u32[]{:S(2)}) collective-permute-start(f32[256,256]{1,0:T(8,128)S(1)} %bitcast.48), channel_id=1, source_target_pairs={{0,24},{4,28},{8,16},{12,20},{16,8},{20,12},{24,0},{28,4},{1,25},{... | collective-permute-start | bytes 786440 | tf_op jit(solution)/shard_map/ppermute | solution.py:451
  139.3 44.5 %collective-permute-start.10 = (f32[4000,128]{1,0:T(8,128)}, f32[4000,128]{1,0:T(8,128)}, u32[]{:S(2)}, u32[]{:S(2)}) collective-permute-start(f32[4000,128]{1,0:T(8,128)} %get-tuple-element.24.refs_3_.refs_0_), channel_id=1, source_target_pairs={{1,0},{2,1},{5,4},{6,5},{9,8},{10,9},{13,12},{14,13},{17,16},{18,1... | collective-permute-start | bytes 6144008 | tf_op jit(solution)/shard_map/ppermute | solution.py:425
  140.6 43.2 %collective-permute-start.11 = (f32[4000,128]{1,0:T(8,128)S(1)}, f32[4000,128]{1,0:T(8,128)}, u32[]{:S(2)}, u32[]{:S(2)}) collective-permute-start(f32[4000,128]{1,0:T(8,128)S(1)} %copy-done.4), channel_id=1, source_target_pairs={{1,2},{2,3},{5,6},{6,7},{9,10},{10,11},{13,14},{14,15},{17,18},{18... | collective-permute-start | bytes 6144008 | tf_op jit(solution)/shard_map/ppermute | solution.py:425
  142.7 1.0 copy-start.2
  142.8 2.9 collective-permute-start.9
  183.8 59.6 %collective-permute-start.16 = (f32[4000,128]{1,0:T(8,128)}, f32[4000,128]{1,0:T(8,128)S(1)}, u32[]{:S(2)}, u32[]{:S(2)}) collective-permute-start(f32[4000,128]{1,0:T(8,128)} %get-tuple-element.30.refs_9_.refs_8_), channel_id=1, source_target_pairs={{1,0},{5,4},{9,8},{13,12},{17,16},{21,20},{25,24},{29,28}} | collective-permute-start | bytes 6144008 | tf_op jit(solution)/shard_map/ppermute | solution.py:425
  185.3 58.1 %collective-permute-start.17 = (f32[4000,128]{1,0:T(8,128)}, f32[4000,128]{1,0:T(8,128)}, u32[]{:S(2)}, u32[]{:S(2)}) collective-permute-start(f32[4000,128]{1,0:T(8,128)} %get-tuple-element.31.refs_10_.refs_9_), channel_id=1, source_target_pairs={{2,3},{6,7},{10,11},{14,15},{18,19},{22,23},{26,27},{30,31}} | collective-permute-start | bytes 6144008 | tf_op jit(solution)/shard_map/ppermute | solution.py:425
  211.8 55.2 %collective-permute-start.12 = (f32[4,128,256]{2,1,0:T(8,128)}, f32[4,128,256]{2,1,0:T(8,128)S(1)}, u32[]{:S(2)}, u32[]{:S(2)}) collective-permute-start(f32[4,128,256]{2,1,0:T(8,128)} %get-tuple-element.33), channel_id=1, source_target_pairs={{0,4},{4,0},{8,12},{12,8},{16,20},{20,16},{24,28},{28,24},{1,5},{5... | collective-permute-start | bytes 1572872 | tf_op jit(solution)/shard_map/ppermute | solution.py:451
  243.4 23.6 %copy-start.5 = (f32[4,128,256]{2,1,0:T(8,128)S(1)}, f32[4,128,256]{2,1,0:T(8,128)}, u32[]{:S(2)}) copy-start(f32[4,128,256]{2,1,0:T(8,128)} %get-tuple-element.32.after_ref) | copy-start | bytes 1572868
  243.4 1.3 copy-start.6
  266.5 10.7 %copy-start.8 = (f32[64,256]{1,0:T(8,128)S(1)}, f32[64,256]{1,0:T(8,128)}, u32[]{:S(2)}) copy-start(f32[64,256]{1,0:T(8,128)} %all-gather) | copy-start | bytes 196612
  266.5 4.7 %collective-permute-start.18 = (f32[4,128,256]{2,1,0:T(8,128)}, f32[4,128,256]{2,1,0:T(8,128)S(1)}, u32[]{:S(2)}, u32[]{:S(2)}) collective-permute-start(f32[4,128,256]{2,1,0:T(8,128)} %get-tuple-element.35), channel_id=1, source_target_pairs={{0,4},{4,0},{8,12},{12,8},{16,20},{20,16},{24,28},{28,24},{1,5},{5... | collective-permute-start | bytes 1572872 | tf_op jit(solution)/shard_map/ppermute | solution.py:451
  267.8 8.1 %collective-permute-start.15 = (f32[128,256]{1,0:T(8,128)S(1)}, f32[128,256]{1,0:T(8,128)S(1)}, u32[]{:S(2)}, u32[]{:S(2)}) collective-permute-start(f32[128,256]{1,0:T(8,128)S(1)} %get-tuple-element.44), channel_id=1, source_target_pairs={{0,24},{4,28},{8,16},{12,20},{16,8},{20,12},{24,0},{28,4},{1,25},{... | collective-permute-start | bytes 393224 | tf_op jit(solution)/shard_map/ppermute | solution.py:451
  270.2 18.6 %collective-permute-start.14 = (f32[128,256]{1,0:T(8,128)S(1)}, f32[128,256]{1,0:T(8,128)S(1)}, u32[]{:S(2)}, u32[]{:S(2)}) collective-permute-start(f32[128,256]{1,0:T(8,128)S(1)} %get-tuple-element.45), channel_id=1, source_target_pairs={{0,16},{4,20},{8,24},{12,28},{16,0},{20,4},{24,8},{28,12},{1,17},{... | collective-permute-start | bytes 393224 | tf_op jit(solution)/shard_map/ppermute | solution.py:451
  270.6 18.2 %collective-permute-start.13 = (f32[128,256]{1,0:T(8,128)S(1)}, f32[128,256]{1,0:T(8,128)S(1)}, u32[]{:S(2)}, u32[]{:S(2)}) collective-permute-start(f32[128,256]{1,0:T(8,128)S(1)} %get-tuple-element.46), channel_id=1, source_target_pairs={{0,8},{4,12},{8,0},{12,4},{16,24},{20,28},{24,16},{28,20},{1,9},{5... | collective-permute-start | bytes 393224 | tf_op jit(solution)/shard_map/ppermute | solution.py:451
  271.3 21.7 %copy-start.1 = (f32[256,256]{1,0:T(8,128)S(1)}, f32[256,256]{1,0:T(8,128)}, u32[]{:S(2)}) copy-start(f32[256,256]{1,0:T(8,128)} %param.6) | copy-start | bytes 786436
  273.1 15.6 %collective-permute-start.21 = (f32[128,256]{1,0:T(8,128)S(1)}, f32[128,256]{1,0:T(8,128)S(1)}, u32[]{:S(2)}, u32[]{:S(2)}) collective-permute-start(f32[128,256]{1,0:T(8,128)S(1)} %get-tuple-element.40), channel_id=1, source_target_pairs={{0,24},{4,28},{8,16},{12,20},{16,8},{20,12},{24,0},{28,4},{1,25},{... | collective-permute-start | bytes 393224 | tf_op jit(solution)/shard_map/ppermute | solution.py:451
  275.5 13.3 %collective-permute-start.20 = (f32[128,256]{1,0:T(8,128)S(1)}, f32[128,256]{1,0:T(8,128)S(1)}, u32[]{:S(2)}, u32[]{:S(2)}) collective-permute-start(f32[128,256]{1,0:T(8,128)S(1)} %get-tuple-element.41), channel_id=1, source_target_pairs={{0,16},{4,20},{8,24},{12,28},{16,0},{20,4},{24,8},{28,12},{1,17},{... | collective-permute-start | bytes 393224 | tf_op jit(solution)/shard_map/ppermute | solution.py:451
  275.9 12.9 %copy-start.9 = (f32[128,256]{1,0:T(8,128)}, f32[128,256]{1,0:T(8,128)S(1)}, u32[]{:S(2)}) copy-start(f32[128,256]{1,0:T(8,128)S(1)} %collective-permute-done.15.refs_3_) | copy-start | bytes 393220
  275.9 12.9 %collective-permute-start.19 = (f32[128,256]{1,0:T(8,128)S(1)}, f32[128,256]{1,0:T(8,128)S(1)}, u32[]{:S(2)}, u32[]{:S(2)}) collective-permute-start(f32[128,256]{1,0:T(8,128)S(1)} %get-tuple-element.42), channel_id=1, source_target_pairs={{0,8},{4,12},{8,0},{12,4},{16,24},{20,28},{24,16},{28,20},{1,9},{5... | collective-permute-start | bytes 393224 | tf_op jit(solution)/shard_map/ppermute | solution.py:451
  288.7 0.7 copy-start.10
  288.7 0.7 copy-start.11
  288.8 0.7 copy-start.12
  288.8 0.8 copy-start.13
  288.8 0.8 copy-start.14
Sparse Core Ops, SparseCore 0:
  22.1 36.9 reduce-scatter.2
  154.4 56.1 reduce-scatter.4

commit v2 on v0

v2 whole, which is shorter than its diff:
```python
import functools

import jax
import jax.numpy as jnp
from jax import lax
from jax.experimental import pallas as pl
from jax.experimental.pallas import tpu as pltpu
from jax.sharding import PartitionSpec as P

FB = 512
OFF = 256
CHUNKS = 1
VMEM = 56 * 1024 * 1024

F32 = jnp.float32
BF16 = jnp.bfloat16
LONG = pl.CostEstimate(flops=10**11, bytes_accessed=1024, transcendentals=0)
SHORT = pl.CostEstimate(flops=1024, bytes_accessed=1024, transcendentals=0)


def split(x):
    high = x.astype(BF16)
    return high, (x - high.astype(F32)).astype(BF16)


def mul(left, right):
    return jnp.dot(left, right, preferred_element_type=F32)


def three(left, right):
    (lh, ll), (rh, rl) = left, right
    return mul(lh, rh) + mul(ll, rh) + mul(lh, rl)


def stacked(both, high, right):
    rh, rl = right
    m = high.shape[0]
    top = mul(both, rh)
    return top[:m] + top[m:] + mul(high, rl)


def params():
    return pltpu.CompilerParams(
        dimension_semantics=("arbitrary",), vmem_limit_bytes=VMEM
    )


def width(columns, wide):
    return 256 if columns % 256 == 0 and 256 % (columns // wide) == 0 else columns // wide


def whole(shape):
    return pl.BlockSpec(shape, lambda j, *_: (0,) * len(shape), pipeline_mode=pl.Buffered(1))


ANY = pl.BlockSpec(memory_space=pl.ANY)


def gate_kernel(*refs):
    del refs


def gate(held, *others, cost=SHORT):
    count = len(held)
    return pl.pallas_call(
        gate_kernel,
        in_specs=[ANY] * (count + len(others)),
        out_specs=[ANY] * count,
        out_shape=[jax.ShapeDtypeStruct(x.shape, x.dtype) for x in held],
        input_output_aliases={k: k for k in range(count)},
        cost_estimate=cost,
        name="gate",
    )(*held, *others)


def place(value, index, even_ref, odd_ref):
    half = index // 2

    @pl.when(index % 2 == 0)
    def _():
        even_ref[half] = value

    @pl.when(index % 2 == 1)
    def _():
        odd_ref[half] = value


def take(index, even_ref, odd_ref):
    half = index // 2
    return jnp.where(index % 2 == 0, even_ref[half], odd_ref[half])


def first_kernel(per, me_ref, v_ref, r_ref, e_ref, x_ref, even_ref, odd_ref, out_ref, small_ref, both_ref):
    j = pl.program_id(0)
    nb = r_ref.shape[1]
    m = both_ref.shape[0] // 2

    @pl.when(j == 0)
    def _():
        turned = r_ref[...].T
        parts = [turned, turned * e_ref[...], x_ref[...].T]
        first = 0
        for part in parts:
            size = part.shape[0]
            both_ref[first : first + size], both_ref[m + first : m + first + size] = split(part)
            first += size
        small_ref[...] = three((both_ref[nb:m], both_ref[m + nb :]), split(r_ref[...]))

    value = stacked(both_ref[...], both_ref[:m], split(v_ref[...]))
    step = v_ref.shape[1]
    for g in range(step // per):
        w = j * (step // per) + g
        part = value[:, g * per : (g + 1) * per]
        place(part[:nb], w ^ me_ref[0], even_ref, odd_ref)
        out_ref[g] = part[nb:]


def first_pass(me, vectors, reflectors, e_row, block, wide):
    rows, columns = vectors.shape
    nb = reflectors.shape[1]
    per = columns // wide
    step = width(columns, wide)
    k = nb + block.shape[1]
    half = jax.ShapeDtypeStruct((wide // 2, nb, per), F32)
    return pl.pallas_call(
        functools.partial(first_kernel, per),
        grid_spec=pltpu.PrefetchScalarGridSpec(
            num_scalar_prefetch=1,
            grid=(columns // step,),
            in_specs=[
                pl.BlockSpec((rows, step), lambda j, *_: (0, j)),
                whole((rows, nb)),
                whole((1, rows)),
                whole(block.shape),
            ],
            out_specs=[
                whole(half.shape),
                whole(half.shape),
                pl.BlockSpec((step // per, k, per), lambda j, *_: (j, 0, 0)),
                whole((k, nb)),
            ],
            scratch_shapes=[pltpu.VMEM((2 * (nb + k), rows), BF16)],
        ),
        out_shape=[
            half,
            half,
            jax.ShapeDtypeStruct((wide, k, per), F32),
            jax.ShapeDtypeStruct((k, nb), F32),
        ],
        compiler_params=params(),
        cost_estimate=SHORT,
        name="first_pass",
    )(me, vectors, reflectors, e_row, block)


def update_kernel(per, offset, me_ref, v_ref, r_ref, even_ref, odd_ref, *refs):
    out_ref, token_ref, left_ref = refs[-3:]
    j = pl.program_id(0)
    nb = r_ref.shape[1]

    @pl.when(j == 0)
    def _():
        token_ref[...] = jnp.zeros_like(token_ref)
        high, low = split(r_ref[...])
        left_ref[:, :nb] = high
        left_ref[:, nb : 2 * nb] = low
        left_ref[:, 2 * nb :] = high

    count = v_ref.shape[1] // per
    blocks = [take(((j + offset) * count + g) ^ me_ref[0], even_ref, odd_ref) for g in range(count)]
    high, low = split(blocks[0] if count == 1 else jnp.concatenate(blocks, axis=1))
    right = jnp.concatenate([high, high, low], axis=0)
    out_ref[...] = v_ref[...] - mul(left_ref[...], right)


def update(me, vectors, reflectors, even, odd, wide, offset, blocks, after, before):
    rows, columns = vectors.shape
    nb = reflectors.shape[1]
    per = columns // wide
    step = width(columns, wide)
    operands = [me, vectors, reflectors, even, odd, *after]
    aliases = {}
    if before is not None:
        aliases = {len(operands): 0}
        operands.append(before)
    columns_of = pl.BlockSpec((rows, step), lambda j, *_: (0, j + offset))
    return pl.pallas_call(
        functools.partial(update_kernel, per, offset),
        grid_spec=pltpu.PrefetchScalarGridSpec(
            num_scalar_prefetch=1,
            grid=(blocks,),
            in_specs=[columns_of, whole((rows, nb)), whole(even.shape), whole(odd.shape)]
            + [ANY] * (len(operands) - 5),
            out_specs=[columns_of, whole((8, 128))],
            scratch_shapes=[pltpu.VMEM((rows, 3 * nb), BF16)],
        ),
        out_shape=[
            jax.ShapeDtypeStruct(vectors.shape, F32),
            jax.ShapeDtypeStruct((8, 128), F32),
        ],
        input_output_aliases=aliases,
        compiler_params=params(),
        cost_estimate=SHORT,
        name="update",
    )(*operands)


def gather(choice, groups, block_ref):
    first = 0
    for group in groups:
        rows = group[0].shape[0]
        for k, ref in enumerate(group):

            @pl.when(choice == k)
            def _(ref=ref, first=first, rows=rows):
                pltpu.sync_copy(ref, block_ref.at[pl.ds(first, rows)])

        first += rows


def regroup(refs, groups):
    refs = list(refs)
    return [[refs.pop(0) for _ in range(count)] for count in groups]


def late_kernel(per, slots, me_ref, v_ref, r_ref, even_ref, odd_ref, after_ref, *refs):
    *refs, even_out, odd_out, both_ref, small_ref, block_ref = refs
    j = pl.program_id(0)
    m = both_ref.shape[0] // 2
    each = block_ref.shape[1]

    @pl.when(j == 0)
    def _():
        left = list(refs)
        for s, groups in enumerate(slots):
            used = sum(groups)
            gather(me_ref[1 + s], regroup(left[:used], groups), block_ref)
            left = left[used:]
            high, low = split(block_ref[...].T)
            both_ref[s * each : (s + 1) * each] = high
            both_ref[m + s * each : m + (s + 1) * each] = low
        small_ref[...] = stacked(both_ref[...], both_ref[:m], split(r_ref[...]))

    value = stacked(both_ref[...], both_ref[:m], split(v_ref[...]))
    small = split(small_ref[...])
    count = v_ref.shape[1] // per
    for g in range(count):
        index = (j * count + g) ^ me_ref[0]
        c = split(take(index, even_ref, odd_ref))
        place(value[:, g * per : (g + 1) * per] - three(small, c), index, even_out, odd_out)


def late(me, vectors, reflectors, slots, even, odd, after, wide):
    rows, columns = vectors.shape
    nb = reflectors.shape[1]
    per = columns // wide
    step = width(columns, wide)
    flat = [x for groups, _ in slots for group in groups for x in group]
    counts = [[len(group) for group in groups] for groups, _ in slots]
    each = flat[0].shape[1]
    m = each * len(slots)
    which = jnp.stack([me[0]] + [choice.astype(jnp.int32) for _, choice in slots])
    half = jax.ShapeDtypeStruct((wide // 2, m, per), F32)
    return pl.pallas_call(
        functools.partial(late_kernel, per, counts),
        grid_spec=pltpu.PrefetchScalarGridSpec(
            num_scalar_prefetch=1,
            grid=(columns // step,),
            in_specs=[
                pl.BlockSpec((rows, step), lambda j, *_: (0, j)),
                whole((rows, nb)),
                whole(even.shape),
                whole(odd.shape),
                ANY,
            ]
            + [ANY] * len(flat),
            out_specs=[whole(half.shape)] * 2,
            scratch_shapes=[
                pltpu.VMEM((2 * m, rows), BF16),
                pltpu.VMEM((m, nb), F32),
                pltpu.VMEM((rows, each), F32),
            ],
        ),
        out_shape=[half, half],
        compiler_params=params(),
        cost_estimate=SHORT,
        name="late",
    )(which, vectors, reflectors, even, odd, after, *flat)


def share_kernel(rows, me_ref, even_ref, odd_ref, out_ref, all_ref):
    per = even_ref.shape[2]
    block = take((OFF // per) ^ me_ref[0], even_ref, odd_ref)
    first = OFF % per
    all_ref[...] = block[:, first : first + all_ref.shape[0]].T
    start = pl.multiple_of((me_ref[0] % (all_ref.shape[0] // rows)) * rows, rows)
    out_ref[...] = all_ref[pl.ds(start, rows), :]


def share(me, even, odd, block_width, rows):
    nb = even.shape[1]
    return pl.pallas_call(
        functools.partial(share_kernel, rows),
        grid_spec=pltpu.PrefetchScalarGridSpec(
            num_scalar_prefetch=1,
            grid=(1,),
            in_specs=[whole(even.shape), whole(odd.shape)],
            out_specs=whole((rows, nb)),
            scratch_shapes=[pltpu.VMEM((block_width, nb), F32)],
        ),
        out_shape=jax.ShapeDtypeStruct((rows, nb), F32),
        compiler_params=params(),
        cost_estimate=SHORT,
        name="share",
    )(me, even, odd)


def base_kernel(n, each, terms, at_ref, ready_ref, small_ref, c_ref, ce_ref, co_ref, *refs):
    *refs, out_ref, coef_ref = refs
    me, z = at_ref[0], at_ref[1]
    nb = c_ref.shape[0]
    half, _, rows, _ = ce_ref.shape
    for h in range(half):
        for p, ref in enumerate((ce_ref, co_ref)):
            owner = (me ^ (2 * h + p)) % (2 * half)
            for s in range(n):
                home = (z + n - s) % n
                first = pl.multiple_of(home * each + owner * rows, rows)
                coef_ref[pl.ds(first, rows), :] = ref[h, s]
    corrected = ready_ref[...] - three(split(small_ref[...]), split(c_ref[...]))
    out_ref[...] = -three(split(coef_ref[...]), split(corrected[:nb]))
    pieces = [corrected[nb:]]
    if terms:
        total = functools.reduce(jnp.add, [ref[...] for ref in refs])
        pieces += [total[k * each : (k + 1) * each] for k in range(total.shape[0] // each)]
    for slot, piece in enumerate(pieces):
        first = pl.multiple_of(at_ref[2 + slot] * each, each)
        out_ref[pl.ds(first, each), :] += piece


def base(at, ready, small, c, ce, co, terms, n, each):
    operands = [ready, small, c, ce, co, *terms]
    per = ready.shape[1]
    return pl.pallas_call(
        functools.partial(base_kernel, n, each, len(terms)),
        grid_spec=pltpu.PrefetchScalarGridSpec(
            num_scalar_prefetch=1,
            grid=(1,),
            in_specs=[whole(x.shape) for x in operands],
            out_specs=whole((FB, per)),
            scratch_shapes=[pltpu.VMEM((FB, c.shape[0]), F32)],
        ),
        out_shape=jax.ShapeDtypeStruct((FB, per), F32),
        compiler_params=params(),
        cost_estimate=SHORT,
        name="base",
    )(at, *operands)


def last_kernel(n, at_ref, base_ref, *refs):
    *refs, out_ref, total_ref = refs
    total = functools.reduce(jnp.add, [ref[...] for ref in refs])
    each = total.shape[0]
    first = pl.multiple_of(at_ref[1 + n] * each, each)
    total_ref[...] = base_ref[...]
    total_ref[pl.ds(first, each), :] += total
    out_ref[...] = total_ref[...].T


def last(at, held, terms, n):
    per = held.shape[1]
    operands = [held, *terms]
    return pl.pallas_call(
        functools.partial(last_kernel, n),
        grid_spec=pltpu.PrefetchScalarGridSpec(
            num_scalar_prefetch=1,
            grid=(1,),
            in_specs=[whole(x.shape) for x in operands],
            out_specs=whole((per, FB)),
            scratch_shapes=[pltpu.VMEM((FB, per), F32)],
        ),
        out_shape=jax.ShapeDtypeStruct((per, FB), F32),
        compiler_params=params(),
        cost_estimate=SHORT,
        name="last",
    )(at, *operands)


def arrivals(n):
    order = []
    for z in range(n):
        found = [(hops, 0) for hops in range(1, n) if z + hops < n]
        found += [(hops, 1) for hops in range(1, n) if z - hops >= 0]
        order.append(sorted(found))
    return [[order[z][slot] for z in range(n)] for slot in range(n - 1)]


def hop(held, n, hops, after):
    if after:
        count = len(held[0])
        both = gate(held[0] + held[1], *after, cost=LONG)
        held = [both[:count], both[count:]]
    pairs = [
        [(p, p - 1) for p in range(1, n - hops + 1)],
        [(p, p + 1) for p in range(hops - 1, n - 1)],
    ]
    return held, [[lax.ppermute(x, "narrow", pairs[d]) for x in held[d]] for d in (0, 1)]


def options(came, places, z):
    choices = sorted(set(places))
    which = jnp.int32(0)
    for p, place in enumerate(places):
        which = jnp.where(z == p, choices.index(place), which)
    return [[came[choice][c] for choice in choices] for c in range(CHUNKS)], which


def source(places, z):
    value = jnp.int32(0)
    for p, (hops, direction) in enumerate(places):
        value = jnp.where(z == p, p - hops if direction else p + hops, value)
    return value


def swap(x, wide, distance):
    return lax.ppermute(x, "wide", [(i, i ^ distance) for i in range(wide)])


def scatter_terms(even, odd, wide):
    other = swap(odd, wide, 1)
    sums = [even[h] + other[h] for h in range(wide // 2)]
    return [sums[0]] + [swap(sums[h], wide, 2 * h) for h in range(1, wide // 2)]


def collect(x, count):
    even = jnp.stack([x] + [swap(x, lax.axis_size("wide"), 2 * h) for h in range(1, count // 2)])
    return even, swap(even, lax.axis_size("wide"), 1)


def on_device(vectors, reflectors, triangle, energies):
    n = lax.axis_size("narrow")
    wide = lax.axis_size("wide")
    z = lax.axis_index("narrow").astype(jnp.int32)
    me = lax.axis_index("wide").astype(jnp.int32).reshape(1)
    each = FB // n
    rows, columns = vectors.shape
    step = rows // CHUNKS
    e_row = energies.reshape(1, rows)

    chunks = [
        energies[c * step : (c + 1) * step, None]
        * vectors[c * step : (c + 1) * step, OFF : OFF + each]
        for c in range(CHUNKS)
    ]
    came = {}

    def travel(held, hops, after):
        held, passed = hop(held, n, hops, after)
        for d in (0, 1):
            if hops > 1:
                came[(hops - 1, d)] = held[d]
            came[(hops, d)] = passed[d]
        return passed

    held = travel([chunks, chunks], 1, [])
    table = arrivals(n)
    at = jnp.stack([me[0], z, z] + [source(places, z) for places in table])

    own = chunks[0] if CHUNKS == 1 else jnp.concatenate(chunks, axis=0)
    even, odd, sums, small = first_pass(me, vectors, reflectors, e_row, own, wide)
    if n > 2:
        held = travel(held, 2, [small])
    ready = lax.psum_scatter(sums, "wide", scatter_dimension=0)
    small = lax.psum(small, "wide")

    terms = scatter_terms(even, odd, wide)
    projected = functools.reduce(jnp.add, terms)
    coefficients = jnp.dot(triangle, projected, precision=lax.Precision.HIGHEST)
    c_even, c_odd = collect(coefficients, wide)

    sharers = wide
    while (each // sharers) % 8:
        sharers //= 2
    mine = share(me, c_even, c_odd, each, each // sharers)
    shares = [mine] + [
        lax.ppermute(mine, "narrow", [(p, (p + s) % n) for p in range(n)]) for s in range(1, n)
    ]
    blocks = columns // width(columns, wide)
    updated, token = update(
        me, vectors, reflectors, c_even, c_odd, wide, 0, blocks // 2, [mine], None
    )
    for hops in range(3, n):
        held = travel(held, hops, [token])
    updated, token = update(
        me, vectors, reflectors, c_even, c_odd, wide, blocks // 2, blocks - blocks // 2,
        [x for d in (0, 1) for x in came[(n - 2, d)]] if n > 2 else [mine], updated,
    )
    share_even, share_odd = collect(jnp.stack(shares), sharers)

    middle = []
    if n > 2:
        slots = [options(came, table[slot], z) for slot in range(n - 2)]
        halves = late(me, vectors, reflectors, slots, c_even, c_odd, token, wide)
        middle = scatter_terms(*halves, wide)
    (token,) = gate([token], share_even, share_odd, *middle[:1])
    halves = late(
        me, vectors, reflectors, [options(came, table[n - 2], z)], c_even, c_odd, token, wide
    )
    held = base(at, ready, small, coefficients, share_even, share_odd, middle, n, each)
    fock_block = last(at, held, scatter_terms(*halves, wide), n)
    return (updated, fock_block)


def solution(mesh):
    return jax.shard_map(
        on_device,
        mesh=mesh,
        in_specs=(P("wide", "narrow"), P("wide", None), P(), P("wide")),
        out_specs=(P("wide", "narrow"), P(("narrow", "wide"), None)),
        check_vma=False,
    )
```

time: 322 us -> 252 us (0.78)
  matrix products: 144 us -> 0.44 us
  Pallas kernels: 0 us -> 138 us
  waiting for transfers between devices: 131 us -> 41.3 us
  starting transfers between devices: 0.12 us -> 43.7 us
  blocking collectives: 28.3 us -> 0 us
  other arithmetic: 0 us -> 8.19 us
    dot_general x5 -> x1, matrix products: 144 us -> 0.44 us  [on_device(): coefficients = jnp.dot(triangle, projected, precision=lax.Precision.HIGHEST)]
    pallas_call x0 -> x11, Pallas kernels: none -> 138 us  [the longest x2 50.6 us: late(): pl.pallas_call(functools.partial(late_kernel, per, counts), grid_spec=plt...]
    psum x1, waiting for transfers between devices: 61.1 us -> 0.01 us  [on_device(): small = lax.psum(small, 'wide')]
    reduce_scatter x1, waiting for transfers between devices: 49.7 us -> 0.01 us  [on_device(): ready = lax.psum_scatter(sums, 'wide', scatter_dimension=0)]
    ppermute x0 -> x29, starting transfers between devices: none -> 43.6 us  [the longest x20 18.6 us: swap(): return lax.ppermute(x, 'wide', [(i, i ^ distance) for i in range(wide)])]
    ppermute x0 -> x29, waiting for transfers between devices: none -> 41.3 us  [the longest x20 34.5 us: swap(): return lax.ppermute(x, 'wide', [(i, i ^ distance) for i in range(wide)])]
    all_gather x1 -> x0, blocking collectives: 28.3 us -> none  [on_device(): lax.all_gather(coefficients[:, OFF:OFF + block_width], 'narrow', axis=1,...]
    all_gather x1 -> x0, waiting for transfers between devices: 20.6 us -> none  [on_device(): lax.all_gather(vectors[:, OFF:OFF + block_width], 'narrow', axis=1, tiled...]
  transfers between devices with their start and end apart: 3 -> 31, of which waited for: 3 -> 13; matrix products, arithmetic and copies ran while one was open for 15% -> 3% of each run, Pallas kernels for 0% -> 54%
where the time goes in v2:
time: 252 us; the launch traced here: 251 us
  Pallas kernels  138 us (55%)
  starting transfers between devices  43.7 us (17%)
  waiting for transfers between devices  41.3 us (16%)
  between operations  14.3 us (6%)
  other arithmetic  8.19 us (3%)
  local copies, waits for them, and re-layouts  5.13 us (2%)
    pallas_call x2, Pallas kernels, late(): pl.pallas_call(functools.partial(late_kernel, per, counts), grid_spec=plt...  50.6 us
    pallas_call x1, Pallas kernels, first_pass(): pl.pallas_call(functools.partial(first_kernel, per), grid_spec=pltpu.Pref...  43.7 us
    ppermute x20, waiting for transfers between devices, swap(): return lax.ppermute(x, 'wide', [(i, i ^ distance) for i in range(wide)])  34.5 us
    pallas_call x2, Pallas kernels, update(): pl.pallas_call(functools.partial(update_kernel, per, offset), grid_spec=p...  34.3 us
    ppermute x20, starting transfers between devices, swap(): return lax.ppermute(x, 'wide', [(i, i ^ distance) for i in range(wide)])  18.6 us
    ppermute x6, starting transfers between devices, hop(): lax.ppermute(x, 'narrow', pairs[d])  14.5 us
    ppermute x3, starting transfers between devices, on_device(): lax.ppermute(mine, 'narrow', [(p, (p + s) % n) for p in range(n)])  10.6 us
  transfers between devices with their start and end apart: 31, of which 13 were waited for; matrix products, arithmetic and copies ran while one was open for 3% of the time, Pallas kernels for 54%

profile of v2, /device:TPU:0, one launch (start us, length us, event | category | flops | bytes accessed | tf_op | source)
XLA Modules:
  0.0 250.9 jit_solution(2523554676323421802)
XLA Ops:
  7.2 2.8 %slice_multiply_fusion.x_ref = f32[4000,128]{1,0:T(8,128)S(1)} fusion(f32[4000,2048]{1,0:T(8,128)} %v_ref.9, f32[4000]{0:T(1024)} %param.7), kind=kLoop, calls=%fused_computation | loop fusion | flops 512000 | bytes 4112000 | tf_op jit(solution)/shard_map/mul | solution.py:451
  10.0 6.3 %collective-permute-start.9 = (f32[4000,128]{1,0:T(8,128)S(1)}, f32[4000,128]{1,0:T(8,128)}, u32[]{:S(2)}, u32[]{:S(2)}) collective-permute-start(f32[4000,128]{1,0:T(8,128)S(1)} %slice_multiply_fusion.x_ref), channel_id=1, source_target_pairs={{0,1},{1,2},{2,3},{4,5},{5,6},{6,7},{8,9},{9,10},{10,11},{12,13},{... | collective-permute-start | bytes 6144008 | tf_op jit(solution)/shard_map/ppermute | solution.py:407
  16.2 1.3 collective-permute-start.8
  17.5 43.7 %first_pass.1 = (f32[4,256,256]{2,1,0:T(8,128)}, f32[4,256,256]{2,1,0:T(8,128)}, f32[8,384,256]{2,1,0:T(8,128)}, f32[384,256]{1,0:T(8,128)}) custom-call(s32[1]{0:T(128)} %bitcast.me_ref, f32[4000,2048]{1,0:T(8,128)} %v_ref.9, f32[4000,256]{1,0:T(8,128)} %r_ref.9, f32[1,4000]{1,0:T(1,128)} %bitcast.67, f32[4000,128]{1,0:T(8,128)} %copy-done.4), custom_call_target="tpu_custom_call" | custom-call | flops 1024 | bytes 1024 | tf_op jit(solution)/shard_map/first_pass/pallas_call | solution.py:125
  61.2 3.0 %collective-permute-done.8.refs_0_ = f32[4000,128]{1,0:T(8,128)} collective-permute-done((f32[4000,128]{1,0:T(8,128)S(1)}, f32[4000,128]{1,0:T(8,128)}, u32[]{:S(2)}, u32[]{:S(2)}) %collective-permute-start.8) | collective-permute-done | bytes 2048032 | tf_op jit(solution)/shard_map/ppermute | solution.py:407
  64.3 1.4 collective-permute-start.10
  65.7 2.1 collective-permute-start.11
  67.9 1.6 collective-permute-start.1
  69.4 1.5 collective-permute-start.3
  71.4 5.8 %collective-permute-done.1 = f32[256,256]{1,0:T(8,128)S(1)} collective-permute-done((f32[256,256]{1,0:T(8,128)S(1)}, f32[256,256]{1,0:T(8,128)S(1)}, u32[]{:S(2)}, u32[]{:S(2)}) %collective-permute-start.1) | collective-permute-done | bytes 262176 | tf_op jit(solution)/shard_map/ppermute | solution.py:426
  77.2 4.3 %collective-permute-done.3 = f32[256,256]{1,0:T(8,128)S(1)} collective-permute-done((f32[256,256]{1,0:T(8,128)S(1)}, f32[256,256]{1,0:T(8,128)S(1)}, u32[]{:S(2)}, u32[]{:S(2)}) %collective-permute-start.3) | collective-permute-done | bytes 262176 | tf_op jit(solution)/shard_map/ppermute | solution.py:426
  81.5 1.4 collective-permute-done.2
  83.3 1.5 collective-permute-start.6
  84.8 1.9 collective-permute-start.5
  86.8 4.8 %collective-permute-done.6 = f32[256,256]{1,0:T(8,128)S(1)} collective-permute-done((f32[256,256]{1,0:T(8,128)S(1)}, f32[256,256]{1,0:T(8,128)S(1)}, u32[]{:S(2)}, u32[]{:S(2)}) %collective-permute-start.6) | collective-permute-done | bytes 262176 | tf_op jit(solution)/shard_map/ppermute | solution.py:426
  91.7 2.7 %collective-permute-done.5 = f32[256,256]{1,0:T(8,128)S(1)} collective-permute-done((f32[256,256]{1,0:T(8,128)S(1)}, f32[256,256]{1,0:T(8,128)S(1)}, u32[]{:S(2)}, u32[]{:S(2)}) %collective-permute-start.5) | collective-permute-done | bytes 262176 | tf_op jit(solution)/shard_map/ppermute | solution.py:426
  94.6 2.6 %collective-permute-done.7.odd_ref = f32[4,256,256]{2,1,0:T(8,128)S(1)} collective-permute-done((f32[4,256,256]{2,1,0:T(8,128)S(1)}, f32[4,256,256]{2,1,0:T(8,128)S(1)}, u32[]{:S(2)}, u32[]{:S(2)}) %collective-permute-start.7) | collective-permute-done | bytes 1048608 | tf_op jit(solution)/shard_map/ppermute | solution.py:426
  97.2 1.0 copy-done.3
  98.2 2.2 share.1.refs_0_
  100.5 17.2 %update.2 = (f32[4000,2048]{1,0:T(8,128)}, f32[8,128]{1,0:T(8,128)}) custom-call(s32[1]{0:T(128)} %bitcast.me_ref, f32[4000,2048]{1,0:T(8,128)} %v_ref.9, f32[4000,256]{1,0:T(8,128)} %r_ref.9, f32[4,256,256]{2,1,0:T(8,128)} %copy-done.2, f32[4,256,256]{2,1,0:T(8,128)} %copy-done.3, f32[16,256]{1,0:T(8,128)} %share.1.refs_0_), custom_call_target="tpu_custom_call" | custom-call | flops 1024 | bytes 1024 | tf_op jit(solution)/shard_map/update/pallas_call | solution.py:187
  117.6 1.5 collective-permute-start.23
  119.1 2.0 collective-permute-start.24
  121.7 17.1 %update.3 = (f32[4000,2048]{1,0:T(8,128)}, f32[8,128]{1,0:T(8,128)}) custom-call(s32[1]{0:T(128)} %bitcast.me_ref, f32[4000,2048]{1,0:T(8,128)} %v_ref.9, f32[4000,256]{1,0:T(8,128)} %r_ref.9, f32[4,256,256]{2,1,0:T(8,128)} %copy-done.2, f32[4,256,256]{2,1,0:T(8,128)} %copy-done.3, ...), custom_call_target="tpu_custom_call", output_to_operand_aliasing={{0}: (7, {})} | custom-call | flops 1024 | bytes 1024 | tf_op jit(solution)/shard_map/update/pallas_call | solution.py:187
  138.8 28.9 %late.2 = (f32[4,256,256]{2,1,0:T(8,128)}, f32[4,256,256]{2,1,0:T(8,128)}) custom-call(s32[3]{0:T(128)} %pad_add_fusion.me_ref, f32[4000,2048]{1,0:T(8,128)} %v_ref.9, f32[4000,256]{1,0:T(8,128)} %r_ref.9, f32[4,256,256]{2,1,0:T(8,128)} %copy-done.2, f32[4,256,256]{2,1,0:T(8,128)} %copy-done.3, f32[8,128]{1,0:T(8,128)} %get-tuple-element.29.after_ref.refs_0_, ...), custom_call_target="tpu_custom_call" | custom-call | flops 1024 | bytes 1024 | tf_op jit(solution)/shard_map/late/pallas_call | solution.py:264
  167.9 5.3 %collective-permute-start.14 = (f32[16,256]{1,0:T(8,128)S(1)}, f32[16,256]{1,0:T(8,128)S(1)}, u32[]{:S(2)}, u32[]{:S(2)}) collective-permute-start(f32[16,256]{1,0:T(8,128)S(1)} %copy-done.16), channel_id=1, source_target_pairs={{0,3},{1,0},{2,1},{3,2},{4,7},{5,4},{6,5},{7,6},{8,11},{9,8},{10,9... | collective-permute-start | bytes 49160 | tf_op jit(solution)/shard_map/ppermute | solution.py:486
  173.2 3.3 %collective-permute-start.13 = (f32[16,256]{1,0:T(8,128)S(1)}, f32[16,256]{1,0:T(8,128)S(1)}, u32[]{:S(2)}, u32[]{:S(2)}) collective-permute-start(f32[16,256]{1,0:T(8,128)S(1)} %copy-done.16), channel_id=1, source_target_pairs={{0,2},{1,3},{2,0},{3,1},{4,6},{5,7},{6,4},{7,5},{8,10},{9,11},{10,... | collective-permute-start | bytes 49160 | tf_op jit(solution)/shard_map/ppermute | solution.py:486
  176.7 2.0 collective-permute-start.12
  178.7 3.5 %collective-permute-done.12 = f32[16,256]{1,0:T(8,128)S(1)} collective-permute-done((f32[16,256]{1,0:T(8,128)S(1)}, f32[16,256]{1,0:T(8,128)S(1)}, u32[]{:S(2)}, u32[]{:S(2)}) %collective-permute-start.12) | collective-permute-done | bytes 16416 | tf_op jit(solution)/shard_map/ppermute | solution.py:486
  182.2 0.8 collective-permute-start.16
  183.1 1.5 collective-permute-start.15
  184.5 3.4 %collective-permute-done.16 = f32[4,16,256]{2,1,0:T(8,128)S(1)} collective-permute-done((f32[4,16,256]{2,1,0:T(8,128)S(1)}, f32[4,16,256]{2,1,0:T(8,128)S(1)}, u32[]{:S(2)}, u32[]{:S(2)}) %collective-permute-start.16) | collective-permute-done | bytes 65568 | tf_op jit(solution)/shard_map/ppermute | solution.py:426
  187.9 1.7 collective-permute-start.17
  190.2 2.9 %collective-permute-done.17 = f32[4,16,256]{2,1,0:T(8,128)S(1)} collective-permute-done((f32[4,16,256]{2,1,0:T(8,128)S(1)}, f32[4,16,256]{2,1,0:T(8,128)S(1)}, u32[]{:S(2)}, u32[]{:S(2)}) %collective-permute-start.17) | collective-permute-done | bytes 65568 | tf_op jit(solution)/shard_map/ppermute | solution.py:426
  193.2 2.3 fusion
  195.5 0.7 copy-done.9
  196.2 1.3 copy-done.7
  197.5 21.7 %late.3 = (f32[4,128,256]{2,1,0:T(8,128)}, f32[4,128,256]{2,1,0:T(8,128)}) custom-call(s32[2]{0:T(128)} %pad_add_fusion.1.me_ref, f32[4000,2048]{1,0:T(8,128)} %v_ref.9, f32[4000,256]{1,0:T(8,128)} %r_ref.9, f32[4,256,256]{2,1,0:T(8,128)} %copy-done.2, f32[4,256,256]{2,1,0:T(8,128)} %copy-done.3, f32[8,128]{1,0:T(8,128)} %gate.5.after_ref, ...), custom_call_target="tpu_custom_call" | custom-call | flops 1024 | bytes 1024 | tf_op jit(solution)/shard_map/late/pallas_call | solution.py:264
  219.7 1.7 collective-permute-start.22
  221.4 0.6 collective-permute-start.21
  222.0 1.2 collective-permute-start.20
  223.2 1.8 fusion.14
  225.0 1.7 collective-permute-start.28
  227.3 2.5 collective-permute-done.22.refs_3_
  229.8 0.9 collective-permute-start.26
  231.2 4.2 %collective-permute-done.21.refs_2_ = f32[256,256]{1,0:T(8,128)S(1)} collective-permute-done((f32[256,256]{1,0:T(8,128)S(1)}, f32[256,256]{1,0:T(8,128)S(1)}, u32[]{:S(2)}, u32[]{:S(2)}) %collective-permute-start.21) | collective-permute-done | bytes 262176 | tf_op jit(solution)/shard_map/ppermute | solution.py:426
  235.5 0.7 copy-done.14
  236.2 4.1 %base.1.base_ref = f32[512,256]{1,0:T(8,128)} custom-call(s32[6]{0:T(128)} %stack.85.at_ref, f32[384,256]{1,0:T(8,128)} %bitcast.62, f32[384,256]{1,0:T(8,128)} %all-reduce.2.cloned.1.call-done.small_ref, f32[256,256]{1,0:T(8,128)} %bitcast.61, f32[4,4,16,256]{3,2,1,0:T(8,128)} %copy-done.5, f32[4,4,16,256]{3,2,1,0:T(8,128)} %copy-done.9, ...), custom_call_target="tpu_custom_call" | custom-call | flops 1024 | bytes 1024 | tf_op jit(solution)/shard_map/base/pallas_call | solution.py:344
  241.1 3.0 %last.1 = f32[256,512]{1,0:T(8,128)} custom-call(s32[6]{0:T(128)} %stack.85.at_ref, f32[512,256]{1,0:T(8,128)} %base.1.base_ref, f32[128,256]{1,0:T(8,128)} %get-tuple-element.44.refs_0_, f32[128,256]{1,0:T(8,128)} %copy-done.19, f32[128,256]{1,0:T(8,128)} %copy-done.18, f32[128,256]{1,0:T(8,128)} %copy-done.17), custom_call_target="tpu_custom_call" | custom-call | flops 1024 | bytes 1024 | tf_op jit(solution)/shard_map/last/pallas_call | solution.py:373
  (78 shorter events, 5.7 us)
Async XLA Ops:
  7.2 75.7 %copy-start = (f32[256,256]{1,0:T(8,128)S(1)}, f32[256,256]{1,0:T(8,128)}, u32[]{:S(2)}) copy-start(f32[256,256]{1,0:T(8,128)} %param.6) | copy-start | bytes 786436
  9.9 7.6 %copy-start.4 = (f32[4000,128]{1,0:T(8,128)}, f32[4000,128]{1,0:T(8,128)S(1)}, u32[]{:S(2)}) copy-start(f32[4000,128]{1,0:T(8,128)S(1)} %slice_multiply_fusion.x_ref) | copy-start | bytes 6144004
  10.0 51.3 %collective-permute-start.9 = (f32[4000,128]{1,0:T(8,128)S(1)}, f32[4000,128]{1,0:T(8,128)}, u32[]{:S(2)}, u32[]{:S(2)}) collective-permute-start(f32[4000,128]{1,0:T(8,128)S(1)} %slice_multiply_fusion.x_ref), channel_id=1, source_target_pairs={{0,1},{1,2},{2,3},{4,5},{5,6},{6,7},{8,9},{9,10},{10,11},{12,13},{... | collective-permute-start | bytes 6144008 | tf_op jit(solution)/shard_map/ppermute | solution.py:407
  16.2 48.0 %collective-permute-start.8 = (f32[4000,128]{1,0:T(8,128)S(1)}, f32[4000,128]{1,0:T(8,128)}, u32[]{:S(2)}, u32[]{:S(2)}) collective-permute-start(f32[4000,128]{1,0:T(8,128)S(1)} %slice_multiply_fusion.x_ref), channel_id=1, source_target_pairs={{1,0},{2,1},{3,2},{5,4},{6,5},{7,6},{9,8},{10,9},{11,10},{13,12},{... | collective-permute-start | bytes 6144008 | tf_op jit(solution)/shard_map/ppermute | solution.py:407
  61.2 6.5 %collective-permute-start = (f32[4,256,256]{2,1,0:T(8,128)}, f32[4,256,256]{2,1,0:T(8,128)S(1)}, u32[]{:S(2)}, u32[]{:S(2)}) collective-permute-start(f32[4,256,256]{2,1,0:T(8,128)} %get-tuple-element.19), channel_id=1, source_target_pairs={{0,4},{4,0},{8,12},{12,8},{16,20},{20,16},{24,28},{28,24},{1,5},{5... | collective-permute-start | bytes 3145736 | tf_op jit(solution)/shard_map/ppermute | solution.py:426
  64.3 3.5 %copy-start.8 = (f32[4,256,256]{2,1,0:T(8,128)S(1)}, f32[4,256,256]{2,1,0:T(8,128)}, u32[]{:S(2)}) copy-start(f32[4,256,256]{2,1,0:T(8,128)} %get-tuple-element.18) | copy-start | bytes 3145732
  64.3 167.0 %all-reduce.2.cloned.1.call-start = ((), (), s32[]{:S(2)}) async-start(), calls=%async_computation.2 | async-start | bytes 786432 | tf_op jit(solution)/shard_map/psum | solution.py:474
  64.3 53.3 %collective-permute-start.10 = (f32[4000,128]{1,0:T(8,128)}, f32[4000,128]{1,0:T(8,128)}, u32[]{:S(2)}, u32[]{:S(2)}) collective-permute-start(f32[4000,128]{1,0:T(8,128)} %get-tuple-element.21.refs_0_), channel_id=1, source_target_pairs={{1,0},{2,1},{5,4},{6,5},{9,8},{10,9},{13,12},{14,13},{17,16},{18,1... | collective-permute-start | bytes 6144008 | tf_op jit(solution)/shard_map/ppermute | solution.py:407
  65.7 51.9 %collective-permute-start.11 = (f32[4000,128]{1,0:T(8,128)}, f32[4000,128]{1,0:T(8,128)}, u32[]{:S(2)}, u32[]{:S(2)}) collective-permute-start(f32[4000,128]{1,0:T(8,128)} %get-tuple-element.22.refs_1_.refs_2_), channel_id=1, source_target_pairs={{1,2},{2,3},{5,6},{6,7},{9,10},{10,11},{13,14},{14,15},{17,18},{18... | collective-permute-start | bytes 6144008 | tf_op jit(solution)/shard_map/ppermute | solution.py:407
  67.9 9.3 %collective-permute-start.1 = (f32[256,256]{1,0:T(8,128)S(1)}, f32[256,256]{1,0:T(8,128)S(1)}, u32[]{:S(2)}, u32[]{:S(2)}) collective-permute-start(f32[256,256]{1,0:T(8,128)S(1)} %get-tuple-element.38), channel_id=1, source_target_pairs={{0,8},{4,12},{8,0},{12,4},{16,24},{20,28},{24,16},{28,20},{1,9},{5... | collective-permute-start | bytes 786440 | tf_op jit(solution)/shard_map/ppermute | solution.py:426
  69.4 12.0 %collective-permute-start.3 = (f32[256,256]{1,0:T(8,128)S(1)}, f32[256,256]{1,0:T(8,128)S(1)}, u32[]{:S(2)}, u32[]{:S(2)}) collective-permute-start(f32[256,256]{1,0:T(8,128)S(1)} %get-tuple-element.39), channel_id=1, source_target_pairs={{0,24},{4,28},{8,16},{12,20},{16,8},{20,12},{24,0},{28,4},{1,25},{... | collective-permute-start | bytes 786440 | tf_op jit(solution)/shard_map/ppermute | solution.py:426
  70.9 11.9 %collective-permute-start.2 = (f32[256,256]{1,0:T(8,128)S(1)}, f32[256,256]{1,0:T(8,128)S(1)}, u32[]{:S(2)}, u32[]{:S(2)}) collective-permute-start(f32[256,256]{1,0:T(8,128)S(1)} %get-tuple-element.40), channel_id=1, source_target_pairs={{0,16},{4,20},{8,24},{12,28},{16,0},{20,4},{24,8},{28,12},{1,17},{... | collective-permute-start | bytes 786440 | tf_op jit(solution)/shard_map/ppermute | solution.py:426
  83.3 11.1 %copy-start.6 = (f32[256,256]{0,1:T(8,128)}, f32[256,256]{0,1:T(8,128)S(1)}, u32[]{:S(2)}) copy-start(f32[256,256]{0,1:T(8,128)S(1)} %fusion.11) | copy-start | bytes 786436
  83.3 8.4 %collective-permute-start.6 = (f32[256,256]{1,0:T(8,128)S(1)}, f32[256,256]{1,0:T(8,128)S(1)}, u32[]{:S(2)}, u32[]{:S(2)}) collective-permute-start(f32[256,256]{1,0:T(8,128)S(1)} %bitcast.57), channel_id=1, source_target_pairs={{0,24},{4,28},{8,16},{12,20},{16,8},{20,12},{24,0},{28,4},{1,25},{... | collective-permute-start | bytes 786440 | tf_op jit(solution)/shard_map/ppermute | solution.py:426
  84.8 9.6 %collective-permute-start.5 = (f32[256,256]{1,0:T(8,128)S(1)}, f32[256,256]{1,0:T(8,128)S(1)}, u32[]{:S(2)}, u32[]{:S(2)}) collective-permute-start(f32[256,256]{1,0:T(8,128)S(1)} %bitcast.58), channel_id=1, source_target_pairs={{0,16},{4,20},{8,24},{12,28},{16,0},{20,4},{24,8},{28,12},{1,17},{... | collective-permute-start | bytes 786440 | tf_op jit(solution)/shard_map/ppermute | solution.py:426
  86.7 7.7 %collective-permute-start.4 = (f32[256,256]{1,0:T(8,128)S(1)}, f32[256,256]{1,0:T(8,128)S(1)}, u32[]{:S(2)}, u32[]{:S(2)}) collective-permute-start(f32[256,256]{1,0:T(8,128)S(1)} %bitcast.59), channel_id=1, source_target_pairs={{0,8},{4,12},{8,0},{12,4},{16,24},{20,28},{24,16},{28,20},{1,9},{5... | collective-permute-start | bytes 786440 | tf_op jit(solution)/shard_map/ppermute | solution.py:426
  94.4 2.7 %copy-start.2 = (f32[4,256,256]{2,1,0:T(8,128)}, f32[4,256,256]{2,1,0:T(8,128)S(1)}, u32[]{:S(2)}) copy-start(f32[4,256,256]{2,1,0:T(8,128)S(1)} %pad_maximum_fusion.even_ref) | copy-start | bytes 3145732
  94.4 2.7 %collective-permute-start.7 = (f32[4,256,256]{2,1,0:T(8,128)S(1)}, f32[4,256,256]{2,1,0:T(8,128)S(1)}, u32[]{:S(2)}, u32[]{:S(2)}) collective-permute-start(f32[4,256,256]{2,1,0:T(8,128)S(1)} %pad_maximum_fusion.even_ref), channel_id=1, source_target_pairs={{0,4},{4,0},{8,12},{12,8},{16,20},{20,16},{24,28},{28,24},{1,5},{5... | collective-permute-start | bytes 3145736 | tf_op jit(solution)/shard_map/ppermute | solution.py:426
  94.5 136.7 %reduce-scatter.2.cloned.1.call-start = ((), (), s32[]{:S(2)}) async-start(), calls=%async_computation.1 | async-start | bytes 3538944 | tf_op jit(solution)/shard_map/reduce_scatter | solution.py:473
  97.2 1.0 copy-start.3
  117.6 78.6 %collective-permute-start.23 = (f32[4000,128]{1,0:T(8,128)}, f32[4000,128]{1,0:T(8,128)S(1)}, u32[]{:S(2)}, u32[]{:S(2)}) collective-permute-start(f32[4000,128]{1,0:T(8,128)} %get-tuple-element.24.refs_0_.refs_3_), channel_id=1, source_target_pairs={{1,0},{5,4},{9,8},{13,12},{17,16},{21,20},{25,24},{29,28}} | collective-permute-start | bytes 6144008 | tf_op jit(solution)/shard_map/ppermute | solution.py:407
  119.1 77.1 %collective-permute-start.24 = (f32[4000,128]{1,0:T(8,128)}, f32[4000,128]{1,0:T(8,128)}, u32[]{:S(2)}, u32[]{:S(2)}) collective-permute-start(f32[4000,128]{1,0:T(8,128)} %get-tuple-element.25.refs_1_.refs_4_), channel_id=1, source_target_pairs={{2,3},{6,7},{10,11},{14,15},{18,19},{22,23},{26,27},{30,31}} | collective-permute-start | bytes 6144008 | tf_op jit(solution)/shard_map/ppermute | solution.py:407
  138.8 29.1 %copy-start.16 = (f32[16,256]{1,0:T(8,128)S(1)}, f32[16,256]{1,0:T(8,128)}, u32[]{:S(2)}) copy-start(f32[16,256]{1,0:T(8,128)} %share.1.refs_0_) | copy-start | bytes 49156
  167.7 25.5 %collective-permute-start.19 = (f32[4,256,256]{2,1,0:T(8,128)}, f32[4,256,256]{2,1,0:T(8,128)S(1)}, u32[]{:S(2)}, u32[]{:S(2)}) collective-permute-start(f32[4,256,256]{2,1,0:T(8,128)} %get-tuple-element.31), channel_id=1, source_target_pairs={{0,4},{4,0},{8,12},{12,8},{16,20},{20,16},{24,28},{28,24},{1,5},{5... | collective-permute-start | bytes 3145736 | tf_op jit(solution)/shard_map/ppermute | solution.py:426
  167.9 8.8 %collective-permute-start.14 = (f32[16,256]{1,0:T(8,128)S(1)}, f32[16,256]{1,0:T(8,128)S(1)}, u32[]{:S(2)}, u32[]{:S(2)}) collective-permute-start(f32[16,256]{1,0:T(8,128)S(1)} %copy-done.16), channel_id=1, source_target_pairs={{0,3},{1,0},{2,1},{3,2},{4,7},{5,4},{6,5},{7,6},{8,11},{9,8},{10,9... | collective-permute-start | bytes 49160 | tf_op jit(solution)/shard_map/ppermute | solution.py:486
  173.2 5.5 %collective-permute-start.13 = (f32[16,256]{1,0:T(8,128)S(1)}, f32[16,256]{1,0:T(8,128)S(1)}, u32[]{:S(2)}, u32[]{:S(2)}) collective-permute-start(f32[16,256]{1,0:T(8,128)S(1)} %copy-done.16), channel_id=1, source_target_pairs={{0,2},{1,3},{2,0},{3,1},{4,6},{5,7},{6,4},{7,5},{8,10},{9,11},{10,... | collective-permute-start | bytes 49160 | tf_op jit(solution)/shard_map/ppermute | solution.py:486
  176.7 5.5 %collective-permute-start.12 = (f32[16,256]{1,0:T(8,128)S(1)}, f32[16,256]{1,0:T(8,128)S(1)}, u32[]{:S(2)}, u32[]{:S(2)}) collective-permute-start(f32[16,256]{1,0:T(8,128)S(1)} %copy-done.16), channel_id=1, source_target_pairs={{0,1},{1,2},{2,3},{3,0},{4,5},{5,6},{6,7},{7,4},{8,9},{9,10},{10,1... | collective-permute-start | bytes 49160 | tf_op jit(solution)/shard_map/ppermute | solution.py:486
  182.2 5.7 %collective-permute-start.16 = (f32[4,16,256]{2,1,0:T(8,128)S(1)}, f32[4,16,256]{2,1,0:T(8,128)S(1)}, u32[]{:S(2)}, u32[]{:S(2)}) collective-permute-start(f32[4,16,256]{2,1,0:T(8,128)S(1)} %get-tuple-element.46), channel_id=1, source_target_pairs={{0,16},{4,20},{8,24},{12,28},{16,0},{20,4},{24,8},{28,12},{1,17},{... | collective-permute-start | bytes 196616 | tf_op jit(solution)/shard_map/ppermute | solution.py:426
  183.1 7.1 %collective-permute-start.15 = (f32[4,16,256]{2,1,0:T(8,128)S(1)}, f32[4,16,256]{2,1,0:T(8,128)S(1)}, u32[]{:S(2)}, u32[]{:S(2)}) collective-permute-start(f32[4,16,256]{2,1,0:T(8,128)S(1)} %get-tuple-element.46), channel_id=1, source_target_pairs={{0,8},{4,12},{8,0},{12,4},{16,24},{20,28},{24,16},{28,20},{1,9},{5... | collective-permute-start | bytes 196616 | tf_op jit(solution)/shard_map/ppermute | solution.py:426
  187.9 5.2 %collective-permute-start.17 = (f32[4,16,256]{2,1,0:T(8,128)S(1)}, f32[4,16,256]{2,1,0:T(8,128)S(1)}, u32[]{:S(2)}, u32[]{:S(2)}) collective-permute-start(f32[4,16,256]{2,1,0:T(8,128)S(1)} %get-tuple-element.46), channel_id=1, source_target_pairs={{0,24},{4,28},{8,16},{12,20},{16,8},{20,12},{24,0},{28,4},{1,25},{... | collective-permute-start | bytes 196616 | tf_op jit(solution)/shard_map/ppermute | solution.py:426
  193.1 3.1 %copy-start.5 = (f32[4,4,16,256]{3,2,1,0:T(8,128)}, f32[4,4,16,256]{3,2,1,0:T(8,128)S(1)}, u32[]{:S(2)}) copy-start(f32[4,4,16,256]{3,2,1,0:T(8,128)S(1)} %pad_maximum_fusion.1.ce_ref.refs_1_) | copy-start | bytes 786436
  193.1 2.4 collective-permute-start.18
  195.5 0.7 copy-start.9
  196.2 23.5 %copy-start.12 = (f32[256,256]{1,0:T(8,128)S(1)}, f32[256,256]{1,0:T(8,128)}, u32[]{:S(2)}) copy-start(f32[256,256]{1,0:T(8,128)} %get-tuple-element.34) | copy-start | bytes 786436
  196.2 25.2 %copy-start.11 = (f32[256,256]{1,0:T(8,128)S(1)}, f32[256,256]{1,0:T(8,128)}, u32[]{:S(2)}) copy-start(f32[256,256]{1,0:T(8,128)} %get-tuple-element.35) | copy-start | bytes 786436
  196.2 25.8 %copy-start.10 = (f32[256,256]{1,0:T(8,128)S(1)}, f32[256,256]{1,0:T(8,128)}, u32[]{:S(2)}) copy-start(f32[256,256]{1,0:T(8,128)} %get-tuple-element.36) | copy-start | bytes 786436
  196.2 1.3 copy-start.7
  219.2 4.0 %collective-permute-start.25 = (f32[4,128,256]{2,1,0:T(8,128)}, f32[4,128,256]{2,1,0:T(8,128)S(1)}, u32[]{:S(2)}, u32[]{:S(2)}) collective-permute-start(f32[4,128,256]{2,1,0:T(8,128)} %get-tuple-element.33), channel_id=1, source_target_pairs={{0,4},{4,0},{8,12},{12,8},{16,20},{20,16},{24,28},{28,24},{1,5},{5... | collective-permute-start | bytes 1572872 | tf_op jit(solution)/shard_map/ppermute | solution.py:426
  219.7 10.1 %collective-permute-start.22 = (f32[256,256]{1,0:T(8,128)S(1)}, f32[256,256]{1,0:T(8,128)S(1)}, u32[]{:S(2)}, u32[]{:S(2)}) collective-permute-start(f32[256,256]{1,0:T(8,128)S(1)} %copy-done.12), channel_id=1, source_target_pairs={{0,24},{4,28},{8,16},{12,20},{16,8},{20,12},{24,0},{28,4},{1,25},{... | collective-permute-start | bytes 786440 | tf_op jit(solution)/shard_map/ppermute | solution.py:426
  221.4 14.1 %collective-permute-start.21 = (f32[256,256]{1,0:T(8,128)S(1)}, f32[256,256]{1,0:T(8,128)S(1)}, u32[]{:S(2)}, u32[]{:S(2)}) collective-permute-start(f32[256,256]{1,0:T(8,128)S(1)} %copy-done.11), channel_id=1, source_target_pairs={{0,16},{4,20},{8,24},{12,28},{16,0},{20,4},{24,8},{28,12},{1,17},{... | collective-permute-start | bytes 786440 | tf_op jit(solution)/shard_map/ppermute | solution.py:426
  222.0 13.4 %collective-permute-start.20 = (f32[256,256]{1,0:T(8,128)S(1)}, f32[256,256]{1,0:T(8,128)S(1)}, u32[]{:S(2)}, u32[]{:S(2)}) collective-permute-start(f32[256,256]{1,0:T(8,128)S(1)} %copy-done.10), channel_id=1, source_target_pairs={{0,8},{4,12},{8,0},{12,4},{16,24},{20,28},{24,16},{28,20},{1,9},{5... | collective-permute-start | bytes 786440 | tf_op jit(solution)/shard_map/ppermute | solution.py:426
  225.0 15.4 %collective-permute-start.28 = (f32[128,256]{1,0:T(8,128)S(1)}, f32[128,256]{1,0:T(8,128)S(1)}, u32[]{:S(2)}, u32[]{:S(2)}) collective-permute-start(f32[128,256]{1,0:T(8,128)S(1)} %get-tuple-element.41), channel_id=1, source_target_pairs={{0,24},{4,28},{8,16},{12,20},{16,8},{20,12},{24,0},{28,4},{1,25},{... | collective-permute-start | bytes 393224 | tf_op jit(solution)/shard_map/ppermute | solution.py:426
  226.7 13.7 %collective-permute-start.27 = (f32[128,256]{1,0:T(8,128)S(1)}, f32[128,256]{1,0:T(8,128)S(1)}, u32[]{:S(2)}, u32[]{:S(2)}) collective-permute-start(f32[128,256]{1,0:T(8,128)S(1)} %get-tuple-element.42), channel_id=1, source_target_pairs={{0,16},{4,20},{8,24},{12,28},{16,0},{20,4},{24,8},{28,12},{1,17},{... | collective-permute-start | bytes 393224 | tf_op jit(solution)/shard_map/ppermute | solution.py:426
  229.8 5.7 %copy-start.13 = (f32[256,256]{1,0:T(8,128)}, f32[256,256]{1,0:T(8,128)S(1)}, u32[]{:S(2)}) copy-start(f32[256,256]{1,0:T(8,128)S(1)} %collective-permute-done.22.refs_3_) | copy-start | bytes 786436
  229.8 10.6 %collective-permute-start.26 = (f32[128,256]{1,0:T(8,128)S(1)}, f32[128,256]{1,0:T(8,128)S(1)}, u32[]{:S(2)}, u32[]{:S(2)}) collective-permute-start(f32[128,256]{1,0:T(8,128)S(1)} %get-tuple-element.43), channel_id=1, source_target_pairs={{0,8},{4,12},{8,0},{12,4},{16,24},{20,28},{24,16},{28,20},{1,9},{5... | collective-permute-start | bytes 393224 | tf_op jit(solution)/shard_map/ppermute | solution.py:426
  235.5 0.8 copy-start.15
  235.5 8.6 %copy-start.1 = (f32[256,256]{1,0:T(8,128)S(1)}, f32[256,256]{1,0:T(8,128)}, u32[]{:S(2)}) copy-start(f32[256,256]{1,0:T(8,128)} %param.6) | copy-start | bytes 786436
  240.4 0.7 copy-start.19
  (3 other events, 2.0 us)
Sparse Core Ops, SparseCore 0:
  94.7 57.9 all-reduce.1
  156.0 48.3 reduce-scatter.1

commit v3 on v2

v3 whole, which is shorter than its diff:
```python
import functools

import jax
import jax.numpy as jnp
from jax import lax
from jax.experimental import pallas as pl
from jax.experimental.pallas import tpu as pltpu
from jax.sharding import PartitionSpec as P

FB = 512
OFF = 256
CHUNKS = 1
VMEM = 56 * 1024 * 1024

F32 = jnp.float32
BF16 = jnp.bfloat16
LONG = pl.CostEstimate(flops=10**11, bytes_accessed=1024, transcendentals=0)
SHORT = pl.CostEstimate(flops=1024, bytes_accessed=1024, transcendentals=0)


def split(x):
    high = x.astype(BF16)
    return high, (x - high.astype(F32)).astype(BF16)


def mul(left, right):
    return jnp.dot(left, right, preferred_element_type=F32)


def three(left, right):
    (lh, ll), (rh, rl) = left, right
    return mul(lh, rh) + mul(ll, rh) + mul(lh, rl)


def stacked(both, high, right):
    rh, rl = right
    m = high.shape[0]
    top = mul(both, rh)
    return top[:m] + top[m:] + mul(high, rl)


def params():
    return pltpu.CompilerParams(
        dimension_semantics=("arbitrary",), vmem_limit_bytes=VMEM
    )


def width(columns, wide):
    return 256 if columns % 256 == 0 and 256 % (columns // wide) == 0 else columns // wide


def whole(shape):
    return pl.BlockSpec(shape, lambda j, *_: (0,) * len(shape), pipeline_mode=pl.Buffered(1))


ANY = pl.BlockSpec(memory_space=pl.ANY)


def gate_kernel(*refs):
    del refs


def gate(held, *others, cost=SHORT):
    count = len(held)
    return pl.pallas_call(
        gate_kernel,
        in_specs=[ANY] * (count + len(others)),
        out_specs=[ANY] * count,
        out_shape=[jax.ShapeDtypeStruct(x.shape, x.dtype) for x in held],
        input_output_aliases={k: k for k in range(count)},
        cost_estimate=cost,
        name="gate",
    )(*held, *others)


def place(value, index, even_ref, odd_ref):
    half = index // 2

    @pl.when(index % 2 == 0)
    def _():
        even_ref[half] = value

    @pl.when(index % 2 == 1)
    def _():
        odd_ref[half] = value


def take(index, even_ref, odd_ref):
    half = index // 2
    return jnp.where(index % 2 == 0, even_ref[half], odd_ref[half])


def project_kernel(per, me_ref, v_ref, r_ref, e_ref, even_ref, odd_ref, scaled_ref, both_ref):
    j = pl.program_id(0)
    nb = r_ref.shape[1]

    @pl.when(j == 0)
    def _():
        turned = r_ref[...].T
        both_ref[:nb], both_ref[nb:] = split(turned)
        scaled_ref[:nb], scaled_ref[nb:] = split(turned * e_ref[...])

    value = stacked(both_ref[...], both_ref[:nb], split(v_ref[...]))
    step = v_ref.shape[1]
    for g in range(step // per):
        w = j * (step // per) + g
        place(value[:, g * per : (g + 1) * per], w ^ me_ref[0], even_ref, odd_ref)


def project(me, vectors, reflectors, e_row, wide):
    rows, columns = vectors.shape
    nb = reflectors.shape[1]
    per = columns // wide
    step = width(columns, wide)
    half = jax.ShapeDtypeStruct((wide // 2, nb, per), F32)
    return pl.pallas_call(
        functools.partial(project_kernel, per),
        grid_spec=pltpu.PrefetchScalarGridSpec(
            num_scalar_prefetch=1,
            grid=(columns // step,),
            in_specs=[
                pl.BlockSpec((rows, step), lambda j, *_: (0, j)),
                whole((rows, nb)),
                whole((1, rows)),
            ],
            out_specs=[whole(half.shape), whole(half.shape), whole((2 * nb, rows))],
            scratch_shapes=[pltpu.VMEM((2 * nb, rows), BF16)],
        ),
        out_shape=[half, half, jax.ShapeDtypeStruct((2 * nb, rows), BF16)],
        compiler_params=params(),
        cost_estimate=SHORT,
        name="project",
    )(me, vectors, reflectors, e_row)


def update_kernel(per, me_ref, v_ref, r_ref, even_ref, odd_ref, after_ref, out_ref, token_ref, left_ref):
    j = pl.program_id(0)
    nb = r_ref.shape[1]

    @pl.when(j == 0)
    def _():
        token_ref[...] = jnp.zeros_like(token_ref)
        high, low = split(r_ref[...])
        left_ref[:, :nb] = high
        left_ref[:, nb : 2 * nb] = low
        left_ref[:, 2 * nb :] = high

    count = v_ref.shape[1] // per
    blocks = [take((j * count + g) ^ me_ref[0], even_ref, odd_ref) for g in range(count)]
    high, low = split(blocks[0] if count == 1 else jnp.concatenate(blocks, axis=1))
    right = jnp.concatenate([high, high, low], axis=0)
    out_ref[...] = v_ref[...] - mul(left_ref[...], right)


def update(me, vectors, reflectors, even, odd, wide, after):
    rows, columns = vectors.shape
    nb = reflectors.shape[1]
    per = columns // wide
    step = width(columns, wide)
    columns_of = pl.BlockSpec((rows, step), lambda j, *_: (0, j))
    return pl.pallas_call(
        functools.partial(update_kernel, per),
        grid_spec=pltpu.PrefetchScalarGridSpec(
            num_scalar_prefetch=1,
            grid=(columns // step,),
            in_specs=[columns_of, whole((rows, nb)), whole(even.shape), whole(odd.shape), ANY],
            out_specs=[columns_of, whole((8, 128))],
            scratch_shapes=[pltpu.VMEM((rows, 3 * nb), BF16)],
        ),
        out_shape=[
            jax.ShapeDtypeStruct(vectors.shape, F32),
            jax.ShapeDtypeStruct((8, 128), F32),
        ],
        compiler_params=params(),
        cost_estimate=SHORT,
        name="update",
    )(me, vectors, reflectors, even, odd, after)


def gather(choice, groups, block_ref):
    first = 0
    for group in groups:
        rows = group[0].shape[0]
        for k, ref in enumerate(group):

            @pl.when(choice == k)
            def _(ref=ref, first=first, rows=rows):
                pltpu.sync_copy(ref, block_ref.at[pl.ds(first, rows)])

        first += rows


def regroup(refs, groups):
    refs = list(refs)
    return [[refs.pop(0) for _ in range(count)] for count in groups]


def late_kernel(n, per, slots, at_ref, u_ref, scaled_ref, ce_ref, co_ref, after_ref, *refs):
    *refs, even_out, odd_out, both_ref, coef_ref, block_ref = refs
    j = pl.program_id(0)
    m = both_ref.shape[0] // 2
    each = block_ref.shape[1]
    me, z = at_ref[0], at_ref[1]

    @pl.when(j == 0)
    def _():
        nb = scaled_ref.shape[0] // 2
        half, _, rows, _ = ce_ref.shape
        left = list(refs)
        for s, groups in enumerate(slots):
            used = sum(groups)
            gather(at_ref[2 + 2 * s], regroup(left[:used], groups), block_ref)
            left = left[used:]
            away = (z + n - at_ref[3 + 2 * s]) % n
            for h in range(half):
                for p, ref in enumerate((ce_ref, co_ref)):
                    owner = (me ^ (2 * h + p)) % (2 * half)
                    first = pl.multiple_of(owner * rows, rows)
                    coef_ref[pl.ds(first, rows), :] = ref[h, away]
            scaled = (scaled_ref[:nb], scaled_ref[nb:])
            block = block_ref[...].T - three(split(coef_ref[...]), scaled)
            high, low = split(block)
            both_ref[s * each : (s + 1) * each] = high
            both_ref[m + s * each : m + (s + 1) * each] = low

    value = stacked(both_ref[...], both_ref[:m], split(u_ref[...]))
    count = u_ref.shape[1] // per
    for g in range(count):
        place(value[:, g * per : (g + 1) * per], (j * count + g) ^ me, even_out, odd_out)


def late(me, z, n, updated, scaled, slots, coef, after, wide):
    rows, columns = updated.shape
    per = columns // wide
    step = width(columns, wide)
    flat = [x for groups, _, _ in slots for group in groups for x in group]
    counts = [[len(group) for group in groups] for groups, _, _ in slots]
    each = flat[0].shape[1]
    m = each * len(slots)
    at = [me[0], z]
    for _, choice, home in slots:
        at += [choice, home]
    at = jnp.stack([x.astype(jnp.int32) for x in at])
    half = jax.ShapeDtypeStruct((wide // 2, m, per), F32)
    return pl.pallas_call(
        functools.partial(late_kernel, n, per, counts),
        grid_spec=pltpu.PrefetchScalarGridSpec(
            num_scalar_prefetch=1,
            grid=(columns // step,),
            in_specs=[
                pl.BlockSpec((rows, step), lambda j, *_: (0, j)),
                whole(scaled.shape),
                whole(coef[0].shape),
                whole(coef[1].shape),
                ANY,
            ]
            + [ANY] * len(flat),
            out_specs=[whole(half.shape)] * 2,
            scratch_shapes=[
                pltpu.VMEM((2 * m, rows), BF16),
                pltpu.VMEM((each, scaled.shape[0] // 2), F32),
                pltpu.VMEM((rows, each), F32),
            ],
        ),
        out_shape=[half, half],
        compiler_params=params(),
        cost_estimate=SHORT,
        name="late",
    )(at, updated, scaled, *coef, after, *flat)


def share_kernel(rows, me_ref, even_ref, odd_ref, out_ref, all_ref):
    per = even_ref.shape[2]
    block = take((OFF // per) ^ me_ref[0], even_ref, odd_ref)
    first = OFF % per
    all_ref[...] = block[:, first : first + all_ref.shape[0]].T
    start = pl.multiple_of((me_ref[0] % (all_ref.shape[0] // rows)) * rows, rows)
    out_ref[...] = all_ref[pl.ds(start, rows), :]


def share(me, even, odd, block_width, rows):
    nb = even.shape[1]
    return pl.pallas_call(
        functools.partial(share_kernel, rows),
        grid_spec=pltpu.PrefetchScalarGridSpec(
            num_scalar_prefetch=1,
            grid=(1,),
            in_specs=[whole(even.shape), whole(odd.shape)],
            out_specs=whole((rows, nb)),
            scratch_shapes=[pltpu.VMEM((block_width, nb), F32)],
        ),
        out_shape=jax.ShapeDtypeStruct((rows, nb), F32),
        compiler_params=params(),
        cost_estimate=SHORT,
        name="share",
    )(me, even, odd)


def base_kernel(at_ref, *refs):
    *refs, out_ref = refs
    total = functools.reduce(jnp.add, [ref[...] for ref in refs])
    count = total.shape[0] * at_ref.shape[0] // out_ref.shape[0]
    each = total.shape[0] // count
    for slot in range(count):
        first = pl.multiple_of(at_ref[slot] * each, each)
        out_ref[pl.ds(first, each), :] = total[slot * each : (slot + 1) * each]


def base(at, terms):
    per = terms[0].shape[1]
    return pl.pallas_call(
        base_kernel,
        grid_spec=pltpu.PrefetchScalarGridSpec(
            num_scalar_prefetch=1,
            grid=(1,),
            in_specs=[whole(x.shape) for x in terms],
            out_specs=whole((FB, per)),
        ),
        out_shape=jax.ShapeDtypeStruct((FB, per), F32),
        compiler_params=params(),
        cost_estimate=LONG,
        name="base",
    )(at, *terms)


def last_kernel(at_ref, base_ref, *refs):
    *refs, out_ref, total_ref = refs
    total = functools.reduce(jnp.add, [ref[...] for ref in refs])
    each = total.shape[0]
    first = pl.multiple_of(at_ref[at_ref.shape[0] - 1] * each, each)
    total_ref[...] = base_ref[...]
    total_ref[pl.ds(first, each), :] = total
    out_ref[...] = total_ref[...].T


def last(at, held, terms):
    per = held.shape[1]
    operands = [held, *terms]
    return pl.pallas_call(
        last_kernel,
        grid_spec=pltpu.PrefetchScalarGridSpec(
            num_scalar_prefetch=1,
            grid=(1,),
            in_specs=[whole(x.shape) for x in operands],
            out_specs=whole((per, FB)),
            scratch_shapes=[pltpu.VMEM((FB, per), F32)],
        ),
        out_shape=jax.ShapeDtypeStruct((per, FB), F32),
        compiler_params=params(),
        cost_estimate=SHORT,
        name="last",
    )(at, *operands)


def arrivals(n):
    order = []
    for z in range(n):
        found = [(hops, 0) for hops in range(1, n) if z + hops < n]
        found += [(hops, 1) for hops in range(1, n) if z - hops >= 0]
        order.append(sorted(found))
    return [[order[z][slot] for z in range(n)] for slot in range(n - 1)]


def hop(held, n, hops, after):
    if after:
        count = len(held[0])
        both = gate(held[0] + held[1], *after, cost=LONG)
        held = [both[:count], both[count:]]
    pairs = [
        [(p, p - 1) for p in range(1, n - hops + 1)],
        [(p, p + 1) for p in range(hops - 1, n - 1)],
    ]
    return held, [[lax.ppermute(x, "narrow", pairs[d]) for x in held[d]] for d in (0, 1)]


def options(came, places, z):
    choices = sorted(set(places))
    which = jnp.int32(0)
    for p, place in enumerate(places):
        which = jnp.where(z == p, choices.index(place), which)
    return [[came[choice][c] for choice in choices] for c in range(CHUNKS)], which


def source(places, z):
    value = jnp.int32(0)
    for p, (hops, direction) in enumerate(places):
        value = jnp.where(z == p, p - hops if direction else p + hops, value)
    return value


def swap(x, wide, distance):
    return lax.ppermute(x, "wide", [(i, i ^ distance) for i in range(wide)])


def scatter_terms(even, odd, wide, after=None):
    other = swap(odd, wide, 1)
    if after is not None:
        (other,) = gate([other], after)
    sums = [even[h] + other[h] for h in range(wide // 2)]
    return [sums[0]] + [swap(sums[h], wide, 2 * h) for h in range(1, wide // 2)]


def collect(x, count):
    even = jnp.stack([x] + [swap(x, lax.axis_size("wide"), 2 * h) for h in range(1, count // 2)])
    return even, swap(even, lax.axis_size("wide"), 1)


def on_device(vectors, reflectors, triangle, energies):
    n = lax.axis_size("narrow")
    wide = lax.axis_size("wide")
    z = lax.axis_index("narrow").astype(jnp.int32)
    me = lax.axis_index("wide").astype(jnp.int32).reshape(1)
    each = FB // n
    rows, columns = vectors.shape
    step = rows // CHUNKS
    e_row = energies.reshape(1, rows)

    chunks = [
        energies[c * step : (c + 1) * step, None]
        * vectors[c * step : (c + 1) * step, OFF : OFF + each]
        for c in range(CHUNKS)
    ]
    came = {}

    def travel(held, hops, after):
        held, passed = hop(held, n, hops, after)
        for d in (0, 1):
            if hops > 1:
                came[(hops - 1, d)] = held[d]
            came[(hops, d)] = passed[d]
        return passed

    held = travel([chunks, chunks], 1, [])
    table = arrivals(n)
    at = jnp.stack([z] + [source(places, z) for places in table])

    even, odd, scaled = project(me, vectors, reflectors, e_row, wide)
    if n > 2:
        held = travel(held, 2, [scaled])

    projected = functools.reduce(jnp.add, scatter_terms(even, odd, wide))
    coefficients = jnp.dot(triangle, projected, precision=lax.Precision.HIGHEST)
    c_even, c_odd = collect(coefficients, wide)

    sharers = wide
    while (each // sharers) % 8:
        sharers //= 2
    mine = share(me, c_even, c_odd, each, each // sharers)
    shares = jnp.stack(
        [mine]
        + [lax.ppermute(mine, "narrow", [(p, (p + s) % n) for p in range(n)]) for s in range(1, n)]
    )
    updated, token = update(me, vectors, reflectors, c_even, c_odd, wide, shares)
    for hops in range(3, n):
        held = travel(held, hops, [token])
    coef = collect(shares, sharers)

    slots = [([[chunk] for chunk in chunks], jnp.int32(0), z)]
    for slot in range(n - 1):
        slots.append((*options(came, table[slot], z), at[1 + slot]))
    halves = late(me, z, n, updated, scaled, slots[:-1], coef, token, wide)
    middle = scatter_terms(*halves, wide)
    (token,) = gate([token], middle[0])
    halves = late(me, z, n, updated, scaled, slots[-1:], coef, token, wide)
    held = base(at, middle)
    fock_block = last(at, held, scatter_terms(*halves, wide, held))
    return (updated, fock_block)


def solution(mesh):
    return jax.shard_map(
        on_device,
        mesh=mesh,
        in_specs=(P("wide", "narrow"), P("wide", None), P(), P("wide")),
        out_specs=(P("wide", "narrow"), P(("narrow", "wide"), None)),
        check_vma=False,
    )
```

time: 252 us -> 271 us (1.075)
  waiting for transfers between devices: 41.3 us -> 88.5 us
  Pallas kernels: 138 us -> 119 us
  between operations: 14.3 us -> 0.87 us
  other arithmetic: 8.19 us -> 10.9 us
    ppermute x6, waiting for transfers between devices: 3.04 us -> 48.8 us  [hop(): lax.ppermute(x, 'narrow', pairs[d])]
    pallas_call x7 -> x6, Pallas kernels: 136 us -> 117 us  [the longest x2 56.5 us: late(): pl.pallas_call(functools.partial(late_kernel, n, per, counts), grid_spec=...]
    ppermute x3, waiting for transfers between devices: 3.77 us -> 17.4 us  [on_device(): lax.ppermute(mine, 'narrow', [(p, (p + s) % n) for p in range(n)])]
    ppermute x20, waiting for transfers between devices: 34.5 us -> 22.2 us  [swap(): return lax.ppermute(x, 'wide', [(i, i ^ distance) for i in range(wide)])]
  transfers between devices with their start and end apart: 31 -> 29, of which waited for: 13 -> 12; matrix products, arithmetic and copies ran while one was open for 3% -> 3% of each run, Pallas kernels for 54% -> 30%
where the time goes in v3:
time: 271 us; the launch traced here: 268 us
  Pallas kernels  119 us (44%)
  waiting for transfers between devices  88.5 us (33%)
  starting transfers between devices  41.4 us (15%)
  other arithmetic  10.9 us (4%)
  local copies, waits for them, and re-layouts  5.11 us (2%)
    pallas_call x2, Pallas kernels, late(): pl.pallas_call(functools.partial(late_kernel, n, per, counts), grid_spec=...  56.5 us
    ppermute x6, waiting for transfers between devices, hop(): lax.ppermute(x, 'narrow', pairs[d])  48.8 us
    pallas_call x1, Pallas kernels, update(): pl.pallas_call(functools.partial(update_kernel, per), grid_spec=pltpu.Pre...  30.9 us
    pallas_call x1, Pallas kernels, project(): pl.pallas_call(functools.partial(project_kernel, per), grid_spec=pltpu.Pr...  23.6 us
    ppermute x20, waiting for transfers between devices, swap(): return lax.ppermute(x, 'wide', [(i, i ^ distance) for i in range(wide)])  22.2 us
    ppermute x20, starting transfers between devices, swap(): return lax.ppermute(x, 'wide', [(i, i ^ distance) for i in range(wide)])  18 us
    ppermute x3, waiting for transfers between devices, on_device(): lax.ppermute(mine, 'narrow', [(p, (p + s) % n) for p in range(n)])  17.4 us
    ppermute x6, starting transfers between devices, hop(): lax.ppermute(x, 'narrow', pairs[d])  14.8 us
  transfers between devices with their start and end apart: 29, of which 12 were waited for; matrix products, arithmetic and copies ran while one was open for 3% of the time, Pallas kernels for 30%

profile of v3, /device:TPU:0, one launch (start us, length us, event | category | flops | bytes accessed | tf_op | source)
XLA Modules:
  0.0 267.6 jit_solution(12653715082218277225)
XLA Ops:
  0.6 2.8 %slice_multiply_fusion.refs_0_ = f32[4000,128]{1,0:T(8,128)S(1)} fusion(f32[4000,2048]{1,0:T(8,128)} %v_ref.3, f32[4000]{0:T(1024)} %param.7), kind=kLoop, calls=%fused_computation | loop fusion | flops 512000 | bytes 4112000 | tf_op jit(solution)/shard_map/mul | solution.py:419
  3.4 1.3 collective-permute-start.15
  4.7 6.9 %collective-permute-start.16 = (f32[4000,128]{1,0:T(8,128)S(1)}, f32[4000,128]{1,0:T(8,128)}, u32[]{:S(2)}, u32[]{:S(2)}) collective-permute-start(f32[4000,128]{1,0:T(8,128)S(1)} %slice_multiply_fusion.refs_0_), channel_id=1, source_target_pairs={{0,1},{1,2},{2,3},{4,5},{5,6},{6,7},{8,9},{9,10},{10,11},{12,13},{... | collective-permute-start | bytes 6144008 | tf_op jit(solution)/shard_map/ppermute | solution.py:373
  11.6 23.6 %project.1 = (f32[4,256,256]{2,1,0:T(8,128)}, f32[4,256,256]{2,1,0:T(8,128)}, bf16[512,4000]{1,0:T(8,128)(2,1)}) custom-call(s32[1]{0:T(128)} %bitcast.me_ref, f32[4000,2048]{1,0:T(8,128)} %v_ref.3, f32[4000,256]{1,0:T(8,128)} %r_ref.3, f32[1,4000]{1,0:T(1,128)} %bitcast.63), custom_call_target="tpu_custom_call" | custom-call | flops 1024 | bytes 1024 | tf_op jit(solution)/shard_map/project/pallas_call | solution.py:116
  35.3 2.9 %collective-permute-done = f32[4,256,256]{2,1,0:T(8,128)S(1)} collective-permute-done((f32[4,256,256]{2,1,0:T(8,128)}, f32[4,256,256]{2,1,0:T(8,128)S(1)}, u32[]{:S(2)}, u32[]{:S(2)}) %collective-permute-start) | collective-permute-done | bytes 1048608 | tf_op jit(solution)/shard_map/ppermute | solution.py:392
  38.1 2.0 fusion.6
  40.2 1.9 collective-permute-start.1
  42.1 1.5 collective-permute-start.2
  43.7 9.4 %collective-permute-done.15.refs_0_ = f32[4000,128]{1,0:T(8,128)} collective-permute-done((f32[4000,128]{1,0:T(8,128)S(1)}, f32[4000,128]{1,0:T(8,128)}, u32[]{:S(2)}, u32[]{:S(2)}) %collective-permute-start.15) | collective-permute-done | bytes 2048032 | tf_op jit(solution)/shard_map/ppermute | solution.py:373
  53.0 1.1 collective-permute-done.16.refs_1_
  54.1 1.3 collective-permute-start.17
  55.4 2.0 collective-permute-start.18
  57.4 1.6 fusion.11
  59.0 2.7 collective-permute-start.6
  62.6 6.7 %collective-permute-done.6 = f32[256,256]{1,0:T(8,128)S(1)} collective-permute-done((f32[256,256]{1,0:T(8,128)S(1)}, f32[256,256]{1,0:T(8,128)S(1)}, u32[]{:S(2)}, u32[]{:S(2)}) %collective-permute-start.6) | collective-permute-done | bytes 262176 | tf_op jit(solution)/shard_map/ppermute | solution.py:392
  69.3 3.4 %collective-permute-done.4 = f32[256,256]{1,0:T(8,128)S(1)} collective-permute-done((f32[256,256]{1,0:T(8,128)S(1)}, f32[256,256]{1,0:T(8,128)S(1)}, u32[]{:S(2)}, u32[]{:S(2)}) %collective-permute-start.4) | collective-permute-done | bytes 262176 | tf_op jit(solution)/shard_map/ppermute | solution.py:392
  73.0 2.6 collective-permute-done.7.odd_ref
  75.6 1.0 copy-done.6
  76.6 2.2 share.1
  78.9 6.0 %collective-permute-start.8 = (f32[16,256]{1,0:T(8,128)}, f32[16,256]{1,0:T(8,128)S(1)}, u32[]{:S(2)}, u32[]{:S(2)}) collective-permute-start(f32[16,256]{1,0:T(8,128)} %share.1), channel_id=1, source_target_pairs={{0,1},{1,2},{2,3},{3,0},{4,5},{5,6},{6,7},{7,4},{8,9},{9,10},{10,1... | collective-permute-start | bytes 49160 | tf_op jit(solution)/shard_map/ppermute | solution.py:451
  84.9 2.5 collective-permute-start.10
  87.4 17.4 %collective-permute-done.9 = f32[16,256]{1,0:T(8,128)S(1)} collective-permute-done((f32[16,256]{1,0:T(8,128)}, f32[16,256]{1,0:T(8,128)S(1)}, u32[]{:S(2)}, u32[]{:S(2)}) %collective-permute-start.9) | collective-permute-done | bytes 16416 | tf_op jit(solution)/shard_map/ppermute | solution.py:451
  104.9 0.7 fusion.18
  105.6 1.4 collective-permute-start.11
  107.0 1.5 collective-permute-start.12
  108.6 0.6 collective-permute-start.13
  109.8 30.9 %update.1 = (f32[4000,2048]{1,0:T(8,128)}, f32[8,128]{1,0:T(8,128)}) custom-call(s32[1]{0:T(128)} %bitcast.me_ref, f32[4000,2048]{1,0:T(8,128)} %v_ref.3, f32[4000,256]{1,0:T(8,128)} %r_ref.3, f32[4,256,256]{2,1,0:T(8,128)} %copy-done.2, f32[4,256,256]{2,1,0:T(8,128)} %copy-done.6, f32[4,16,256]{2,1,0:T(8,128)} %copy-done.11), custom_call_target="tpu_custom_call" | custom-call | flops 1024 | bytes 1024 | tf_op jit(solution)/shard_map/update/pallas_call | solution.py:161
  140.8 1.3 copy-done.4
  142.3 0.7 copy-done.9
  143.0 35.7 %late.2 = (f32[4,384,256]{2,1,0:T(8,128)}, f32[4,384,256]{2,1,0:T(8,128)}) custom-call(s32[8]{0:T(128)} %stack.95.at_ref, f32[4000,2048]{1,0:T(8,128)} %get-tuple-element.13.u_ref, bf16[512,4000]{1,0:T(8,128)(2,1)} %get-tuple-element.18.refs_2_.scaled_ref, f32[4,4,16,256]{3,2,1,0:T(8,128)} %copy-done.7, f32[4,4,16,256]{3,2,1,0:T(8,128)} %copy-done.9, ...), custom_call_target="tpu_custom_call" | custom-call | flops 1024 | bytes 1024 | tf_op jit(solution)/shard_map/late/pallas_call | solution.py:245
  179.0 1.3 collective-permute-start.23
  180.3 2.1 collective-permute-start.24
  182.4 2.3 fusion
  184.7 1.3 collective-permute-start.20
  186.0 1.5 collective-permute-start.21
  187.5 0.6 collective-permute-start.22
  189.4 38.4 %collective-permute-done.23.refs_2_ = f32[4000,128]{1,0:T(8,128)} collective-permute-done((f32[4000,128]{1,0:T(8,128)S(1)}, f32[4000,128]{1,0:T(8,128)}, u32[]{:S(2)}, u32[]{:S(2)}) %collective-permute-start.23) | collective-permute-done | bytes 2048032 | tf_op jit(solution)/shard_map/ppermute | solution.py:373
  227.7 20.8 %late.3 = (f32[4,128,256]{2,1,0:T(8,128)}, f32[4,128,256]{2,1,0:T(8,128)}) custom-call(s32[4]{0:T(128)} %add_add_fusion.1.at_ref, f32[4000,2048]{1,0:T(8,128)} %get-tuple-element.13.u_ref, bf16[512,4000]{1,0:T(8,128)(2,1)} %get-tuple-element.18.refs_2_.scaled_ref, f32[4,4,16,256]{3,2,1,0:T(8,128)} %copy-done.7, f32[4,4,16,256]{3,2,1,0:T(8,128)} %copy-done.9, ...), custom_call_target="tpu_custom_call" | custom-call | flops 1024 | bytes 1024 | tf_op jit(solution)/shard_map/late/pallas_call | solution.py:245
  248.5 3.0 %base.1.refs_1_.base_ref = f32[512,256]{1,0:T(8,128)} custom-call(s32[4]{0:T(128)} %add_add_fusion.at_ref, f32[384,256]{1,0:T(8,128)} %get-tuple-element.31.refs_0_.refs_1_, f32[384,256]{1,0:T(8,128)} %collective-permute-done.20.refs_1_, f32[384,256]{1,0:T(8,128)} %collective-permute-done.21.refs_2_, f32[384,256]{1,0:T(8,128)} %collective-permute-done.22.refs_3_), custom_call_target="tpu_custom_call" | custom-call | flops 99999997952 | bytes 1024 | tf_op jit(solution)/shard_map/base/pallas_call | solution.py:311
  251.5 0.8 copy-done.8
  252.4 1.8 fusion.14
  254.2 1.3 collective-permute-start.26
  255.5 1.5 collective-permute-start.27
  257.0 0.6 collective-permute-start.28
  257.7 2.8 %collective-permute-done.26.refs_1_ = f32[128,256]{1,0:T(8,128)S(1)} collective-permute-done((f32[128,256]{1,0:T(8,128)S(1)}, f32[128,256]{1,0:T(8,128)S(1)}, u32[]{:S(2)}, u32[]{:S(2)}) %collective-permute-start.26) | collective-permute-done | bytes 131104 | tf_op jit(solution)/shard_map/ppermute | solution.py:392
  260.5 3.5 %collective-permute-done.27.refs_2_ = f32[128,256]{1,0:T(8,128)S(1)} collective-permute-done((f32[128,256]{1,0:T(8,128)S(1)}, f32[128,256]{1,0:T(8,128)S(1)}, u32[]{:S(2)}, u32[]{:S(2)}) %collective-permute-start.27) | collective-permute-done | bytes 131104 | tf_op jit(solution)/shard_map/ppermute | solution.py:392
  263.9 0.6 copy-done.13
  264.6 3.0 %last.1 = f32[256,512]{1,0:T(8,128)} custom-call(s32[4]{0:T(128)} %add_add_fusion.at_ref, f32[512,256]{1,0:T(8,128)} %base.1.refs_1_.base_ref, f32[128,256]{1,0:T(8,128)} %get-tuple-element.38.refs_0_, f32[128,256]{1,0:T(8,128)} %copy-done.12, f32[128,256]{1,0:T(8,128)} %copy-done.13, f32[128,256]{1,0:T(8,128)} %copy-done.14), custom_call_target="tpu_custom_call" | custom-call | flops 1024 | bytes 1024 | tf_op jit(solution)/shard_map/last/pallas_call | solution.py:339
  (62 shorter events, 3.7 us)
Async XLA Ops:
  0.6 56.8 %copy-start = (f32[256,256]{1,0:T(8,128)S(1)}, f32[256,256]{1,0:T(8,128)}, u32[]{:S(2)}) copy-start(f32[256,256]{1,0:T(8,128)} %param.6) | copy-start | bytes 786436
  3.4 31.9 %copy-start.3 = (f32[4000,128]{1,0:T(8,128)}, f32[4000,128]{1,0:T(8,128)S(1)}, u32[]{:S(2)}) copy-start(f32[4000,128]{1,0:T(8,128)S(1)} %slice_multiply_fusion.refs_0_) | copy-start | bytes 6144004
  3.4 49.6 %collective-permute-start.15 = (f32[4000,128]{1,0:T(8,128)S(1)}, f32[4000,128]{1,0:T(8,128)}, u32[]{:S(2)}, u32[]{:S(2)}) collective-permute-start(f32[4000,128]{1,0:T(8,128)S(1)} %slice_multiply_fusion.refs_0_), channel_id=1, source_target_pairs={{1,0},{2,1},{3,2},{5,4},{6,5},{7,6},{9,8},{10,9},{11,10},{13,12},{... | collective-permute-start | bytes 6144008 | tf_op jit(solution)/shard_map/ppermute | solution.py:373
  4.7 49.4 %collective-permute-start.16 = (f32[4000,128]{1,0:T(8,128)S(1)}, f32[4000,128]{1,0:T(8,128)}, u32[]{:S(2)}, u32[]{:S(2)}) collective-permute-start(f32[4000,128]{1,0:T(8,128)S(1)} %slice_multiply_fusion.refs_0_), channel_id=1, source_target_pairs={{0,1},{1,2},{2,3},{4,5},{5,6},{6,7},{8,9},{9,10},{10,11},{12,13},{... | collective-permute-start | bytes 6144008 | tf_op jit(solution)/shard_map/ppermute | solution.py:373
  35.3 2.9 %collective-permute-start = (f32[4,256,256]{2,1,0:T(8,128)}, f32[4,256,256]{2,1,0:T(8,128)S(1)}, u32[]{:S(2)}, u32[]{:S(2)}) collective-permute-start(f32[4,256,256]{2,1,0:T(8,128)} %get-tuple-element.16), channel_id=1, source_target_pairs={{0,4},{4,0},{8,12},{12,8},{16,20},{20,16},{24,28},{28,24},{1,5},{5... | collective-permute-start | bytes 3145736 | tf_op jit(solution)/shard_map/ppermute | solution.py:392
  40.2 17.2 %collective-permute-start.1 = (f32[256,256]{1,0:T(8,128)}, f32[256,256]{1,0:T(8,128)}, u32[]{:S(2)}, u32[]{:S(2)}) collective-permute-start(f32[256,256]{1,0:T(8,128)} %get-tuple-element.32), channel_id=1, source_target_pairs={{0,8},{4,12},{8,0},{12,4},{16,24},{20,28},{24,16},{28,20},{1,9},{5... | collective-permute-start | bytes 786440 | tf_op jit(solution)/shard_map/ppermute | solution.py:392
  42.1 15.3 %collective-permute-start.2 = (f32[256,256]{1,0:T(8,128)}, f32[256,256]{1,0:T(8,128)}, u32[]{:S(2)}, u32[]{:S(2)}) collective-permute-start(f32[256,256]{1,0:T(8,128)} %get-tuple-element.34), channel_id=1, source_target_pairs={{0,16},{4,20},{8,24},{12,28},{16,0},{20,4},{24,8},{28,12},{1,17},{... | collective-permute-start | bytes 786440 | tf_op jit(solution)/shard_map/ppermute | solution.py:392
  43.6 13.8 %collective-permute-start.3 = (f32[256,256]{1,0:T(8,128)}, f32[256,256]{1,0:T(8,128)}, u32[]{:S(2)}, u32[]{:S(2)}) collective-permute-start(f32[256,256]{1,0:T(8,128)} %get-tuple-element.33), channel_id=1, source_target_pairs={{0,24},{4,28},{8,16},{12,20},{16,8},{20,12},{24,0},{28,4},{1,25},{... | collective-permute-start | bytes 786440 | tf_op jit(solution)/shard_map/ppermute | solution.py:392
  54.1 86.7 %collective-permute-start.17 = (f32[4000,128]{1,0:T(8,128)}, f32[4000,128]{1,0:T(8,128)S(1)}, u32[]{:S(2)}, u32[]{:S(2)}) collective-permute-start(f32[4000,128]{1,0:T(8,128)} %get-tuple-element.20.refs_1_), channel_id=1, source_target_pairs={{1,0},{2,1},{5,4},{6,5},{9,8},{10,9},{13,12},{14,13},{17,16},{18,1... | collective-permute-start | bytes 6144008 | tf_op jit(solution)/shard_map/ppermute | solution.py:373
  55.4 85.5 %collective-permute-start.18 = (f32[4000,128]{1,0:T(8,128)}, f32[4000,128]{1,0:T(8,128)}, u32[]{:S(2)}, u32[]{:S(2)}) collective-permute-start(f32[4000,128]{1,0:T(8,128)} %get-tuple-element.21.refs_2_.refs_3_), channel_id=1, source_target_pairs={{1,2},{2,3},{5,6},{6,7},{9,10},{10,11},{13,14},{14,15},{17,18},{18... | collective-permute-start | bytes 6144008 | tf_op jit(solution)/shard_map/ppermute | solution.py:373
  59.0 10.3 %collective-permute-start.6 = (f32[256,256]{1,0:T(8,128)S(1)}, f32[256,256]{1,0:T(8,128)S(1)}, u32[]{:S(2)}, u32[]{:S(2)}) collective-permute-start(f32[256,256]{1,0:T(8,128)S(1)} %bitcast.56), channel_id=1, source_target_pairs={{0,24},{4,28},{8,16},{12,20},{16,8},{20,12},{24,0},{28,4},{1,25},{... | collective-permute-start | bytes 786440 | tf_op jit(solution)/shard_map/ppermute | solution.py:392
  61.7 11.0 %collective-permute-start.4 = (f32[256,256]{1,0:T(8,128)S(1)}, f32[256,256]{1,0:T(8,128)S(1)}, u32[]{:S(2)}, u32[]{:S(2)}) collective-permute-start(f32[256,256]{1,0:T(8,128)S(1)} %bitcast.57), channel_id=1, source_target_pairs={{0,8},{4,12},{8,0},{12,4},{16,24},{20,28},{24,16},{28,20},{1,9},{5... | collective-permute-start | bytes 786440 | tf_op jit(solution)/shard_map/ppermute | solution.py:392
  62.2 10.6 %collective-permute-start.5 = (f32[256,256]{1,0:T(8,128)S(1)}, f32[256,256]{1,0:T(8,128)S(1)}, u32[]{:S(2)}, u32[]{:S(2)}) collective-permute-start(f32[256,256]{1,0:T(8,128)S(1)} %bitcast.58), channel_id=1, source_target_pairs={{0,16},{4,20},{8,24},{12,28},{16,0},{20,4},{24,8},{28,12},{1,17},{... | collective-permute-start | bytes 786440 | tf_op jit(solution)/shard_map/ppermute | solution.py:392
  72.9 2.7 %copy-start.2 = (f32[4,256,256]{2,1,0:T(8,128)}, f32[4,256,256]{2,1,0:T(8,128)S(1)}, u32[]{:S(2)}) copy-start(f32[4,256,256]{2,1,0:T(8,128)S(1)} %pad_maximum_fusion.even_ref) | copy-start | bytes 3145732
  72.9 2.7 %collective-permute-start.7 = (f32[4,256,256]{2,1,0:T(8,128)S(1)}, f32[4,256,256]{2,1,0:T(8,128)S(1)}, u32[]{:S(2)}, u32[]{:S(2)}) collective-permute-start(f32[4,256,256]{2,1,0:T(8,128)S(1)} %pad_maximum_fusion.even_ref), channel_id=1, source_target_pairs={{0,4},{4,0},{8,12},{12,8},{16,20},{20,16},{24,28},{28,24},{1,5},{5... | collective-permute-start | bytes 3145736 | tf_op jit(solution)/shard_map/ppermute | solution.py:392
  75.6 1.0 copy-start.6
  78.9 8.6 %collective-permute-start.8 = (f32[16,256]{1,0:T(8,128)}, f32[16,256]{1,0:T(8,128)S(1)}, u32[]{:S(2)}, u32[]{:S(2)}) collective-permute-start(f32[16,256]{1,0:T(8,128)} %share.1), channel_id=1, source_target_pairs={{0,1},{1,2},{2,3},{3,0},{4,5},{5,6},{6,7},{7,4},{8,9},{9,10},{10,1... | collective-permute-start | bytes 49160 | tf_op jit(solution)/shard_map/ppermute | solution.py:451
  84.9 20.0 %collective-permute-start.9 = (f32[16,256]{1,0:T(8,128)}, f32[16,256]{1,0:T(8,128)S(1)}, u32[]{:S(2)}, u32[]{:S(2)}) collective-permute-start(f32[16,256]{1,0:T(8,128)} %share.1), channel_id=1, source_target_pairs={{0,2},{1,3},{2,0},{3,1},{4,6},{5,7},{6,4},{7,5},{8,10},{9,11},{10,... | collective-permute-start | bytes 49160 | tf_op jit(solution)/shard_map/ppermute | solution.py:451
  84.9 20.0 %collective-permute-start.10 = (f32[16,256]{1,0:T(8,128)}, f32[16,256]{1,0:T(8,128)S(1)}, u32[]{:S(2)}, u32[]{:S(2)}) collective-permute-start(f32[16,256]{1,0:T(8,128)} %share.1), channel_id=1, source_target_pairs={{0,3},{1,0},{2,1},{3,2},{4,7},{5,4},{6,5},{7,6},{8,11},{9,8},{10,9... | collective-permute-start | bytes 49160 | tf_op jit(solution)/shard_map/ppermute | solution.py:451
  105.6 4.2 %copy-start.11 = (f32[4,16,256]{2,1,0:T(8,128)}, f32[4,16,256]{2,1,0:T(8,128)S(1)}, u32[]{:S(2)}) copy-start(f32[4,16,256]{2,1,0:T(8,128)S(1)} %get-tuple-element.40.after_ref) | copy-start | bytes 196612
  105.6 35.0 %collective-permute-start.11 = (f32[4,16,256]{2,1,0:T(8,128)S(1)}, f32[4,16,256]{2,1,0:T(8,128)S(1)}, u32[]{:S(2)}, u32[]{:S(2)}) collective-permute-start(f32[4,16,256]{2,1,0:T(8,128)S(1)} %get-tuple-element.40.after_ref), channel_id=1, source_target_pairs={{0,8},{4,12},{8,0},{12,4},{16,24},{20,28},{24,16},{28,20},{1,9},{5... | collective-permute-start | bytes 196616 | tf_op jit(solution)/shard_map/ppermute | solution.py:392
  107.0 33.7 %collective-permute-start.12 = (f32[4,16,256]{2,1,0:T(8,128)S(1)}, f32[4,16,256]{2,1,0:T(8,128)S(1)}, u32[]{:S(2)}, u32[]{:S(2)}) collective-permute-start(f32[4,16,256]{2,1,0:T(8,128)S(1)} %get-tuple-element.40.after_ref), channel_id=1, source_target_pairs={{0,16},{4,20},{8,24},{12,28},{16,0},{20,4},{24,8},{28,12},{1,17},{... | collective-permute-start | bytes 196616 | tf_op jit(solution)/shard_map/ppermute | solution.py:392
  108.6 32.1 %collective-permute-start.13 = (f32[4,16,256]{2,1,0:T(8,128)S(1)}, f32[4,16,256]{2,1,0:T(8,128)S(1)}, u32[]{:S(2)}, u32[]{:S(2)}) collective-permute-start(f32[4,16,256]{2,1,0:T(8,128)S(1)} %get-tuple-element.40.after_ref), channel_id=1, source_target_pairs={{0,24},{4,28},{8,16},{12,20},{16,8},{20,12},{24,0},{28,4},{1,25},{... | collective-permute-start | bytes 196616 | tf_op jit(solution)/shard_map/ppermute | solution.py:392
  140.7 1.4 copy-start.7
  140.7 1.6 collective-permute-start.14
  140.8 1.3 copy-start.4
  142.3 0.7 copy-start.9
  143.0 36.0 %copy-start.5 = (f32[4000,128]{1,0:T(8,128)S(1)}, f32[4000,128]{1,0:T(8,128)}, u32[]{:S(2)}) copy-start(f32[4000,128]{1,0:T(8,128)} %get-tuple-element.22.refs_4_.refs_0_) | copy-start | bytes 6144004
  178.8 3.6 %collective-permute-start.19 = (f32[4,384,256]{2,1,0:T(8,128)}, f32[4,384,256]{2,1,0:T(8,128)S(1)}, u32[]{:S(2)}, u32[]{:S(2)}) collective-permute-start(f32[4,384,256]{2,1,0:T(8,128)} %get-tuple-element.25), channel_id=1, source_target_pairs={{0,4},{4,0},{8,12},{12,8},{16,20},{20,16},{24,28},{28,24},{1,5},{5... | collective-permute-start | bytes 4718600 | tf_op jit(solution)/shard_map/ppermute | solution.py:392
  179.0 48.7 %collective-permute-start.23 = (f32[4000,128]{1,0:T(8,128)S(1)}, f32[4000,128]{1,0:T(8,128)}, u32[]{:S(2)}, u32[]{:S(2)}) collective-permute-start(f32[4000,128]{1,0:T(8,128)S(1)} %copy-done.5), channel_id=1, source_target_pairs={{1,0},{5,4},{9,8},{13,12},{17,16},{21,20},{25,24},{29,28}} | collective-permute-start | bytes 6144008 | tf_op jit(solution)/shard_map/ppermute | solution.py:373
  180.3 47.4 %collective-permute-start.24 = (f32[4000,128]{1,0:T(8,128)}, f32[4000,128]{1,0:T(8,128)}, u32[]{:S(2)}, u32[]{:S(2)}) collective-permute-start(f32[4000,128]{1,0:T(8,128)} %get-tuple-element.23.refs_5_.refs_1_), channel_id=1, source_target_pairs={{2,3},{6,7},{10,11},{14,15},{18,19},{22,23},{26,27},{30,31}} | collective-permute-start | bytes 6144008 | tf_op jit(solution)/shard_map/ppermute | solution.py:373
  184.7 63.8 %collective-permute-start.20 = (f32[384,256]{1,0:T(8,128)S(1)}, f32[384,256]{1,0:T(8,128)}, u32[]{:S(2)}, u32[]{:S(2)}) collective-permute-start(f32[384,256]{1,0:T(8,128)S(1)} %get-tuple-element.30), channel_id=1, source_target_pairs={{0,8},{4,12},{8,0},{12,4},{16,24},{20,28},{24,16},{28,20},{1,9},{5... | collective-permute-start | bytes 1179656 | tf_op jit(solution)/shard_map/ppermute | solution.py:392
  186.0 62.5 %collective-permute-start.21 = (f32[384,256]{1,0:T(8,128)S(1)}, f32[384,256]{1,0:T(8,128)}, u32[]{:S(2)}, u32[]{:S(2)}) collective-permute-start(f32[384,256]{1,0:T(8,128)S(1)} %get-tuple-element.29), channel_id=1, source_target_pairs={{0,16},{4,20},{8,24},{12,28},{16,0},{20,4},{24,8},{28,12},{1,17},{... | collective-permute-start | bytes 1179656 | tf_op jit(solution)/shard_map/ppermute | solution.py:392
  187.5 61.0 %collective-permute-start.22 = (f32[384,256]{1,0:T(8,128)S(1)}, f32[384,256]{1,0:T(8,128)}, u32[]{:S(2)}, u32[]{:S(2)}) collective-permute-start(f32[384,256]{1,0:T(8,128)S(1)} %get-tuple-element.28), channel_id=1, source_target_pairs={{0,24},{4,28},{8,16},{12,20},{16,8},{20,12},{24,0},{28,4},{1,25},{... | collective-permute-start | bytes 1179656 | tf_op jit(solution)/shard_map/ppermute | solution.py:392
  248.5 3.9 %copy-start.10 = (f32[4,128,256]{2,1,0:T(8,128)S(1)}, f32[4,128,256]{2,1,0:T(8,128)}, u32[]{:S(2)}) copy-start(f32[4,128,256]{2,1,0:T(8,128)} %get-tuple-element.26) | copy-start | bytes 1572868
  248.5 3.0 %collective-permute-start.25 = (f32[4,128,256]{2,1,0:T(8,128)}, f32[4,128,256]{2,1,0:T(8,128)S(1)}, u32[]{:S(2)}, u32[]{:S(2)}) collective-permute-start(f32[4,128,256]{2,1,0:T(8,128)} %get-tuple-element.27), channel_id=1, source_target_pairs={{0,4},{4,0},{8,12},{12,8},{16,20},{20,16},{24,28},{28,24},{1,5},{5... | collective-permute-start | bytes 1572872 | tf_op jit(solution)/shard_map/ppermute | solution.py:392
  248.5 19.1 %copy-start.1 = (f32[256,256]{1,0:T(8,128)S(1)}, f32[256,256]{1,0:T(8,128)}, u32[]{:S(2)}) copy-start(f32[256,256]{1,0:T(8,128)} %param.6) | copy-start | bytes 786436
  251.5 0.8 copy-start.8
  254.2 6.3 %collective-permute-start.26 = (f32[128,256]{1,0:T(8,128)S(1)}, f32[128,256]{1,0:T(8,128)S(1)}, u32[]{:S(2)}, u32[]{:S(2)}) collective-permute-start(f32[128,256]{1,0:T(8,128)S(1)} %get-tuple-element.37), channel_id=1, source_target_pairs={{0,8},{4,12},{8,0},{12,4},{16,24},{20,28},{24,16},{28,20},{1,9},{5... | collective-permute-start | bytes 393224 | tf_op jit(solution)/shard_map/ppermute | solution.py:392
  255.5 8.4 %collective-permute-start.27 = (f32[128,256]{1,0:T(8,128)S(1)}, f32[128,256]{1,0:T(8,128)S(1)}, u32[]{:S(2)}, u32[]{:S(2)}) collective-permute-start(f32[128,256]{1,0:T(8,128)S(1)} %get-tuple-element.36), channel_id=1, source_target_pairs={{0,16},{4,20},{8,24},{12,28},{16,0},{20,4},{24,8},{28,12},{1,17},{... | collective-permute-start | bytes 393224 | tf_op jit(solution)/shard_map/ppermute | solution.py:392
  257.0 6.9 %collective-permute-start.28 = (f32[128,256]{1,0:T(8,128)S(1)}, f32[128,256]{1,0:T(8,128)S(1)}, u32[]{:S(2)}, u32[]{:S(2)}) collective-permute-start(f32[128,256]{1,0:T(8,128)S(1)} %get-tuple-element.35), channel_id=1, source_target_pairs={{0,24},{4,28},{8,16},{12,20},{16,8},{20,12},{24,0},{28,4},{1,25},{... | collective-permute-start | bytes 393224 | tf_op jit(solution)/shard_map/ppermute | solution.py:392
  260.5 3.5 %copy-start.12 = (f32[128,256]{1,0:T(8,128)}, f32[128,256]{1,0:T(8,128)S(1)}, u32[]{:S(2)}) copy-start(f32[128,256]{1,0:T(8,128)S(1)} %collective-permute-done.26.refs_1_) | copy-start | bytes 393220
  263.9 0.6 copy-start.13
  263.9 0.7 copy-start.14

commit v4 on v3

v4 whole, which is shorter than its diff:
```python
import functools

import jax
import jax.numpy as jnp
from jax import lax
from jax.experimental import pallas as pl
from jax.experimental.pallas import tpu as pltpu
from jax.sharding import PartitionSpec as P

FB = 512
OFF = 256
VMEM = 60 * 1024 * 1024

F32 = jnp.float32
BF16 = jnp.bfloat16
LONG = pl.CostEstimate(flops=10**11, bytes_accessed=1024, transcendentals=0)
SHORT = pl.CostEstimate(flops=1024, bytes_accessed=1024, transcendentals=0)


def split(x):
    high = x.astype(BF16)
    return high, (x - high.astype(F32)).astype(BF16)


def mul(left, right):
    return jnp.dot(left, right, preferred_element_type=F32)


def three(left, right):
    (lh, ll), (rh, rl) = left, right
    return mul(lh, rh) + mul(ll, rh) + mul(lh, rl)


def stacked(both, high, right):
    rh, rl = right
    m = high.shape[0]
    top = mul(both, rh)
    return top[:m] + top[m:] + mul(high, rl)


def params():
    return pltpu.CompilerParams(
        dimension_semantics=("arbitrary",), vmem_limit_bytes=VMEM
    )


def width(columns, wide):
    return 256 if columns % 256 == 0 and 256 % (columns // wide) == 0 else columns // wide


def whole(shape):
    return pl.BlockSpec(shape, lambda j, *_: (0,) * len(shape), pipeline_mode=pl.Buffered(1))


ANY = pl.BlockSpec(memory_space=pl.ANY)


def gate_kernel(*refs):
    del refs


def gate(held, *others, cost=SHORT):
    count = len(held)
    return pl.pallas_call(
        gate_kernel,
        in_specs=[ANY] * (count + len(others)),
        out_specs=[ANY] * count,
        out_shape=[jax.ShapeDtypeStruct(x.shape, x.dtype) for x in held],
        input_output_aliases={k: k for k in range(count)},
        cost_estimate=cost,
        name="gate",
    )(*held, *others)


def place(value, index, even_ref, odd_ref, first):
    half = index // 2
    rows = value.shape[0]

    @pl.when(index % 2 == 0)
    def _():
        even_ref[half, first : first + rows] = value

    @pl.when(index % 2 == 1)
    def _():
        odd_ref[half, first : first + rows] = value


def take(index, even_ref, odd_ref, rows):
    half = index // 2
    return jnp.where(index % 2 == 0, even_ref[half, rows], odd_ref[half, rows])


def project_kernel(per, each, wide, me_ref, v_ref, r_ref, e_ref, after_ref, even_ref, odd_ref, scaled_ref, own_ref, both_ref):
    j = pl.program_id(0)
    nb = r_ref.shape[1]
    step = v_ref.shape[1]

    @pl.when(j == 0)
    def _():
        turned = r_ref[...].T
        both_ref[:nb], both_ref[nb:] = split(turned)
        scaled_ref[:nb], scaled_ref[nb:] = split(turned * e_ref[...])

    value = stacked(both_ref[...], both_ref[:nb], split(v_ref[...]))
    for g in range(step // per):
        index = (j * (step // per) + g) ^ me_ref[0]
        place(value[:, g * per : (g + 1) * per], index, even_ref, odd_ref, 0)

    @pl.when(j == OFF // step)
    def _():
        own = value[:, OFF % step : OFF % step + each].T
        own_ref[...] = own
        rows = even_ref.shape[1] - nb
        if rows:
            for w in range(wide):
                place(own[w * rows : (w + 1) * rows], w ^ me_ref[0], even_ref, odd_ref, nb)


def project(me, vectors, reflectors, e_row, after, wide, each, rows):
    height, columns = vectors.shape
    nb = reflectors.shape[1]
    per = columns // wide
    step = width(columns, wide)
    half = jax.ShapeDtypeStruct((wide // 2, nb + rows, per), F32)
    return pl.pallas_call(
        functools.partial(project_kernel, per, each, wide),
        grid_spec=pltpu.PrefetchScalarGridSpec(
            num_scalar_prefetch=1,
            grid=(columns // step,),
            in_specs=[
                pl.BlockSpec((height, step), lambda j, *_: (0, j)),
                whole((height, nb)),
                whole((1, height)),
                ANY,
            ],
            out_specs=[
                whole(half.shape),
                whole(half.shape),
                whole((2 * nb, height)),
                whole((each, nb)),
            ],
            scratch_shapes=[pltpu.VMEM((2 * nb, height), BF16)],
        ),
        out_shape=[
            half,
            half,
            jax.ShapeDtypeStruct((2 * nb, height), BF16),
            jax.ShapeDtypeStruct((each, nb), F32),
        ],
        compiler_params=params(),
        cost_estimate=SHORT,
        name="project",
    )(me, vectors, reflectors, e_row, after)


def gather(choice, groups, block_ref):
    first = 0
    for group in groups:
        rows = group[0].shape[0]
        for k, ref in enumerate(group):

            @pl.when(choice == k)
            def _(ref=ref, first=first, rows=rows):
                pltpu.sync_copy(ref, block_ref.at[pl.ds(first, rows)])

        first += rows


def regroup(refs, groups):
    refs = list(refs)
    return [[refs.pop(0) for _ in range(count)] for count in groups]


def load_slots(n, slots, at_ref, scaled, ce_ref, co_ref, coef_in, refs, both_ref, coef_ref, block_ref):
    m = both_ref.shape[0] // 2
    each = block_ref.shape[1]
    nb = coef_ref.shape[1]
    me, z = at_ref[0], at_ref[1]
    left = list(refs)
    for s, groups in enumerate(slots):
        used = sum(groups)
        gather(at_ref[2 + 2 * s], regroup(left[:used], groups), block_ref)
        left = left[used:]
        home = at_ref[3 + 2 * s]
        if coef_in is not None:
            coef_ref[...] = coef_in[home]
        else:
            wide = 2 * ce_ref.shape[0]
            rows = each // wide
            first = pl.multiple_of(nb + (z + n - home) % n * rows, rows)
            for w in range(wide):
                coef_ref[w * rows : (w + 1) * rows] = take(
                    w ^ me, ce_ref, co_ref, pl.ds(first, rows)
                )
        high, low = split(block_ref[...].T - three(split(coef_ref[...]), scaled))
        both_ref[s * each : (s + 1) * each] = high
        both_ref[m + s * each : m + (s + 1) * each] = low


def merged_kernel(n, per, slots, has_coef, at_ref, v_ref, r_ref, scaled_ref, ce_ref, co_ref, after_ref, *refs):
    *refs, out_ref, even_out, odd_out, token_ref, left_ref, both_ref, coef_ref, block_ref = refs
    coef_in, refs = (refs[0], refs[1:]) if has_coef else (None, refs)
    j = pl.program_id(0)
    nb = r_ref.shape[1]
    m = both_ref.shape[0] // 2

    @pl.when(j == 0)
    def _():
        token_ref[...] = jnp.zeros_like(token_ref)
        high, low = split(r_ref[...])
        left_ref[:, :nb] = high
        left_ref[:, nb : 2 * nb] = low
        left_ref[:, 2 * nb :] = high
        scaled = (scaled_ref[:nb], scaled_ref[nb:])
        load_slots(
            n, slots, at_ref, scaled, ce_ref, co_ref, coef_in, refs, both_ref, coef_ref, block_ref
        )

    count = v_ref.shape[1] // per
    indices = [(j * count + g) ^ at_ref[0] for g in range(count)]
    blocks = [take(index, ce_ref, co_ref, slice(0, nb)) for index in indices]
    high, low = split(blocks[0] if count == 1 else jnp.concatenate(blocks, axis=1))
    u = v_ref[...] - mul(left_ref[...], jnp.concatenate([high, high, low], axis=0))
    out_ref[...] = u
    value = stacked(both_ref[...], both_ref[:m], split(u))
    for g, index in enumerate(indices):
        place(value[:, g * per : (g + 1) * per], index, even_out, odd_out, 0)


def late_kernel(n, per, slots, has_coef, has_before, chunk, at_ref, u_ref, scaled_ref, ce_ref, co_ref, after_ref, *refs):
    *refs, even_out, odd_out, both_ref, coef_ref, block_ref = refs
    coef_in, refs = (refs[0], refs[1:]) if has_coef else (None, refs)
    before, refs = (refs[:2], refs[2:]) if has_before else (None, refs)
    j = pl.program_id(0)
    rows = both_ref.shape[1]
    m = both_ref.shape[0] // 2

    @pl.when(j == 0)
    def _():
        nb = coef_ref.shape[1]
        first = chunk * u_ref.shape[0]
        scaled = (scaled_ref[:nb, first : first + rows], scaled_ref[nb:, first : first + rows])
        load_slots(
            n, slots, at_ref, scaled, ce_ref, co_ref, coef_in, refs, both_ref, coef_ref, block_ref
        )

    value = stacked(both_ref[...], both_ref[:m], split(u_ref[:rows]))
    count = u_ref.shape[1] // per
    for g in range(count):
        index = (j * count + g) ^ at_ref[0]
        part = value[:, g * per : (g + 1) * per]
        if before is not None:
            part = part + take(index, *before, slice(0, m))
        place(part, index, even_out, odd_out, 0)


def slot_operands(me, z, slots):
    flat = [x for groups, _, _ in slots for group in groups for x in group]
    counts = [[len(group) for group in groups] for groups, _, _ in slots]
    at = [me[0], z]
    for _, choice, home in slots:
        at += [choice, home]
    return jnp.stack([x.astype(jnp.int32) for x in at]), flat, counts


def merged(me, z, n, vectors, reflectors, scaled, slots, c, coef, after, wide):
    rows, columns = vectors.shape
    nb = reflectors.shape[1]
    per = columns // wide
    step = width(columns, wide)
    at, flat, counts = slot_operands(me, z, slots)
    each = flat[0].shape[1]
    m = each * len(slots)
    half = jax.ShapeDtypeStruct((wide // 2, m, per), F32)
    columns_of = pl.BlockSpec((rows, step), lambda j, *_: (0, j))
    return pl.pallas_call(
        functools.partial(merged_kernel, n, per, counts, bool(coef)),
        grid_spec=pltpu.PrefetchScalarGridSpec(
            num_scalar_prefetch=1,
            grid=(columns // step,),
            in_specs=[columns_of]
            + [whole(x.shape) for x in (reflectors, scaled, *c)]
            + [ANY]
            + [whole(x.shape) for x in coef]
            + [ANY] * len(flat),
            out_specs=[columns_of, whole(half.shape), whole(half.shape), whole((8, 128))],
            scratch_shapes=[
                pltpu.VMEM((rows, 3 * nb), BF16),
                pltpu.VMEM((2 * m, rows), BF16),
                pltpu.VMEM((each, nb), F32),
                pltpu.VMEM((rows, each), F32),
            ],
        ),
        out_shape=[
            jax.ShapeDtypeStruct(vectors.shape, F32),
            half,
            half,
            jax.ShapeDtypeStruct((8, 128), F32),
        ],
        compiler_params=params(),
        cost_estimate=SHORT,
        name="merged",
    )(at, vectors, reflectors, scaled, *c, after, *coef, *flat)


def late(me, z, n, updated, scaled, slots, c, coef, before, after, chunk, wide):
    columns = updated.shape[1]
    per = columns // wide
    step = width(columns, wide)
    at, flat, counts = slot_operands(me, z, slots)
    rows, each = flat[0].shape
    m = each * len(slots)
    half = jax.ShapeDtypeStruct((wide // 2, m, per), F32)
    height = updated.shape[0] - rows if chunk else rows
    return pl.pallas_call(
        functools.partial(late_kernel, n, per, counts, bool(coef), bool(before), chunk),
        grid_spec=pltpu.PrefetchScalarGridSpec(
            num_scalar_prefetch=1,
            grid=(columns // step,),
            in_specs=[pl.BlockSpec((height, step), lambda j, *_: (chunk, j))]
            + [whole(x.shape) for x in (scaled, *c)]
            + [ANY]
            + [whole(x.shape) for x in (*coef, *before)]
            + [ANY] * len(flat),
            out_specs=[whole(half.shape)] * 2,
            scratch_shapes=[
                pltpu.VMEM((2 * m, rows), BF16),
                pltpu.VMEM((each, scaled.shape[0] // 2), F32),
                pltpu.VMEM((rows, each), F32),
            ],
        ),
        out_shape=[half, half],
        compiler_params=params(),
        cost_estimate=SHORT,
        name="late",
    )(at, updated, scaled, *c, after, *coef, *before, *flat)


def fill(at_ref, first_slot, total, each, out_ref):
    for k in range(total.shape[0] // each):
        first = pl.multiple_of(at_ref[first_slot + k] * each, each)
        out_ref[pl.ds(first, each), :] = total[k * each : (k + 1) * each]


def base_kernel(each, at_ref, *refs):
    *refs, out_ref = refs
    out_ref[...] = jnp.zeros_like(out_ref)
    fill(at_ref, 0, functools.reduce(jnp.add, [ref[...] for ref in refs]), each, out_ref)


def base(at, terms, each):
    per = terms[0].shape[1]
    return pl.pallas_call(
        functools.partial(base_kernel, each),
        grid_spec=pltpu.PrefetchScalarGridSpec(
            num_scalar_prefetch=1,
            grid=(1,),
            in_specs=[whole(x.shape) for x in terms],
            out_specs=whole((FB, per)),
        ),
        out_shape=jax.ShapeDtypeStruct((FB, per), F32),
        compiler_params=params(),
        cost_estimate=LONG,
        name="base",
    )(at, *terms)


def last_kernel(each, at_ref, base_ref, *refs):
    *refs, out_ref, total_ref = refs
    total_ref[...] = base_ref[...]
    total = functools.reduce(jnp.add, [ref[...] for ref in refs])
    fill(at_ref, at_ref.shape[0] - total.shape[0] // each, total, each, total_ref)
    out_ref[...] = total_ref[...].T


def last(at, held, terms, each):
    per = held.shape[1]
    operands = [held, *terms]
    return pl.pallas_call(
        functools.partial(last_kernel, each),
        grid_spec=pltpu.PrefetchScalarGridSpec(
            num_scalar_prefetch=1,
            grid=(1,),
            in_specs=[whole(x.shape) for x in operands],
            out_specs=whole((per, FB)),
            scratch_shapes=[pltpu.VMEM((FB, per), F32)],
        ),
        out_shape=jax.ShapeDtypeStruct((per, FB), F32),
        compiler_params=params(),
        cost_estimate=SHORT,
        name="last",
    )(at, *operands)


def arrivals(n):
    order = []
    for z in range(n):
        found = [(hops, 0) for hops in range(1, n) if z + hops < n]
        found += [(hops, 1) for hops in range(1, n) if z - hops >= 0]
        order.append(sorted(found))
    return [[order[z][slot] for z in range(n)] for slot in range(n - 1)]


def hop(held, n, hops, after):
    if hops > 1:
        held = gate(held, *after)
    pairs = [
        [(p, p - 1) for p in range(1, n - hops + 1)],
        [(p, p + 1) for p in range(hops - 1, n - 1)],
    ]
    return held, [lax.ppermute(held[d], "narrow", pairs[d]) for d in (0, 1)]


def options(came, places, z, chunks):
    choices = sorted(set(places))
    which = jnp.int32(0)
    for p, place in enumerate(places):
        which = jnp.where(z == p, choices.index(place), which)
    return [[came[(c, *choice)] for choice in choices] for c in chunks], which


def source(places, z):
    value = jnp.int32(0)
    for p, (hops, direction) in enumerate(places):
        value = jnp.where(z == p, p - hops if direction else p + hops, value)
    return value


def swap(x, wide, distance):
    return lax.ppermute(x, "wide", [(i, i ^ distance) for i in range(wide)])


def scatter_terms(even, odd, wide, after=None):
    other = swap(odd, wide, 1)
    if after is not None:
        (other,) = gate([other], after)
    sums = [even[h] + other[h] for h in range(wide // 2)]
    return [sums[0]] + [swap(sums[h], wide, 2 * h) for h in range(1, wide // 2)]


def collect(x, count):
    even = jnp.stack([x] + [swap(x, lax.axis_size("wide"), 2 * h) for h in range(1, count // 2)])
    return even, swap(even, lax.axis_size("wide"), 1)


def on_device(vectors, reflectors, triangle, energies):
    n = lax.axis_size("narrow")
    wide = lax.axis_size("wide")
    z = lax.axis_index("narrow").astype(jnp.int32)
    me = lax.axis_index("wide").astype(jnp.int32).reshape(1)
    each = FB // n
    height, columns = vectors.shape
    nb = reflectors.shape[1]
    per = columns // wide
    e_row = energies.reshape(1, height)

    cut = -(-height * 4 // 7 // 128) * 128
    bounds = [(0, cut), (cut, height)]
    chunks = [
        energies[first:end, None] * vectors[first:end, OFF : OFF + each] for first, end in bounds
    ]
    came = {}

    def travel(c, held, hops, after):
        held, passed = hop(held, n, hops, after)
        for d in (0, 1):
            if hops > 1:
                came[(c, hops - 1, d)] = held[d]
            came[(c, hops, d)] = passed[d]
        return passed

    held = [travel(c, [chunk, chunk], 1, []) for c, chunk in enumerate(chunks)]
    table = arrivals(n)
    at = jnp.stack([z] + [source(places, z) for places in table])

    rows = each // wide if per == nb and (each // wide) % 8 == 0 else 0
    even, odd, scaled, own = project(me, vectors, reflectors, e_row, chunks[1], wide, each, rows)
    (odd,) = gate([odd], *held[0])
    terms = scatter_terms(even, odd, wide)
    terms[0] = gate(terms[:1], *held[1])[0]
    projected = functools.reduce(jnp.add, terms)
    highest = lax.Precision.HIGHEST
    coefficients = jnp.dot(triangle, projected[:nb], precision=highest)
    turn = (((1,), (1,)), ((), ()))
    if rows:
        mine = lax.dot_general(projected[nb:], triangle, turn, precision=highest)
        shares = [mine] + [
            lax.ppermute(mine, "narrow", [(p, (p + s) % n) for p in range(n)]) for s in range(1, n)
        ]
        coefficients = jnp.concatenate([coefficients, *shares], axis=0)
        ready, coef = shares[1:], []
    else:
        own = lax.dot_general(lax.psum(own, "wide"), triangle, turn, precision=highest)
        coef = [lax.all_gather(own, "narrow")]
        ready = coef
    c = collect(coefficients, wide)

    for hops in range(2, n):
        for k in range(len(chunks)):
            if hops == 2:
                held[k] = travel(k, held[k], hops, ready)
            elif k == 0:
                held[k] = travel(k, held[k], hops, [])
    slots = [([[chunk] for chunk in chunks], jnp.int32(0), z)]
    slots.append((*options(came, table[0], z, (0, 1)), at[1]))
    updated, *halves, token = merged(
        me, z, n, vectors, reflectors, scaled, slots, c, coef, came[(0, min(2, n - 1), 0)], wide
    )
    for hops in range(3, n):
        held[1] = travel(1, held[1], hops, [token])
    even, odd = halves
    (odd,) = gate([odd], *held[0])
    middle = scatter_terms(even, odd, wide)
    (token,) = gate([token], middle[0])
    halves = []
    for k in (0, 1):
        slots = [
            (*options(came, table[slot], z, (k,)), at[1 + slot]) for slot in range(1, n - 1)
        ]
        halves = late(me, z, n, updated, scaled, slots, c, coef, halves, token, k, wide)
    held = base(at, middle, each)
    fock_block = last(at, held, scatter_terms(*halves, wide, held), each)
    return (updated, fock_block)


def solution(mesh):
    return jax.shard_map(
        on_device,
        mesh=mesh,
        in_specs=(P("wide", "narrow"), P("wide", None), P(), P("wide")),
        out_specs=(P("wide", "narrow"), P(("narrow", "wide"), None)),
        check_vma=False,
    )
```

time: 271 us -> 257 us (0.948)
  the two profiles are of different devices: /device:TPU:0 before, /device:TPU:8 now
where the time goes in v4:
time: 257 us; the launch traced here: 255 us
  Pallas kernels  133 us (52%)
  starting transfers between devices  52 us (20%)
  waiting for transfers between devices  42.3 us (16%)
  local copies, waits for them, and re-layouts  13.5 us (5%)
  other arithmetic  13.3 us (5%)
    pallas_call x1, Pallas kernels, merged(): pl.pallas_call(functools.partial(merged_kernel, n, per, counts, bool(coef...  62.6 us
    pallas_call x2, Pallas kernels, late(): pl.pallas_call(functools.partial(late_kernel, n, per, counts, bool(coef),...  40.3 us
    ppermute x12, starting transfers between devices, hop(): return (held, [lax.ppermute(held[d], 'narrow', pairs[d]) for d in (0, 1)])  32.9 us
    pallas_call x1, Pallas kernels, project(): pl.pallas_call(functools.partial(project_kernel, per, each, wide), grid_s...  23.9 us
    ppermute x16, waiting for transfers between devices, swap(): return lax.ppermute(x, 'wide', [(i, i ^ distance) for i in range(wide)])  22.7 us
    ppermute x12, waiting for transfers between devices, hop(): return (held, [lax.ppermute(held[d], 'narrow', pairs[d]) for d in (0, 1)])  17.8 us
    ppermute x16, starting transfers between devices, swap(): return lax.ppermute(x, 'wide', [(i, i ^ distance) for i in range(wide)])  14.1 us
    unnamed x48, local copies, waits for them, and re-layouts  10.7 us
  transfers between devices with their start and end apart: 31, of which 12 were waited for; matrix products, arithmetic and copies ran while one was open for 4% of the time, Pallas kernels for 51%

profile of v4, /device:TPU:8, one launch (start us, length us, event | category | flops | bytes accessed | tf_op | source)
XLA Modules:
  0.0 255.4 jit_solution(15010105980605705212)
XLA Ops:
  1.4 2.7 %slice_multiply_fusion.refs_0_ = f32[2304,128]{1,0:T(8,128)} fusion(f32[4000,2048]{1,0:T(8,128)} %v_ref.3, f32[2304]{0:T(1024)S(1)} %slice.93), kind=kLoop, calls=%fused_computation.1 | loop fusion | flops 294912 | bytes 2368512 | tf_op jit(solution)/shard_map/mul | solution.py:460
  4.1 1.9 collective-permute-start
  6.0 3.9 %collective-permute-start.1 = (f32[2304,128]{1,0:T(8,128)}, f32[2304,128]{1,0:T(8,128)S(1)}, u32[]{:S(2)}, u32[]{:S(2)}) collective-permute-start(f32[2304,128]{1,0:T(8,128)} %slice_multiply_fusion.refs_0_), channel_id=1, source_target_pairs={{0,1},{1,2},{2,3},{4,5},{5,6},{6,7},{8,9},{9,10},{10,11},{12,13},{... | collective-permute-start | bytes 3538952 | tf_op jit(solution)/shard_map/ppermute | solution.py:411
  9.9 2.4 slice_multiply_fusion.1.after_ref.refs_1_
  12.3 23.9 %project.1 = (f32[4,272,256]{2,1,0:T(8,128)}, f32[4,272,256]{2,1,0:T(8,128)}, bf16[512,4000]{1,0:T(8,128)(2,1)}, f32[128,256]{1,0:T(8,128)}) custom-call(s32[1]{0:T(128)} %bitcast.me_ref, f32[4000,2048]{1,0:T(8,128)} %v_ref.3, f32[4000,256]{1,0:T(8,128)} %r_ref.3, f32[1,4000]{1,0:T(1,128)} %bitcast.47, f32[1696,128]{1,0:T(8,128)} %slice_multiply_fusion.1.after_ref.refs_1_), custom_call_target="tpu_custom_call" | custom-call | flops 1024 | bytes 1024 | tf_op jit(solution)/shard_map/project/pallas_call | solution.py:125
  36.2 1.0 copy-done.6
  37.7 1.2 copy-done.7
  38.9 2.0 collective-permute-start.3
  40.8 3.9 %collective-permute-start.4 = (f32[1696,128]{1,0:T(8,128)S(1)}, f32[1696,128]{1,0:T(8,128)S(1)}, u32[]{:S(2)}, u32[]{:S(2)}) collective-permute-start(f32[1696,128]{1,0:T(8,128)S(1)} %copy-done.7), channel_id=1, source_target_pairs={{0,1},{1,2},{2,3},{4,5},{5,6},{6,7},{8,9},{9,10},{10,11},{12,13},{... | collective-permute-start | bytes 2605064 | tf_op jit(solution)/shard_map/ppermute | solution.py:411
  44.7 2.2 fusion.3
  46.9 2.4 collective-permute-start.7
  50.4 10.9 %collective-permute-done.3.refs_1_.refs_0_ = f32[1696,128]{1,0:T(8,128)S(1)} collective-permute-done((f32[1696,128]{1,0:T(8,128)S(1)}, f32[1696,128]{1,0:T(8,128)S(1)}, u32[]{:S(2)}, u32[]{:S(2)}) %collective-permute-start.3) | collective-permute-done | bytes 868384 | tf_op jit(solution)/shard_map/ppermute | solution.py:411
  61.3 1.9 collective-permute-done.4.refs_2_.refs_1_
  63.2 0.9 copy-done.5
  64.2 1.3 add_add_fusion
  66.1 1.8 collective-permute-start.8
  67.9 1.2 collective-permute-start.9
  69.1 1.9 collective-permute-start.10
  71.1 1.5 collective-permute-done.9.refs_3_
  73.8 3.6 %collective-permute-start.15 = (f32[2304,128]{1,0:T(8,128)}, f32[2304,128]{1,0:T(8,128)S(1)}, u32[]{:S(2)}, u32[]{:S(2)}) collective-permute-start(f32[2304,128]{1,0:T(8,128)} %get-tuple-element.24.refs_2_), channel_id=1, source_target_pairs={{1,0},{2,1},{5,4},{6,5},{9,8},{10,9},{13,12},{14,13},{17,16},{18,1... | collective-permute-start | bytes 3538952 | tf_op jit(solution)/shard_map/ppermute | solution.py:411
  77.3 3.4 %collective-permute-start.16 = (f32[2304,128]{1,0:T(8,128)}, f32[2304,128]{1,0:T(8,128)}, u32[]{:S(2)}, u32[]{:S(2)}) collective-permute-start(f32[2304,128]{1,0:T(8,128)} %get-tuple-element.25.refs_3_.refs_0_), channel_id=1, source_target_pairs={{1,2},{2,3},{5,6},{6,7},{9,10},{10,11},{13,14},{14,15},{17,18},{18... | collective-permute-start | bytes 3538952 | tf_op jit(solution)/shard_map/ppermute | solution.py:411
  82.8 2.5 collective-permute-start.13
  86.3 7.0 %collective-permute-done.13 = f32[320,256]{1,0:T(8,128)S(1)} collective-permute-done((f32[320,256]{1,0:T(8,128)S(1)}, f32[320,256]{1,0:T(8,128)S(1)}, u32[]{:S(2)}, u32[]{:S(2)}) %collective-permute-start.13) | collective-permute-done | bytes 327712 | tf_op jit(solution)/shard_map/ppermute | solution.py:430
  93.3 3.4 %collective-permute-done.12 = f32[320,256]{1,0:T(8,128)S(1)} collective-permute-done((f32[320,256]{1,0:T(8,128)S(1)}, f32[320,256]{1,0:T(8,128)S(1)}, u32[]{:S(2)}, u32[]{:S(2)}) %collective-permute-start.12) | collective-permute-done | bytes 327712 | tf_op jit(solution)/shard_map/ppermute | solution.py:430
  97.0 3.6 %collective-permute-done.15.refs_0_ = f32[2304,128]{1,0:T(8,128)S(1)} collective-permute-done((f32[2304,128]{1,0:T(8,128)}, f32[2304,128]{1,0:T(8,128)S(1)}, u32[]{:S(2)}, u32[]{:S(2)}) %collective-permute-start.15) | collective-permute-done | bytes 1179680 | tf_op jit(solution)/shard_map/ppermute | solution.py:411
  100.6 1.4 collective-permute-done.16.refs_1_
  101.9 4.3 %collective-permute-start.17 = (f32[2304,128]{1,0:T(8,128)}, f32[2304,128]{1,0:T(8,128)}, u32[]{:S(2)}, u32[]{:S(2)}) collective-permute-start(f32[2304,128]{1,0:T(8,128)} %get-tuple-element.26.after_ref.refs_1_.refs_3_), channel_id=1, source_target_pairs={{1,0},{5,4},{9,8},{13,12},{17,16},{21,20},{25,24},{29,28}} | collective-permute-start | bytes 3538952 | tf_op jit(solution)/shard_map/ppermute | solution.py:411
  106.2 1.7 collective-permute-start.18
  107.9 1.9 collective-permute-start.23
  109.8 4.2 %collective-permute-start.24 = (f32[1696,128]{1,0:T(8,128)}, f32[1696,128]{1,0:T(8,128)S(1)}, u32[]{:S(2)}, u32[]{:S(2)}) collective-permute-start(f32[1696,128]{1,0:T(8,128)} %get-tuple-element.28.refs_5_.refs_2_), channel_id=1, source_target_pairs={{1,2},{2,3},{5,6},{6,7},{9,10},{10,11},{13,14},{14,15},{17,18},{18... | collective-permute-start | bytes 2605064 | tf_op jit(solution)/shard_map/ppermute | solution.py:411
  114.7 62.6 %merged.1 = (f32[4000,2048]{1,0:T(8,128)}, f32[4,256,256]{2,1,0:T(8,128)}, f32[4,256,256]{2,1,0:T(8,128)}, f32[8,128]{1,0:T(8,128)}) custom-call(s32[6]{0:T(128)} %stack.55.at_ref, f32[4000,2048]{1,0:T(8,128)} %v_ref.3, f32[4000,256]{1,0:T(8,128)} %r_ref.3, bf16[512,4000]{1,0:T(8,128)(2,1)} %get-tuple-element.21.scaled_ref, f32[4,320,256]{2,1,0:T(8,128)} %copy-done.2, ...), custom_call_target="tpu_custom_call" | custom-call | flops 1024 | bytes 1024 | tf_op jit(solution)/shard_map/merged/pallas_call | solution.py:276
  177.5 0.9 copy-done.9
  178.7 1.3 collective-permute-start.25
  180.0 0.9 collective-permute-start.26
  181.0 2.1 fusion.9
  183.1 1.5 collective-permute-start.20
  184.6 1.5 collective-permute-start.21
  187.9 21.0 %late.2 = (f32[4,256,256]{2,1,0:T(8,128)}, f32[4,256,256]{2,1,0:T(8,128)}) custom-call(s32[6]{0:T(128)} %stack.66.at_ref, f32[4000,2048]{1,0:T(8,128)} %get-tuple-element.19.u_ref, bf16[512,4000]{1,0:T(8,128)(2,1)} %get-tuple-element.21.scaled_ref, f32[4,320,256]{2,1,0:T(8,128)} %copy-done.2, f32[4,320,256]{2,1,0:T(8,128)} %collective-permute-done.14.co_ref, ...), custom_call_target="tpu_custom_call" | custom-call | flops 1024 | bytes 1024 | tf_op jit(solution)/shard_map/late/pallas_call | solution.py:315
  208.8 0.9 copy-done.14
  210.1 19.4 %late.3 = (f32[4,256,256]{2,1,0:T(8,128)}, f32[4,256,256]{2,1,0:T(8,128)}) custom-call(s32[6]{0:T(128)} %stack.66.at_ref, f32[4000,2048]{1,0:T(8,128)} %get-tuple-element.19.u_ref, bf16[512,4000]{1,0:T(8,128)(2,1)} %get-tuple-element.21.scaled_ref, f32[4,320,256]{2,1,0:T(8,128)} %copy-done.2, f32[4,320,256]{2,1,0:T(8,128)} %collective-permute-done.14.co_ref, ...), custom_call_target="tpu_custom_call" | custom-call | flops 1024 | bytes 1024 | tf_op jit(solution)/shard_map/late/pallas_call | solution.py:315
  229.5 2.7 %base.1.refs_1_.base_ref = f32[512,256]{1,0:T(8,128)} custom-call(s32[4]{0:T(128)} %pad_add_fusion.at_ref, f32[256,256]{1,0:T(8,128)} %get-tuple-element.51.refs_0_.refs_1_, f32[256,256]{1,0:T(8,128)} %collective-permute-done.20.refs_1_, f32[256,256]{1,0:T(8,128)} %collective-permute-done.21.refs_2_, f32[256,256]{1,0:T(8,128)} %collective-permute-done.22.refs_3_), custom_call_target="tpu_custom_call" | custom-call | flops 99999997952 | bytes 1024 | tf_op jit(solution)/shard_map/base/pallas_call | solution.py:353
  232.4 1.0 copy-done.11
  233.8 2.1 fusion.5
  235.9 1.5 collective-permute-start.28
  237.4 1.5 collective-permute-start.29
  239.4 5.6 %collective-permute-done.28.refs_1_ = f32[256,256]{1,0:T(8,128)S(1)} collective-permute-done((f32[256,256]{1,0:T(8,128)S(1)}, f32[256,256]{1,0:T(8,128)S(1)}, u32[]{:S(2)}, u32[]{:S(2)}) %collective-permute-start.28) | collective-permute-done | bytes 262176 | tf_op jit(solution)/shard_map/ppermute | solution.py:430
  245.0 6.4 %collective-permute-done.29.refs_2_ = f32[256,256]{1,0:T(8,128)S(1)} collective-permute-done((f32[256,256]{1,0:T(8,128)S(1)}, f32[256,256]{1,0:T(8,128)S(1)}, u32[]{:S(2)}, u32[]{:S(2)}) %collective-permute-start.29) | collective-permute-done | bytes 262176 | tf_op jit(solution)/shard_map/ppermute | solution.py:430
  252.3 3.1 %last.1 = f32[256,512]{1,0:T(8,128)} custom-call(s32[4]{0:T(128)} %pad_add_fusion.at_ref, f32[512,256]{1,0:T(8,128)} %base.1.refs_1_.base_ref, f32[256,256]{1,0:T(8,128)} %get-tuple-element.47.refs_0_, f32[256,256]{1,0:T(8,128)} %copy-done.16, f32[256,256]{1,0:T(8,128)} %copy-done.17, f32[256,256]{1,0:T(8,128)} %copy-done.18), custom_call_target="tpu_custom_call" | custom-call | flops 1024 | bytes 1024 | tf_op jit(solution)/shard_map/last/pallas_call | solution.py:379
  (92 shorter events, 12.7 us)
Async XLA Ops:
  0.6 64.8 %copy-start = (f32[256,256]{1,0:T(8,128)S(1)}, f32[256,256]{1,0:T(8,128)}, u32[]{:S(2)}) copy-start(f32[256,256]{1,0:T(8,128)} %param.6) | copy-start | bytes 786436
  1.4 8.5 %copy-start.22 = (f32[4000]{0:T(1024)S(1)}, f32[4000]{0:T(1024)}, u32[]{:S(2)}) copy-start(f32[4000]{0:T(1024)} %param.7) | copy-start | bytes 48004
  4.1 32.1 %collective-permute-start = (f32[2304,128]{1,0:T(8,128)}, f32[2304,128]{1,0:T(8,128)S(1)}, u32[]{:S(2)}, u32[]{:S(2)}) collective-permute-start(f32[2304,128]{1,0:T(8,128)} %slice_multiply_fusion.refs_0_), channel_id=1, source_target_pairs={{1,0},{2,1},{3,2},{5,4},{6,5},{7,6},{9,8},{10,9},{11,10},{13,12},{... | collective-permute-start | bytes 3538952 | tf_op jit(solution)/shard_map/ppermute | solution.py:411
  6.0 30.2 %collective-permute-start.1 = (f32[2304,128]{1,0:T(8,128)}, f32[2304,128]{1,0:T(8,128)S(1)}, u32[]{:S(2)}, u32[]{:S(2)}) collective-permute-start(f32[2304,128]{1,0:T(8,128)} %slice_multiply_fusion.refs_0_), channel_id=1, source_target_pairs={{0,1},{1,2},{2,3},{4,5},{5,6},{6,7},{8,9},{9,10},{10,11},{12,13},{... | collective-permute-start | bytes 3538952 | tf_op jit(solution)/shard_map/ppermute | solution.py:411
  36.2 1.0 copy-start.6
  36.2 1.5 copy-start.4
  37.7 1.2 copy-start.7
  37.7 7.0 %collective-permute-start.2 = (f32[4,272,256]{2,1,0:T(8,128)}, f32[4,272,256]{2,1,0:T(8,128)S(1)}, u32[]{:S(2)}, u32[]{:S(2)}) collective-permute-start(f32[4,272,256]{2,1,0:T(8,128)} %gate.9), channel_id=1, source_target_pairs={{0,4},{4,0},{8,12},{12,8},{16,20},{20,16},{24,28},{28,24},{1,5},{5... | collective-permute-start | bytes 3342344 | tf_op jit(solution)/shard_map/ppermute | solution.py:430
  38.9 22.4 %collective-permute-start.3 = (f32[1696,128]{1,0:T(8,128)S(1)}, f32[1696,128]{1,0:T(8,128)S(1)}, u32[]{:S(2)}, u32[]{:S(2)}) collective-permute-start(f32[1696,128]{1,0:T(8,128)S(1)} %copy-done.7), channel_id=1, source_target_pairs={{1,0},{2,1},{3,2},{5,4},{6,5},{7,6},{9,8},{10,9},{11,10},{13,12},{... | collective-permute-start | bytes 2605064 | tf_op jit(solution)/shard_map/ppermute | solution.py:411
  40.8 22.4 %collective-permute-start.4 = (f32[1696,128]{1,0:T(8,128)S(1)}, f32[1696,128]{1,0:T(8,128)S(1)}, u32[]{:S(2)}, u32[]{:S(2)}) collective-permute-start(f32[1696,128]{1,0:T(8,128)S(1)} %copy-done.7), channel_id=1, source_target_pairs={{0,1},{1,2},{2,3},{4,5},{5,6},{6,7},{8,9},{9,10},{10,11},{12,13},{... | collective-permute-start | bytes 2605064 | tf_op jit(solution)/shard_map/ppermute | solution.py:411
  46.9 17.3 %collective-permute-start.7 = (f32[272,256]{1,0:T(8,128)}, f32[272,256]{1,0:T(8,128)}, u32[]{:S(2)}, u32[]{:S(2)}) collective-permute-start(f32[272,256]{1,0:T(8,128)} %get-tuple-element.41), channel_id=1, source_target_pairs={{0,24},{4,28},{8,16},{12,20},{16,8},{20,12},{24,0},{28,4},{1,25},{... | collective-permute-start | bytes 835592 | tf_op jit(solution)/shard_map/ppermute | solution.py:430
  49.3 14.8 %collective-permute-start.6 = (f32[272,256]{1,0:T(8,128)S(1)}, f32[272,256]{1,0:T(8,128)}, u32[]{:S(2)}, u32[]{:S(2)}) collective-permute-start(f32[272,256]{1,0:T(8,128)S(1)} %get-tuple-element.42), channel_id=1, source_target_pairs={{0,16},{4,20},{8,24},{12,28},{16,0},{20,4},{24,8},{28,12},{1,17},{... | collective-permute-start | bytes 835592 | tf_op jit(solution)/shard_map/ppermute | solution.py:430
  49.8 14.3 %collective-permute-start.5 = (f32[272,256]{1,0:T(8,128)S(1)}, f32[272,256]{1,0:T(8,128)}, u32[]{:S(2)}, u32[]{:S(2)}) collective-permute-start(f32[272,256]{1,0:T(8,128)S(1)} %get-tuple-element.40), channel_id=1, source_target_pairs={{0,8},{4,12},{8,0},{12,4},{16,24},{20,28},{24,16},{28,20},{1,9},{5... | collective-permute-start | bytes 835592 | tf_op jit(solution)/shard_map/ppermute | solution.py:430
  61.3 1.9 copy-start.8
  66.1 4.9 %collective-permute-start.8 = (f32[16,256]{1,0:T(8,128)S(1)}, f32[16,256]{1,0:T(8,128)S(1)}, u32[]{:S(2)}, u32[]{:S(2)}) collective-permute-start(f32[16,256]{1,0:T(8,128)S(1)} %get-tuple-element.53), channel_id=1, source_target_pairs={{0,1},{1,2},{2,3},{3,0},{4,5},{5,6},{6,7},{7,4},{8,9},{9,10},{10,1... | collective-permute-start | bytes 49160 | tf_op jit(solution)/shard_map/ppermute | solution.py:488
  67.9 4.6 %collective-permute-start.9 = (f32[16,256]{1,0:T(8,128)S(1)}, f32[16,256]{1,0:T(8,128)S(1)}, u32[]{:S(2)}, u32[]{:S(2)}) collective-permute-start(f32[16,256]{1,0:T(8,128)S(1)} %get-tuple-element.53), channel_id=1, source_target_pairs={{0,2},{1,3},{2,0},{3,1},{4,6},{5,7},{6,4},{7,5},{8,10},{9,11},{10,... | collective-permute-start | bytes 49160 | tf_op jit(solution)/shard_map/ppermute | solution.py:488
  69.1 3.7 %collective-permute-start.10 = (f32[16,256]{1,0:T(8,128)S(1)}, f32[16,256]{1,0:T(8,128)S(1)}, u32[]{:S(2)}, u32[]{:S(2)}) collective-permute-start(f32[16,256]{1,0:T(8,128)S(1)} %get-tuple-element.53), channel_id=1, source_target_pairs={{0,3},{1,0},{2,1},{3,2},{4,7},{5,4},{6,5},{7,6},{8,11},{9,8},{10,9... | collective-permute-start | bytes 49160 | tf_op jit(solution)/shard_map/ppermute | solution.py:488
  71.1 1.8 copy-start.19
  73.8 26.8 %collective-permute-start.15 = (f32[2304,128]{1,0:T(8,128)}, f32[2304,128]{1,0:T(8,128)S(1)}, u32[]{:S(2)}, u32[]{:S(2)}) collective-permute-start(f32[2304,128]{1,0:T(8,128)} %get-tuple-element.24.refs_2_), channel_id=1, source_target_pairs={{1,0},{2,1},{5,4},{6,5},{9,8},{10,9},{13,12},{14,13},{17,16},{18,1... | collective-permute-start | bytes 3538952 | tf_op jit(solution)/shard_map/ppermute | solution.py:411
  77.3 24.6 %collective-permute-start.16 = (f32[2304,128]{1,0:T(8,128)}, f32[2304,128]{1,0:T(8,128)}, u32[]{:S(2)}, u32[]{:S(2)}) collective-permute-start(f32[2304,128]{1,0:T(8,128)} %get-tuple-element.25.refs_3_.refs_0_), channel_id=1, source_target_pairs={{1,2},{2,3},{5,6},{6,7},{9,10},{10,11},{13,14},{14,15},{17,18},{18... | collective-permute-start | bytes 3538952 | tf_op jit(solution)/shard_map/ppermute | solution.py:411
  82.8 10.4 %collective-permute-start.13 = (f32[320,256]{1,0:T(8,128)S(1)}, f32[320,256]{1,0:T(8,128)S(1)}, u32[]{:S(2)}, u32[]{:S(2)}) collective-permute-start(f32[320,256]{1,0:T(8,128)S(1)} %constant_dynamic-update-slice_fusion), channel_id=1, source_target_pairs={{0,24},{4,28},{8,16},{12,20},{16,8},{20,12},{24,0},{28,4},{1,25},{... | collective-permute-start | bytes 983048 | tf_op jit(solution)/shard_map/ppermute | solution.py:430
  85.3 11.4 %collective-permute-start.12 = (f32[320,256]{1,0:T(8,128)S(1)}, f32[320,256]{1,0:T(8,128)S(1)}, u32[]{:S(2)}, u32[]{:S(2)}) collective-permute-start(f32[320,256]{1,0:T(8,128)S(1)} %constant_dynamic-update-slice_fusion), channel_id=1, source_target_pairs={{0,16},{4,20},{8,24},{12,28},{16,0},{20,4},{24,8},{28,12},{1,17},{... | collective-permute-start | bytes 983048 | tf_op jit(solution)/shard_map/ppermute | solution.py:430
  85.8 11.0 %collective-permute-start.11 = (f32[320,256]{1,0:T(8,128)S(1)}, f32[320,256]{1,0:T(8,128)S(1)}, u32[]{:S(2)}, u32[]{:S(2)}) collective-permute-start(f32[320,256]{1,0:T(8,128)S(1)} %constant_dynamic-update-slice_fusion), channel_id=1, source_target_pairs={{0,8},{4,12},{8,0},{12,4},{16,24},{20,28},{24,16},{28,20},{1,9},{5... | collective-permute-start | bytes 983048 | tf_op jit(solution)/shard_map/ppermute | solution.py:430
  96.9 5.0 %copy-start.2 = (f32[4,320,256]{2,1,0:T(8,128)}, f32[4,320,256]{2,1,0:T(8,128)S(1)}, u32[]{:S(2)}) copy-start(f32[4,320,256]{2,1,0:T(8,128)S(1)} %pad_maximum_fusion.ce_ref) | copy-start | bytes 3932164
  96.9 17.9 %collective-permute-start.14 = (f32[4,320,256]{2,1,0:T(8,128)S(1)}, f32[4,320,256]{2,1,0:T(8,128)}, u32[]{:S(2)}, u32[]{:S(2)}) collective-permute-start(f32[4,320,256]{2,1,0:T(8,128)S(1)} %pad_maximum_fusion.ce_ref), channel_id=1, source_target_pairs={{0,4},{4,0},{8,12},{12,8},{16,20},{20,16},{24,28},{28,24},{1,5},{5... | collective-permute-start | bytes 3932168 | tf_op jit(solution)/shard_map/ppermute | solution.py:430
  100.6 1.4 copy-start.3
  101.9 75.4 %collective-permute-start.17 = (f32[2304,128]{1,0:T(8,128)}, f32[2304,128]{1,0:T(8,128)}, u32[]{:S(2)}, u32[]{:S(2)}) collective-permute-start(f32[2304,128]{1,0:T(8,128)} %get-tuple-element.26.after_ref.refs_1_.refs_3_), channel_id=1, source_target_pairs={{1,0},{5,4},{9,8},{13,12},{17,16},{21,20},{25,24},{29,28}} | collective-permute-start | bytes 3538952 | tf_op jit(solution)/shard_map/ppermute | solution.py:411
  106.2 71.1 %collective-permute-start.18 = (f32[2304,128]{1,0:T(8,128)}, f32[2304,128]{1,0:T(8,128)}, u32[]{:S(2)}, u32[]{:S(2)}) collective-permute-start(f32[2304,128]{1,0:T(8,128)} %get-tuple-element.32.refs_2_.refs_4_), channel_id=1, source_target_pairs={{2,3},{6,7},{10,11},{14,15},{18,19},{22,23},{26,27},{30,31}} | collective-permute-start | bytes 3538952 | tf_op jit(solution)/shard_map/ppermute | solution.py:411
  107.9 69.6 %collective-permute-start.23 = (f32[1696,128]{1,0:T(8,128)}, f32[1696,128]{1,0:T(8,128)S(1)}, u32[]{:S(2)}, u32[]{:S(2)}) collective-permute-start(f32[1696,128]{1,0:T(8,128)} %get-tuple-element.27.refs_4_), channel_id=1, source_target_pairs={{1,0},{2,1},{5,4},{6,5},{9,8},{10,9},{13,12},{14,13},{17,16},{18,1... | collective-permute-start | bytes 2605064 | tf_op jit(solution)/shard_map/ppermute | solution.py:411
  109.8 67.7 %collective-permute-start.24 = (f32[1696,128]{1,0:T(8,128)}, f32[1696,128]{1,0:T(8,128)S(1)}, u32[]{:S(2)}, u32[]{:S(2)}) collective-permute-start(f32[1696,128]{1,0:T(8,128)} %get-tuple-element.28.refs_5_.refs_2_), channel_id=1, source_target_pairs={{1,2},{2,3},{5,6},{6,7},{9,10},{10,11},{13,14},{14,15},{17,18},{18... | collective-permute-start | bytes 2605064 | tf_op jit(solution)/shard_map/ppermute | solution.py:411
  177.4 3.6 %copy-start.12 = (f32[4,256,256]{2,1,0:T(8,128)S(1)}, f32[4,256,256]{2,1,0:T(8,128)}, u32[]{:S(2)}) copy-start(f32[4,256,256]{2,1,0:T(8,128)} %get-tuple-element.30) | copy-start | bytes 3145732
  177.4 3.6 %collective-permute-start.19 = (f32[4,256,256]{2,1,0:T(8,128)}, f32[4,256,256]{2,1,0:T(8,128)}, u32[]{:S(2)}, u32[]{:S(2)}) collective-permute-start(f32[4,256,256]{2,1,0:T(8,128)} %gate.14), channel_id=1, source_target_pairs={{0,4},{4,0},{8,12},{12,8},{16,20},{20,16},{24,28},{28,24},{1,5},{5... | collective-permute-start | bytes 3145736 | tf_op jit(solution)/shard_map/ppermute | solution.py:430
  177.5 1.2 copy-start.10
  178.7 30.1 %collective-permute-start.25 = (f32[1696,128]{1,0:T(8,128)}, f32[1696,128]{1,0:T(8,128)S(1)}, u32[]{:S(2)}, u32[]{:S(2)}) collective-permute-start(f32[1696,128]{1,0:T(8,128)} %get-tuple-element.36.refs_3_.refs_5_), channel_id=1, source_target_pairs={{1,0},{5,4},{9,8},{13,12},{17,16},{21,20},{25,24},{29,28}} | collective-permute-start | bytes 2605064 | tf_op jit(solution)/shard_map/ppermute | solution.py:411
  180.0 28.8 %collective-permute-start.26 = (f32[1696,128]{1,0:T(8,128)}, f32[1696,128]{1,0:T(8,128)S(1)}, u32[]{:S(2)}, u32[]{:S(2)}) collective-permute-start(f32[1696,128]{1,0:T(8,128)} %get-tuple-element.37.refs_4_.refs_6_), channel_id=1, source_target_pairs={{2,3},{6,7},{10,11},{14,15},{18,19},{22,23},{26,27},{30,31}} | collective-permute-start | bytes 2605064 | tf_op jit(solution)/shard_map/ppermute | solution.py:411
  183.1 46.4 %collective-permute-start.20 = (f32[256,256]{1,0:T(8,128)}, f32[256,256]{1,0:T(8,128)}, u32[]{:S(2)}, u32[]{:S(2)}) collective-permute-start(f32[256,256]{1,0:T(8,128)} %get-tuple-element.50), channel_id=1, source_target_pairs={{0,8},{4,12},{8,0},{12,4},{16,24},{20,28},{24,16},{28,20},{1,9},{5... | collective-permute-start | bytes 786440 | tf_op jit(solution)/shard_map/ppermute | solution.py:430
  184.6 44.9 %collective-permute-start.21 = (f32[256,256]{1,0:T(8,128)S(1)}, f32[256,256]{1,0:T(8,128)}, u32[]{:S(2)}, u32[]{:S(2)}) collective-permute-start(f32[256,256]{1,0:T(8,128)S(1)} %get-tuple-element.49), channel_id=1, source_target_pairs={{0,16},{4,20},{8,24},{12,28},{16,0},{20,4},{24,8},{28,12},{1,17},{... | collective-permute-start | bytes 786440 | tf_op jit(solution)/shard_map/ppermute | solution.py:430
  186.1 43.4 %collective-permute-start.22 = (f32[256,256]{1,0:T(8,128)S(1)}, f32[256,256]{1,0:T(8,128)}, u32[]{:S(2)}, u32[]{:S(2)}) collective-permute-start(f32[256,256]{1,0:T(8,128)S(1)} %get-tuple-element.48), channel_id=1, source_target_pairs={{0,24},{4,28},{8,16},{12,20},{16,8},{20,12},{24,0},{28,4},{1,25},{... | collective-permute-start | bytes 786440 | tf_op jit(solution)/shard_map/ppermute | solution.py:430
  208.8 0.9 copy-start.14
  208.8 1.3 copy-start.15
  229.5 2.9 %collective-permute-start.27 = (f32[4,256,256]{2,1,0:T(8,128)}, f32[4,256,256]{2,1,0:T(8,128)S(1)}, u32[]{:S(2)}, u32[]{:S(2)}) collective-permute-start(f32[4,256,256]{2,1,0:T(8,128)} %get-tuple-element.39), channel_id=1, source_target_pairs={{0,4},{4,0},{8,12},{12,8},{16,20},{20,16},{24,28},{28,24},{1,5},{5... | collective-permute-start | bytes 3145736 | tf_op jit(solution)/shard_map/ppermute | solution.py:430
  232.2 1.6 copy-start.13
  232.4 1.0 copy-start.11
  233.8 21.5 %copy-start.1 = (f32[256,256]{1,0:T(8,128)S(1)}, f32[256,256]{1,0:T(8,128)}, u32[]{:S(2)}) copy-start(f32[256,256]{1,0:T(8,128)} %param.6) | copy-start | bytes 786436
  235.9 9.1 %collective-permute-start.28 = (f32[256,256]{1,0:T(8,128)S(1)}, f32[256,256]{1,0:T(8,128)S(1)}, u32[]{:S(2)}, u32[]{:S(2)}) collective-permute-start(f32[256,256]{1,0:T(8,128)S(1)} %get-tuple-element.46), channel_id=1, source_target_pairs={{0,8},{4,12},{8,0},{12,4},{16,24},{20,28},{24,16},{28,20},{1,9},{5... | collective-permute-start | bytes 786440 | tf_op jit(solution)/shard_map/ppermute | solution.py:430
  237.4 14.0 %collective-permute-start.29 = (f32[256,256]{1,0:T(8,128)S(1)}, f32[256,256]{1,0:T(8,128)S(1)}, u32[]{:S(2)}, u32[]{:S(2)}) collective-permute-start(f32[256,256]{1,0:T(8,128)S(1)} %get-tuple-element.45), channel_id=1, source_target_pairs={{0,16},{4,20},{8,24},{12,28},{16,0},{20,4},{24,8},{28,12},{1,17},{... | collective-permute-start | bytes 786440 | tf_op jit(solution)/shard_map/ppermute | solution.py:430
  238.9 12.5 %collective-permute-start.30 = (f32[256,256]{1,0:T(8,128)S(1)}, f32[256,256]{1,0:T(8,128)S(1)}, u32[]{:S(2)}, u32[]{:S(2)}) collective-permute-start(f32[256,256]{1,0:T(8,128)S(1)} %get-tuple-element.44), channel_id=1, source_target_pairs={{0,24},{4,28},{8,16},{12,20},{16,8},{20,12},{24,0},{28,4},{1,25},{... | collective-permute-start | bytes 786440 | tf_op jit(solution)/shard_map/ppermute | solution.py:430
  245.0 6.4 %copy-start.16 = (f32[256,256]{1,0:T(8,128)}, f32[256,256]{1,0:T(8,128)S(1)}, u32[]{:S(2)}) copy-start(f32[256,256]{1,0:T(8,128)S(1)} %collective-permute-done.28.refs_1_) | copy-start | bytes 786436
  (6 other events, 4.6 us)

commit v5 on v3

v5 whole, which is shorter than its diff:
```python
import functools

import jax
import jax.numpy as jnp
from jax import lax
from jax.experimental import pallas as pl
from jax.experimental.pallas import tpu as pltpu
from jax.sharding import PartitionSpec as P

FB = 512
OFF = 256
VMEM = 60 * 1024 * 1024

F32 = jnp.float32
BF16 = jnp.bfloat16
LONG = pl.CostEstimate(flops=10**11, bytes_accessed=1024, transcendentals=0)
SHORT = pl.CostEstimate(flops=1024, bytes_accessed=1024, transcendentals=0)


def split(x):
    high = x.astype(BF16)
    return high, (x - high.astype(F32)).astype(BF16)


def mul(left, right):
    return jnp.dot(left, right, preferred_element_type=F32)


def three(left, right):
    (lh, ll), (rh, rl) = left, right
    return mul(lh, rh) + mul(ll, rh) + mul(lh, rl)


def stacked(both, high, right):
    rh, rl = right
    m = high.shape[0]
    top = mul(both, rh)
    return top[:m] + top[m:] + mul(high, rl)


def params():
    return pltpu.CompilerParams(
        dimension_semantics=("arbitrary",), vmem_limit_bytes=VMEM
    )


def width(columns, wide):
    return 256 if columns % 256 == 0 and 256 % (columns // wide) == 0 else columns // wide


def whole(shape):
    return pl.BlockSpec(shape, lambda j, *_: (0,) * len(shape), pipeline_mode=pl.Buffered(1))


ANY = pl.BlockSpec(memory_space=pl.ANY)


def gate_kernel(*refs):
    del refs


def gate(held, *others, cost=SHORT):
    count = len(held)
    return pl.pallas_call(
        gate_kernel,
        in_specs=[ANY] * (count + len(others)),
        out_specs=[ANY] * count,
        out_shape=[jax.ShapeDtypeStruct(x.shape, x.dtype) for x in held],
        input_output_aliases={k: k for k in range(count)},
        cost_estimate=cost,
        name="gate",
    )(*held, *others)


def place(value, index, even_ref, odd_ref, first):
    half = index // 2
    rows = value.shape[0]

    @pl.when(index % 2 == 0)
    def _():
        even_ref[half, first : first + rows] = value

    @pl.when(index % 2 == 1)
    def _():
        odd_ref[half, first : first + rows] = value


def take(index, even_ref, odd_ref, rows):
    half = index // 2
    return jnp.where(index % 2 == 0, even_ref[half, rows], odd_ref[half, rows])


def project_kernel(per, wide, me_ref, v_ref, r_ref, e_ref, x_ref, even_ref, odd_ref, left_ref, own_ref, small_ref, both_ref):
    j = pl.program_id(0)
    nb = r_ref.shape[1]
    each = x_ref.shape[1]
    step = v_ref.shape[1]
    ride = even_ref.shape[1] - nb

    @pl.when(j == 0)
    def _():
        turned = r_ref[...].T
        both_ref[:nb], both_ref[nb:] = split(turned)
        k = nb + each
        left_ref[:nb], left_ref[k : k + nb] = split(turned * e_ref[...])
        left_ref[nb:k], left_ref[k + nb :] = split(x_ref[...].T)
        small = three((left_ref[:k], left_ref[k:]), split(r_ref[...]))
        small_ref[...] = small
        if ride:
            rows = k // wide
            for w in range(wide):
                place(small[w * rows : (w + 1) * rows], w ^ me_ref[0], even_ref, odd_ref, nb)

    value = stacked(both_ref[...], both_ref[:nb], split(v_ref[...]))
    for g in range(step // per):
        index = (j * (step // per) + g) ^ me_ref[0]
        place(value[:, g * per : (g + 1) * per], index, even_ref, odd_ref, 0)

    @pl.when(j == OFF // step)
    def _():
        own = value[:, OFF % step : OFF % step + each].T
        own_ref[...] = own
        if ride:
            rows = each // wide
            for w in range(wide):
                place(
                    own[w * rows : (w + 1) * rows], w ^ me_ref[0], even_ref, odd_ref,
                    nb + ride - rows,
                )


def project(me, vectors, reflectors, e_row, block, wide, ride):
    rows, columns = vectors.shape
    nb = reflectors.shape[1]
    each = block.shape[1]
    k = nb + each
    per = columns // wide
    step = width(columns, wide)
    shapes = [(wide // 2, nb + ride, per)] * 2 + [(2 * k, rows), (each, nb), (k, nb)]
    kinds = [F32, F32, BF16, F32, F32]
    return pl.pallas_call(
        functools.partial(project_kernel, per, wide),
        grid_spec=pltpu.PrefetchScalarGridSpec(
            num_scalar_prefetch=1,
            grid=(columns // step,),
            in_specs=[pl.BlockSpec((rows, step), lambda j, *_: (0, j))]
            + [whole(x) for x in ((rows, nb), (1, rows), block.shape)],
            out_specs=[whole(x) for x in shapes],
            scratch_shapes=[pltpu.VMEM((2 * nb, rows), BF16)],
        ),
        out_shape=[jax.ShapeDtypeStruct(x, kind) for x, kind in zip(shapes, kinds)],
        compiler_params=params(),
        cost_estimate=SHORT,
        name="project",
    )(me, vectors, reflectors, e_row, block)


def early_kernel(per, v_ref, left_ref, *refs):
    out_ref, token_ref = refs[-2:]
    k = left_ref.shape[0] // 2
    token_ref[...] = jnp.zeros_like(token_ref)
    value = stacked(left_ref[...], left_ref[:k], split(v_ref[...]))
    for g in range(v_ref.shape[1] // per):
        out_ref[g] = value[:, g * per : (g + 1) * per]


def early(vectors, left, offset, blocks, after, before, wide):
    rows, columns = vectors.shape
    per = columns // wide
    step = width(columns, wide)
    count = step // per
    k = left.shape[0] // 2
    operands = [vectors, left, after] + before
    return pl.pallas_call(
        functools.partial(early_kernel, per),
        grid=(blocks,),
        in_specs=[pl.BlockSpec((rows, step), lambda j: (0, j + offset)), whole(left.shape)]
        + [ANY] * (len(operands) - 2),
        out_specs=[
            pl.BlockSpec((count, k, per), lambda j: (j + offset, 0, 0)),
            whole((8, 128)),
        ],
        out_shape=[
            jax.ShapeDtypeStruct((wide, k, per), F32),
            jax.ShapeDtypeStruct((8, 128), F32),
        ],
        input_output_aliases={3: 0} if before else {},
        compiler_params=params(),
        cost_estimate=SHORT,
        name="early",
    )(*operands)


def update_kernel(per, offset, me_ref, v_ref, r_ref, even_ref, odd_ref, *refs):
    out_ref, token_ref, left_ref = refs[-3:]
    j = pl.program_id(0)
    nb = r_ref.shape[1]

    @pl.when(j == 0)
    def _():
        token_ref[...] = jnp.zeros_like(token_ref)
        high, low = split(r_ref[...])
        left_ref[:, :nb] = high
        left_ref[:, nb : 2 * nb] = low
        left_ref[:, 2 * nb :] = high

    count = v_ref.shape[1] // per
    blocks = [
        take(((j + offset) * count + g) ^ me_ref[0], even_ref, odd_ref, slice(0, nb))
        for g in range(count)
    ]
    high, low = split(blocks[0] if count == 1 else jnp.concatenate(blocks, axis=1))
    right = jnp.concatenate([high, high, low], axis=0)
    out_ref[...] = v_ref[...] - mul(left_ref[...], right)


def update(me, vectors, reflectors, c, offset, blocks, after, before, wide):
    rows, columns = vectors.shape
    nb = reflectors.shape[1]
    per = columns // wide
    step = width(columns, wide)
    operands = [me, vectors, reflectors, *c, *after]
    aliases = {len(operands): 0} if before else {}
    operands += before
    columns_of = pl.BlockSpec((rows, step), lambda j, *_: (0, j + offset))
    return pl.pallas_call(
        functools.partial(update_kernel, per, offset),
        grid_spec=pltpu.PrefetchScalarGridSpec(
            num_scalar_prefetch=1,
            grid=(blocks,),
            in_specs=[columns_of]
            + [whole(x.shape) for x in (reflectors, *c)]
            + [ANY] * (len(operands) - 5),
            out_specs=[columns_of, whole((8, 128))],
            scratch_shapes=[pltpu.VMEM((rows, 3 * nb), BF16)],
        ),
        out_shape=[
            jax.ShapeDtypeStruct(vectors.shape, F32),
            jax.ShapeDtypeStruct((8, 128), F32),
        ],
        input_output_aliases=aliases,
        compiler_params=params(),
        cost_estimate=SHORT,
        name="update",
    )(*operands)


def late_kernel(per, counts, at_ref, u_ref, after_ref, *refs):
    *refs, even_out, odd_out, both_ref, block_ref, sem_ref = refs
    j = pl.program_id(0)
    m = both_ref.shape[0] // 2
    each = block_ref.shape[2]

    @pl.when(j == 0)
    def _():
        first = 0
        for s, count in enumerate(counts):
            for k, ref in enumerate(refs[first : first + count]):

                @pl.when(at_ref[1 + s] == k)
                def _(ref=ref, s=s):
                    pltpu.make_async_copy(ref, block_ref.at[s], sem_ref.at[s]).start()

            first += count
        for s in range(len(counts)):
            pltpu.make_async_copy(block_ref.at[s], block_ref.at[s], sem_ref.at[s]).wait()
            high, low = split(block_ref[s].T)
            both_ref[s * each : (s + 1) * each] = high
            both_ref[m + s * each : m + (s + 1) * each] = low

    value = stacked(both_ref[...], both_ref[:m], split(u_ref[...]))
    count = u_ref.shape[1] // per
    for g in range(count):
        index = (j * count + g) ^ at_ref[0]
        place(value[:, g * per : (g + 1) * per], index, even_out, odd_out, 0)


def late(me, updated, slots, after, wide):
    rows, columns = updated.shape
    per = columns // wide
    step = width(columns, wide)
    flat = [x for choices, _ in slots for x in choices]
    counts = [len(choices) for choices, _ in slots]
    each = flat[0].shape[1]
    m = each * len(slots)
    at = jnp.stack([me[0]] + [which.astype(jnp.int32) for _, which in slots])
    half = jax.ShapeDtypeStruct((wide // 2, m, per), F32)
    return pl.pallas_call(
        functools.partial(late_kernel, per, counts),
        grid_spec=pltpu.PrefetchScalarGridSpec(
            num_scalar_prefetch=1,
            grid=(columns // step,),
            in_specs=[pl.BlockSpec((rows, step), lambda j, *_: (0, j))] + [ANY] * (1 + len(flat)),
            out_specs=[whole(half.shape)] * 2,
            scratch_shapes=[
                pltpu.VMEM((2 * m, rows), BF16),
                pltpu.VMEM((len(slots), rows, each), F32),
                pltpu.SemaphoreType.DMA((len(slots),)),
            ],
        ),
        out_shape=[half, half],
        compiler_params=params(),
        cost_estimate=SHORT,
        name="late",
    )(at, updated, after, *flat)


def base_kernel(n, each, ride, at_ref, ready_ref, c_ref, *refs):
    *refs, out_ref, coef_ref, small_ref = refs
    me, z = at_ref[0], at_ref[1]
    nb = c_ref.shape[0]
    k = small_ref.shape[0]
    if ride:
        c_even, c_odd, ce_ref, co_ref, *refs = refs
        half, _, rows, _ = ce_ref.shape
        wide = 2 * half
        for w in range(wide):
            index = w ^ me
            small_ref[w * (k // wide) : (w + 1) * (k // wide)] = take(
                index, c_even, c_odd, slice(nb, nb + k // wide)
            )
            for s in range(n):
                first = pl.multiple_of((z + n - s) % n * each + w * rows, rows)
                coef_ref[pl.ds(first, rows), :] = take(index, ce_ref, co_ref, s)
    else:
        all_small, all_coef, *refs = refs
        small_ref[...] = all_small[...]
        for s in range(n):
            coef_ref[s * each : (s + 1) * each] = all_coef[s]
    corrected = ready_ref[...] - three(split(small_ref[...]), split(c_ref[...]))
    out_ref[...] = -three(split(coef_ref[...]), split(corrected[:nb]))
    total = functools.reduce(jnp.add, [ref[...] for ref in refs])
    for slot in range(1 + total.shape[0] // each):
        piece = corrected[nb:] if slot == 0 else total[(slot - 1) * each : slot * each]
        first = pl.multiple_of(at_ref[1 + slot] * each, each)
        out_ref[pl.ds(first, each), :] += piece


def base(at, ready, c, extra, terms, n, each, ride):
    operands = [ready, c, *extra, *terms]
    k, per = ready.shape
    nb = c.shape[0]
    return pl.pallas_call(
        functools.partial(base_kernel, n, each, ride),
        grid_spec=pltpu.PrefetchScalarGridSpec(
            num_scalar_prefetch=1,
            grid=(1,),
            in_specs=[whole(x.shape) for x in operands],
            out_specs=whole((FB, per)),
            scratch_shapes=[pltpu.VMEM((FB, nb), F32), pltpu.VMEM((k, nb), F32)],
        ),
        out_shape=jax.ShapeDtypeStruct((FB, per), F32),
        compiler_params=params(),
        cost_estimate=LONG,
        name="base",
    )(at, *operands)


def last_kernel(each, at_ref, base_ref, *refs):
    *refs, out_ref, total_ref = refs
    total_ref[...] = base_ref[...]
    total = functools.reduce(jnp.add, [ref[...] for ref in refs])
    first = pl.multiple_of(at_ref[at_ref.shape[0] - 1] * each, each)
    total_ref[pl.ds(first, each), :] += total
    out_ref[...] = total_ref[...].T


def last(at, held, terms, each):
    per = held.shape[1]
    operands = [held, *terms]
    return pl.pallas_call(
        functools.partial(last_kernel, each),
        grid_spec=pltpu.PrefetchScalarGridSpec(
            num_scalar_prefetch=1,
            grid=(1,),
            in_specs=[whole(x.shape) for x in operands],
            out_specs=whole((per, FB)),
            scratch_shapes=[pltpu.VMEM((FB, per), F32)],
        ),
        out_shape=jax.ShapeDtypeStruct((per, FB), F32),
        compiler_params=params(),
        cost_estimate=SHORT,
        name="last",
    )(at, *operands)


def arrivals(n):
    order = []
    for z in range(n):
        found = [(hops, 0) for hops in range(1, n) if z + hops < n]
        found += [(hops, 1) for hops in range(1, n) if z - hops >= 0]
        order.append(sorted(found))
    return [[order[z][slot] for z in range(n)] for slot in range(n - 1)]


def travel(came, held, n, hops, after):
    if hops > 1:
        held = gate(held, *after, cost=LONG)
        came[(hops - 1, 0)], came[(hops - 1, 1)] = held
    pairs = [
        [(p, p - 1) for p in range(1, n - hops + 1)],
        [(p, p + 1) for p in range(hops - 1, n - 1)],
    ]
    held = [lax.ppermute(held[d], "narrow", pairs[d]) for d in (0, 1)]
    came[(hops, 0)], came[(hops, 1)] = held
    return held


def options(came, places, z):
    choices = sorted(set(places))
    which = jnp.int32(0)
    for p, place in enumerate(places):
        which = jnp.where(z == p, choices.index(place), which)
    return [came[choice] for choice in choices], which


def source(places, z):
    value = jnp.int32(0)
    for p, (hops, direction) in enumerate(places):
        value = jnp.where(z == p, p - hops if direction else p + hops, value)
    return value


def swap(x, wide, distance):
    return lax.ppermute(x, "wide", [(i, i ^ distance) for i in range(wide)])


def scatter_terms(even, odd, wide, after=None):
    other = swap(odd, wide, 1)
    if after is not None:
        (other,) = gate([other], after)
    sums = [even[h] + other[h] for h in range(wide // 2)]
    return [sums[0]] + [swap(sums[h], wide, 2 * h) for h in range(1, wide // 2)]


def collect(x, wide, after=()):
    pieces = [swap(x, wide, 2 * h) for h in range(1, wide // 2)]
    if after:
        (x,) = gate([x], *after)
    even = jnp.stack([x, *pieces])
    return even, swap(even, wide, 1)


def on_device(vectors, reflectors, triangle, energies):
    n = lax.axis_size("narrow")
    wide = lax.axis_size("wide")
    z = lax.axis_index("narrow").astype(jnp.int32)
    me = lax.axis_index("wide").astype(jnp.int32).reshape(1)
    each = FB // n
    rows, columns = vectors.shape
    nb = reflectors.shape[1]
    k = nb + each
    per = columns // wide
    blocks = columns // width(columns, wide)
    half = blocks // 2
    e_row = energies.reshape(1, rows)

    own = energies[:, None] * vectors[:, OFF : OFF + each]
    came = {}
    held = travel(came, [own, own], n, 1, [])
    table = arrivals(n)
    at = jnp.stack([me[0], z] + [source(places, z) for places in table])

    fits = per == nb and each % (8 * wide) == 0 and k % (8 * wide) == 0
    ride = (k + each) // wide if fits else 0
    even, odd, left, own_part, small = project(me, vectors, reflectors, e_row, own, wide, ride)
    terms = scatter_terms(even, odd, wide)
    if n > 2:
        held = travel(came, held, n, 2, [left, terms[0]])
    highest = lax.Precision.HIGHEST
    turn = (((1,), (1,)), ((), ()))
    sums, token = early(vectors, left, 0, half, came[(1, 0)], [], wide)
    terms[0] = gate(terms[:1], token)[0]
    projected = functools.reduce(jnp.add, terms)
    coefficients = jnp.dot(triangle, projected[:nb], precision=highest)
    payload = coefficients
    if ride:
        payload = jnp.concatenate([coefficients, projected[nb : nb + k // wide]], axis=0)
    sums, token = early(vectors, left, half, blocks - half, payload, [sums], wide)
    ready = lax.psum_scatter(sums, "wide", scatter_dimension=0)
    c = collect(payload, wide, [token])
    ready_shares = []
    if ride:
        (mine,) = gate([projected[nb + k // wide :]], c[0])
        mine = lax.dot_general(mine, triangle, turn, precision=highest)
        shares = jnp.stack(
            [mine]
            + [
                lax.ppermute(mine, "narrow", [(p, (p + s) % n) for p in range(n)])
                for s in range(1, n)
            ]
        )
        ready_shares = [shares]

    for hops in range(3, n):
        held = travel(came, held, n, hops, [token, *ready_shares])
    after = came[(min(2, n - 1), 0)]
    updated, token = update(me, vectors, reflectors, c, 0, blocks, [after], [], wide)
    if ride:
        share_even, share_odd = collect(shares, wide, [token])
        extra = [*c, share_even, share_odd]
        (token,) = gate([token], share_even)
    else:
        own_part = lax.dot_general(lax.psum(own_part, "wide"), triangle, turn, precision=highest)
        extra = [lax.psum(small, "wide"), lax.all_gather(own_part, "narrow")]
    slots = [options(came, places, z) for places in table]
    even, odd = late(me, updated, slots[:-1], token, wide)
    middle = scatter_terms(even, odd, wide)
    (token,) = gate([token], middle[0], extra[-1])
    even, odd = late(me, updated, slots[-1:], token, wide)
    base_block = base(at, ready, coefficients, extra, middle, n, each, ride)
    tail = scatter_terms(even, odd, wide, base_block)
    return (updated, last(at, base_block, tail, each))


def solution(mesh):
    return jax.shard_map(
        on_device,
        mesh=mesh,
        in_specs=(P("wide", "narrow"), P("wide", None), P(), P("wide")),
        out_specs=(P("wide", "narrow"), P(("narrow", "wide"), None)),
        check_vma=False,
    )
```

time: 271 us -> 248 us (0.915)
  waiting for transfers between devices: 88.5 us -> 27.1 us
  Pallas kernels: 119 us -> 139 us
  between operations: 0.87 us -> 14.3 us
  other arithmetic: 10.9 us -> 16.3 us
    ppermute x6, waiting for transfers between devices: 48.8 us -> 9.29 us  [travel(): held = [lax.ppermute(held[d], 'narrow', pairs[d]) for d in (0, 1)]]
    pallas_call x7 -> x8, Pallas kernels: 119 us -> 139 us  [the longest x2 42.3 us: late(): pl.pallas_call(functools.partial(late_kernel, per, counts), grid_spec=plt...]
    ppermute x3, waiting for transfers between devices: 17.4 us -> 5.53 us  [on_device(): lax.ppermute(mine, 'narrow', [(p, (p + s) % n) for p in range(n)])]
    ppermute x20, waiting for transfers between devices: 22.2 us -> 12.3 us  [swap(): return lax.ppermute(x, 'wide', [(i, i ^ distance) for i in range(wide)])]
    another operation x5, other arithmetic: 2.02 us -> 6.23 us  [the longest x2 3.69 us: collect(): even = jnp.stack([x, *pieces])]
  transfers between devices with their start and end apart: 29 -> 30, of which waited for: 12 -> 9; matrix products, arithmetic and copies ran while one was open for 3% -> 6% of each run, Pallas kernels for 30% -> 55%
where the time goes in v5:
time: 248 us; the launch traced here: 247 us
  Pallas kernels  139 us (56%)
  starting transfers between devices  41.4 us (17%)
  waiting for transfers between devices  27.1 us (11%)
  other arithmetic  16.3 us (7%)
  between operations  14.3 us (6%)
  local copies, waits for them, and re-layouts  6.07 us (2%)
    pallas_call x2, Pallas kernels, late(): pl.pallas_call(functools.partial(late_kernel, per, counts), grid_spec=plt...  42.3 us
    pallas_call x1, Pallas kernels, update(): pl.pallas_call(functools.partial(update_kernel, per, offset), grid_spec=p...  31.2 us
    pallas_call x2, Pallas kernels, early(): pl.pallas_call(functools.partial(early_kernel, per), grid=(blocks,), in_s...  30.5 us
    pallas_call x1, Pallas kernels, project(): pl.pallas_call(functools.partial(project_kernel, per, wide), grid_spec=pl...  27.6 us
    ppermute x20, starting transfers between devices, swap(): return lax.ppermute(x, 'wide', [(i, i ^ distance) for i in range(wide)])  18.4 us
    ppermute x6, starting transfers between devices, travel(): held = [lax.ppermute(held[d], 'narrow', pairs[d]) for d in (0, 1)]  14.7 us
    ppermute x20, waiting for transfers between devices, swap(): return lax.ppermute(x, 'wide', [(i, i ^ distance) for i in range(wide)])  12.3 us
    ppermute x6, waiting for transfers between devices, travel(): held = [lax.ppermute(held[d], 'narrow', pairs[d]) for d in (0, 1)]  9.29 us
  transfers between devices with their start and end apart: 30, of which 9 were waited for; matrix products, arithmetic and copies ran while one was open for 6% of the time, Pallas kernels for 55%

profile of v5, /device:TPU:0, one launch (start us, length us, event | category | flops | bytes accessed | tf_op | source)
XLA Modules:
  0.0 246.8 jit_solution(68498385305070795)
XLA Ops:
  7.2 2.7 %slice_multiply_fusion.x_ref = f32[4000,128]{1,0:T(8,128)S(1)} fusion(f32[4000,2048]{1,0:T(8,128)} %v_ref.7, f32[4000]{0:T(1024)} %param.7), kind=kLoop, calls=%fused_computation | loop fusion | flops 512000 | bytes 4112000 | tf_op jit(solution)/shard_map/mul | solution.py:458
  10.0 1.3 collective-permute-start.1
  11.3 6.9 %collective-permute-start.2 = (f32[4000,128]{1,0:T(8,128)S(1)}, f32[4000,128]{1,0:T(8,128)}, u32[]{:S(2)}, u32[]{:S(2)}) collective-permute-start(f32[4000,128]{1,0:T(8,128)S(1)} %slice_multiply_fusion.x_ref), channel_id=1, source_target_pairs={{0,1},{1,2},{2,3},{4,5},{5,6},{6,7},{8,9},{9,10},{10,11},{12,13},{... | collective-permute-start | bytes 6144008 | tf_op jit(solution)/shard_map/ppermute | solution.py:404
  18.2 27.6 %project.1 = (f32[4,320,256]{2,1,0:T(8,128)}, f32[4,320,256]{2,1,0:T(8,128)}, bf16[768,4000]{1,0:T(8,128)(2,1)}, f32[128,256]{1,0:T(8,128)}, f32[384,256]{1,0:T(8,128)}) custom-call(s32[1]{0:T(128)} %bitcast.me_ref, f32[4000,2048]{1,0:T(8,128)} %v_ref.7, f32[4000,256]{1,0:T(8,128)} %r_ref.3, f32[1,4000]{1,0:T(1,128)} %bitcast.56, f32[4000,128]{1,0:T(8,128)} %copy-done.4), custom_call_target="tpu_custom_call" | custom-call | flops 1024 | bytes 1024 | tf_op jit(solution)/shard_map/project/pallas_call | solution.py:141
  45.8 3.2 %collective-permute-done = f32[4,320,256]{2,1,0:T(8,128)S(1)} collective-permute-done((f32[4,320,256]{2,1,0:T(8,128)}, f32[4,320,256]{2,1,0:T(8,128)S(1)}, u32[]{:S(2)}, u32[]{:S(2)}) %collective-permute-start) | collective-permute-done | bytes 1310752 | tf_op jit(solution)/shard_map/ppermute | solution.py:425
  49.0 2.4 fusion.2
  51.4 8.2 %collective-permute-done.1.refs_0_ = f32[4000,128]{1,0:T(8,128)} collective-permute-done((f32[4000,128]{1,0:T(8,128)S(1)}, f32[4000,128]{1,0:T(8,128)}, u32[]{:S(2)}, u32[]{:S(2)}) %collective-permute-start.1) | collective-permute-done | bytes 2048032 | tf_op jit(solution)/shard_map/ppermute | solution.py:404
  59.6 1.1 collective-permute-done.2.refs_1_
  60.7 1.3 collective-permute-start.10
  62.0 2.0 collective-permute-start.11
  63.9 2.6 %collective-permute-start.5 = (f32[320,256]{1,0:T(8,128)}, f32[320,256]{1,0:T(8,128)S(1)}, u32[]{:S(2)}, u32[]{:S(2)}) collective-permute-start(f32[320,256]{1,0:T(8,128)} %get-tuple-element.37), channel_id=1, source_target_pairs={{0,24},{4,28},{8,16},{12,20},{16,8},{20,12},{24,0},{28,4},{1,25},{... | collective-permute-start | bytes 983048 | tf_op jit(solution)/shard_map/ppermute | solution.py:425
  67.4 15.3 %early.2 = (f32[8,384,256]{2,1,0:T(8,128)}, f32[8,128]{1,0:T(8,128)}) custom-call(f32[4000,2048]{1,0:T(8,128)} %v_ref.7, bf16[768,4000]{1,0:T(8,128)(2,1)} %get-tuple-element.21.refs_2_.left_ref, f32[4000,128]{1,0:T(8,128)} %get-tuple-element.22.refs_0_), custom_call_target="tpu_custom_call" | custom-call | flops 1024 | bytes 1024 | tf_op jit(solution)/shard_map/early/pallas_call | solution.py:174
  82.7 1.1 add_add_fusion
  84.3 2.7 %collective-permute-start.8 = (f32[304,256]{1,0:T(8,128)S(1)}, f32[304,256]{1,0:T(8,128)S(1)}, u32[]{:S(2)}, u32[]{:S(2)}) collective-permute-start(f32[304,256]{1,0:T(8,128)S(1)} %pad_maximum_fusion.1.refs_0_), channel_id=1, source_target_pairs={{0,24},{4,28},{8,16},{12,20},{16,8},{20,12},{24,0},{28,4},{1,25},{... | collective-permute-start | bytes 933896 | tf_op jit(solution)/shard_map/ppermute | solution.py:425
  88.1 15.3 %early.3 = (f32[8,384,256]{2,1,0:T(8,128)}, f32[8,128]{1,0:T(8,128)}) custom-call(f32[4000,2048]{1,0:T(8,128)} %v_ref.7, bf16[768,4000]{1,0:T(8,128)(2,1)} %get-tuple-element.21.refs_2_.left_ref, f32[304,256]{1,0:T(8,128)} %copy-done.5, f32[8,384,256]{2,1,0:T(8,128)} %get-tuple-element.24.refs_1_), custom_call_target="tpu_custom_call", output_to_operand_aliasing={{0}: (3, {})} | custom-call | flops 1024 | bytes 1024 | tf_op jit(solution)/shard_map/early/pallas_call | solution.py:174
  104.0 2.1 pad_maximum_fusion.refs_1_.even_ref.refs_0_
  106.1 1.7 fusion.13
  107.8 5.1 %collective-permute-start.14 = (f32[16,256]{1,0:T(8,128)}, f32[16,256]{1,0:T(8,128)S(1)}, u32[]{:S(2)}, u32[]{:S(2)}) collective-permute-start(f32[16,256]{1,0:T(8,128)} %fusion.13), channel_id=1, source_target_pairs={{0,3},{1,0},{2,1},{3,2},{4,7},{5,4},{6,5},{7,6},{8,11},{9,8},{10,9... | collective-permute-start | bytes 49160 | tf_op jit(solution)/shard_map/ppermute | solution.py:489
  112.9 3.0 %collective-permute-start.13 = (f32[16,256]{1,0:T(8,128)}, f32[16,256]{1,0:T(8,128)S(1)}, u32[]{:S(2)}, u32[]{:S(2)}) collective-permute-start(f32[16,256]{1,0:T(8,128)} %fusion.13), channel_id=1, source_target_pairs={{0,2},{1,3},{2,0},{3,1},{4,6},{5,7},{6,4},{7,5},{8,10},{9,11},{10,... | collective-permute-start | bytes 49160 | tf_op jit(solution)/shard_map/ppermute | solution.py:489
  116.4 1.6 collective-permute-done.13
  118.0 3.6 %collective-permute-done.12 = f32[16,256]{1,0:T(8,128)S(1)} collective-permute-done((f32[16,256]{1,0:T(8,128)}, f32[16,256]{1,0:T(8,128)S(1)}, u32[]{:S(2)}, u32[]{:S(2)}) %collective-permute-start.12) | collective-permute-done | bytes 16416 | tf_op jit(solution)/shard_map/ppermute | solution.py:489
  121.7 1.4 pad_maximum_fusion.3.refs_3_.refs_0_
  123.0 1.3 copy-done.2
  124.4 1.3 collective-permute-start.23
  125.7 2.0 collective-permute-start.24
  127.7 2.3 collective-permute-start.17
  130.5 0.7 collective-permute-start.15
  131.1 31.2 %update.1 = (f32[4000,2048]{1,0:T(8,128)}, f32[8,128]{1,0:T(8,128)}) custom-call(s32[1]{0:T(128)} %bitcast.me_ref, f32[4000,2048]{1,0:T(8,128)} %v_ref.7, f32[4000,256]{1,0:T(8,128)} %r_ref.3, f32[4,304,256]{2,1,0:T(8,128)} %pad_maximum_fusion.refs_1_.even_ref.refs_0_, f32[4,304,256]{2,1,0:T(8,128)} %collective-permute-done.9.odd_ref.refs_1_, ...), custom_call_target="tpu_custom_call" | custom-call | flops 1024 | bytes 1024 | tf_op jit(solution)/shard_map/update/pallas_call | solution.py:226
  162.4 1.6 pad_maximum_fusion.2.refs_1_.refs_2_
  164.5 23.4 %late.2 = (f32[4,256,256]{2,1,0:T(8,128)}, f32[4,256,256]{2,1,0:T(8,128)}) custom-call(s32[3]{0:T(128)} %pad_add_fusion.at_ref, f32[4000,2048]{1,0:T(8,128)} %get-tuple-element.17.u_ref, f32[8,128]{1,0:T(8,128)} %gate.15.after_ref.refs_0_, f32[4000,128]{1,0:T(8,128)} %get-tuple-element.22.refs_0_, f32[4000,128]{1,0:T(8,128)} %get-tuple-element.26.refs_1_.refs_2_, ...), custom_call_target="tpu_custom_call" | custom-call | flops 1024 | bytes 1024 | tf_op jit(solution)/shard_map/late/pallas_call | solution.py:288
  188.5 2.7 %collective-permute-done.19 = f32[4,256,256]{2,1,0:T(8,128)S(1)} collective-permute-done((f32[4,256,256]{2,1,0:T(8,128)}, f32[4,256,256]{2,1,0:T(8,128)S(1)}, u32[]{:S(2)}, u32[]{:S(2)}) %collective-permute-start.19) | collective-permute-done | bytes 1048608 | tf_op jit(solution)/shard_map/ppermute | solution.py:425
  191.2 2.0 fusion.4
  193.3 1.3 collective-permute-start.20
  194.6 1.5 collective-permute-start.21
  196.1 0.6 collective-permute-start.22
  198.0 1.4 copy-done.7
  199.3 18.9 %late.3 = (f32[4,128,256]{2,1,0:T(8,128)}, f32[4,128,256]{2,1,0:T(8,128)}) custom-call(s32[2]{0:T(128)} %pad_add_fusion.1.at_ref, f32[4000,2048]{1,0:T(8,128)} %get-tuple-element.17.u_ref, f32[8,128]{1,0:T(8,128)} %gate.16.after_ref, f32[4000,128]{1,0:T(8,128)} %get-tuple-element.27.refs_0_.refs_3_, f32[4000,128]{1,0:T(8,128)} %get-tuple-element.31.refs_4_.refs_1_, ...), custom_call_target="tpu_custom_call" | custom-call | flops 1024 | bytes 1024 | tf_op jit(solution)/shard_map/late/pallas_call | solution.py:288
  218.4 0.7 copy-done.16
  219.1 4.9 %base.1.refs_1_.base_ref = f32[512,256]{1,0:T(8,128)} custom-call(s32[5]{0:T(128)} %stack.89.at_ref, f32[384,256]{1,0:T(8,128)} %bitcast.63, f32[256,256]{1,0:T(8,128)} %copy-done.8, f32[4,304,256]{2,1,0:T(8,128)} %pad_maximum_fusion.refs_1_.even_ref.refs_0_, f32[4,304,256]{2,1,0:T(8,128)} %collective-permute-done.9.odd_ref.refs_1_, ...), custom_call_target="tpu_custom_call" | custom-call | flops 99999997952 | bytes 1024 | tf_op jit(solution)/shard_map/base/pallas_call | solution.py:343
  223.9 0.8 copy-done.6
  224.7 1.8 fusion.9
  226.5 1.3 collective-permute-start.26
  227.9 1.5 collective-permute-start.27
  229.4 0.6 collective-permute-start.28
  230.0 2.8 %collective-permute-done.26.refs_1_ = f32[128,256]{1,0:T(8,128)S(1)} collective-permute-done((f32[128,256]{1,0:T(8,128)S(1)}, f32[128,256]{1,0:T(8,128)S(1)}, u32[]{:S(2)}, u32[]{:S(2)}) %collective-permute-start.26) | collective-permute-done | bytes 131104 | tf_op jit(solution)/shard_map/ppermute | solution.py:425
  232.8 3.4 %collective-permute-done.27.refs_2_ = f32[128,256]{1,0:T(8,128)S(1)} collective-permute-done((f32[128,256]{1,0:T(8,128)S(1)}, f32[128,256]{1,0:T(8,128)S(1)}, u32[]{:S(2)}, u32[]{:S(2)}) %collective-permute-start.27) | collective-permute-done | bytes 131104 | tf_op jit(solution)/shard_map/ppermute | solution.py:425
  236.3 0.6 copy-done.14
  237.0 3.0 %last.1 = f32[256,512]{1,0:T(8,128)} custom-call(s32[5]{0:T(128)} %stack.89.at_ref, f32[512,256]{1,0:T(8,128)} %base.1.refs_1_.base_ref, f32[128,256]{1,0:T(8,128)} %get-tuple-element.47.refs_0_, f32[128,256]{1,0:T(8,128)} %copy-done.13, f32[128,256]{1,0:T(8,128)} %copy-done.14, f32[128,256]{1,0:T(8,128)} %copy-done.15), custom_call_target="tpu_custom_call" | custom-call | flops 1024 | bytes 1024 | tf_op jit(solution)/shard_map/last/pallas_call | solution.py:371
  (80 shorter events, 6.7 us)
Async XLA Ops:
  7.2 76.6 %copy-start = (f32[256,256]{1,0:T(8,128)S(1)}, f32[256,256]{1,0:T(8,128)}, u32[]{:S(2)}) copy-start(f32[256,256]{1,0:T(8,128)} %param.6) | copy-start | bytes 786436
  7.2 211.2 %reduce-scatter.2.cloned.1.call-start = ((), (), s32[]{:S(2)}) async-start(), calls=%async_computation.1 | async-start | bytes 3538944 | tf_op jit(solution)/shard_map/reduce_scatter | solution.py:480
  10.0 8.2 %copy-start.4 = (f32[4000,128]{1,0:T(8,128)}, f32[4000,128]{1,0:T(8,128)S(1)}, u32[]{:S(2)}) copy-start(f32[4000,128]{1,0:T(8,128)S(1)} %slice_multiply_fusion.x_ref) | copy-start | bytes 6144004
  10.0 49.6 %collective-permute-start.1 = (f32[4000,128]{1,0:T(8,128)S(1)}, f32[4000,128]{1,0:T(8,128)}, u32[]{:S(2)}, u32[]{:S(2)}) collective-permute-start(f32[4000,128]{1,0:T(8,128)S(1)} %slice_multiply_fusion.x_ref), channel_id=1, source_target_pairs={{1,0},{2,1},{3,2},{5,4},{6,5},{7,6},{9,8},{10,9},{11,10},{13,12},{... | collective-permute-start | bytes 6144008 | tf_op jit(solution)/shard_map/ppermute | solution.py:404
  11.3 49.4 %collective-permute-start.2 = (f32[4000,128]{1,0:T(8,128)S(1)}, f32[4000,128]{1,0:T(8,128)}, u32[]{:S(2)}, u32[]{:S(2)}) collective-permute-start(f32[4000,128]{1,0:T(8,128)S(1)} %slice_multiply_fusion.x_ref), channel_id=1, source_target_pairs={{0,1},{1,2},{2,3},{4,5},{5,6},{6,7},{8,9},{9,10},{10,11},{12,13},{... | collective-permute-start | bytes 6144008 | tf_op jit(solution)/shard_map/ppermute | solution.py:404
  45.8 3.2 %collective-permute-start = (f32[4,320,256]{2,1,0:T(8,128)}, f32[4,320,256]{2,1,0:T(8,128)S(1)}, u32[]{:S(2)}, u32[]{:S(2)}) collective-permute-start(f32[4,320,256]{2,1,0:T(8,128)} %get-tuple-element.20), channel_id=1, source_target_pairs={{0,4},{4,0},{8,12},{12,8},{16,20},{20,16},{24,28},{28,24},{1,5},{5... | collective-permute-start | bytes 3932168 | tf_op jit(solution)/shard_map/ppermute | solution.py:425
  60.7 62.3 %collective-permute-start.10 = (f32[4000,128]{1,0:T(8,128)}, f32[4000,128]{1,0:T(8,128)S(1)}, u32[]{:S(2)}, u32[]{:S(2)}) collective-permute-start(f32[4000,128]{1,0:T(8,128)} %get-tuple-element.22.refs_0_), channel_id=1, source_target_pairs={{1,0},{2,1},{5,4},{6,5},{9,8},{10,9},{13,12},{14,13},{17,16},{18,1... | collective-permute-start | bytes 6144008 | tf_op jit(solution)/shard_map/ppermute | solution.py:404
  62.0 61.1 %collective-permute-start.11 = (f32[4000,128]{1,0:T(8,128)}, f32[4000,128]{1,0:T(8,128)}, u32[]{:S(2)}, u32[]{:S(2)}) collective-permute-start(f32[4000,128]{1,0:T(8,128)} %get-tuple-element.26.refs_1_.refs_2_), channel_id=1, source_target_pairs={{1,2},{2,3},{5,6},{6,7},{9,10},{10,11},{13,14},{14,15},{17,18},{18... | collective-permute-start | bytes 6144008 | tf_op jit(solution)/shard_map/ppermute | solution.py:404
  63.9 18.8 %collective-permute-start.5 = (f32[320,256]{1,0:T(8,128)}, f32[320,256]{1,0:T(8,128)S(1)}, u32[]{:S(2)}, u32[]{:S(2)}) collective-permute-start(f32[320,256]{1,0:T(8,128)} %get-tuple-element.37), channel_id=1, source_target_pairs={{0,24},{4,28},{8,16},{12,20},{16,8},{20,12},{24,0},{28,4},{1,25},{... | collective-permute-start | bytes 983048 | tf_op jit(solution)/shard_map/ppermute | solution.py:425
  66.5 16.2 %collective-permute-start.4 = (f32[320,256]{1,0:T(8,128)}, f32[320,256]{1,0:T(8,128)S(1)}, u32[]{:S(2)}, u32[]{:S(2)}) collective-permute-start(f32[320,256]{1,0:T(8,128)} %get-tuple-element.38), channel_id=1, source_target_pairs={{0,16},{4,20},{8,24},{12,28},{16,0},{20,4},{24,8},{28,12},{1,17},{... | collective-permute-start | bytes 983048 | tf_op jit(solution)/shard_map/ppermute | solution.py:425
  67.0 15.7 %collective-permute-start.3 = (f32[320,256]{1,0:T(8,128)}, f32[320,256]{1,0:T(8,128)S(1)}, u32[]{:S(2)}, u32[]{:S(2)}) collective-permute-start(f32[320,256]{1,0:T(8,128)} %get-tuple-element.36), channel_id=1, source_target_pairs={{0,8},{4,12},{8,0},{12,4},{16,24},{20,28},{24,16},{28,20},{1,9},{5... | collective-permute-start | bytes 983048 | tf_op jit(solution)/shard_map/ppermute | solution.py:425
  84.2 2.7 %copy-start.8 = (f32[256,256]{1,0:T(8,128)}, f32[256,256]{1,0:T(8,128)S(1)}, u32[]{:S(2)}) copy-start(f32[256,256]{1,0:T(8,128)S(1)} %convolution_bitcast_fusion.c_ref) | copy-start | bytes 786436
  84.2 3.8 %copy-start.5 = (f32[304,256]{1,0:T(8,128)}, f32[304,256]{1,0:T(8,128)S(1)}, u32[]{:S(2)}) copy-start(f32[304,256]{1,0:T(8,128)S(1)} %pad_maximum_fusion.1.refs_0_) | copy-start | bytes 933892
  84.3 19.7 %collective-permute-start.8 = (f32[304,256]{1,0:T(8,128)S(1)}, f32[304,256]{1,0:T(8,128)S(1)}, u32[]{:S(2)}, u32[]{:S(2)}) collective-permute-start(f32[304,256]{1,0:T(8,128)S(1)} %pad_maximum_fusion.1.refs_0_), channel_id=1, source_target_pairs={{0,24},{4,28},{8,16},{12,20},{16,8},{20,12},{24,0},{28,4},{1,25},{... | collective-permute-start | bytes 933896 | tf_op jit(solution)/shard_map/ppermute | solution.py:425
  86.9 17.0 %collective-permute-start.7 = (f32[304,256]{1,0:T(8,128)S(1)}, f32[304,256]{1,0:T(8,128)S(1)}, u32[]{:S(2)}, u32[]{:S(2)}) collective-permute-start(f32[304,256]{1,0:T(8,128)S(1)} %pad_maximum_fusion.1.refs_0_), channel_id=1, source_target_pairs={{0,16},{4,20},{8,24},{12,28},{16,0},{20,4},{24,8},{28,12},{1,17},{... | collective-permute-start | bytes 933896 | tf_op jit(solution)/shard_map/ppermute | solution.py:425
  87.4 16.5 %collective-permute-start.6 = (f32[304,256]{1,0:T(8,128)S(1)}, f32[304,256]{1,0:T(8,128)S(1)}, u32[]{:S(2)}, u32[]{:S(2)}) collective-permute-start(f32[304,256]{1,0:T(8,128)S(1)} %pad_maximum_fusion.1.refs_0_), channel_id=1, source_target_pairs={{0,8},{4,12},{8,0},{12,4},{16,24},{20,28},{24,16},{28,20},{1,9},{5... | collective-permute-start | bytes 933896 | tf_op jit(solution)/shard_map/ppermute | solution.py:425
  106.1 10.3 %copy-start.3 = (f32[4,304,256]{2,1,0:T(8,128)S(1)}, f32[4,304,256]{2,1,0:T(8,128)}, u32[]{:S(2)}) copy-start(f32[4,304,256]{2,1,0:T(8,128)} %pad_maximum_fusion.refs_1_.even_ref.refs_0_) | copy-start | bytes 3735556
  107.8 8.5 %collective-permute-start.14 = (f32[16,256]{1,0:T(8,128)}, f32[16,256]{1,0:T(8,128)S(1)}, u32[]{:S(2)}, u32[]{:S(2)}) collective-permute-start(f32[16,256]{1,0:T(8,128)} %fusion.13), channel_id=1, source_target_pairs={{0,3},{1,0},{2,1},{3,2},{4,7},{5,4},{6,5},{7,6},{8,11},{9,8},{10,9... | collective-permute-start | bytes 49160 | tf_op jit(solution)/shard_map/ppermute | solution.py:489
  112.9 5.1 %collective-permute-start.13 = (f32[16,256]{1,0:T(8,128)}, f32[16,256]{1,0:T(8,128)S(1)}, u32[]{:S(2)}, u32[]{:S(2)}) collective-permute-start(f32[16,256]{1,0:T(8,128)} %fusion.13), channel_id=1, source_target_pairs={{0,2},{1,3},{2,0},{3,1},{4,6},{5,7},{6,4},{7,5},{8,10},{9,11},{10,... | collective-permute-start | bytes 49160 | tf_op jit(solution)/shard_map/ppermute | solution.py:489
  115.9 5.7 %collective-permute-start.12 = (f32[16,256]{1,0:T(8,128)}, f32[16,256]{1,0:T(8,128)S(1)}, u32[]{:S(2)}, u32[]{:S(2)}) collective-permute-start(f32[16,256]{1,0:T(8,128)} %fusion.13), channel_id=1, source_target_pairs={{0,1},{1,2},{2,3},{3,0},{4,5},{5,6},{6,7},{7,4},{8,9},{9,10},{10,1... | collective-permute-start | bytes 49160 | tf_op jit(solution)/shard_map/ppermute | solution.py:489
  116.4 14.1 %collective-permute-start.9 = (f32[4,304,256]{2,1,0:T(8,128)S(1)}, f32[4,304,256]{2,1,0:T(8,128)}, u32[]{:S(2)}, u32[]{:S(2)}) collective-permute-start(f32[4,304,256]{2,1,0:T(8,128)S(1)} %copy-done.3), channel_id=1, source_target_pairs={{0,4},{4,0},{8,12},{12,8},{16,20},{20,16},{24,28},{28,24},{1,5},{5... | collective-permute-start | bytes 3735560 | tf_op jit(solution)/shard_map/ppermute | solution.py:425
  123.0 4.6 %copy-start.10 = (f32[4,16,256]{2,1,0:T(8,128)S(1)}, f32[4,16,256]{2,1,0:T(8,128)}, u32[]{:S(2)}) copy-start(f32[4,16,256]{2,1,0:T(8,128)} %pad_maximum_fusion.3.refs_3_.refs_0_) | copy-start | bytes 196612
  123.0 1.3 copy-start.2
  124.4 73.6 %collective-permute-start.23 = (f32[4000,128]{1,0:T(8,128)}, f32[4000,128]{1,0:T(8,128)S(1)}, u32[]{:S(2)}, u32[]{:S(2)}) collective-permute-start(f32[4000,128]{1,0:T(8,128)} %get-tuple-element.27.refs_0_.refs_3_), channel_id=1, source_target_pairs={{1,0},{5,4},{9,8},{13,12},{17,16},{21,20},{25,24},{29,28}} | collective-permute-start | bytes 6144008 | tf_op jit(solution)/shard_map/ppermute | solution.py:404
  125.7 72.3 %collective-permute-start.24 = (f32[4000,128]{1,0:T(8,128)}, f32[4000,128]{1,0:T(8,128)}, u32[]{:S(2)}, u32[]{:S(2)}) collective-permute-start(f32[4000,128]{1,0:T(8,128)} %get-tuple-element.31.refs_4_.refs_1_), channel_id=1, source_target_pairs={{2,3},{6,7},{10,11},{14,15},{18,19},{22,23},{26,27},{30,31}} | collective-permute-start | bytes 6144008 | tf_op jit(solution)/shard_map/ppermute | solution.py:404
  127.7 34.7 %collective-permute-start.17 = (f32[4,16,256]{2,1,0:T(8,128)S(1)}, f32[4,16,256]{2,1,0:T(8,128)S(1)}, u32[]{:S(2)}, u32[]{:S(2)}) collective-permute-start(f32[4,16,256]{2,1,0:T(8,128)S(1)} %copy-done.10), channel_id=1, source_target_pairs={{0,24},{4,28},{8,16},{12,20},{16,8},{20,12},{24,0},{28,4},{1,25},{... | collective-permute-start | bytes 196616 | tf_op jit(solution)/shard_map/ppermute | solution.py:425
  130.0 32.4 %collective-permute-start.16 = (f32[4,16,256]{2,1,0:T(8,128)S(1)}, f32[4,16,256]{2,1,0:T(8,128)S(1)}, u32[]{:S(2)}, u32[]{:S(2)}) collective-permute-start(f32[4,16,256]{2,1,0:T(8,128)S(1)} %copy-done.10), channel_id=1, source_target_pairs={{0,16},{4,20},{8,24},{12,28},{16,0},{20,4},{24,8},{28,12},{1,17},{... | collective-permute-start | bytes 196616 | tf_op jit(solution)/shard_map/ppermute | solution.py:425
  130.5 31.8 %collective-permute-start.15 = (f32[4,16,256]{2,1,0:T(8,128)S(1)}, f32[4,16,256]{2,1,0:T(8,128)S(1)}, u32[]{:S(2)}, u32[]{:S(2)}) collective-permute-start(f32[4,16,256]{2,1,0:T(8,128)S(1)} %copy-done.10), channel_id=1, source_target_pairs={{0,8},{4,12},{8,0},{12,4},{16,24},{20,28},{24,16},{28,20},{1,9},{5... | collective-permute-start | bytes 196616 | tf_op jit(solution)/shard_map/ppermute | solution.py:425
  164.5 23.5 %copy-start.9 = (f32[4,4,16,256]{3,2,1,0:T(8,128)S(1)}, f32[4,4,16,256]{3,2,1,0:T(8,128)}, u32[]{:S(2)}) copy-start(f32[4,4,16,256]{3,2,1,0:T(8,128)} %pad_maximum_fusion.2.refs_1_.refs_2_) | copy-start | bytes 786436
  187.9 3.3 %collective-permute-start.19 = (f32[4,256,256]{2,1,0:T(8,128)}, f32[4,256,256]{2,1,0:T(8,128)S(1)}, u32[]{:S(2)}, u32[]{:S(2)}) collective-permute-start(f32[4,256,256]{2,1,0:T(8,128)} %get-tuple-element.33), channel_id=1, source_target_pairs={{0,4},{4,0},{8,12},{12,8},{16,20},{20,16},{24,28},{28,24},{1,5},{5... | collective-permute-start | bytes 3145736 | tf_op jit(solution)/shard_map/ppermute | solution.py:425
  188.0 8.1 %collective-permute-start.18 = (f32[4,4,16,256]{3,2,1,0:T(8,128)S(1)}, f32[4,4,16,256]{3,2,1,0:T(8,128)S(1)}, u32[]{:S(2)}, u32[]{:S(2)}) collective-permute-start(f32[4,4,16,256]{3,2,1,0:T(8,128)S(1)} %copy-done.9), channel_id=1, source_target_pairs={{0,4},{4,0},{8,12},{12,8},{16,20},{20,16},{24,28},{28,24},{1,5},{5... | collective-permute-start | bytes 786440 | tf_op jit(solution)/shard_map/ppermute | solution.py:425
  193.3 25.1 %collective-permute-start.20 = (f32[256,256]{1,0:T(8,128)S(1)}, f32[256,256]{1,0:T(8,128)}, u32[]{:S(2)}, u32[]{:S(2)}) collective-permute-start(f32[256,256]{1,0:T(8,128)S(1)} %get-tuple-element.42), channel_id=1, source_target_pairs={{0,8},{4,12},{8,0},{12,4},{16,24},{20,28},{24,16},{28,20},{1,9},{5... | collective-permute-start | bytes 786440 | tf_op jit(solution)/shard_map/ppermute | solution.py:425
  194.6 23.7 %collective-permute-start.21 = (f32[256,256]{1,0:T(8,128)S(1)}, f32[256,256]{1,0:T(8,128)}, u32[]{:S(2)}, u32[]{:S(2)}) collective-permute-start(f32[256,256]{1,0:T(8,128)S(1)} %get-tuple-element.41), channel_id=1, source_target_pairs={{0,16},{4,20},{8,24},{12,28},{16,0},{20,4},{24,8},{28,12},{1,17},{... | collective-permute-start | bytes 786440 | tf_op jit(solution)/shard_map/ppermute | solution.py:425
  196.1 1.8 copy-start.12
  196.1 22.2 %collective-permute-start.22 = (f32[256,256]{1,0:T(8,128)S(1)}, f32[256,256]{1,0:T(8,128)S(1)}, u32[]{:S(2)}, u32[]{:S(2)}) collective-permute-start(f32[256,256]{1,0:T(8,128)S(1)} %get-tuple-element.40), channel_id=1, source_target_pairs={{0,24},{4,28},{8,16},{12,20},{16,8},{20,12},{24,0},{28,4},{1,25},{... | collective-permute-start | bytes 786440 | tf_op jit(solution)/shard_map/ppermute | solution.py:425
  198.0 1.4 copy-start.7
  218.2 5.7 %collective-permute-start.25 = (f32[4,128,256]{2,1,0:T(8,128)}, f32[4,128,256]{2,1,0:T(8,128)S(1)}, u32[]{:S(2)}, u32[]{:S(2)}) collective-permute-start(f32[4,128,256]{2,1,0:T(8,128)} %get-tuple-element.35), channel_id=1, source_target_pairs={{0,4},{4,0},{8,12},{12,8},{16,20},{20,16},{24,28},{28,24},{1,5},{5... | collective-permute-start | bytes 1572872 | tf_op jit(solution)/shard_map/ppermute | solution.py:425
  218.4 0.7 copy-start.16
  219.1 5.7 %copy-start.11 = (f32[4,128,256]{2,1,0:T(8,128)S(1)}, f32[4,128,256]{2,1,0:T(8,128)}, u32[]{:S(2)}) copy-start(f32[4,128,256]{2,1,0:T(8,128)} %get-tuple-element.34) | copy-start | bytes 1572868
  219.1 20.9 %copy-start.1 = (f32[256,256]{1,0:T(8,128)S(1)}, f32[256,256]{1,0:T(8,128)}, u32[]{:S(2)}) copy-start(f32[256,256]{1,0:T(8,128)} %param.6) | copy-start | bytes 786436
  223.9 0.8 copy-start.6
  226.5 6.3 %collective-permute-start.26 = (f32[128,256]{1,0:T(8,128)S(1)}, f32[128,256]{1,0:T(8,128)S(1)}, u32[]{:S(2)}, u32[]{:S(2)}) collective-permute-start(f32[128,256]{1,0:T(8,128)S(1)} %get-tuple-element.46), channel_id=1, source_target_pairs={{0,8},{4,12},{8,0},{12,4},{16,24},{20,28},{24,16},{28,20},{1,9},{5... | collective-permute-start | bytes 393224 | tf_op jit(solution)/shard_map/ppermute | solution.py:425
  227.9 8.4 %collective-permute-start.27 = (f32[128,256]{1,0:T(8,128)S(1)}, f32[128,256]{1,0:T(8,128)S(1)}, u32[]{:S(2)}, u32[]{:S(2)}) collective-permute-start(f32[128,256]{1,0:T(8,128)S(1)} %get-tuple-element.45), channel_id=1, source_target_pairs={{0,16},{4,20},{8,24},{12,28},{16,0},{20,4},{24,8},{28,12},{1,17},{... | collective-permute-start | bytes 393224 | tf_op jit(solution)/shard_map/ppermute | solution.py:425
  229.4 6.9 %collective-permute-start.28 = (f32[128,256]{1,0:T(8,128)S(1)}, f32[128,256]{1,0:T(8,128)S(1)}, u32[]{:S(2)}, u32[]{:S(2)}) collective-permute-start(f32[128,256]{1,0:T(8,128)S(1)} %get-tuple-element.44), channel_id=1, source_target_pairs={{0,24},{4,28},{8,16},{12,20},{16,8},{20,12},{24,0},{28,4},{1,25},{... | collective-permute-start | bytes 393224 | tf_op jit(solution)/shard_map/ppermute | solution.py:425
  232.8 3.5 %copy-start.13 = (f32[128,256]{1,0:T(8,128)}, f32[128,256]{1,0:T(8,128)S(1)}, u32[]{:S(2)}) copy-start(f32[128,256]{1,0:T(8,128)S(1)} %collective-permute-done.26.refs_1_) | copy-start | bytes 393220
  236.3 0.7 copy-start.14
  236.3 0.7 copy-start.15
Sparse Core Ops, SparseCore 0:
  116.2 47.3 reduce-scatter.1

commit v6 on v5

--- a/solution.py
+++ b/solution.py
@@ -191,58 +191,49 @@
     )(*operands)
 
 
-def update_kernel(per, offset, me_ref, v_ref, r_ref, even_ref, odd_ref, *refs):
-    out_ref, token_ref, left_ref = refs[-3:]
-    j = pl.program_id(0)
+def update_kernel(me_ref, v_ref, r_ref, even_ref, odd_ref, after_ref, out_ref, token_ref, right_ref):
     nb = r_ref.shape[1]
-
-    @pl.when(j == 0)
+    per = even_ref.shape[2]
+
+    @pl.when(pl.program_id(0) == 0)
     def _():
         token_ref[...] = jnp.zeros_like(token_ref)
-        high, low = split(r_ref[...])
-        left_ref[:, :nb] = high
-        left_ref[:, nb : 2 * nb] = low
-        left_ref[:, 2 * nb :] = high
-
-    count = v_ref.shape[1] // per
-    blocks = [
-        take(((j + offset) * count + g) ^ me_ref[0], even_ref, odd_ref, slice(0, nb))
-        for g in range(count)
-    ]
-    high, low = split(blocks[0] if count == 1 else jnp.concatenate(blocks, axis=1))
-    right = jnp.concatenate([high, high, low], axis=0)
-    out_ref[...] = v_ref[...] - mul(left_ref[...], right)
-
-
-def update(me, vectors, reflectors, c, offset, blocks, after, before, wide):
+        for w in range(2 * even_ref.shape[0]):
+            high, low = split(take(w ^ me_ref[0], even_ref, odd_ref, slice(0, nb)))
+            here = slice(w * per, (w + 1) * per)
+            right_ref[:nb, here] = high
+            right_ref[nb : 2 * nb, here] = high
+            right_ref[2 * nb :, here] = low
+
+    high, low = split(r_ref[...])
+    left = jnp.concatenate([high, low, high], axis=1)
+    out_ref[...] = v_ref[...] - mul(left, right_ref[...])
+
+
+def update(me, vectors, reflectors, c, after):
     rows, columns = vectors.shape
     nb = reflectors.shape[1]
-    per = columns // wide
-    step = width(columns, wide)
-    operands = [me, vectors, reflectors, *c, *after]
-    aliases = {len(operands): 0} if before else {}
-    operands += before
-    columns_of = pl.BlockSpec((rows, step), lambda j, *_: (0, j + offset))
-    return pl.pallas_call(
-        functools.partial(update_kernel, per, offset),
+    count = next(x for x in range(4, rows) if rows % (16 * x) == 0)
+    rows_of = pl.BlockSpec((rows // count, columns), lambda j, *_: (j, 0))
+    return pl.pallas_call(
+        update_kernel,
         grid_spec=pltpu.PrefetchScalarGridSpec(
             num_scalar_prefetch=1,
-            grid=(blocks,),
-            in_specs=[columns_of]
-            + [whole(x.shape) for x in (reflectors, *c)]
-            + [ANY] * (len(operands) - 5),
-            out_specs=[columns_of, whole((8, 128))],
-            scratch_shapes=[pltpu.VMEM((rows, 3 * nb), BF16)],
+            grid=(count,),
+            in_specs=[rows_of, pl.BlockSpec((rows // count, nb), lambda j, *_: (j, 0))]
+            + [whole(x.shape) for x in c]
+            + [ANY],
+            out_specs=[rows_of, whole((8, 128))],
+            scratch_shapes=[pltpu.VMEM((3 * nb, columns), BF16)],
         ),
         out_shape=[
             jax.ShapeDtypeStruct(vectors.shape, F32),
             jax.ShapeDtypeStruct((8, 128), F32),
         ],
-        input_output_aliases=aliases,
         compiler_params=params(),
         cost_estimate=SHORT,
         name="update",
-    )(*operands)
+    )(me, vectors, reflectors, *c, after)
 
 
 def late_kernel(per, counts, at_ref, u_ref, after_ref, *refs):
@@ -305,13 +296,31 @@
     )(at, updated, after, *flat)
 
 
+def total_kernel(*refs):
+    refs[-1][...] = functools.reduce(jnp.add, [ref[...] for ref in refs[:-1]])
+
+
+def total(terms):
+    shape = terms[0].shape
+    return pl.pallas_call(
+        total_kernel,
+        grid=(1,),
+        in_specs=[pl.BlockSpec(shape, lambda j: (0, 0))] * len(terms),
+        out_specs=pl.BlockSpec(shape, lambda j: (0, 0)),
+        out_shape=jax.ShapeDtypeStruct(shape, F32),
+        compiler_params=params(),
+        cost_estimate=LONG,
+        name="total",
+    )(*terms)
+
+
 def base_kernel(n, each, ride, at_ref, ready_ref, c_ref, *refs):
     *refs, out_ref, coef_ref, small_ref = refs
     me, z = at_ref[0], at_ref[1]
     nb = c_ref.shape[0]
     k = small_ref.shape[0]
     if ride:
-        c_even, c_odd, ce_ref, co_ref, *refs = refs
+        c_even, c_odd, ce_ref, co_ref = refs[1:]
         half, _, rows, _ = ce_ref.shape
         wide = 2 * half
         for w in range(wide):
@@ -323,21 +332,21 @@
                 first = pl.multiple_of((z + n - s) % n * each + w * rows, rows)
                 coef_ref[pl.ds(first, rows), :] = take(index, ce_ref, co_ref, s)
     else:
-        all_small, all_coef, *refs = refs
+        all_small, all_coef = refs[1:]
         small_ref[...] = all_small[...]
         for s in range(n):
             coef_ref[s * each : (s + 1) * each] = all_coef[s]
     corrected = ready_ref[...] - three(split(small_ref[...]), split(c_ref[...]))
     out_ref[...] = -three(split(coef_ref[...]), split(corrected[:nb]))
-    total = functools.reduce(jnp.add, [ref[...] for ref in refs])
+    total = refs[0]
     for slot in range(1 + total.shape[0] // each):
         piece = corrected[nb:] if slot == 0 else total[(slot - 1) * each : slot * each]
         first = pl.multiple_of(at_ref[1 + slot] * each, each)
         out_ref[pl.ds(first, each), :] += piece
 
 
-def base(at, ready, c, extra, terms, n, each, ride):
-    operands = [ready, c, *extra, *terms]
+def base(at, ready, c, middle, extra, n, each, ride):
+    operands = [ready, c, middle, *extra]
     k, per = ready.shape
     nb = c.shape[0]
     return pl.pallas_call(
@@ -465,10 +474,10 @@
     ride = (k + each) // wide if fits else 0
     even, odd, left, own_part, small = project(me, vectors, reflectors, e_row, own, wide, ride)
     terms = scatter_terms(even, odd, wide)
+    highest = lax.Precision.HIGHEST
+    turn = (((1,), (1,)), ((), ()))
     if n > 2:
         held = travel(came, held, n, 2, [left, terms[0]])
-    highest = lax.Precision.HIGHEST
-    turn = (((1,), (1,)), ((), ()))
     sums, token = early(vectors, left, 0, half, came[(1, 0)], [], wide)
     terms[0] = gate(terms[:1], token)[0]
     projected = functools.reduce(jnp.add, terms)
@@ -479,37 +488,34 @@
     sums, token = early(vectors, left, half, blocks - half, payload, [sums], wide)
     ready = lax.psum_scatter(sums, "wide", scatter_dimension=0)
     c = collect(payload, wide, [token])
-    ready_shares = []
+    for hops in range(3, n):
+        held = travel(came, held, n, hops, [token])
+    after = came[(min(2, n - 1), 0)]
+    updated, token = update(me, vectors, reflectors, c, after)
+
     if ride:
-        (mine,) = gate([projected[nb + k // wide :]], c[0])
+        (mine,) = gate([projected[nb + k // wide :]], after)
         mine = lax.dot_general(mine, triangle, turn, precision=highest)
-        shares = jnp.stack(
-            [mine]
-            + [
-                lax.ppermute(mine, "narrow", [(p, (p + s) % n) for p in range(n)])
-                for s in range(1, n)
-            ]
-        )
-        ready_shares = [shares]
-
-    for hops in range(3, n):
-        held = travel(came, held, n, hops, [token, *ready_shares])
-    after = came[(min(2, n - 1), 0)]
-    updated, token = update(me, vectors, reflectors, c, 0, blocks, [after], [], wide)
+        shares = [
+            lax.ppermute(mine, "narrow", [(p, (p + s) % n) for p in range(n)]) for s in range(1, n)
+        ]
+        shares = jnp.stack([*gate([mine], token), *shares])
+        token = shares
+    slots = [options(came, places, z) for places in table]
+    even, odd = late(me, updated, slots[:-1], token, wide)
     if ride:
-        share_even, share_odd = collect(shares, wide, [token])
-        extra = [*c, share_even, share_odd]
-        (token,) = gate([token], share_even)
+        extra = [*c, *collect(shares, wide, [even])]
+        token = extra[-2]
     else:
         own_part = lax.dot_general(lax.psum(own_part, "wide"), triangle, turn, precision=highest)
         extra = [lax.psum(small, "wide"), lax.all_gather(own_part, "narrow")]
-    slots = [options(came, places, z) for places in table]
-    even, odd = late(me, updated, slots[:-1], token, wide)
     middle = scatter_terms(even, odd, wide)
-    (token,) = gate([token], middle[0], extra[-1])
-    even, odd = late(me, updated, slots[-1:], token, wide)
-    base_block = base(at, ready, coefficients, extra, middle, n, each, ride)
-    tail = scatter_terms(even, odd, wide, base_block)
+    (ready,) = gate([ready], middle[0], token)
+    even, odd = late(me, updated, slots[-1:], ready, wide)
+    middle = total(middle)
+    tail = scatter_terms(even, odd, wide, middle)
+    (ready,) = gate([ready], tail[0])
+    base_block = base(at, ready, coefficients, middle, extra, n, each, ride)
     return (updated, last(at, base_block, tail, each))
 
 

time: 248 us -> 246 us (level)
  waiting for transfers between devices: 27.1 us -> 23.9 us
    ppermute x20, waiting for transfers between devices: 12.3 us -> 4.82 us  [swap(): return lax.ppermute(x, 'wide', [(i, i ^ distance) for i in range(wide)])]
    ppermute x6, waiting for transfers between devices: 9.29 us -> 12.8 us  [travel(): held = [lax.ppermute(held[d], 'narrow', pairs[d]) for d in (0, 1)]]
    pallas_call x1 -> x2, Pallas kernels: 31.2 us -> 32.3 us  [the longest x1 30.4 us: update(): pl.pallas_call(update_kernel, grid_spec=pltpu.PrefetchScalarGridSpec(num_...]
    unnamed x34 -> x40, local copies, waits for them, and re-layouts: 4.89 us -> 5.71 us
  transfers between devices with their start and end apart: 30 -> 30, of which waited for: 9 -> 7; matrix products, arithmetic and copies ran while one was open for 6% -> 7% of each run, Pallas kernels for 55% -> 56%
where the time goes in v6:
time: 246 us; the launch traced here: 245 us
  Pallas kernels  140 us (57%)
  starting transfers between devices  41.4 us (17%)
  waiting for transfers between devices  23.9 us (10%)
  other arithmetic  15.5 us (6%)
  between operations  14.4 us (6%)
  local copies, waits for them, and re-layouts  7.61 us (3%)
    pallas_call x2, Pallas kernels, late(): pl.pallas_call(functools.partial(late_kernel, per, counts), grid_spec=plt...  42.3 us
    pallas_call x2, Pallas kernels, early(): pl.pallas_call(functools.partial(early_kernel, per), grid=(blocks,), in_s...  30.6 us
    pallas_call x1, Pallas kernels, update(): pl.pallas_call(update_kernel, grid_spec=pltpu.PrefetchScalarGridSpec(num_...  30.4 us
    pallas_call x1, Pallas kernels, project(): pl.pallas_call(functools.partial(project_kernel, per, wide), grid_spec=pl...  27.6 us
    ppermute x20, starting transfers between devices, swap(): return lax.ppermute(x, 'wide', [(i, i ^ distance) for i in range(wide)])  18.8 us
    ppermute x6, starting transfers between devices, travel(): held = [lax.ppermute(held[d], 'narrow', pairs[d]) for d in (0, 1)]  14.7 us
    ppermute x6, waiting for transfers between devices, travel(): held = [lax.ppermute(held[d], 'narrow', pairs[d]) for d in (0, 1)]  12.8 us
    ppermute x3, starting transfers between devices, on_device(): lax.ppermute(mine, 'narrow', [(p, (p + s) % n) for p in range(n)])  7.92 us
  transfers between devices with their start and end apart: 30, of which 7 were waited for; matrix products, arithmetic and copies ran while one was open for 7% of the time, Pallas kernels for 56%

profile of v6, /device:TPU:0, one launch (start us, length us, event | category | flops | bytes accessed | tf_op | source)
XLA Modules:
  0.0 244.6 jit_solution(11583463297847306254)
XLA Ops:
  7.2 2.7 %slice_multiply_fusion.x_ref = f32[4000,128]{1,0:T(8,128)S(1)} fusion(f32[4000,2048]{1,0:T(8,128)} %v_ref.7, f32[4000]{0:T(1024)} %param.7), kind=kLoop, calls=%fused_computation | loop fusion | flops 512000 | bytes 4112000 | tf_op jit(solution)/shard_map/mul | solution.py:467
  10.0 1.3 collective-permute-start.1
  11.3 6.8 %collective-permute-start.2 = (f32[4000,128]{1,0:T(8,128)S(1)}, f32[4000,128]{1,0:T(8,128)}, u32[]{:S(2)}, u32[]{:S(2)}) collective-permute-start(f32[4000,128]{1,0:T(8,128)S(1)} %slice_multiply_fusion.x_ref), channel_id=1, source_target_pairs={{0,1},{1,2},{2,3},{4,5},{5,6},{6,7},{8,9},{9,10},{10,11},{12,13},{... | collective-permute-start | bytes 6144008 | tf_op jit(solution)/shard_map/ppermute | solution.py:413
  18.1 27.6 %project.1 = (f32[4,320,256]{2,1,0:T(8,128)}, f32[4,320,256]{2,1,0:T(8,128)}, bf16[768,4000]{1,0:T(8,128)(2,1)}, f32[128,256]{1,0:T(8,128)}, f32[384,256]{1,0:T(8,128)}) custom-call(s32[1]{0:T(128)} %bitcast.me_ref, f32[4000,2048]{1,0:T(8,128)} %v_ref.7, f32[4000,256]{1,0:T(8,128)} %r_ref.3, f32[1,4000]{1,0:T(1,128)} %bitcast.58, f32[4000,128]{1,0:T(8,128)} %copy-done.3), custom_call_target="tpu_custom_call" | custom-call | flops 1024 | bytes 1024 | tf_op jit(solution)/shard_map/project/pallas_call | solution.py:141
  45.8 3.2 %collective-permute-done = f32[4,320,256]{2,1,0:T(8,128)S(1)} collective-permute-done((f32[4,320,256]{2,1,0:T(8,128)}, f32[4,320,256]{2,1,0:T(8,128)S(1)}, u32[]{:S(2)}, u32[]{:S(2)}) %collective-permute-start) | collective-permute-done | bytes 1310752 | tf_op jit(solution)/shard_map/ppermute | solution.py:434
  49.0 2.4 fusion.2
  51.4 8.2 %collective-permute-done.1.refs_0_ = f32[4000,128]{1,0:T(8,128)} collective-permute-done((f32[4000,128]{1,0:T(8,128)S(1)}, f32[4000,128]{1,0:T(8,128)}, u32[]{:S(2)}, u32[]{:S(2)}) %collective-permute-start.1) | collective-permute-done | bytes 2048032 | tf_op jit(solution)/shard_map/ppermute | solution.py:413
  59.6 1.1 collective-permute-done.2.refs_1_
  60.7 1.3 collective-permute-start.10
  62.0 2.0 collective-permute-start.11
  64.0 2.6 %collective-permute-start.5 = (f32[320,256]{1,0:T(8,128)}, f32[320,256]{1,0:T(8,128)S(1)}, u32[]{:S(2)}, u32[]{:S(2)}) collective-permute-start(f32[320,256]{1,0:T(8,128)} %get-tuple-element.37), channel_id=1, source_target_pairs={{0,24},{4,28},{8,16},{12,20},{16,8},{20,12},{24,0},{28,4},{1,25},{... | collective-permute-start | bytes 983048 | tf_op jit(solution)/shard_map/ppermute | solution.py:434
  67.4 15.3 %early.2 = (f32[8,384,256]{2,1,0:T(8,128)}, f32[8,128]{1,0:T(8,128)}) custom-call(f32[4000,2048]{1,0:T(8,128)} %v_ref.7, bf16[768,4000]{1,0:T(8,128)(2,1)} %get-tuple-element.21.refs_2_.left_ref, f32[4000,128]{1,0:T(8,128)} %get-tuple-element.22.refs_0_), custom_call_target="tpu_custom_call" | custom-call | flops 1024 | bytes 1024 | tf_op jit(solution)/shard_map/early/pallas_call | solution.py:174
  82.7 1.1 add_add_fusion
  84.3 2.7 %collective-permute-start.8 = (f32[304,256]{1,0:T(8,128)S(1)}, f32[304,256]{1,0:T(8,128)S(1)}, u32[]{:S(2)}, u32[]{:S(2)}) collective-permute-start(f32[304,256]{1,0:T(8,128)S(1)} %pad_maximum_fusion.1.refs_0_), channel_id=1, source_target_pairs={{0,24},{4,28},{8,16},{12,20},{16,8},{20,12},{24,0},{28,4},{1,25},{... | collective-permute-start | bytes 933896 | tf_op jit(solution)/shard_map/ppermute | solution.py:434
  87.8 15.3 %early.3 = (f32[8,384,256]{2,1,0:T(8,128)}, f32[8,128]{1,0:T(8,128)}) custom-call(f32[4000,2048]{1,0:T(8,128)} %v_ref.7, bf16[768,4000]{1,0:T(8,128)(2,1)} %get-tuple-element.21.refs_2_.left_ref, f32[304,256]{1,0:T(8,128)} %copy-done.5, f32[8,384,256]{2,1,0:T(8,128)} %get-tuple-element.24.refs_1_), custom_call_target="tpu_custom_call", output_to_operand_aliasing={{0}: (3, {})} | custom-call | flops 1024 | bytes 1024 | tf_op jit(solution)/shard_map/early/pallas_call | solution.py:174
  104.1 1.3 pad_maximum_fusion.even_ref.refs_1_
  105.6 3.5 %collective-permute-done.10.refs_0_ = f32[4000,128]{1,0:T(8,128)S(1)} collective-permute-done((f32[4000,128]{1,0:T(8,128)}, f32[4000,128]{1,0:T(8,128)S(1)}, u32[]{:S(2)}, u32[]{:S(2)}) %collective-permute-start.10) | collective-permute-done | bytes 2048032 | tf_op jit(solution)/shard_map/ppermute | solution.py:413
  109.1 1.3 copy-done.2
  110.4 1.3 collective-permute-start.19
  111.7 2.0 collective-permute-start.20
  113.7 1.3 slice.118.refs_0_
  115.0 1.0 fusion.13.refs_0_
  116.1 3.4 %collective-permute-start.14 = (f32[16,256]{1,0:T(8,128)S(1)}, f32[16,256]{1,0:T(8,128)S(1)}, u32[]{:S(2)}, u32[]{:S(2)}) collective-permute-start(f32[16,256]{1,0:T(8,128)S(1)} %fusion.13.refs_0_), channel_id=1, source_target_pairs={{0,3},{1,0},{2,1},{3,2},{4,7},{5,4},{6,5},{7,6},{8,11},{9,8},{10,9... | collective-permute-start | bytes 49160 | tf_op jit(solution)/shard_map/ppermute | solution.py:500
  119.5 2.5 %collective-permute-start.13 = (f32[16,256]{1,0:T(8,128)S(1)}, f32[16,256]{1,0:T(8,128)S(1)}, u32[]{:S(2)}, u32[]{:S(2)}) collective-permute-start(f32[16,256]{1,0:T(8,128)S(1)} %fusion.13.refs_0_), channel_id=1, source_target_pairs={{0,2},{1,3},{2,0},{3,1},{4,6},{5,7},{6,4},{7,5},{8,10},{9,11},{10,... | collective-permute-start | bytes 49160 | tf_op jit(solution)/shard_map/ppermute | solution.py:500
  122.0 1.9 collective-permute-start.12
  124.6 30.4 %update.1 = (f32[4000,2048]{1,0:T(8,128)}, f32[8,128]{1,0:T(8,128)}) custom-call(s32[1]{0:T(128)} %bitcast.me_ref, f32[4000,2048]{1,0:T(8,128)} %v_ref.7, f32[4000,256]{1,0:T(8,128)} %r_ref.3, f32[4,304,256]{2,1,0:T(8,128)} %copy-done.4, f32[4,304,256]{2,1,0:T(8,128)} %collective-permute-done.9.odd_ref.refs_2_, ...), custom_call_target="tpu_custom_call" | custom-call | flops 1024 | bytes 1024 | tf_op jit(solution)/shard_map/update/pallas_call | solution.py:218
  155.0 6.3 %collective-permute-done.14 = f32[16,256]{1,0:T(8,128)S(1)} collective-permute-done((f32[16,256]{1,0:T(8,128)S(1)}, f32[16,256]{1,0:T(8,128)S(1)}, u32[]{:S(2)}, u32[]{:S(2)}) %collective-permute-start.14) | collective-permute-done | bytes 16416 | tf_op jit(solution)/shard_map/ppermute | solution.py:500
  161.3 1.4 pad_maximum_fusion.3.after_ref.refs_0_
  162.6 23.4 %late.2 = (f32[4,256,256]{2,1,0:T(8,128)}, f32[4,256,256]{2,1,0:T(8,128)}) custom-call(s32[3]{0:T(128)} %pad_add_fusion.at_ref, f32[4000,2048]{1,0:T(8,128)} %get-tuple-element.17.u_ref, f32[4,16,256]{2,1,0:T(8,128)} %pad_maximum_fusion.3.after_ref.refs_0_, f32[4000,128]{1,0:T(8,128)} %get-tuple-element.22.refs_0_, ...), custom_call_target="tpu_custom_call" | custom-call | flops 1024 | bytes 1024 | tf_op jit(solution)/shard_map/late/pallas_call | solution.py:279
  186.1 2.7 %collective-permute-start.18 = (f32[4,16,256]{2,1,0:T(8,128)S(1)}, f32[4,16,256]{2,1,0:T(8,128)S(1)}, u32[]{:S(2)}, u32[]{:S(2)}) collective-permute-start(f32[4,16,256]{2,1,0:T(8,128)S(1)} %copy-done.9), channel_id=1, source_target_pairs={{0,24},{4,28},{8,16},{12,20},{16,8},{20,12},{24,0},{28,4},{1,25},{... | collective-permute-start | bytes 196616 | tf_op jit(solution)/shard_map/ppermute | solution.py:434
  189.3 1.3 collective-permute-start.16
  190.6 2.0 fusion.4
  192.6 0.7 collective-permute-start.22
  193.3 1.5 collective-permute-start.23
  194.9 1.3 collective-permute-start.24
  197.3 1.6 pad_maximum_fusion.2.refs_2_.refs_3_
  198.9 1.2 copy-done.7
  200.2 18.9 %late.3 = (f32[4,128,256]{2,1,0:T(8,128)}, f32[4,128,256]{2,1,0:T(8,128)}) custom-call(s32[2]{0:T(128)} %pad_add_fusion.1.at_ref, f32[4000,2048]{1,0:T(8,128)} %get-tuple-element.17.u_ref, f32[384,256]{1,0:T(8,128)} %gate.17.after_ref.refs_0_, f32[4000,128]{1,0:T(8,128)} %get-tuple-element.27.after_ref.refs_1_.refs_3_.refs_0_, ...), custom_call_target="tpu_custom_call" | custom-call | flops 1024 | bytes 1024 | tf_op jit(solution)/shard_map/late/pallas_call | solution.py:279
  219.2 0.7 copy-done.19
  219.9 1.9 total.1.refs_1_.refs_0_
  221.8 0.8 copy-done.6
  222.6 1.8 fusion.9
  224.4 0.7 collective-permute-start.26
  225.2 1.5 collective-permute-start.27
  226.7 1.3 collective-permute-start.28
  227.9 4.6 %base.1.base_ref = f32[512,256]{1,0:T(8,128)} custom-call(s32[5]{0:T(128)} %stack.84.at_ref, f32[384,256]{1,0:T(8,128)} %gate.19.ready_ref, f32[256,256]{1,0:T(8,128)} %copy-done.10, f32[256,256]{1,0:T(8,128)} %total.1.refs_1_.refs_0_, f32[4,304,256]{2,1,0:T(8,128)} %copy-done.4, f32[4,304,256]{2,1,0:T(8,128)} %collective-permute-done.9.odd_ref.refs_2_, ...), custom_call_target="tpu_custom_call" | custom-call | flops 99999997952 | bytes 1024 | tf_op jit(solution)/shard_map/base/pallas_call | solution.py:352
  232.7 1.5 collective-permute-done.28.refs_3_
  234.8 3.0 %last.1 = f32[256,512]{1,0:T(8,128)} custom-call(s32[5]{0:T(128)} %stack.84.at_ref, f32[512,256]{1,0:T(8,128)} %base.1.base_ref, f32[128,256]{1,0:T(8,128)} %get-tuple-element.47.refs_1_.refs_0_, f32[128,256]{1,0:T(8,128)} %copy-done.16, f32[128,256]{1,0:T(8,128)} %copy-done.17, f32[128,256]{1,0:T(8,128)} %copy-done.18), custom_call_target="tpu_custom_call" | custom-call | flops 1024 | bytes 1024 | tf_op jit(solution)/shard_map/last/pallas_call | solution.py:380
  (88 shorter events, 6.6 us)
Async XLA Ops:
  7.2 76.7 %copy-start = (f32[256,256]{1,0:T(8,128)S(1)}, f32[256,256]{1,0:T(8,128)}, u32[]{:S(2)}) copy-start(f32[256,256]{1,0:T(8,128)} %param.6) | copy-start | bytes 786436
  7.2 191.7 %reduce-scatter.2.cloned.1.call-start = ((), (), s32[]{:S(2)}) async-start(), calls=%async_computation.1 | async-start | bytes 3538944 | tf_op jit(solution)/shard_map/reduce_scatter | solution.py:489
  10.0 8.2 %copy-start.3 = (f32[4000,128]{1,0:T(8,128)}, f32[4000,128]{1,0:T(8,128)S(1)}, u32[]{:S(2)}) copy-start(f32[4000,128]{1,0:T(8,128)S(1)} %slice_multiply_fusion.x_ref) | copy-start | bytes 6144004
  10.0 49.6 %collective-permute-start.1 = (f32[4000,128]{1,0:T(8,128)S(1)}, f32[4000,128]{1,0:T(8,128)}, u32[]{:S(2)}, u32[]{:S(2)}) collective-permute-start(f32[4000,128]{1,0:T(8,128)S(1)} %slice_multiply_fusion.x_ref), channel_id=1, source_target_pairs={{1,0},{2,1},{3,2},{5,4},{6,5},{7,6},{9,8},{10,9},{11,10},{13,12},{... | collective-permute-start | bytes 6144008 | tf_op jit(solution)/shard_map/ppermute | solution.py:413
  11.3 49.4 %collective-permute-start.2 = (f32[4000,128]{1,0:T(8,128)S(1)}, f32[4000,128]{1,0:T(8,128)}, u32[]{:S(2)}, u32[]{:S(2)}) collective-permute-start(f32[4000,128]{1,0:T(8,128)S(1)} %slice_multiply_fusion.x_ref), channel_id=1, source_target_pairs={{0,1},{1,2},{2,3},{4,5},{5,6},{6,7},{8,9},{9,10},{10,11},{12,13},{... | collective-permute-start | bytes 6144008 | tf_op jit(solution)/shard_map/ppermute | solution.py:413
  45.7 3.2 %collective-permute-start = (f32[4,320,256]{2,1,0:T(8,128)}, f32[4,320,256]{2,1,0:T(8,128)S(1)}, u32[]{:S(2)}, u32[]{:S(2)}) collective-permute-start(f32[4,320,256]{2,1,0:T(8,128)} %get-tuple-element.20), channel_id=1, source_target_pairs={{0,4},{4,0},{8,12},{12,8},{16,20},{20,16},{24,28},{28,24},{1,5},{5... | collective-permute-start | bytes 3932168 | tf_op jit(solution)/shard_map/ppermute | solution.py:434
  60.7 48.4 %collective-permute-start.10 = (f32[4000,128]{1,0:T(8,128)}, f32[4000,128]{1,0:T(8,128)S(1)}, u32[]{:S(2)}, u32[]{:S(2)}) collective-permute-start(f32[4000,128]{1,0:T(8,128)} %get-tuple-element.22.refs_0_), channel_id=1, source_target_pairs={{1,0},{2,1},{5,4},{6,5},{9,8},{10,9},{13,12},{14,13},{17,16},{18,1... | collective-permute-start | bytes 6144008 | tf_op jit(solution)/shard_map/ppermute | solution.py:413
  62.0 47.1 %collective-permute-start.11 = (f32[4000,128]{1,0:T(8,128)}, f32[4000,128]{1,0:T(8,128)}, u32[]{:S(2)}, u32[]{:S(2)}) collective-permute-start(f32[4000,128]{1,0:T(8,128)} %get-tuple-element.26.refs_1_.refs_2_), channel_id=1, source_target_pairs={{1,2},{2,3},{5,6},{6,7},{9,10},{10,11},{13,14},{14,15},{17,18},{18... | collective-permute-start | bytes 6144008 | tf_op jit(solution)/shard_map/ppermute | solution.py:413
  64.0 18.8 %collective-permute-start.5 = (f32[320,256]{1,0:T(8,128)}, f32[320,256]{1,0:T(8,128)S(1)}, u32[]{:S(2)}, u32[]{:S(2)}) collective-permute-start(f32[320,256]{1,0:T(8,128)} %get-tuple-element.37), channel_id=1, source_target_pairs={{0,24},{4,28},{8,16},{12,20},{16,8},{20,12},{24,0},{28,4},{1,25},{... | collective-permute-start | bytes 983048 | tf_op jit(solution)/shard_map/ppermute | solution.py:434
  66.6 16.2 %collective-permute-start.4 = (f32[320,256]{1,0:T(8,128)}, f32[320,256]{1,0:T(8,128)S(1)}, u32[]{:S(2)}, u32[]{:S(2)}) collective-permute-start(f32[320,256]{1,0:T(8,128)} %get-tuple-element.38), channel_id=1, source_target_pairs={{0,16},{4,20},{8,24},{12,28},{16,0},{20,4},{24,8},{28,12},{1,17},{... | collective-permute-start | bytes 983048 | tf_op jit(solution)/shard_map/ppermute | solution.py:434
  67.1 15.7 %collective-permute-start.3 = (f32[320,256]{1,0:T(8,128)}, f32[320,256]{1,0:T(8,128)S(1)}, u32[]{:S(2)}, u32[]{:S(2)}) collective-permute-start(f32[320,256]{1,0:T(8,128)} %get-tuple-element.36), channel_id=1, source_target_pairs={{0,8},{4,12},{8,0},{12,4},{16,24},{20,28},{24,16},{28,20},{1,9},{5... | collective-permute-start | bytes 983048 | tf_op jit(solution)/shard_map/ppermute | solution.py:434
  83.8 3.2 %copy-start.8 = (f32[320,256]{1,0:T(8,128)}, f32[320,256]{1,0:T(8,128)S(1)}, u32[]{:S(2)}) copy-start(f32[320,256]{1,0:T(8,128)S(1)} %add_add_fusion) | copy-start | bytes 983044
  84.2 3.2 %copy-start.10 = (f32[256,256]{1,0:T(8,128)}, f32[256,256]{1,0:T(8,128)S(1)}, u32[]{:S(2)}) copy-start(f32[256,256]{1,0:T(8,128)S(1)} %convolution_bitcast_fusion.c_ref) | copy-start | bytes 786436
  84.3 3.6 %copy-start.5 = (f32[304,256]{1,0:T(8,128)}, f32[304,256]{1,0:T(8,128)S(1)}, u32[]{:S(2)}) copy-start(f32[304,256]{1,0:T(8,128)S(1)} %pad_maximum_fusion.1.refs_0_) | copy-start | bytes 933892
  84.3 18.9 %collective-permute-start.8 = (f32[304,256]{1,0:T(8,128)S(1)}, f32[304,256]{1,0:T(8,128)S(1)}, u32[]{:S(2)}, u32[]{:S(2)}) collective-permute-start(f32[304,256]{1,0:T(8,128)S(1)} %pad_maximum_fusion.1.refs_0_), channel_id=1, source_target_pairs={{0,24},{4,28},{8,16},{12,20},{16,8},{20,12},{24,0},{28,4},{1,25},{... | collective-permute-start | bytes 933896 | tf_op jit(solution)/shard_map/ppermute | solution.py:434
  87.0 16.2 %collective-permute-start.7 = (f32[304,256]{1,0:T(8,128)S(1)}, f32[304,256]{1,0:T(8,128)S(1)}, u32[]{:S(2)}, u32[]{:S(2)}) collective-permute-start(f32[304,256]{1,0:T(8,128)S(1)} %pad_maximum_fusion.1.refs_0_), channel_id=1, source_target_pairs={{0,16},{4,20},{8,24},{12,28},{16,0},{20,4},{24,8},{28,12},{1,17},{... | collective-permute-start | bytes 933896 | tf_op jit(solution)/shard_map/ppermute | solution.py:434
  87.5 15.8 %collective-permute-start.6 = (f32[304,256]{1,0:T(8,128)S(1)}, f32[304,256]{1,0:T(8,128)S(1)}, u32[]{:S(2)}, u32[]{:S(2)}) collective-permute-start(f32[304,256]{1,0:T(8,128)S(1)} %pad_maximum_fusion.1.refs_0_), channel_id=1, source_target_pairs={{0,8},{4,12},{8,0},{12,4},{16,24},{20,28},{24,16},{28,20},{1,9},{5... | collective-permute-start | bytes 933896 | tf_op jit(solution)/shard_map/ppermute | solution.py:434
  103.2 0.7 copy-start.12
  103.2 0.8 copy-start.13
  103.2 0.9 copy-start.14
  105.5 4.9 %copy-start.4 = (f32[4,304,256]{2,1,0:T(8,128)}, f32[4,304,256]{2,1,0:T(8,128)S(1)}, u32[]{:S(2)}) copy-start(f32[4,304,256]{2,1,0:T(8,128)S(1)} %pad_maximum_fusion.even_ref.refs_1_) | copy-start | bytes 3735556
  105.5 16.6 %collective-permute-start.9 = (f32[4,304,256]{2,1,0:T(8,128)S(1)}, f32[4,304,256]{2,1,0:T(8,128)}, u32[]{:S(2)}, u32[]{:S(2)}) collective-permute-start(f32[4,304,256]{2,1,0:T(8,128)S(1)} %pad_maximum_fusion.even_ref.refs_1_), channel_id=1, source_target_pairs={{0,4},{4,0},{8,12},{12,8},{16,20},{20,16},{24,28},{28,24},{1,5},{5... | collective-permute-start | bytes 3735560 | tf_op jit(solution)/shard_map/ppermute | solution.py:434
  109.1 1.3 copy-start.2
  110.4 88.4 %collective-permute-start.19 = (f32[4000,128]{1,0:T(8,128)}, f32[4000,128]{1,0:T(8,128)S(1)}, u32[]{:S(2)}, u32[]{:S(2)}) collective-permute-start(f32[4000,128]{1,0:T(8,128)} %get-tuple-element.27.after_ref.refs_1_.refs_3_.refs_0_), channel_id=1, source_target_pairs={{1,0},{5,4},{9,8},{13,12},{17,16},{21,20},{25,24},{29,28}} | collective-permute-start | bytes 6144008 | tf_op jit(solution)/shard_map/ppermute | solution.py:413
  111.7 87.2 %collective-permute-start.20 = (f32[4000,128]{1,0:T(8,128)}, f32[4000,128]{1,0:T(8,128)}, u32[]{:S(2)}, u32[]{:S(2)}) collective-permute-start(f32[4000,128]{1,0:T(8,128)} %get-tuple-element.31.refs_4_.refs_1_), channel_id=1, source_target_pairs={{2,3},{6,7},{10,11},{14,15},{18,19},{22,23},{26,27},{30,31}} | collective-permute-start | bytes 6144008 | tf_op jit(solution)/shard_map/ppermute | solution.py:413
  116.0 39.0 %copy-start.15 = (f32[16,256]{1,0:T(8,128)}, f32[16,256]{1,0:T(8,128)S(1)}, u32[]{:S(2)}) copy-start(f32[16,256]{1,0:T(8,128)S(1)} %fusion.13.refs_0_) | copy-start | bytes 49156
  116.1 45.2 %collective-permute-start.14 = (f32[16,256]{1,0:T(8,128)S(1)}, f32[16,256]{1,0:T(8,128)S(1)}, u32[]{:S(2)}, u32[]{:S(2)}) collective-permute-start(f32[16,256]{1,0:T(8,128)S(1)} %fusion.13.refs_0_), channel_id=1, source_target_pairs={{0,3},{1,0},{2,1},{3,2},{4,7},{5,4},{6,5},{7,6},{8,11},{9,8},{10,9... | collective-permute-start | bytes 49160 | tf_op jit(solution)/shard_map/ppermute | solution.py:500
  119.5 41.8 %collective-permute-start.13 = (f32[16,256]{1,0:T(8,128)S(1)}, f32[16,256]{1,0:T(8,128)S(1)}, u32[]{:S(2)}, u32[]{:S(2)}) collective-permute-start(f32[16,256]{1,0:T(8,128)S(1)} %fusion.13.refs_0_), channel_id=1, source_target_pairs={{0,2},{1,3},{2,0},{3,1},{4,6},{5,7},{6,4},{7,5},{8,10},{9,11},{10,... | collective-permute-start | bytes 49160 | tf_op jit(solution)/shard_map/ppermute | solution.py:500
  122.0 39.2 %collective-permute-start.12 = (f32[16,256]{1,0:T(8,128)S(1)}, f32[16,256]{1,0:T(8,128)S(1)}, u32[]{:S(2)}, u32[]{:S(2)}) collective-permute-start(f32[16,256]{1,0:T(8,128)S(1)} %fusion.13.refs_0_), channel_id=1, source_target_pairs={{0,1},{1,2},{2,3},{3,0},{4,5},{5,6},{6,7},{7,4},{8,9},{9,10},{10,1... | collective-permute-start | bytes 49160 | tf_op jit(solution)/shard_map/ppermute | solution.py:500
  162.6 23.5 %copy-start.9 = (f32[4,16,256]{2,1,0:T(8,128)S(1)}, f32[4,16,256]{2,1,0:T(8,128)}, u32[]{:S(2)}) copy-start(f32[4,16,256]{2,1,0:T(8,128)} %pad_maximum_fusion.3.after_ref.refs_0_) | copy-start | bytes 196612
  186.0 3.3 %collective-permute-start.15 = (f32[4,256,256]{2,1,0:T(8,128)}, f32[4,256,256]{2,1,0:T(8,128)S(1)}, u32[]{:S(2)}, u32[]{:S(2)}) collective-permute-start(f32[4,256,256]{2,1,0:T(8,128)} %get-tuple-element.33), channel_id=1, source_target_pairs={{0,4},{4,0},{8,12},{12,8},{16,20},{20,16},{24,28},{28,24},{1,5},{5... | collective-permute-start | bytes 3145736 | tf_op jit(solution)/shard_map/ppermute | solution.py:434
  186.1 6.5 %collective-permute-start.18 = (f32[4,16,256]{2,1,0:T(8,128)S(1)}, f32[4,16,256]{2,1,0:T(8,128)S(1)}, u32[]{:S(2)}, u32[]{:S(2)}) collective-permute-start(f32[4,16,256]{2,1,0:T(8,128)S(1)} %copy-done.9), channel_id=1, source_target_pairs={{0,24},{4,28},{8,16},{12,20},{16,8},{20,12},{24,0},{28,4},{1,25},{... | collective-permute-start | bytes 196616 | tf_op jit(solution)/shard_map/ppermute | solution.py:434
  188.8 4.6 %collective-permute-start.17 = (f32[4,16,256]{2,1,0:T(8,128)S(1)}, f32[4,16,256]{2,1,0:T(8,128)S(1)}, u32[]{:S(2)}, u32[]{:S(2)}) collective-permute-start(f32[4,16,256]{2,1,0:T(8,128)S(1)} %copy-done.9), channel_id=1, source_target_pairs={{0,16},{4,20},{8,24},{12,28},{16,0},{20,4},{24,8},{28,12},{1,17},{... | collective-permute-start | bytes 196616 | tf_op jit(solution)/shard_map/ppermute | solution.py:434
  189.3 5.6 %collective-permute-start.16 = (f32[4,16,256]{2,1,0:T(8,128)S(1)}, f32[4,16,256]{2,1,0:T(8,128)S(1)}, u32[]{:S(2)}, u32[]{:S(2)}) collective-permute-start(f32[4,16,256]{2,1,0:T(8,128)S(1)} %copy-done.9), channel_id=1, source_target_pairs={{0,8},{4,12},{8,0},{12,4},{16,24},{20,28},{24,16},{28,20},{1,9},{5... | collective-permute-start | bytes 196616 | tf_op jit(solution)/shard_map/ppermute | solution.py:434
  192.6 26.5 %collective-permute-start.22 = (f32[256,256]{1,0:T(8,128)S(1)}, f32[256,256]{1,0:T(8,128)S(1)}, u32[]{:S(2)}, u32[]{:S(2)}) collective-permute-start(f32[256,256]{1,0:T(8,128)S(1)} %get-tuple-element.42), channel_id=1, source_target_pairs={{0,8},{4,12},{8,0},{12,4},{16,24},{20,28},{24,16},{28,20},{1,9},{5... | collective-permute-start | bytes 786440 | tf_op jit(solution)/shard_map/ppermute | solution.py:434
  193.3 25.8 %collective-permute-start.23 = (f32[256,256]{1,0:T(8,128)S(1)}, f32[256,256]{1,0:T(8,128)}, u32[]{:S(2)}, u32[]{:S(2)}) collective-permute-start(f32[256,256]{1,0:T(8,128)S(1)} %get-tuple-element.41), channel_id=1, source_target_pairs={{0,16},{4,20},{8,24},{12,28},{16,0},{20,4},{24,8},{28,12},{1,17},{... | collective-permute-start | bytes 786440 | tf_op jit(solution)/shard_map/ppermute | solution.py:434
  194.9 24.3 %collective-permute-start.24 = (f32[256,256]{1,0:T(8,128)S(1)}, f32[256,256]{1,0:T(8,128)}, u32[]{:S(2)}, u32[]{:S(2)}) collective-permute-start(f32[256,256]{1,0:T(8,128)S(1)} %get-tuple-element.40), channel_id=1, source_target_pairs={{0,24},{4,28},{8,16},{12,20},{16,8},{20,12},{24,0},{28,4},{1,25},{... | collective-permute-start | bytes 786440 | tf_op jit(solution)/shard_map/ppermute | solution.py:434
  198.8 1.3 copy-start.7
  198.8 29.1 %collective-permute-start.25 = (f32[4,4,16,256]{3,2,1,0:T(8,128)}, f32[4,4,16,256]{3,2,1,0:T(8,128)}, u32[]{:S(2)}, u32[]{:S(2)}) collective-permute-start(f32[4,4,16,256]{3,2,1,0:T(8,128)} %pad_maximum_fusion.2.refs_2_.refs_3_), channel_id=1, source_target_pairs={{0,4},{4,0},{8,12},{12,8},{16,20},{20,16},{24,28},{28,24},{1,5},{5... | collective-permute-start | bytes 786440 | tf_op jit(solution)/shard_map/ppermute | solution.py:434
  219.1 3.6 %copy-start.11 = (f32[4,128,256]{2,1,0:T(8,128)S(1)}, f32[4,128,256]{2,1,0:T(8,128)}, u32[]{:S(2)}) copy-start(f32[4,128,256]{2,1,0:T(8,128)} %get-tuple-element.34) | copy-start | bytes 1572868
  219.1 2.7 %collective-permute-start.21 = (f32[4,128,256]{2,1,0:T(8,128)}, f32[4,128,256]{2,1,0:T(8,128)S(1)}, u32[]{:S(2)}, u32[]{:S(2)}) collective-permute-start(f32[4,128,256]{2,1,0:T(8,128)} %get-tuple-element.35), channel_id=1, source_target_pairs={{0,4},{4,0},{8,12},{12,8},{16,20},{20,16},{24,28},{28,24},{1,5},{5... | collective-permute-start | bytes 1572872 | tf_op jit(solution)/shard_map/ppermute | solution.py:434
  221.8 0.8 copy-start.6
  224.4 8.1 %collective-permute-start.26 = (f32[128,256]{1,0:T(8,128)S(1)}, f32[128,256]{1,0:T(8,128)S(1)}, u32[]{:S(2)}, u32[]{:S(2)}) collective-permute-start(f32[128,256]{1,0:T(8,128)S(1)} %get-tuple-element.46), channel_id=1, source_target_pairs={{0,8},{4,12},{8,0},{12,4},{16,24},{20,28},{24,16},{28,20},{1,9},{5... | collective-permute-start | bytes 393224 | tf_op jit(solution)/shard_map/ppermute | solution.py:434
  225.2 7.5 %collective-permute-start.27 = (f32[128,256]{1,0:T(8,128)S(1)}, f32[128,256]{1,0:T(8,128)S(1)}, u32[]{:S(2)}, u32[]{:S(2)}) collective-permute-start(f32[128,256]{1,0:T(8,128)S(1)} %get-tuple-element.45), channel_id=1, source_target_pairs={{0,16},{4,20},{8,24},{12,28},{16,0},{20,4},{24,8},{28,12},{1,17},{... | collective-permute-start | bytes 393224 | tf_op jit(solution)/shard_map/ppermute | solution.py:434
  226.7 7.4 %collective-permute-start.28 = (f32[128,256]{1,0:T(8,128)S(1)}, f32[128,256]{1,0:T(8,128)S(1)}, u32[]{:S(2)}, u32[]{:S(2)}) collective-permute-start(f32[128,256]{1,0:T(8,128)S(1)} %get-tuple-element.44), channel_id=1, source_target_pairs={{0,24},{4,28},{8,16},{12,20},{16,8},{20,12},{24,0},{28,4},{1,25},{... | collective-permute-start | bytes 393224 | tf_op jit(solution)/shard_map/ppermute | solution.py:434
  227.9 9.8 %copy-start.1 = (f32[256,256]{1,0:T(8,128)S(1)}, f32[256,256]{1,0:T(8,128)}, u32[]{:S(2)}) copy-start(f32[256,256]{1,0:T(8,128)} %param.6) | copy-start | bytes 786436
  232.6 1.5 copy-start.16
  232.6 1.5 copy-start.17
  (2 other events, 1.4 us)
Sparse Core Ops, SparseCore 0:
  103.3 50.6 reduce-scatter.1

commit v7 on v6

--- a/solution.py
+++ b/solution.py
@@ -90,7 +90,7 @@
     return jnp.where(index % 2 == 0, even_ref[half, rows], odd_ref[half, rows])
 
 
-def project_kernel(per, wide, me_ref, v_ref, r_ref, e_ref, x_ref, even_ref, odd_ref, left_ref, own_ref, small_ref, both_ref):
+def project_kernel(per, wide, me_ref, v_ref, r_ref, e_ref, x_ref, even_ref, odd_ref, left_ref, small_ref, both_ref):
     j = pl.program_id(0)
     nb = r_ref.shape[1]
     each = x_ref.shape[1]
@@ -116,18 +116,6 @@
         index = (j * (step // per) + g) ^ me_ref[0]
         place(value[:, g * per : (g + 1) * per], index, even_ref, odd_ref, 0)
 
-    @pl.when(j == OFF // step)
-    def _():
-        own = value[:, OFF % step : OFF % step + each].T
-        own_ref[...] = own
-        if ride:
-            rows = each // wide
-            for w in range(wide):
-                place(
-                    own[w * rows : (w + 1) * rows], w ^ me_ref[0], even_ref, odd_ref,
-                    nb + ride - rows,
-                )
-
 
 def project(me, vectors, reflectors, e_row, block, wide, ride):
     rows, columns = vectors.shape
@@ -136,8 +124,8 @@
     k = nb + each
     per = columns // wide
     step = width(columns, wide)
-    shapes = [(wide // 2, nb + ride, per)] * 2 + [(2 * k, rows), (each, nb), (k, nb)]
-    kinds = [F32, F32, BF16, F32, F32]
+    shapes = [(wide // 2, nb + ride, per)] * 2 + [(2 * k, rows), (k, nb)]
+    kinds = [F32, F32, BF16, F32]
     return pl.pallas_call(
         functools.partial(project_kernel, per, wide),
         grid_spec=pltpu.PrefetchScalarGridSpec(
@@ -296,22 +284,27 @@
     )(at, updated, after, *flat)
 
 
-def total_kernel(*refs):
-    refs[-1][...] = functools.reduce(jnp.add, [ref[...] for ref in refs[:-1]])
-
-
-def total(terms):
-    shape = terms[0].shape
-    return pl.pallas_call(
-        total_kernel,
-        grid=(1,),
-        in_specs=[pl.BlockSpec(shape, lambda j: (0, 0))] * len(terms),
-        out_specs=pl.BlockSpec(shape, lambda j: (0, 0)),
-        out_shape=jax.ShapeDtypeStruct(shape, F32),
-        compiler_params=params(),
-        cost_estimate=LONG,
-        name="total",
-    )(*terms)
+def own_kernel(me_ref, even_ref, odd_ref, after_ref, out_ref):
+    each, nb = out_ref.shape
+    per = even_ref.shape[2]
+    block = take((OFF // per) ^ me_ref[0], even_ref, odd_ref, slice(0, nb))
+    out_ref[...] = block[:, OFF % per : OFF % per + each].T
+
+
+def own_columns(me, c, after, nb, each):
+    return pl.pallas_call(
+        own_kernel,
+        grid_spec=pltpu.PrefetchScalarGridSpec(
+            num_scalar_prefetch=1,
+            grid=(1,),
+            in_specs=[whole(x.shape) for x in c] + [ANY],
+            out_specs=whole((each, nb)),
+        ),
+        out_shape=jax.ShapeDtypeStruct((each, nb), F32),
+        compiler_params=params(),
+        cost_estimate=SHORT,
+        name="own_columns",
+    )(me, *c, after)
 
 
 def base_kernel(n, each, ride, at_ref, ready_ref, c_ref, *refs):
@@ -319,34 +312,24 @@
     me, z = at_ref[0], at_ref[1]
     nb = c_ref.shape[0]
     k = small_ref.shape[0]
+    for s in range(n):
+        first = pl.multiple_of((z + n - s) % n * each, each)
+        coef_ref[pl.ds(first, each), :] = refs[s][...]
     if ride:
-        c_even, c_odd, ce_ref, co_ref = refs[1:]
-        half, _, rows, _ = ce_ref.shape
-        wide = 2 * half
+        wide = 2 * refs[n].shape[0]
         for w in range(wide):
-            index = w ^ me
             small_ref[w * (k // wide) : (w + 1) * (k // wide)] = take(
-                index, c_even, c_odd, slice(nb, nb + k // wide)
+                w ^ me, *refs[n:], slice(nb, nb + k // wide)
             )
-            for s in range(n):
-                first = pl.multiple_of((z + n - s) % n * each + w * rows, rows)
-                coef_ref[pl.ds(first, rows), :] = take(index, ce_ref, co_ref, s)
     else:
-        all_small, all_coef = refs[1:]
-        small_ref[...] = all_small[...]
-        for s in range(n):
-            coef_ref[s * each : (s + 1) * each] = all_coef[s]
+        small_ref[...] = refs[n][...]
     corrected = ready_ref[...] - three(split(small_ref[...]), split(c_ref[...]))
     out_ref[...] = -three(split(coef_ref[...]), split(corrected[:nb]))
-    total = refs[0]
-    for slot in range(1 + total.shape[0] // each):
-        piece = corrected[nb:] if slot == 0 else total[(slot - 1) * each : slot * each]
-        first = pl.multiple_of(at_ref[1 + slot] * each, each)
-        out_ref[pl.ds(first, each), :] += piece
-
-
-def base(at, ready, c, middle, extra, n, each, ride):
-    operands = [ready, c, middle, *extra]
+    out_ref[pl.ds(pl.multiple_of(z * each, each), each), :] += corrected[nb:]
+
+
+def base(at, ready, c, coef, small, n, each, ride):
+    operands = [ready, c, *coef, *small]
     k, per = ready.shape
     nb = c.shape[0]
     return pl.pallas_call(
@@ -369,8 +352,9 @@
     *refs, out_ref, total_ref = refs
     total_ref[...] = base_ref[...]
     total = functools.reduce(jnp.add, [ref[...] for ref in refs])
-    first = pl.multiple_of(at_ref[at_ref.shape[0] - 1] * each, each)
-    total_ref[pl.ds(first, each), :] += total
+    for slot in range(total.shape[0] // each):
+        first = pl.multiple_of(at_ref[2 + slot] * each, each)
+        total_ref[pl.ds(first, each), :] += total[slot * each : (slot + 1) * each]
     out_ref[...] = total_ref[...].T
 
 
@@ -470,12 +454,10 @@
     table = arrivals(n)
     at = jnp.stack([me[0], z] + [source(places, z) for places in table])
 
-    fits = per == nb and each % (8 * wide) == 0 and k % (8 * wide) == 0
-    ride = (k + each) // wide if fits else 0
-    even, odd, left, own_part, small = project(me, vectors, reflectors, e_row, own, wide, ride)
+    ride = k // wide if per == nb and k % (8 * wide) == 0 else 0
+    even, odd, left, small = project(me, vectors, reflectors, e_row, own, wide, ride)
     terms = scatter_terms(even, odd, wide)
     highest = lax.Precision.HIGHEST
-    turn = (((1,), (1,)), ((), ()))
     if n > 2:
         held = travel(came, held, n, 2, [left, terms[0]])
     sums, token = early(vectors, left, 0, half, came[(1, 0)], [], wide)
@@ -484,38 +466,26 @@
     coefficients = jnp.dot(triangle, projected[:nb], precision=highest)
     payload = coefficients
     if ride:
-        payload = jnp.concatenate([coefficients, projected[nb : nb + k // wide]], axis=0)
+        payload = jnp.concatenate([coefficients, projected[nb:]], axis=0)
     sums, token = early(vectors, left, half, blocks - half, payload, [sums], wide)
     ready = lax.psum_scatter(sums, "wide", scatter_dimension=0)
     c = collect(payload, wide, [token])
     for hops in range(3, n):
-        held = travel(came, held, n, hops, [token])
+        held = travel(came, held, n, hops, [token, c[0]])
     after = came[(min(2, n - 1), 0)]
     updated, token = update(me, vectors, reflectors, c, after)
 
-    if ride:
-        (mine,) = gate([projected[nb + k // wide :]], after)
-        mine = lax.dot_general(mine, triangle, turn, precision=highest)
-        shares = [
-            lax.ppermute(mine, "narrow", [(p, (p + s) % n) for p in range(n)]) for s in range(1, n)
-        ]
-        shares = jnp.stack([*gate([mine], token), *shares])
-        token = shares
+    mine = own_columns(me, c, token, nb, each)
+    coef = [mine] + [
+        lax.ppermute(mine, "narrow", [(p, (p + s) % n) for p in range(n)]) for s in range(1, n)
+    ]
     slots = [options(came, places, z) for places in table]
-    even, odd = late(me, updated, slots[:-1], token, wide)
-    if ride:
-        extra = [*c, *collect(shares, wide, [even])]
-        token = extra[-2]
-    else:
-        own_part = lax.dot_general(lax.psum(own_part, "wide"), triangle, turn, precision=highest)
-        extra = [lax.psum(small, "wide"), lax.all_gather(own_part, "narrow")]
-    middle = scatter_terms(even, odd, wide)
-    (ready,) = gate([ready], middle[0], token)
-    even, odd = late(me, updated, slots[-1:], ready, wide)
-    middle = total(middle)
-    tail = scatter_terms(even, odd, wide, middle)
+    even, odd = late(me, updated, slots, token, wide)
+    (odd,) = gate([odd], ready, *coef[1:])
+    tail = scatter_terms(even, odd, wide)
     (ready,) = gate([ready], tail[0])
-    base_block = base(at, ready, coefficients, middle, extra, n, each, ride)
+    small = c if ride else [lax.psum(small, "wide")]
+    base_block = base(at, ready, coefficients, coef, small, n, each, ride)
     return (updated, last(at, base_block, tail, each))
 
 

time: 246 us -> 235 us (0.955)
  waiting for transfers between devices: 23.9 us -> 46 us
  starting transfers between devices: 41.4 us -> 29.2 us
  Pallas kernels: 140 us -> 128 us
  other arithmetic: 15.5 us -> 11 us
  local copies, waits for them, and re-layouts: 7.61 us -> 5.1 us
    ppermute x20 -> x12, waiting for transfers between devices: 4.82 us -> 22.2 us  [swap(): return lax.ppermute(x, 'wide', [(i, i ^ distance) for i in range(wide)])]
    pallas_call x2 -> x1, Pallas kernels: 42.3 us -> 29.6 us  [late(): pl.pallas_call(functools.partial(late_kernel, per, counts), grid_spec=plt...]
    ppermute x6, waiting for transfers between devices: 12.8 us -> 23.8 us  [travel(): held = [lax.ppermute(held[d], 'narrow', pairs[d]) for d in (0, 1)]]
    ppermute x20 -> x12, starting transfers between devices: 18.8 us -> 10.8 us  [swap(): return lax.ppermute(x, 'wide', [(i, i ^ distance) for i in range(wide)])]
    ppermute x3, waiting for transfers between devices: 6.29 us -> 0.01 us  [on_device(): lax.ppermute(mine, 'narrow', [(p, (p + s) % n) for p in range(n)])]
    add x3 -> x2, other arithmetic: 6.22 us -> 3.35 us  [scatter_terms(): sums = [even[h] + other[h] for h in range(wide // 2)]]
    ppermute x3, starting transfers between devices: 7.92 us -> 5.28 us  [on_device(): lax.ppermute(mine, 'narrow', [(p, (p + s) % n) for p in range(n)])]
    unnamed x40 -> x30, local copies, waits for them, and re-layouts: 5.71 us -> 4.53 us
  transfers between devices with their start and end apart: 30 -> 22, of which waited for: 7 -> 10; matrix products, arithmetic and copies ran while one was open for 7% -> 3% of each run, Pallas kernels for 56% -> 53%
where the time goes in v7:
time: 235 us; the launch traced here: 234 us
  Pallas kernels  128 us (54%)
  waiting for transfers between devices  46 us (20%)
  starting transfers between devices  29.2 us (12%)
  between operations  14.3 us (6%)
  other arithmetic  11 us (5%)
  local copies, waits for them, and re-layouts  5.1 us (2%)
    pallas_call x1, Pallas kernels, update(): pl.pallas_call(update_kernel, grid_spec=pltpu.PrefetchScalarGridSpec(num_...  30.6 us
    pallas_call x2, Pallas kernels, early(): pl.pallas_call(functools.partial(early_kernel, per), grid=(blocks,), in_s...  30.6 us
    pallas_call x1, Pallas kernels, late(): pl.pallas_call(functools.partial(late_kernel, per, counts), grid_spec=plt...  29.6 us
    pallas_call x1, Pallas kernels, project(): pl.pallas_call(functools.partial(project_kernel, per, wide), grid_spec=pl...  27.4 us
    ppermute x6, waiting for transfers between devices, travel(): held = [lax.ppermute(held[d], 'narrow', pairs[d]) for d in (0, 1)]  23.8 us
    ppermute x12, waiting for transfers between devices, swap(): return lax.ppermute(x, 'wide', [(i, i ^ distance) for i in range(wide)])  22.2 us
    ppermute x6, starting transfers between devices, travel(): held = [lax.ppermute(held[d], 'narrow', pairs[d]) for d in (0, 1)]  13.1 us
    ppermute x12, starting transfers between devices, swap(): return lax.ppermute(x, 'wide', [(i, i ^ distance) for i in range(wide)])  10.8 us
  transfers between devices with their start and end apart: 22, of which 10 were waited for; matrix products, arithmetic and copies ran while one was open for 3% of the time, Pallas kernels for 53%

profile of v7, /device:TPU:0, one launch (start us, length us, event | category | flops | bytes accessed | tf_op | source)
XLA Modules:
  0.0 234.4 jit_solution(5191287520736355764)
XLA Ops:
  7.2 3.7 %slice_multiply_fusion.x_ref = f32[4000,128]{1,0:T(8,128)} fusion(f32[4000,2048]{1,0:T(8,128)} %v_ref.7, f32[4000]{0:T(1024)} %param.7), kind=kLoop, calls=%fused_computation | loop fusion | flops 512000 | bytes 4112000 | tf_op jit(solution)/shard_map/mul | solution.py:451
  10.9 5.0 %collective-permute-start.2 = (f32[4000,128]{1,0:T(8,128)}, f32[4000,128]{1,0:T(8,128)S(1)}, u32[]{:S(2)}, u32[]{:S(2)}) collective-permute-start(f32[4000,128]{1,0:T(8,128)} %slice_multiply_fusion.x_ref), channel_id=1, source_target_pairs={{0,1},{1,2},{2,3},{4,5},{5,6},{6,7},{8,9},{9,10},{10,11},{12,13},{... | collective-permute-start | bytes 6144008 | tf_op jit(solution)/shard_map/ppermute | solution.py:397
  16.0 1.3 collective-permute-start.1
  17.3 27.4 %project.1 = (f32[4,304,256]{2,1,0:T(8,128)}, f32[4,304,256]{2,1,0:T(8,128)}, bf16[768,4000]{1,0:T(8,128)(2,1)}, f32[384,256]{1,0:T(8,128)}) custom-call(s32[1]{0:T(128)} %bitcast.me_ref, f32[4000,2048]{1,0:T(8,128)} %v_ref.7, f32[4000,256]{1,0:T(8,128)} %r_ref.3, f32[1,4000]{1,0:T(1,128)} %bitcast.39, f32[4000,128]{1,0:T(8,128)} %slice_multiply_fusion.x_ref), custom_call_target="tpu_custom_call" | custom-call | flops 1024 | bytes 1024 | tf_op jit(solution)/shard_map/project/pallas_call | solution.py:129
  44.7 3.1 %collective-permute-done = f32[4,304,256]{2,1,0:T(8,128)S(1)} collective-permute-done((f32[4,304,256]{2,1,0:T(8,128)}, f32[4,304,256]{2,1,0:T(8,128)S(1)}, u32[]{:S(2)}, u32[]{:S(2)}) %collective-permute-start) | collective-permute-done | bytes 1245216 | tf_op jit(solution)/shard_map/ppermute | solution.py:418
  47.8 2.1 fusion.6
  50.0 10.0 %collective-permute-done.2.refs_1_ = f32[4000,128]{1,0:T(8,128)S(1)} collective-permute-done((f32[4000,128]{1,0:T(8,128)}, f32[4000,128]{1,0:T(8,128)S(1)}, u32[]{:S(2)}, u32[]{:S(2)}) %collective-permute-start.2) | collective-permute-done | bytes 2048032 | tf_op jit(solution)/shard_map/ppermute | solution.py:397
  60.0 4.2 %collective-permute-done.1.refs_0_ = f32[4000,128]{1,0:T(8,128)} collective-permute-done((f32[4000,128]{1,0:T(8,128)}, f32[4000,128]{1,0:T(8,128)}, u32[]{:S(2)}, u32[]{:S(2)}) %collective-permute-start.1) | collective-permute-done | bytes 2048032 | tf_op jit(solution)/shard_map/ppermute | solution.py:397
  64.2 2.0 collective-permute-start.11
  66.3 1.5 collective-permute-start.10
  67.7 1.6 collective-permute-start.3
  69.3 1.5 collective-permute-start.5
  70.8 0.5 collective-permute-start.4
  71.3 15.3 %early.2 = (f32[8,384,256]{2,1,0:T(8,128)}, f32[8,128]{1,0:T(8,128)}) custom-call(f32[4000,2048]{1,0:T(8,128)} %v_ref.7, bf16[768,4000]{1,0:T(8,128)(2,1)} %get-tuple-element.19.refs_2_.left_ref, f32[4000,128]{1,0:T(8,128)} %get-tuple-element.20.refs_0_), custom_call_target="tpu_custom_call" | custom-call | flops 1024 | bytes 1024 | tf_op jit(solution)/shard_map/early/pallas_call | solution.py:162
  86.6 1.2 add_add_fusion
  87.9 0.4 convolution_bitcast_fusion.c_ref
  88.3 2.5 %collective-permute-start.8 = (f32[304,256]{1,0:T(8,128)S(1)}, f32[304,256]{1,0:T(8,128)S(1)}, u32[]{:S(2)}, u32[]{:S(2)}) collective-permute-start(f32[304,256]{1,0:T(8,128)S(1)} %pad_maximum_fusion.1.refs_0_), channel_id=1, source_target_pairs={{0,24},{4,28},{8,16},{12,20},{16,8},{20,12},{24,0},{28,4},{1,25},{... | collective-permute-start | bytes 933896 | tf_op jit(solution)/shard_map/ppermute | solution.py:418
  90.8 0.5 collective-permute-start.7
  91.4 0.6 collective-permute-start.6
  92.0 15.3 %early.3 = (f32[8,384,256]{2,1,0:T(8,128)}, f32[8,128]{1,0:T(8,128)}) custom-call(f32[4000,2048]{1,0:T(8,128)} %v_ref.7, bf16[768,4000]{1,0:T(8,128)(2,1)} %get-tuple-element.19.refs_2_.left_ref, f32[304,256]{1,0:T(8,128)} %copy-done.6, f32[8,384,256]{2,1,0:T(8,128)} %get-tuple-element.22.refs_1_), custom_call_target="tpu_custom_call", output_to_operand_aliasing={{0}: (3, {})} | custom-call | flops 1024 | bytes 1024 | tf_op jit(solution)/shard_map/early/pallas_call | solution.py:162
  107.3 2.1 pad_maximum_fusion.refs_3_.even_ref.refs_4_
  109.5 6.3 %collective-permute-done.10.refs_0_ = f32[4000,128]{1,0:T(8,128)S(1)} collective-permute-done((f32[4000,128]{1,0:T(8,128)}, f32[4000,128]{1,0:T(8,128)S(1)}, u32[]{:S(2)}, u32[]{:S(2)}) %collective-permute-start.10) | collective-permute-done | bytes 2048032 | tf_op jit(solution)/shard_map/ppermute | solution.py:397
  115.8 1.3 copy-done.2
  117.1 2.0 collective-permute-start.13
  119.0 1.3 collective-permute-start.12
  120.3 0.1 collective-permute-start.9
  120.4 3.3 %collective-permute-done.9.odd_ref.refs_5_ = f32[4,304,256]{2,1,0:T(8,128)S(1)} collective-permute-done((f32[4,304,256]{2,1,0:T(8,128)S(1)}, f32[4,304,256]{2,1,0:T(8,128)S(1)}, u32[]{:S(2)}, u32[]{:S(2)}) %collective-permute-start.9) | collective-permute-done | bytes 1245216 | tf_op jit(solution)/shard_map/ppermute | solution.py:418
  123.7 1.0 copy-done.5
  124.7 30.6 %update.1 = (f32[4000,2048]{1,0:T(8,128)}, f32[8,128]{1,0:T(8,128)}) custom-call(s32[1]{0:T(128)} %bitcast.me_ref, f32[4000,2048]{1,0:T(8,128)} %v_ref.7, f32[4000,256]{1,0:T(8,128)} %r_ref.3, f32[4,304,256]{2,1,0:T(8,128)} %pad_maximum_fusion.refs_3_.even_ref.refs_4_, f32[4,304,256]{2,1,0:T(8,128)} %copy-done.5, ...), custom_call_target="tpu_custom_call" | custom-call | flops 1024 | bytes 1024 | tf_op jit(solution)/shard_map/update/pallas_call | solution.py:206
  155.3 2.4 %own_columns.1.refs_0_ = f32[128,256]{1,0:T(8,128)} custom-call(s32[1]{0:T(128)} %bitcast.me_ref, f32[4,304,256]{2,1,0:T(8,128)} %pad_maximum_fusion.refs_3_.even_ref.refs_4_, f32[4,304,256]{2,1,0:T(8,128)} %copy-done.5, f32[8,128]{1,0:T(8,128)} %get-tuple-element.28.after_ref), custom_call_target="tpu_custom_call" | custom-call | flops 1024 | bytes 1024 | tf_op jit(solution)/shard_map/own_columns/pallas_call | solution.py:295
  157.8 5.3 %collective-permute-start.15 = (f32[128,256]{1,0:T(8,128)}, f32[128,256]{1,0:T(8,128)S(1)}, u32[]{:S(2)}, u32[]{:S(2)}) collective-permute-start(f32[128,256]{1,0:T(8,128)} %own_columns.1.refs_0_), channel_id=1, source_target_pairs={{0,2},{1,3},{2,0},{3,1},{4,6},{5,7},{6,4},{7,5},{8,10},{9,11},{10,... | collective-permute-start | bytes 393224 | tf_op jit(solution)/shard_map/ppermute | solution.py:480
  163.0 0.6 pad_add_fusion.at_ref
  163.6 3.2 %collective-permute-done.12.refs_7_ = f32[4000,128]{1,0:T(8,128)} collective-permute-done((f32[4000,128]{1,0:T(8,128)}, f32[4000,128]{1,0:T(8,128)}, u32[]{:S(2)}, u32[]{:S(2)}) %collective-permute-start.12) | collective-permute-done | bytes 2048032 | tf_op jit(solution)/shard_map/ppermute | solution.py:397
  166.8 29.6 %late.1 = (f32[4,384,256]{2,1,0:T(8,128)}, f32[4,384,256]{2,1,0:T(8,128)}) custom-call(s32[4]{0:T(128)} %pad_add_fusion.at_ref, f32[4000,2048]{1,0:T(8,128)} %get-tuple-element.15.u_ref, f32[8,128]{1,0:T(8,128)} %get-tuple-element.28.after_ref, f32[4000,128]{1,0:T(8,128)} %get-tuple-element.20.refs_0_, f32[4000,128]{1,0:T(8,128)} %get-tuple-element.24.refs_1_.refs_2_, ...), custom_call_target="tpu_custom_call" | custom-call | flops 1024 | bytes 1024 | tf_op jit(solution)/shard_map/late/pallas_call | solution.py:267
  196.5 0.6 copy-done.12
  197.2 0.6 stack.51.at_ref
  197.8 3.1 %collective-permute-done.17 = f32[4,384,256]{2,1,0:T(8,128)S(1)} collective-permute-done((f32[4,384,256]{2,1,0:T(8,128)}, f32[4,384,256]{2,1,0:T(8,128)S(1)}, u32[]{:S(2)}, u32[]{:S(2)}) %collective-permute-start.17) | collective-permute-done | bytes 1572896 | tf_op jit(solution)/shard_map/ppermute | solution.py:418
  200.8 1.2 fusion
  202.0 2.4 %collective-permute-start.20 = (f32[384,256]{1,0:T(8,128)}, f32[384,256]{1,0:T(8,128)S(1)}, u32[]{:S(2)}, u32[]{:S(2)}) collective-permute-start(f32[384,256]{1,0:T(8,128)} %get-tuple-element.32), channel_id=1, source_target_pairs={{0,24},{4,28},{8,16},{12,20},{16,8},{20,12},{24,0},{28,4},{1,25},{... | collective-permute-start | bytes 1179656 | tf_op jit(solution)/shard_map/ppermute | solution.py:418
  204.5 0.5 collective-permute-start.19
  205.0 0.5 collective-permute-start.18
  205.5 4.6 %base.1.base_ref = f32[512,256]{1,0:T(8,128)} custom-call(s32[5]{0:T(128)} %stack.51.at_ref, f32[384,256]{1,0:T(8,128)} %gate.11.ready_ref, f32[256,256]{1,0:T(8,128)} %copy-done.8, f32[128,256]{1,0:T(8,128)} %own_columns.1.refs_0_, f32[128,256]{1,0:T(8,128)} %copy-done.14, f32[128,256]{1,0:T(8,128)} %copy-done.13, f32[128,256]{1,0:T(8,128)} %copy-done.12, ...), custom_call_target="tpu_custom_call" | custom-call | flops 99999997952 | bytes 1024 | tf_op jit(solution)/shard_map/base/pallas_call | solution.py:335
  210.1 5.0 %collective-permute-done.20.refs_3_ = f32[384,256]{1,0:T(8,128)S(1)} collective-permute-done((f32[384,256]{1,0:T(8,128)}, f32[384,256]{1,0:T(8,128)S(1)}, u32[]{:S(2)}, u32[]{:S(2)}) %collective-permute-start.20) | collective-permute-done | bytes 393248 | tf_op jit(solution)/shard_map/ppermute | solution.py:418
  215.2 7.6 %collective-permute-done.19.refs_2_ = f32[384,256]{1,0:T(8,128)S(1)} collective-permute-done((f32[384,256]{1,0:T(8,128)}, f32[384,256]{1,0:T(8,128)S(1)}, u32[]{:S(2)}, u32[]{:S(2)}) %collective-permute-start.19) | collective-permute-done | bytes 393248 | tf_op jit(solution)/shard_map/ppermute | solution.py:418
  222.7 0.1 collective-permute-done.18.refs_1_
  222.8 0.7 copy-done.10
  223.5 0.7 copy-done.11
  224.3 3.3 %last.1 = f32[256,512]{1,0:T(8,128)} custom-call(s32[5]{0:T(128)} %stack.51.at_ref, f32[512,256]{1,0:T(8,128)} %base.1.base_ref, f32[384,256]{1,0:T(8,128)} %get-tuple-element.35.refs_1_.refs_0_, f32[384,256]{1,0:T(8,128)} %copy-done.11, f32[384,256]{1,0:T(8,128)} %copy-done.10, f32[384,256]{1,0:T(8,128)} %copy-done.9), custom_call_target="tpu_custom_call" | custom-call | flops 1024 | bytes 1024 | tf_op jit(solution)/shard_map/last/pallas_call | solution.py:364
  (51 shorter events, 0.3 us)
Async XLA Ops:
  7.2 80.7 %copy-start = (f32[256,256]{1,0:T(8,128)S(1)}, f32[256,256]{1,0:T(8,128)}, u32[]{:S(2)}) copy-start(f32[256,256]{1,0:T(8,128)} %param.6) | copy-start | bytes 786436
  7.2 189.3 %reduce-scatter.2.cloned.1.call-start = ((), (), s32[]{:S(2)}) async-start(), calls=%async_computation.1 | async-start | bytes 3538944 | tf_op jit(solution)/shard_map/reduce_scatter | solution.py:471
  10.9 49.1 %collective-permute-start.2 = (f32[4000,128]{1,0:T(8,128)}, f32[4000,128]{1,0:T(8,128)S(1)}, u32[]{:S(2)}, u32[]{:S(2)}) collective-permute-start(f32[4000,128]{1,0:T(8,128)} %slice_multiply_fusion.x_ref), channel_id=1, source_target_pairs={{0,1},{1,2},{2,3},{4,5},{5,6},{6,7},{8,9},{9,10},{10,11},{12,13},{... | collective-permute-start | bytes 6144008 | tf_op jit(solution)/shard_map/ppermute | solution.py:397
  16.0 48.2 %collective-permute-start.1 = (f32[4000,128]{1,0:T(8,128)}, f32[4000,128]{1,0:T(8,128)}, u32[]{:S(2)}, u32[]{:S(2)}) collective-permute-start(f32[4000,128]{1,0:T(8,128)} %slice_multiply_fusion.x_ref), channel_id=1, source_target_pairs={{1,0},{2,1},{3,2},{5,4},{6,5},{7,6},{9,8},{10,9},{11,10},{13,12},{... | collective-permute-start | bytes 6144008 | tf_op jit(solution)/shard_map/ppermute | solution.py:397
  44.7 3.2 %collective-permute-start = (f32[4,304,256]{2,1,0:T(8,128)}, f32[4,304,256]{2,1,0:T(8,128)S(1)}, u32[]{:S(2)}, u32[]{:S(2)}) collective-permute-start(f32[4,304,256]{2,1,0:T(8,128)} %get-tuple-element.18), channel_id=1, source_target_pairs={{0,4},{4,0},{8,12},{12,8},{16,20},{20,16},{24,28},{28,24},{1,5},{5... | collective-permute-start | bytes 3735560 | tf_op jit(solution)/shard_map/ppermute | solution.py:418
  60.0 4.2 %copy-start.4 = (f32[4000,128]{1,0:T(8,128)}, f32[4000,128]{1,0:T(8,128)S(1)}, u32[]{:S(2)}) copy-start(f32[4000,128]{1,0:T(8,128)S(1)} %collective-permute-done.2.refs_1_) | copy-start | bytes 6144004
  64.2 45.2 %collective-permute-start.11 = (f32[4000,128]{1,0:T(8,128)}, f32[4000,128]{1,0:T(8,128)}, u32[]{:S(2)}, u32[]{:S(2)}) collective-permute-start(f32[4000,128]{1,0:T(8,128)} %get-tuple-element.24.refs_1_.refs_2_), channel_id=1, source_target_pairs={{1,2},{2,3},{5,6},{6,7},{9,10},{10,11},{13,14},{14,15},{17,18},{18... | collective-permute-start | bytes 6144008 | tf_op jit(solution)/shard_map/ppermute | solution.py:397
  66.3 49.5 %collective-permute-start.10 = (f32[4000,128]{1,0:T(8,128)}, f32[4000,128]{1,0:T(8,128)S(1)}, u32[]{:S(2)}, u32[]{:S(2)}) collective-permute-start(f32[4000,128]{1,0:T(8,128)} %get-tuple-element.20.refs_0_), channel_id=1, source_target_pairs={{1,0},{2,1},{5,4},{6,5},{9,8},{10,9},{13,12},{14,13},{17,16},{18,1... | collective-permute-start | bytes 6144008 | tf_op jit(solution)/shard_map/ppermute | solution.py:397
  67.7 18.8 %collective-permute-start.3 = (f32[304,256]{1,0:T(8,128)S(1)}, f32[304,256]{1,0:T(8,128)S(1)}, u32[]{:S(2)}, u32[]{:S(2)}) collective-permute-start(f32[304,256]{1,0:T(8,128)S(1)} %get-tuple-element.36), channel_id=1, source_target_pairs={{0,8},{4,12},{8,0},{12,4},{16,24},{20,28},{24,16},{28,20},{1,9},{5... | collective-permute-start | bytes 933896 | tf_op jit(solution)/shard_map/ppermute | solution.py:418
  69.3 17.3 %collective-permute-start.5 = (f32[304,256]{1,0:T(8,128)S(1)}, f32[304,256]{1,0:T(8,128)}, u32[]{:S(2)}, u32[]{:S(2)}) collective-permute-start(f32[304,256]{1,0:T(8,128)S(1)} %get-tuple-element.37), channel_id=1, source_target_pairs={{0,24},{4,28},{8,16},{12,20},{16,8},{20,12},{24,0},{28,4},{1,25},{... | collective-permute-start | bytes 933896 | tf_op jit(solution)/shard_map/ppermute | solution.py:418
  70.8 15.8 %collective-permute-start.4 = (f32[304,256]{1,0:T(8,128)S(1)}, f32[304,256]{1,0:T(8,128)}, u32[]{:S(2)}, u32[]{:S(2)}) collective-permute-start(f32[304,256]{1,0:T(8,128)S(1)} %get-tuple-element.38), channel_id=1, source_target_pairs={{0,16},{4,20},{8,24},{12,28},{16,0},{20,4},{24,8},{28,12},{1,17},{... | collective-permute-start | bytes 933896 | tf_op jit(solution)/shard_map/ppermute | solution.py:418
  88.3 2.6 %copy-start.8 = (f32[256,256]{1,0:T(8,128)}, f32[256,256]{1,0:T(8,128)S(1)}, u32[]{:S(2)}) copy-start(f32[256,256]{1,0:T(8,128)S(1)} %convolution_bitcast_fusion.c_ref) | copy-start | bytes 786436
  88.3 3.7 %copy-start.6 = (f32[304,256]{1,0:T(8,128)}, f32[304,256]{1,0:T(8,128)S(1)}, u32[]{:S(2)}) copy-start(f32[304,256]{1,0:T(8,128)S(1)} %pad_maximum_fusion.1.refs_0_) | copy-start | bytes 933892
  88.3 19.0 %collective-permute-start.8 = (f32[304,256]{1,0:T(8,128)S(1)}, f32[304,256]{1,0:T(8,128)S(1)}, u32[]{:S(2)}, u32[]{:S(2)}) collective-permute-start(f32[304,256]{1,0:T(8,128)S(1)} %pad_maximum_fusion.1.refs_0_), channel_id=1, source_target_pairs={{0,24},{4,28},{8,16},{12,20},{16,8},{20,12},{24,0},{28,4},{1,25},{... | collective-permute-start | bytes 933896 | tf_op jit(solution)/shard_map/ppermute | solution.py:418
  90.8 16.5 %collective-permute-start.7 = (f32[304,256]{1,0:T(8,128)S(1)}, f32[304,256]{1,0:T(8,128)S(1)}, u32[]{:S(2)}, u32[]{:S(2)}) collective-permute-start(f32[304,256]{1,0:T(8,128)S(1)} %pad_maximum_fusion.1.refs_0_), channel_id=1, source_target_pairs={{0,16},{4,20},{8,24},{12,28},{16,0},{20,4},{24,8},{28,12},{1,17},{... | collective-permute-start | bytes 933896 | tf_op jit(solution)/shard_map/ppermute | solution.py:418
  91.4 16.0 %collective-permute-start.6 = (f32[304,256]{1,0:T(8,128)S(1)}, f32[304,256]{1,0:T(8,128)S(1)}, u32[]{:S(2)}, u32[]{:S(2)}) collective-permute-start(f32[304,256]{1,0:T(8,128)S(1)} %pad_maximum_fusion.1.refs_0_), channel_id=1, source_target_pairs={{0,8},{4,12},{8,0},{12,4},{16,24},{20,28},{24,16},{28,20},{1,9},{5... | collective-permute-start | bytes 933896 | tf_op jit(solution)/shard_map/ppermute | solution.py:418
  109.5 10.8 %copy-start.3 = (f32[4,304,256]{2,1,0:T(8,128)S(1)}, f32[4,304,256]{2,1,0:T(8,128)}, u32[]{:S(2)}) copy-start(f32[4,304,256]{2,1,0:T(8,128)} %pad_maximum_fusion.refs_3_.even_ref.refs_4_) | copy-start | bytes 3735556
  115.8 1.3 copy-start.2
  117.1 46.5 %collective-permute-start.13 = (f32[4000,128]{1,0:T(8,128)}, f32[4000,128]{1,0:T(8,128)}, u32[]{:S(2)}, u32[]{:S(2)}) collective-permute-start(f32[4000,128]{1,0:T(8,128)} %get-tuple-element.29.refs_4_.refs_6_), channel_id=1, source_target_pairs={{2,3},{6,7},{10,11},{14,15},{18,19},{22,23},{26,27},{30,31}} | collective-permute-start | bytes 6144008 | tf_op jit(solution)/shard_map/ppermute | solution.py:397
  119.0 47.8 %collective-permute-start.12 = (f32[4000,128]{1,0:T(8,128)}, f32[4000,128]{1,0:T(8,128)}, u32[]{:S(2)}, u32[]{:S(2)}) collective-permute-start(f32[4000,128]{1,0:T(8,128)} %get-tuple-element.25.after_ref.refs_3_.refs_5_), channel_id=1, source_target_pairs={{1,0},{5,4},{9,8},{13,12},{17,16},{21,20},{25,24},{29,28}} | collective-permute-start | bytes 6144008 | tf_op jit(solution)/shard_map/ppermute | solution.py:397
  120.3 3.4 %collective-permute-start.9 = (f32[4,304,256]{2,1,0:T(8,128)S(1)}, f32[4,304,256]{2,1,0:T(8,128)S(1)}, u32[]{:S(2)}, u32[]{:S(2)}) collective-permute-start(f32[4,304,256]{2,1,0:T(8,128)S(1)} %copy-done.3), channel_id=1, source_target_pairs={{0,4},{4,0},{8,12},{12,8},{16,20},{20,16},{24,28},{28,24},{1,5},{5... | collective-permute-start | bytes 3735560 | tf_op jit(solution)/shard_map/ppermute | solution.py:418
  123.7 1.0 copy-start.5
  157.8 38.7 %collective-permute-start.16 = (f32[128,256]{1,0:T(8,128)}, f32[128,256]{1,0:T(8,128)S(1)}, u32[]{:S(2)}, u32[]{:S(2)}) collective-permute-start(f32[128,256]{1,0:T(8,128)} %own_columns.1.refs_0_), channel_id=1, source_target_pairs={{0,3},{1,0},{2,1},{3,2},{4,7},{5,4},{6,5},{7,6},{8,11},{9,8},{10,9... | collective-permute-start | bytes 393224 | tf_op jit(solution)/shard_map/ppermute | solution.py:480
  157.8 38.7 %collective-permute-start.15 = (f32[128,256]{1,0:T(8,128)}, f32[128,256]{1,0:T(8,128)S(1)}, u32[]{:S(2)}, u32[]{:S(2)}) collective-permute-start(f32[128,256]{1,0:T(8,128)} %own_columns.1.refs_0_), channel_id=1, source_target_pairs={{0,2},{1,3},{2,0},{3,1},{4,6},{5,7},{6,4},{7,5},{8,10},{9,11},{10,... | collective-permute-start | bytes 393224 | tf_op jit(solution)/shard_map/ppermute | solution.py:480
  163.0 33.4 %collective-permute-start.14 = (f32[128,256]{1,0:T(8,128)}, f32[128,256]{1,0:T(8,128)S(1)}, u32[]{:S(2)}, u32[]{:S(2)}) collective-permute-start(f32[128,256]{1,0:T(8,128)} %own_columns.1.refs_0_), channel_id=1, source_target_pairs={{0,1},{1,2},{2,3},{3,0},{4,5},{5,6},{6,7},{7,4},{8,9},{9,10},{10,1... | collective-permute-start | bytes 393224 | tf_op jit(solution)/shard_map/ppermute | solution.py:480
  196.4 4.4 %copy-start.7 = (f32[4,384,256]{2,1,0:T(8,128)S(1)}, f32[4,384,256]{2,1,0:T(8,128)}, u32[]{:S(2)}) copy-start(f32[4,384,256]{2,1,0:T(8,128)} %get-tuple-element.30) | copy-start | bytes 4718596
  196.4 0.7 copy-start.12
  196.5 0.7 copy-start.13
  196.5 0.7 copy-start.14
  197.2 3.6 %collective-permute-start.17 = (f32[4,384,256]{2,1,0:T(8,128)}, f32[4,384,256]{2,1,0:T(8,128)S(1)}, u32[]{:S(2)}, u32[]{:S(2)}) collective-permute-start(f32[4,384,256]{2,1,0:T(8,128)} %gate.10), channel_id=1, source_target_pairs={{0,4},{4,0},{8,12},{12,8},{16,20},{20,16},{24,28},{28,24},{1,5},{5... | collective-permute-start | bytes 4718600 | tf_op jit(solution)/shard_map/ppermute | solution.py:418
  202.0 13.1 %collective-permute-start.20 = (f32[384,256]{1,0:T(8,128)}, f32[384,256]{1,0:T(8,128)S(1)}, u32[]{:S(2)}, u32[]{:S(2)}) collective-permute-start(f32[384,256]{1,0:T(8,128)} %get-tuple-element.32), channel_id=1, source_target_pairs={{0,24},{4,28},{8,16},{12,20},{16,8},{20,12},{24,0},{28,4},{1,25},{... | collective-permute-start | bytes 1179656 | tf_op jit(solution)/shard_map/ppermute | solution.py:418
  204.5 18.2 %collective-permute-start.19 = (f32[384,256]{1,0:T(8,128)}, f32[384,256]{1,0:T(8,128)S(1)}, u32[]{:S(2)}, u32[]{:S(2)}) collective-permute-start(f32[384,256]{1,0:T(8,128)} %get-tuple-element.33), channel_id=1, source_target_pairs={{0,16},{4,20},{8,24},{12,28},{16,0},{20,4},{24,8},{28,12},{1,17},{... | collective-permute-start | bytes 1179656 | tf_op jit(solution)/shard_map/ppermute | solution.py:418
  205.0 17.8 %collective-permute-start.18 = (f32[384,256]{1,0:T(8,128)}, f32[384,256]{1,0:T(8,128)S(1)}, u32[]{:S(2)}, u32[]{:S(2)}) collective-permute-start(f32[384,256]{1,0:T(8,128)} %get-tuple-element.34), channel_id=1, source_target_pairs={{0,8},{4,12},{8,0},{12,4},{16,24},{20,28},{24,16},{28,20},{1,9},{5... | collective-permute-start | bytes 1179656 | tf_op jit(solution)/shard_map/ppermute | solution.py:418
  205.5 22.0 %copy-start.1 = (f32[256,256]{1,0:T(8,128)S(1)}, f32[256,256]{1,0:T(8,128)}, u32[]{:S(2)}) copy-start(f32[256,256]{1,0:T(8,128)} %param.6) | copy-start | bytes 786436
  215.2 7.7 %copy-start.9 = (f32[384,256]{1,0:T(8,128)}, f32[384,256]{1,0:T(8,128)S(1)}, u32[]{:S(2)}) copy-start(f32[384,256]{1,0:T(8,128)S(1)} %collective-permute-done.20.refs_3_) | copy-start | bytes 1179652
  222.7 0.8 copy-start.10
  223.5 0.7 copy-start.11
Sparse Core Ops, SparseCore 0:
  107.4 51.1 reduce-scatter.1

commit v8 on v7

--- a/solution.py
+++ b/solution.py
@@ -90,42 +90,45 @@
     return jnp.where(index % 2 == 0, even_ref[half, rows], odd_ref[half, rows])
 
 
-def project_kernel(per, wide, me_ref, v_ref, r_ref, e_ref, x_ref, even_ref, odd_ref, left_ref, small_ref, both_ref):
+def project_kernel(per, wide, me_ref, v_ref, r_ref, e_ref, x_ref, even_ref, odd_ref, sums_ref, small_ref, both_ref):
     j = pl.program_id(0)
     nb = r_ref.shape[1]
-    each = x_ref.shape[1]
-    step = v_ref.shape[1]
+    m = both_ref.shape[0] // 2
+    k = m - nb
     ride = even_ref.shape[1] - nb
 
     @pl.when(j == 0)
     def _():
         turned = r_ref[...].T
-        both_ref[:nb], both_ref[nb:] = split(turned)
-        k = nb + each
-        left_ref[:nb], left_ref[k : k + nb] = split(turned * e_ref[...])
-        left_ref[nb:k], left_ref[k + nb :] = split(x_ref[...].T)
-        small = three((left_ref[:k], left_ref[k:]), split(r_ref[...]))
+        first = 0
+        for part in (turned, turned * e_ref[...], x_ref[...].T):
+            end = first + part.shape[0]
+            both_ref[first:end], both_ref[m + first : m + end] = split(part)
+            first = end
+        small = three((both_ref[nb:m], both_ref[m + nb :]), split(r_ref[...]))
         small_ref[...] = small
         if ride:
-            rows = k // wide
             for w in range(wide):
-                place(small[w * rows : (w + 1) * rows], w ^ me_ref[0], even_ref, odd_ref, nb)
-
-    value = stacked(both_ref[...], both_ref[:nb], split(v_ref[...]))
-    for g in range(step // per):
-        index = (j * (step // per) + g) ^ me_ref[0]
-        place(value[:, g * per : (g + 1) * per], index, even_ref, odd_ref, 0)
+                share = small[w * ride : (w + 1) * ride]
+                place(share, w ^ me_ref[0], even_ref, odd_ref, nb)
+
+    value = stacked(both_ref[...], both_ref[:m], split(v_ref[...]))
+    count = v_ref.shape[1] // per
+    for g in range(count):
+        part = value[:, g * per : (g + 1) * per]
+        place(part[:nb], (j * count + g) ^ me_ref[0], even_ref, odd_ref, 0)
+        sums_ref[g] = part[nb:]
 
 
 def project(me, vectors, reflectors, e_row, block, wide, ride):
     rows, columns = vectors.shape
     nb = reflectors.shape[1]
-    each = block.shape[1]
-    k = nb + each
+    k = nb + block.shape[1]
     per = columns // wide
     step = width(columns, wide)
-    shapes = [(wide // 2, nb + ride, per)] * 2 + [(2 * k, rows), (k, nb)]
-    kinds = [F32, F32, BF16, F32]
+    shapes = [(wide // 2, nb + ride, per)] * 2 + [(wide, k, per), (k, nb)]
+    specs = [whole(x) for x in shapes]
+    specs[2] = pl.BlockSpec((step // per, k, per), lambda j, *_: (j, 0, 0))
     return pl.pallas_call(
         functools.partial(project_kernel, per, wide),
         grid_spec=pltpu.PrefetchScalarGridSpec(
@@ -133,53 +136,18 @@
             grid=(columns // step,),
             in_specs=[pl.BlockSpec((rows, step), lambda j, *_: (0, j))]
             + [whole(x) for x in ((rows, nb), (1, rows), block.shape)],
-            out_specs=[whole(x) for x in shapes],
-            scratch_shapes=[pltpu.VMEM((2 * nb, rows), BF16)],
+            out_specs=specs,
+            scratch_shapes=[pltpu.VMEM((2 * (nb + k), rows), BF16)],
         ),
-        out_shape=[jax.ShapeDtypeStruct(x, kind) for x, kind in zip(shapes, kinds)],
+        out_shape=[jax.ShapeDtypeStruct(x, F32) for x in shapes],
         compiler_params=params(),
         cost_estimate=SHORT,
         name="project",
     )(me, vectors, reflectors, e_row, block)
 
 
-def early_kernel(per, v_ref, left_ref, *refs):
-    out_ref, token_ref = refs[-2:]
-    k = left_ref.shape[0] // 2
-    token_ref[...] = jnp.zeros_like(token_ref)
-    value = stacked(left_ref[...], left_ref[:k], split(v_ref[...]))
-    for g in range(v_ref.shape[1] // per):
-        out_ref[g] = value[:, g * per : (g + 1) * per]
-
-
-def early(vectors, left, offset, blocks, after, before, wide):
-    rows, columns = vectors.shape
-    per = columns // wide
-    step = width(columns, wide)
-    count = step // per
-    k = left.shape[0] // 2
-    operands = [vectors, left, after] + before
-    return pl.pallas_call(
-        functools.partial(early_kernel, per),
-        grid=(blocks,),
-        in_specs=[pl.BlockSpec((rows, step), lambda j: (0, j + offset)), whole(left.shape)]
-        + [ANY] * (len(operands) - 2),
-        out_specs=[
-            pl.BlockSpec((count, k, per), lambda j: (j + offset, 0, 0)),
-            whole((8, 128)),
-        ],
-        out_shape=[
-            jax.ShapeDtypeStruct((wide, k, per), F32),
-            jax.ShapeDtypeStruct((8, 128), F32),
-        ],
-        input_output_aliases={3: 0} if before else {},
-        compiler_params=params(),
-        cost_estimate=SHORT,
-        name="early",
-    )(*operands)
-
-
-def update_kernel(me_ref, v_ref, r_ref, even_ref, odd_ref, after_ref, out_ref, token_ref, right_ref):
+def update_kernel(me_ref, v_ref, r_ref, even_ref, odd_ref, *refs):
+    out_ref, token_ref, right_ref = refs[-3:]
     nb = r_ref.shape[1]
     per = even_ref.shape[2]
 
@@ -198,30 +166,36 @@
     out_ref[...] = v_ref[...] - mul(left, right_ref[...])
 
 
-def update(me, vectors, reflectors, c, after):
+def update(me, vectors, reflectors, c, first, count, of, others, before):
     rows, columns = vectors.shape
     nb = reflectors.shape[1]
-    count = next(x for x in range(4, rows) if rows % (16 * x) == 0)
-    rows_of = pl.BlockSpec((rows // count, columns), lambda j, *_: (j, 0))
+    operands = [me, vectors, reflectors, *c, *others, *before]
     return pl.pallas_call(
         update_kernel,
         grid_spec=pltpu.PrefetchScalarGridSpec(
             num_scalar_prefetch=1,
             grid=(count,),
-            in_specs=[rows_of, pl.BlockSpec((rows // count, nb), lambda j, *_: (j, 0))]
+            in_specs=[
+                pl.BlockSpec((rows // of, columns), lambda j, *_: (j + first, 0)),
+                pl.BlockSpec((rows // of, nb), lambda j, *_: (j + first, 0)),
+            ]
             + [whole(x.shape) for x in c]
-            + [ANY],
-            out_specs=[rows_of, whole((8, 128))],
+            + [ANY] * (len(operands) - 5),
+            out_specs=[
+                pl.BlockSpec((rows // of, columns), lambda j, *_: (j + first, 0)),
+                whole((8, 128)),
+            ],
             scratch_shapes=[pltpu.VMEM((3 * nb, columns), BF16)],
         ),
         out_shape=[
             jax.ShapeDtypeStruct(vectors.shape, F32),
             jax.ShapeDtypeStruct((8, 128), F32),
         ],
+        input_output_aliases={len(operands) - 1: 0} if before else {},
         compiler_params=params(),
         cost_estimate=SHORT,
         name="update",
-    )(me, vectors, reflectors, *c, after)
+    )(*operands)
 
 
 def late_kernel(per, counts, at_ref, u_ref, after_ref, *refs):
@@ -287,17 +261,23 @@
 def own_kernel(me_ref, even_ref, odd_ref, after_ref, out_ref):
     each, nb = out_ref.shape
     per = even_ref.shape[2]
-    block = take((OFF // per) ^ me_ref[0], even_ref, odd_ref, slice(0, nb))
+    block = jnp.where(
+        ((OFF // per) ^ me_ref[0]) % 2 == 0, even_ref[0, :nb], odd_ref[0, :nb]
+    )
     out_ref[...] = block[:, OFF % per : OFF % per + each].T
 
 
 def own_columns(me, c, after, nb, each):
+    per = c[0].shape[2]
+    block = pl.BlockSpec(
+        (1, *c[0].shape[1:]), lambda j, me_ref: (((OFF // per) ^ me_ref[0]) // 2, 0, 0)
+    )
     return pl.pallas_call(
         own_kernel,
         grid_spec=pltpu.PrefetchScalarGridSpec(
             num_scalar_prefetch=1,
             grid=(1,),
-            in_specs=[whole(x.shape) for x in c] + [ANY],
+            in_specs=[block, block, ANY],
             out_specs=whole((each, nb)),
         ),
         out_shape=jax.ShapeDtypeStruct((each, nb), F32),
@@ -307,7 +287,25 @@
     )(me, *c, after)
 
 
-def base_kernel(n, each, ride, at_ref, ready_ref, c_ref, *refs):
+def total_kernel(*refs):
+    refs[-1][...] = functools.reduce(jnp.add, [ref[...] for ref in refs[:-1]])
+
+
+def total(terms):
+    shape = terms[0].shape
+    return pl.pallas_call(
+        total_kernel,
+        grid=(1,),
+        in_specs=[pl.BlockSpec(shape, lambda j: (0, 0))] * len(terms),
+        out_specs=pl.BlockSpec(shape, lambda j: (0, 0)),
+        out_shape=jax.ShapeDtypeStruct(shape, F32),
+        compiler_params=params(),
+        cost_estimate=LONG,
+        name="total",
+    )(*terms)
+
+
+def base_kernel(n, each, ride, at_ref, ready_ref, c_ref, middle_ref, *refs):
     *refs, out_ref, coef_ref, small_ref = refs
     me, z = at_ref[0], at_ref[1]
     nb = c_ref.shape[0]
@@ -325,11 +323,17 @@
         small_ref[...] = refs[n][...]
     corrected = ready_ref[...] - three(split(small_ref[...]), split(c_ref[...]))
     out_ref[...] = -three(split(coef_ref[...]), split(corrected[:nb]))
-    out_ref[pl.ds(pl.multiple_of(z * each, each), each), :] += corrected[nb:]
-
-
-def base(at, ready, c, coef, small, n, each, ride):
-    operands = [ready, c, *coef, *small]
+    middle = middle_ref[...]
+    pieces = [corrected[nb:]] + [
+        middle[first : first + each] for first in range(0, middle.shape[0], each)
+    ]
+    for slot, piece in enumerate(pieces):
+        first = pl.multiple_of(at_ref[1 + slot] * each, each)
+        out_ref[pl.ds(first, each), :] += piece
+
+
+def base(at, ready, c, middle, coef, small, n, each, ride):
+    operands = [ready, c, middle, *coef, *small]
     k, per = ready.shape
     nb = c.shape[0]
     return pl.pallas_call(
@@ -352,9 +356,8 @@
     *refs, out_ref, total_ref = refs
     total_ref[...] = base_ref[...]
     total = functools.reduce(jnp.add, [ref[...] for ref in refs])
-    for slot in range(total.shape[0] // each):
-        first = pl.multiple_of(at_ref[2 + slot] * each, each)
-        total_ref[pl.ds(first, each), :] += total[slot * each : (slot + 1) * each]
+    first = pl.multiple_of(at_ref[at_ref.shape[0] - 1] * each, each)
+    total_ref[pl.ds(first, each), :] += total
     out_ref[...] = total_ref[...].T
 
 
@@ -444,8 +447,6 @@
     nb = reflectors.shape[1]
     k = nb + each
     per = columns // wide
-    blocks = columns // width(columns, wide)
-    half = blocks // 2
     e_row = energies.reshape(1, rows)
 
     own = energies[:, None] * vectors[:, OFF : OFF + each]
@@ -455,37 +456,42 @@
     at = jnp.stack([me[0], z] + [source(places, z) for places in table])
 
     ride = k // wide if per == nb and k % (8 * wide) == 0 else 0
-    even, odd, left, small = project(me, vectors, reflectors, e_row, own, wide, ride)
-    terms = scatter_terms(even, odd, wide)
+    even, odd, sums, small = project(me, vectors, reflectors, e_row, own, wide, ride)
+    if n > 2:
+        held = travel(came, held, n, 2, [small])
+    ready = lax.psum_scatter(sums, "wide", scatter_dimension=0)
+
+    projected = functools.reduce(jnp.add, scatter_terms(even, odd, wide, came[(1, 0)]))
     highest = lax.Precision.HIGHEST
-    if n > 2:
-        held = travel(came, held, n, 2, [left, terms[0]])
-    sums, token = early(vectors, left, 0, half, came[(1, 0)], [], wide)
-    terms[0] = gate(terms[:1], token)[0]
-    projected = functools.reduce(jnp.add, terms)
     coefficients = jnp.dot(triangle, projected[:nb], precision=highest)
     payload = coefficients
     if ride:
         payload = jnp.concatenate([coefficients, projected[nb:]], axis=0)
-    sums, token = early(vectors, left, half, blocks - half, payload, [sums], wide)
-    ready = lax.psum_scatter(sums, "wide", scatter_dimension=0)
-    c = collect(payload, wide, [token])
+    c = collect(payload, wide)
+
+    of = next(x for x in range(4, rows) if rows % (16 * x) == 0)
+    updated, token = update(me, vectors, reflectors, c, 0, of // 2, of, [], [])
     for hops in range(3, n):
-        held = travel(came, held, n, hops, [token, c[0]])
-    after = came[(min(2, n - 1), 0)]
-    updated, token = update(me, vectors, reflectors, c, after)
-
-    mine = own_columns(me, c, token, nb, each)
+        held = travel(came, held, n, hops, [token])
+    updated, token = update(
+        me, vectors, reflectors, c, of // 2, of - of // 2, of, [came[(n - 2, 0)]], [updated]
+    )
+
+    slots = [options(came, places, z) for places in table]
+    even, odd = late(me, updated, slots[:-1], token, wide)
+    mine = own_columns(me, c, even, nb, each)
     coef = [mine] + [
         lax.ppermute(mine, "narrow", [(p, (p + s) % n) for p in range(n)]) for s in range(1, n)
     ]
-    slots = [options(came, places, z) for places in table]
-    even, odd = late(me, updated, slots, token, wide)
-    (odd,) = gate([odd], ready, *coef[1:])
-    tail = scatter_terms(even, odd, wide)
+    middle = scatter_terms(even, odd, wide)
+    (ready,) = gate([ready], middle[0], mine)
+    even, odd = late(me, updated, slots[-1:], ready, wide)
+    middle = total(middle)
+    (odd,) = gate([odd], *coef[1:])
+    tail = scatter_terms(even, odd, wide, middle)
     (ready,) = gate([ready], tail[0])
     small = c if ride else [lax.psum(small, "wide")]
-    base_block = base(at, ready, coefficients, coef, small, n, each, ride)
+    base_block = base(at, ready, coefficients, middle, coef, small, n, each, ride)
     return (updated, last(at, base_block, tail, each))
 
 

time: 235 us -> 233 us (level)
  waiting for transfers between devices: 46 us -> 32.2 us
  starting transfers between devices: 29.2 us -> 37.3 us
  Pallas kernels: 128 us -> 131 us
    pallas_call x2 -> x1, Pallas kernels: 30.6 us -> 2 us  [total(): pl.pallas_call(total_kernel, grid=(1,), in_specs=[pl.BlockSpec(shape, lam...]
    ppermute x6, waiting for transfers between devices: 23.8 us -> 4.12 us  [travel(): held = [lax.ppermute(held[d], 'narrow', pairs[d]) for d in (0, 1)]]
    pallas_call x1, Pallas kernels: 27.4 us -> 43.9 us  [project(): pl.pallas_call(functools.partial(project_kernel, per, wide), grid_spec=pl...]
    pallas_call x1 -> x2, Pallas kernels: 29.6 us -> 42.3 us  [late(): pl.pallas_call(functools.partial(late_kernel, per, counts), grid_spec=plt...]
    ppermute x12 -> x16, waiting for transfers between devices: 22.2 us -> 28.1 us  [swap(): return lax.ppermute(x, 'wide', [(i, i ^ distance) for i in range(wide)])]
    ppermute x3, starting transfers between devices: 5.28 us -> 9.95 us  [on_device(): lax.ppermute(mine, 'narrow', [(p, (p + s) % n) for p in range(n)])]
    ppermute x12 -> x16, starting transfers between devices: 10.8 us -> 14.2 us  [swap(): return lax.ppermute(x, 'wide', [(i, i ^ distance) for i in range(wide)])]
    pallas_call x1 -> x2, Pallas kernels: 30.6 us -> 33.1 us  [update(): pl.pallas_call(update_kernel, grid_spec=pltpu.PrefetchScalarGridSpec(num_...]
  transfers between devices with their start and end apart: 22 -> 26, of which waited for: 10 -> 13; matrix products, arithmetic and copies ran while one was open for 3% -> 2% of each run, Pallas kernels for 53% -> 55%
where the time goes in v8:
time: 233 us
  Pallas kernels  131 us (56%)
  starting transfers between devices  37.3 us (16%)
  waiting for transfers between devices  32.2 us (14%)
  between operations  14.3 us (6%)
  other arithmetic  10.3 us (4%)
  local copies, waits for them, and re-layouts  7.11 us (3%)
    pallas_call x1, Pallas kernels, project(): pl.pallas_call(functools.partial(project_kernel, per, wide), grid_spec=pl...  43.9 us
    pallas_call x2, Pallas kernels, late(): pl.pallas_call(functools.partial(late_kernel, per, counts), grid_spec=plt...  42.3 us
    pallas_call x2, Pallas kernels, update(): pl.pallas_call(update_kernel, grid_spec=pltpu.PrefetchScalarGridSpec(num_...  33.1 us
    ppermute x16, waiting for transfers between devices, swap(): return lax.ppermute(x, 'wide', [(i, i ^ distance) for i in range(wide)])  28.1 us
    ppermute x16, starting transfers between devices, swap(): return lax.ppermute(x, 'wide', [(i, i ^ distance) for i in range(wide)])  14.2 us
    ppermute x6, starting transfers between devices, travel(): held = [lax.ppermute(held[d], 'narrow', pairs[d]) for d in (0, 1)]  13.1 us
    ppermute x3, starting transfers between devices, on_device(): lax.ppermute(mine, 'narrow', [(p, (p + s) % n) for p in range(n)])  9.95 us
    unnamed x38, local copies, waits for them, and re-layouts  6.43 us
  transfers between devices with their start and end apart: 26, of which 13 were waited for; matrix products, arithmetic and copies ran while one was open for 2% of the time, Pallas kernels for 55%

profile of v8, /device:TPU:0, one launch (start us, length us, event | category | flops | bytes accessed | tf_op | source)
XLA Modules:
  0.0 232.6 jit_solution(9151104673804806867)
XLA Ops:
  7.2 2.7 %slice_multiply_fusion.x_ref = f32[4000,128]{1,0:T(8,128)S(1)} fusion(f32[4000,2048]{1,0:T(8,128)} %v_ref.5, f32[4000]{0:T(1024)} %param.7), kind=kLoop, calls=%fused_computation | loop fusion | flops 512000 | bytes 4112000 | tf_op jit(solution)/shard_map/mul | solution.py:452
  10.0 6.3 %collective-permute-start.2 = (f32[4000,128]{1,0:T(8,128)S(1)}, f32[4000,128]{1,0:T(8,128)}, u32[]{:S(2)}, u32[]{:S(2)}) collective-permute-start(f32[4000,128]{1,0:T(8,128)S(1)} %slice_multiply_fusion.x_ref), channel_id=1, source_target_pairs={{0,1},{1,2},{2,3},{4,5},{5,6},{6,7},{8,9},{9,10},{10,11},{12,13},{... | collective-permute-start | bytes 6144008 | tf_op jit(solution)/shard_map/ppermute | solution.py:400
  16.3 1.3 collective-permute-start.1
  17.6 43.9 %project.1 = (f32[4,304,256]{2,1,0:T(8,128)}, f32[4,304,256]{2,1,0:T(8,128)}, f32[8,384,256]{2,1,0:T(8,128)}, f32[384,256]{1,0:T(8,128)}) custom-call(s32[1]{0:T(128)} %bitcast.me_ref, f32[4000,2048]{1,0:T(8,128)} %v_ref.5, f32[4000,256]{1,0:T(8,128)} %r_ref.5, f32[1,4000]{1,0:T(1,128)} %bitcast.52, f32[4000,128]{1,0:T(8,128)} %copy-done.4), custom_call_target="tpu_custom_call" | custom-call | flops 1024 | bytes 1024 | tf_op jit(solution)/shard_map/project/pallas_call | solution.py:132
  61.6 2.8 %collective-permute-done.1.refs_0_ = f32[4000,128]{1,0:T(8,128)} collective-permute-done((f32[4000,128]{1,0:T(8,128)S(1)}, f32[4000,128]{1,0:T(8,128)}, u32[]{:S(2)}, u32[]{:S(2)}) %collective-permute-start.1) | collective-permute-done | bytes 2048032 | tf_op jit(solution)/shard_map/ppermute | solution.py:400
  64.7 1.0 copy-done.5
  65.7 1.3 copy-done.9
  67.0 1.3 fusion.2
  68.3 1.6 collective-permute-start.3
  69.9 1.5 collective-permute-start.5
  71.9 1.3 collective-permute-start.10
  73.2 2.0 collective-permute-start.11
  75.1 3.4 %collective-permute-done.3 = f32[304,256]{1,0:T(8,128)S(1)} collective-permute-done((f32[304,256]{1,0:T(8,128)S(1)}, f32[304,256]{1,0:T(8,128)S(1)}, u32[]{:S(2)}, u32[]{:S(2)}) %collective-permute-start.3) | collective-permute-done | bytes 311328 | tf_op jit(solution)/shard_map/ppermute | solution.py:421
  78.6 6.9 %collective-permute-done.5 = f32[304,256]{1,0:T(8,128)S(1)} collective-permute-done((f32[304,256]{1,0:T(8,128)S(1)}, f32[304,256]{1,0:T(8,128)S(1)}, u32[]{:S(2)}, u32[]{:S(2)}) %collective-permute-start.5) | collective-permute-done | bytes 311328 | tf_op jit(solution)/shard_map/ppermute | solution.py:421
  85.5 1.4 collective-permute-done.4
  86.9 1.1 fusion.6
  89.0 1.5 collective-permute-start.6
  90.5 1.5 collective-permute-start.8
  92.0 5.9 %collective-permute-done.7 = f32[304,256]{1,0:T(8,128)S(1)} collective-permute-done((f32[304,256]{1,0:T(8,128)S(1)}, f32[304,256]{1,0:T(8,128)S(1)}, u32[]{:S(2)}, u32[]{:S(2)}) %collective-permute-start.7) | collective-permute-done | bytes 311328 | tf_op jit(solution)/shard_map/ppermute | solution.py:421
  97.9 1.3 collective-permute-done.6
  99.2 4.3 %collective-permute-done.8 = f32[304,256]{1,0:T(8,128)S(1)} collective-permute-done((f32[304,256]{1,0:T(8,128)S(1)}, f32[304,256]{1,0:T(8,128)S(1)}, u32[]{:S(2)}, u32[]{:S(2)}) %collective-permute-start.8) | collective-permute-done | bytes 311328 | tf_op jit(solution)/shard_map/ppermute | solution.py:421
  103.7 3.0 %collective-permute-done.9.odd_ref.refs_5_ = f32[4,304,256]{2,1,0:T(8,128)} collective-permute-done((f32[4,304,256]{2,1,0:T(8,128)S(1)}, f32[4,304,256]{2,1,0:T(8,128)}, u32[]{:S(2)}, u32[]{:S(2)}) %collective-permute-start.9) | collective-permute-done | bytes 1245216 | tf_op jit(solution)/shard_map/ppermute | solution.py:421
  106.8 12.5 %update.2 = (f32[4000,2048]{1,0:T(8,128)}, f32[8,128]{1,0:T(8,128)}) custom-call(s32[1]{0:T(128)} %bitcast.me_ref, f32[4000,2048]{1,0:T(8,128)} %v_ref.5, f32[4000,256]{1,0:T(8,128)} %r_ref.5, f32[4,304,256]{2,1,0:T(8,128)} %copy-done.2, f32[4,304,256]{2,1,0:T(8,128)} %collective-permute-done.9.odd_ref.refs_5_), custom_call_target="tpu_custom_call" | custom-call | flops 1024 | bytes 1024 | tf_op jit(solution)/shard_map/update/pallas_call | solution.py:173
  119.3 1.4 collective-permute-done.10.refs_0_
  120.7 1.3 copy-done.3
  122.0 1.0 collective-permute-start.14
  123.0 1.3 collective-permute-start.13
  124.3 0.7 pad_add_fusion.at_ref
  125.0 20.6 %update.3 = (f32[4000,2048]{1,0:T(8,128)}, f32[8,128]{1,0:T(8,128)}) custom-call(s32[1]{0:T(128)} %bitcast.me_ref, f32[4000,2048]{1,0:T(8,128)} %v_ref.5, f32[4000,256]{1,0:T(8,128)} %r_ref.5, f32[4,304,256]{2,1,0:T(8,128)} %copy-done.2, f32[4,304,256]{2,1,0:T(8,128)} %collective-permute-done.9.odd_ref.refs_5_, ...), custom_call_target="tpu_custom_call", output_to_operand_aliasing={{0}: (6, {})} | custom-call | flops 1024 | bytes 1024 | tf_op jit(solution)/shard_map/update/pallas_call | solution.py:173
  145.6 23.3 %late.2 = (f32[4,256,256]{2,1,0:T(8,128)}, f32[4,256,256]{2,1,0:T(8,128)}) custom-call(s32[3]{0:T(128)} %pad_add_fusion.at_ref, f32[4000,2048]{1,0:T(8,128)} %get-tuple-element.16.u_ref, f32[8,128]{1,0:T(8,128)} %get-tuple-element.28.after_ref, f32[4000,128]{1,0:T(8,128)} %get-tuple-element.21.refs_1_.refs_0_, ...), custom_call_target="tpu_custom_call" | custom-call | flops 1024 | bytes 1024 | tf_op jit(solution)/shard_map/late/pallas_call | solution.py:241
  169.0 1.9 own_columns.1.refs_2_.refs_0_
  170.9 5.5 %collective-permute-start.17 = (f32[128,256]{1,0:T(8,128)}, f32[128,256]{1,0:T(8,128)S(1)}, u32[]{:S(2)}, u32[]{:S(2)}) collective-permute-start(f32[128,256]{1,0:T(8,128)} %own_columns.1.refs_2_.refs_0_), channel_id=1, source_target_pairs={{0,3},{1,0},{2,1},{3,2},{4,7},{5,4},{6,5},{7,6},{8,11},{9,8},{10,9... | collective-permute-start | bytes 393224 | tf_op jit(solution)/shard_map/ppermute | solution.py:484
  176.4 2.0 fusion.7
  178.5 2.4 %collective-permute-start.21 = (f32[256,256]{1,0:T(8,128)S(1)}, f32[256,256]{1,0:T(8,128)}, u32[]{:S(2)}, u32[]{:S(2)}) collective-permute-start(f32[256,256]{1,0:T(8,128)S(1)} %get-tuple-element.37), channel_id=1, source_target_pairs={{0,24},{4,28},{8,16},{12,20},{16,8},{20,12},{24,0},{28,4},{1,25},{... | collective-permute-start | bytes 786440 | tf_op jit(solution)/shard_map/ppermute | solution.py:421
  182.0 3.4 %collective-permute-start.16 = (f32[128,256]{1,0:T(8,128)S(1)}, f32[128,256]{1,0:T(8,128)S(1)}, u32[]{:S(2)}, u32[]{:S(2)}) collective-permute-start(f32[128,256]{1,0:T(8,128)S(1)} %copy-done.12), channel_id=1, source_target_pairs={{0,2},{1,3},{2,0},{3,1},{4,6},{5,7},{6,4},{7,5},{8,10},{9,11},{10,... | collective-permute-start | bytes 393224 | tf_op jit(solution)/shard_map/ppermute | solution.py:484
  185.4 1.1 collective-permute-start.15
  187.0 0.7 stack.54.at_ref
  187.7 18.9 %late.3 = (f32[4,128,256]{2,1,0:T(8,128)}, f32[4,128,256]{2,1,0:T(8,128)}) custom-call(s32[2]{0:T(128)} %pad_add_fusion.1.at_ref, f32[4000,2048]{1,0:T(8,128)} %get-tuple-element.16.u_ref, f32[384,256]{1,0:T(8,128)} %gate.10.after_ref.refs_0_, f32[4000,128]{1,0:T(8,128)} %get-tuple-element.24.refs_0_.refs_3_, f32[4000,128]{1,0:T(8,128)} %get-tuple-element.29.refs_4_.refs_1_, ...), custom_call_target="tpu_custom_call" | custom-call | flops 1024 | bytes 1024 | tf_op jit(solution)/shard_map/late/pallas_call | solution.py:241
  206.7 0.6 copy-done.17
  207.4 2.0 total.1.refs_1_.middle_ref
  209.5 0.8 copy-done.7
  210.3 1.8 fusion.12
  212.1 1.5 collective-permute-start.24
  214.1 1.5 collective-permute-start.22
  215.6 4.7 %base.1.base_ref = f32[512,256]{1,0:T(8,128)} custom-call(s32[5]{0:T(128)} %stack.54.at_ref, f32[384,256]{1,0:T(8,128)} %gate.13.ready_ref, f32[256,256]{1,0:T(8,128)} %copy-done.10, f32[256,256]{1,0:T(8,128)} %total.1.refs_1_.middle_ref, f32[128,256]{1,0:T(8,128)} %own_columns.1.refs_2_.refs_0_, f32[128,256]{1,0:T(8,128)} %copy-done.18, ...), custom_call_target="tpu_custom_call" | custom-call | flops 99999997952 | bytes 1024 | tf_op jit(solution)/shard_map/base/pallas_call | solution.py:339
  220.3 1.3 collective-permute-done.23.refs_2_
  222.2 0.7 copy-done.15
  222.8 3.0 %last.1 = f32[256,512]{1,0:T(8,128)} custom-call(s32[5]{0:T(128)} %stack.54.at_ref, f32[512,256]{1,0:T(8,128)} %base.1.base_ref, f32[128,256]{1,0:T(8,128)} %get-tuple-element.44.refs_1_.refs_0_, f32[128,256]{1,0:T(8,128)} %copy-done.15, f32[128,256]{1,0:T(8,128)} %copy-done.14, f32[128,256]{1,0:T(8,128)} %copy-done.13), custom_call_target="tpu_custom_call" | custom-call | flops 1024 | bytes 1024 | tf_op jit(solution)/shard_map/last/pallas_call | solution.py:367
  (71 shorter events, 5.3 us)
Async XLA Ops:
  7.2 80.8 %copy-start = (f32[256,256]{1,0:T(8,128)S(1)}, f32[256,256]{1,0:T(8,128)}, u32[]{:S(2)}) copy-start(f32[256,256]{1,0:T(8,128)} %param.6) | copy-start | bytes 786436
  7.2 179.8 %reduce-scatter.2.cloned.1.call-start = ((), (), s32[]{:S(2)}) async-start(), calls=%async_computation.1 | async-start | bytes 3538944 | tf_op jit(solution)/shard_map/reduce_scatter | solution.py:462
  10.0 7.6 %copy-start.4 = (f32[4000,128]{1,0:T(8,128)}, f32[4000,128]{1,0:T(8,128)S(1)}, u32[]{:S(2)}) copy-start(f32[4000,128]{1,0:T(8,128)S(1)} %slice_multiply_fusion.x_ref) | copy-start | bytes 6144004
  10.0 51.6 %collective-permute-start.2 = (f32[4000,128]{1,0:T(8,128)S(1)}, f32[4000,128]{1,0:T(8,128)}, u32[]{:S(2)}, u32[]{:S(2)}) collective-permute-start(f32[4000,128]{1,0:T(8,128)S(1)} %slice_multiply_fusion.x_ref), channel_id=1, source_target_pairs={{0,1},{1,2},{2,3},{4,5},{5,6},{6,7},{8,9},{9,10},{10,11},{12,13},{... | collective-permute-start | bytes 6144008 | tf_op jit(solution)/shard_map/ppermute | solution.py:400
  16.3 48.0 %collective-permute-start.1 = (f32[4000,128]{1,0:T(8,128)S(1)}, f32[4000,128]{1,0:T(8,128)}, u32[]{:S(2)}, u32[]{:S(2)}) collective-permute-start(f32[4000,128]{1,0:T(8,128)S(1)} %slice_multiply_fusion.x_ref), channel_id=1, source_target_pairs={{1,0},{2,1},{3,2},{5,4},{6,5},{7,6},{9,8},{10,9},{11,10},{13,12},{... | collective-permute-start | bytes 6144008 | tf_op jit(solution)/shard_map/ppermute | solution.py:400
  61.6 3.2 %collective-permute-start = (f32[4,304,256]{2,1,0:T(8,128)}, f32[4,304,256]{2,1,0:T(8,128)S(1)}, u32[]{:S(2)}, u32[]{:S(2)}) collective-permute-start(f32[4,304,256]{2,1,0:T(8,128)} %get-tuple-element.19), channel_id=1, source_target_pairs={{0,4},{4,0},{8,12},{12,8},{16,20},{20,16},{24,28},{28,24},{1,5},{5... | collective-permute-start | bytes 3735560 | tf_op jit(solution)/shard_map/ppermute | solution.py:421
  64.7 1.0 copy-start.5
  65.7 1.3 copy-start.9
  68.3 10.3 %collective-permute-start.3 = (f32[304,256]{1,0:T(8,128)S(1)}, f32[304,256]{1,0:T(8,128)S(1)}, u32[]{:S(2)}, u32[]{:S(2)}) collective-permute-start(f32[304,256]{1,0:T(8,128)S(1)} %get-tuple-element.34), channel_id=1, source_target_pairs={{0,8},{4,12},{8,0},{12,4},{16,24},{20,28},{24,16},{28,20},{1,9},{5... | collective-permute-start | bytes 933896 | tf_op jit(solution)/shard_map/ppermute | solution.py:421
  69.9 15.6 %collective-permute-start.5 = (f32[304,256]{1,0:T(8,128)S(1)}, f32[304,256]{1,0:T(8,128)S(1)}, u32[]{:S(2)}, u32[]{:S(2)}) collective-permute-start(f32[304,256]{1,0:T(8,128)S(1)} %get-tuple-element.35), channel_id=1, source_target_pairs={{0,24},{4,28},{8,16},{12,20},{16,8},{20,12},{24,0},{28,4},{1,25},{... | collective-permute-start | bytes 933896 | tf_op jit(solution)/shard_map/ppermute | solution.py:421
  71.4 15.5 %collective-permute-start.4 = (f32[304,256]{1,0:T(8,128)S(1)}, f32[304,256]{1,0:T(8,128)S(1)}, u32[]{:S(2)}, u32[]{:S(2)}) collective-permute-start(f32[304,256]{1,0:T(8,128)S(1)} %get-tuple-element.36), channel_id=1, source_target_pairs={{0,16},{4,20},{8,24},{12,28},{16,0},{20,4},{24,8},{28,12},{1,17},{... | collective-permute-start | bytes 933896 | tf_op jit(solution)/shard_map/ppermute | solution.py:421
  71.9 48.8 %collective-permute-start.10 = (f32[4000,128]{1,0:T(8,128)}, f32[4000,128]{1,0:T(8,128)S(1)}, u32[]{:S(2)}, u32[]{:S(2)}) collective-permute-start(f32[4000,128]{1,0:T(8,128)} %get-tuple-element.21.refs_1_.refs_0_), channel_id=1, source_target_pairs={{1,0},{2,1},{5,4},{6,5},{9,8},{10,9},{13,12},{14,13},{17,16},{18,1... | collective-permute-start | bytes 6144008 | tf_op jit(solution)/shard_map/ppermute | solution.py:400
  73.2 46.1 %collective-permute-start.11 = (f32[4000,128]{1,0:T(8,128)}, f32[4000,128]{1,0:T(8,128)}, u32[]{:S(2)}, u32[]{:S(2)}) collective-permute-start(f32[4000,128]{1,0:T(8,128)} %get-tuple-element.22.refs_1_.refs_2_), channel_id=1, source_target_pairs={{1,2},{2,3},{5,6},{6,7},{9,10},{10,11},{13,14},{14,15},{17,18},{18... | collective-permute-start | bytes 6144008 | tf_op jit(solution)/shard_map/ppermute | solution.py:400
  88.4 15.1 %copy-start.10 = (f32[256,256]{1,0:T(8,128)}, f32[256,256]{1,0:T(8,128)S(1)}, u32[]{:S(2)}) copy-start(f32[256,256]{1,0:T(8,128)S(1)} %convolution_bitcast_fusion.c_ref) | copy-start | bytes 786436
  88.4 9.5 %collective-permute-start.7 = (f32[304,256]{1,0:T(8,128)S(1)}, f32[304,256]{1,0:T(8,128)S(1)}, u32[]{:S(2)}, u32[]{:S(2)}) collective-permute-start(f32[304,256]{1,0:T(8,128)S(1)} %get-tuple-element.46), channel_id=1, source_target_pairs={{0,16},{4,20},{8,24},{12,28},{16,0},{20,4},{24,8},{28,12},{1,17},{... | collective-permute-start | bytes 933896 | tf_op jit(solution)/shard_map/ppermute | solution.py:421
  89.0 10.2 %collective-permute-start.6 = (f32[304,256]{1,0:T(8,128)S(1)}, f32[304,256]{1,0:T(8,128)S(1)}, u32[]{:S(2)}, u32[]{:S(2)}) collective-permute-start(f32[304,256]{1,0:T(8,128)S(1)} %get-tuple-element.46), channel_id=1, source_target_pairs={{0,8},{4,12},{8,0},{12,4},{16,24},{20,28},{24,16},{28,20},{1,9},{5... | collective-permute-start | bytes 933896 | tf_op jit(solution)/shard_map/ppermute | solution.py:421
  90.5 13.0 %collective-permute-start.8 = (f32[304,256]{1,0:T(8,128)S(1)}, f32[304,256]{1,0:T(8,128)S(1)}, u32[]{:S(2)}, u32[]{:S(2)}) collective-permute-start(f32[304,256]{1,0:T(8,128)S(1)} %get-tuple-element.46), channel_id=1, source_target_pairs={{0,24},{4,28},{8,16},{12,20},{16,8},{20,12},{24,0},{28,4},{1,25},{... | collective-permute-start | bytes 933896 | tf_op jit(solution)/shard_map/ppermute | solution.py:421
  103.6 3.2 %copy-start.2 = (f32[4,304,256]{2,1,0:T(8,128)}, f32[4,304,256]{2,1,0:T(8,128)S(1)}, u32[]{:S(2)}) copy-start(f32[4,304,256]{2,1,0:T(8,128)S(1)} %pad_maximum_fusion.even_ref.refs_4_) | copy-start | bytes 3735556
  103.6 3.1 %collective-permute-start.9 = (f32[4,304,256]{2,1,0:T(8,128)S(1)}, f32[4,304,256]{2,1,0:T(8,128)}, u32[]{:S(2)}, u32[]{:S(2)}) collective-permute-start(f32[4,304,256]{2,1,0:T(8,128)S(1)} %pad_maximum_fusion.even_ref.refs_4_), channel_id=1, source_target_pairs={{0,4},{4,0},{8,12},{12,8},{16,20},{20,16},{24,28},{28,24},{1,5},{5... | collective-permute-start | bytes 3735560 | tf_op jit(solution)/shard_map/ppermute | solution.py:421
  120.7 1.4 copy-start.3
  122.0 60.0 %collective-permute-start.14 = (f32[4000,128]{1,0:T(8,128)}, f32[4000,128]{1,0:T(8,128)S(1)}, u32[]{:S(2)}, u32[]{:S(2)}) collective-permute-start(f32[4000,128]{1,0:T(8,128)} %get-tuple-element.29.refs_4_.refs_1_), channel_id=1, source_target_pairs={{2,3},{6,7},{10,11},{14,15},{18,19},{22,23},{26,27},{30,31}} | collective-permute-start | bytes 6144008 | tf_op jit(solution)/shard_map/ppermute | solution.py:400
  123.0 62.4 %collective-permute-start.13 = (f32[4000,128]{1,0:T(8,128)}, f32[4000,128]{1,0:T(8,128)}, u32[]{:S(2)}, u32[]{:S(2)}) collective-permute-start(f32[4000,128]{1,0:T(8,128)} %get-tuple-element.24.refs_0_.refs_3_), channel_id=1, source_target_pairs={{1,0},{5,4},{9,8},{13,12},{17,16},{21,20},{25,24},{29,28}} | collective-permute-start | bytes 6144008 | tf_op jit(solution)/shard_map/ppermute | solution.py:400
  168.9 7.5 %copy-start.6 = (f32[4,256,256]{2,1,0:T(8,128)S(1)}, f32[4,256,256]{2,1,0:T(8,128)}, u32[]{:S(2)}) copy-start(f32[4,256,256]{2,1,0:T(8,128)} %get-tuple-element.30.after_ref) | copy-start | bytes 3145732
  168.9 7.5 %collective-permute-start.12 = (f32[4,256,256]{2,1,0:T(8,128)}, f32[4,256,256]{2,1,0:T(8,128)}, u32[]{:S(2)}, u32[]{:S(2)}) collective-permute-start(f32[4,256,256]{2,1,0:T(8,128)} %get-tuple-element.31), channel_id=1, source_target_pairs={{0,4},{4,0},{8,12},{12,8},{16,20},{20,16},{24,28},{28,24},{1,5},{5... | collective-permute-start | bytes 3145736 | tf_op jit(solution)/shard_map/ppermute | solution.py:421
  170.9 11.0 %copy-start.12 = (f32[128,256]{1,0:T(8,128)S(1)}, f32[128,256]{1,0:T(8,128)}, u32[]{:S(2)}) copy-start(f32[128,256]{1,0:T(8,128)} %own_columns.1.refs_2_.refs_0_) | copy-start | bytes 393220
  170.9 10.5 %collective-permute-start.17 = (f32[128,256]{1,0:T(8,128)}, f32[128,256]{1,0:T(8,128)S(1)}, u32[]{:S(2)}, u32[]{:S(2)}) collective-permute-start(f32[128,256]{1,0:T(8,128)} %own_columns.1.refs_2_.refs_0_), channel_id=1, source_target_pairs={{0,3},{1,0},{2,1},{3,2},{4,7},{5,4},{6,5},{7,6},{8,11},{9,8},{10,9... | collective-permute-start | bytes 393224 | tf_op jit(solution)/shard_map/ppermute | solution.py:484
  178.5 28.9 %collective-permute-start.21 = (f32[256,256]{1,0:T(8,128)S(1)}, f32[256,256]{1,0:T(8,128)}, u32[]{:S(2)}, u32[]{:S(2)}) collective-permute-start(f32[256,256]{1,0:T(8,128)S(1)} %get-tuple-element.37), channel_id=1, source_target_pairs={{0,24},{4,28},{8,16},{12,20},{16,8},{20,12},{24,0},{28,4},{1,25},{... | collective-permute-start | bytes 786440 | tf_op jit(solution)/shard_map/ppermute | solution.py:421
  180.9 26.5 %collective-permute-start.20 = (f32[256,256]{1,0:T(8,128)S(1)}, f32[256,256]{1,0:T(8,128)}, u32[]{:S(2)}, u32[]{:S(2)}) collective-permute-start(f32[256,256]{1,0:T(8,128)S(1)} %get-tuple-element.38), channel_id=1, source_target_pairs={{0,16},{4,20},{8,24},{12,28},{16,0},{20,4},{24,8},{28,12},{1,17},{... | collective-permute-start | bytes 786440 | tf_op jit(solution)/shard_map/ppermute | solution.py:421
  181.4 3.9 %copy-start.16 = (f32[128,256]{1,0:T(8,128)}, f32[128,256]{1,0:T(8,128)S(1)}, u32[]{:S(2)}) copy-start(f32[128,256]{1,0:T(8,128)S(1)} %collective-permute-done.17.refs_3_) | copy-start | bytes 393220
  181.4 25.9 %collective-permute-start.19 = (f32[256,256]{1,0:T(8,128)S(1)}, f32[256,256]{1,0:T(8,128)}, u32[]{:S(2)}, u32[]{:S(2)}) collective-permute-start(f32[256,256]{1,0:T(8,128)S(1)} %get-tuple-element.39), channel_id=1, source_target_pairs={{0,8},{4,12},{8,0},{12,4},{16,24},{20,28},{24,16},{28,20},{1,9},{5... | collective-permute-start | bytes 786440 | tf_op jit(solution)/shard_map/ppermute | solution.py:421
  182.0 5.7 %copy-start.8 = (f32[4000,128]{1,0:T(8,128)}, f32[4000,128]{1,0:T(8,128)S(1)}, u32[]{:S(2)}) copy-start(f32[4000,128]{1,0:T(8,128)S(1)} %collective-permute-done.14.refs_3_) | copy-start | bytes 6144004
  182.0 24.7 %collective-permute-start.16 = (f32[128,256]{1,0:T(8,128)S(1)}, f32[128,256]{1,0:T(8,128)S(1)}, u32[]{:S(2)}, u32[]{:S(2)}) collective-permute-start(f32[128,256]{1,0:T(8,128)S(1)} %copy-done.12), channel_id=1, source_target_pairs={{0,2},{1,3},{2,0},{3,1},{4,6},{5,7},{6,4},{7,5},{8,10},{9,11},{10,... | collective-permute-start | bytes 393224 | tf_op jit(solution)/shard_map/ppermute | solution.py:484
  185.4 21.3 %collective-permute-start.15 = (f32[128,256]{1,0:T(8,128)S(1)}, f32[128,256]{1,0:T(8,128)S(1)}, u32[]{:S(2)}, u32[]{:S(2)}) collective-permute-start(f32[128,256]{1,0:T(8,128)S(1)} %copy-done.12), channel_id=1, source_target_pairs={{0,1},{1,2},{2,3},{3,0},{4,5},{5,6},{6,7},{7,4},{8,9},{9,10},{10,1... | collective-permute-start | bytes 393224 | tf_op jit(solution)/shard_map/ppermute | solution.py:484
  206.6 0.7 copy-start.17
  206.7 0.7 copy-start.18
  207.3 2.9 %copy-start.11 = (f32[4,128,256]{2,1,0:T(8,128)S(1)}, f32[4,128,256]{2,1,0:T(8,128)}, u32[]{:S(2)}) copy-start(f32[4,128,256]{2,1,0:T(8,128)} %get-tuple-element.32) | copy-start | bytes 1572868
  207.3 2.1 collective-permute-start.18
  209.5 0.8 copy-start.7
  212.1 8.2 %collective-permute-start.24 = (f32[128,256]{1,0:T(8,128)S(1)}, f32[128,256]{1,0:T(8,128)S(1)}, u32[]{:S(2)}, u32[]{:S(2)}) collective-permute-start(f32[128,256]{1,0:T(8,128)S(1)} %get-tuple-element.41), channel_id=1, source_target_pairs={{0,24},{4,28},{8,16},{12,20},{16,8},{20,12},{24,0},{28,4},{1,25},{... | collective-permute-start | bytes 393224 | tf_op jit(solution)/shard_map/ppermute | solution.py:421
  213.6 8.0 %collective-permute-start.23 = (f32[128,256]{1,0:T(8,128)S(1)}, f32[128,256]{1,0:T(8,128)S(1)}, u32[]{:S(2)}, u32[]{:S(2)}) collective-permute-start(f32[128,256]{1,0:T(8,128)S(1)} %get-tuple-element.42), channel_id=1, source_target_pairs={{0,16},{4,20},{8,24},{12,28},{16,0},{20,4},{24,8},{28,12},{1,17},{... | collective-permute-start | bytes 393224 | tf_op jit(solution)/shard_map/ppermute | solution.py:421
  214.1 7.5 %collective-permute-start.22 = (f32[128,256]{1,0:T(8,128)S(1)}, f32[128,256]{1,0:T(8,128)S(1)}, u32[]{:S(2)}, u32[]{:S(2)}) collective-permute-start(f32[128,256]{1,0:T(8,128)S(1)} %get-tuple-element.43), channel_id=1, source_target_pairs={{0,8},{4,12},{8,0},{12,4},{16,24},{20,28},{24,16},{28,20},{1,9},{5... | collective-permute-start | bytes 393224 | tf_op jit(solution)/shard_map/ppermute | solution.py:421
  215.6 10.2 %copy-start.1 = (f32[256,256]{1,0:T(8,128)S(1)}, f32[256,256]{1,0:T(8,128)}, u32[]{:S(2)}) copy-start(f32[256,256]{1,0:T(8,128)} %param.6) | copy-start | bytes 786436
  220.3 1.3 copy-start.13
  221.5 0.6 copy-start.14
  222.2 0.7 copy-start.15
Sparse Core Ops, SparseCore 0:
  103.9 47.6 reduce-scatter.1

commit v9 on v8

--- a/solution.py
+++ b/solution.py
@@ -287,25 +287,7 @@
     )(me, *c, after)
 
 
-def total_kernel(*refs):
-    refs[-1][...] = functools.reduce(jnp.add, [ref[...] for ref in refs[:-1]])
-
-
-def total(terms):
-    shape = terms[0].shape
-    return pl.pallas_call(
-        total_kernel,
-        grid=(1,),
-        in_specs=[pl.BlockSpec(shape, lambda j: (0, 0))] * len(terms),
-        out_specs=pl.BlockSpec(shape, lambda j: (0, 0)),
-        out_shape=jax.ShapeDtypeStruct(shape, F32),
-        compiler_params=params(),
-        cost_estimate=LONG,
-        name="total",
-    )(*terms)
-
-
-def base_kernel(n, each, ride, at_ref, ready_ref, c_ref, middle_ref, *refs):
+def base_kernel(n, each, ride, at_ref, ready_ref, c_ref, *refs):
     *refs, out_ref, coef_ref, small_ref = refs
     me, z = at_ref[0], at_ref[1]
     nb = c_ref.shape[0]
@@ -323,17 +305,11 @@
         small_ref[...] = refs[n][...]
     corrected = ready_ref[...] - three(split(small_ref[...]), split(c_ref[...]))
     out_ref[...] = -three(split(coef_ref[...]), split(corrected[:nb]))
-    middle = middle_ref[...]
-    pieces = [corrected[nb:]] + [
-        middle[first : first + each] for first in range(0, middle.shape[0], each)
-    ]
-    for slot, piece in enumerate(pieces):
-        first = pl.multiple_of(at_ref[1 + slot] * each, each)
-        out_ref[pl.ds(first, each), :] += piece
-
-
-def base(at, ready, c, middle, coef, small, n, each, ride):
-    operands = [ready, c, middle, *coef, *small]
+    out_ref[pl.ds(pl.multiple_of(z * each, each), each), :] += corrected[nb:]
+
+
+def base(at, ready, c, coef, small, n, each, ride):
+    operands = [ready, c, *coef, *small]
     k, per = ready.shape
     nb = c.shape[0]
     return pl.pallas_call(
@@ -356,8 +332,9 @@
     *refs, out_ref, total_ref = refs
     total_ref[...] = base_ref[...]
     total = functools.reduce(jnp.add, [ref[...] for ref in refs])
-    first = pl.multiple_of(at_ref[at_ref.shape[0] - 1] * each, each)
-    total_ref[pl.ds(first, each), :] += total
+    for slot in range(total.shape[0] // each):
+        first = pl.multiple_of(at_ref[2 + slot] * each, each)
+        total_ref[pl.ds(first, each), :] += total[slot * each : (slot + 1) * each]
     out_ref[...] = total_ref[...].T
 
 
@@ -421,11 +398,13 @@
     return lax.ppermute(x, "wide", [(i, i ^ distance) for i in range(wide)])
 
 
-def scatter_terms(even, odd, wide, after=None):
-    other = swap(odd, wide, 1)
-    if after is not None:
-        (other,) = gate([other], after)
-    sums = [even[h] + other[h] for h in range(wide // 2)]
+def scatter_terms(halves, wide, after):
+    others = [swap(odd, wide, 1) for _, odd in halves]
+    others[-1:] = gate(others[-1:], after)
+    sums = [
+        [even[h] + other[h] for (even, _), other in zip(halves, others)] for h in range(wide // 2)
+    ]
+    sums = [x[0] if len(x) == 1 else jnp.concatenate(x, axis=0) for x in sums]
     return [sums[0]] + [swap(sums[h], wide, 2 * h) for h in range(1, wide // 2)]
 
 
@@ -461,7 +440,7 @@
         held = travel(came, held, n, 2, [small])
     ready = lax.psum_scatter(sums, "wide", scatter_dimension=0)
 
-    projected = functools.reduce(jnp.add, scatter_terms(even, odd, wide, came[(1, 0)]))
+    projected = functools.reduce(jnp.add, scatter_terms([(even, odd)], wide, came[(1, 0)]))
     highest = lax.Precision.HIGHEST
     coefficients = jnp.dot(triangle, projected[:nb], precision=highest)
     payload = coefficients
@@ -478,20 +457,17 @@
     )
 
     slots = [options(came, places, z) for places in table]
-    even, odd = late(me, updated, slots[:-1], token, wide)
-    mine = own_columns(me, c, even, nb, each)
+    halves = [late(me, updated, slots[:-1], token, wide)]
+    (ready,) = gate([ready], halves[0][0])
+    halves.append(late(me, updated, slots[-1:], ready, wide))
+    mine = own_columns(me, c, halves[1][0], nb, each)
     coef = [mine] + [
         lax.ppermute(mine, "narrow", [(p, (p + s) % n) for p in range(n)]) for s in range(1, n)
     ]
-    middle = scatter_terms(even, odd, wide)
-    (ready,) = gate([ready], middle[0], mine)
-    even, odd = late(me, updated, slots[-1:], ready, wide)
-    middle = total(middle)
-    (odd,) = gate([odd], *coef[1:])
-    tail = scatter_terms(even, odd, wide, middle)
+    tail = scatter_terms(halves, wide, mine)
     (ready,) = gate([ready], tail[0])
     small = c if ride else [lax.psum(small, "wide")]
-    base_block = base(at, ready, coefficients, middle, coef, small, n, each, ride)
+    base_block = base(at, ready, coefficients, coef, small, n, each, ride)
     return (updated, last(at, base_block, tail, each))
 
 

time: 233 us -> 238 us (1.021)
  waiting for transfers between devices: 32.2 us -> 42.6 us
  starting transfers between devices: 37.3 us -> 33.1 us
    ppermute x16 -> x13, waiting for transfers between devices: 28.1 us -> 33.2 us  [swap(): return lax.ppermute(x, 'wide', [(i, i ^ distance) for i in range(wide)])]
    ppermute x3, waiting for transfers between devices: 0.01 us -> 3.86 us  [on_device(): lax.ppermute(mine, 'narrow', [(p, (p + s) % n) for p in range(n)])]
    ppermute x16 -> x13, starting transfers between devices: 14.2 us -> 11.2 us  [swap(): return lax.ppermute(x, 'wide', [(i, i ^ distance) for i in range(wide)])]
  transfers between devices with their start and end apart: 26 -> 23, of which waited for: 13 -> 13; matrix products, arithmetic and copies ran while one was open for 2% -> 3% of each run, Pallas kernels for 55% -> 53%
where the time goes in v9:
time: 238 us; the launch traced here: 237 us
  Pallas kernels  129 us (54%)
  waiting for transfers between devices  42.6 us (18%)
  starting transfers between devices  33.1 us (14%)
  between operations  14.3 us (6%)
  other arithmetic  9.82 us (4%)
  local copies, waits for them, and re-layouts  7.92 us (3%)
    pallas_call x1, Pallas kernels, project(): pl.pallas_call(functools.partial(project_kernel, per, wide), grid_spec=pl...  43.9 us
    pallas_call x2, Pallas kernels, late(): pl.pallas_call(functools.partial(late_kernel, per, counts), grid_spec=plt...  42.2 us
    ppermute x13, waiting for transfers between devices, swap(): return lax.ppermute(x, 'wide', [(i, i ^ distance) for i in range(wide)])  33.2 us
    pallas_call x2, Pallas kernels, update(): pl.pallas_call(update_kernel, grid_spec=pltpu.PrefetchScalarGridSpec(num_...  33.1 us
    ppermute x6, starting transfers between devices, travel(): held = [lax.ppermute(held[d], 'narrow', pairs[d]) for d in (0, 1)]  13 us
    ppermute x13, starting transfers between devices, swap(): return lax.ppermute(x, 'wide', [(i, i ^ distance) for i in range(wide)])  11.2 us
    ppermute x3, starting transfers between devices, on_device(): lax.ppermute(mine, 'narrow', [(p, (p + s) % n) for p in range(n)])  8.8 us
    unnamed x38, local copies, waits for them, and re-layouts  7.3 us
  transfers between devices with their start and end apart: 23, of which 13 were waited for; matrix products, arithmetic and copies ran while one was open for 3% of the time, Pallas kernels for 53%

profile of v9, /device:TPU:0, one launch (start us, length us, event | category | flops | bytes accessed | tf_op | source)
XLA Modules:
  0.0 237.3 jit_solution(15907969481613664199)
XLA Ops:
  7.2 2.7 %slice_multiply_fusion.x_ref = f32[4000,128]{1,0:T(8,128)S(1)} fusion(f32[4000,2048]{1,0:T(8,128)} %v_ref.5, f32[4000]{0:T(1024)} %param.7), kind=kLoop, calls=%fused_computation | loop fusion | flops 512000 | bytes 4112000 | tf_op jit(solution)/shard_map/mul | solution.py:431
  10.0 6.2 %collective-permute-start.2 = (f32[4000,128]{1,0:T(8,128)S(1)}, f32[4000,128]{1,0:T(8,128)}, u32[]{:S(2)}, u32[]{:S(2)}) collective-permute-start(f32[4000,128]{1,0:T(8,128)S(1)} %slice_multiply_fusion.x_ref), channel_id=1, source_target_pairs={{0,1},{1,2},{2,3},{4,5},{5,6},{6,7},{8,9},{9,10},{10,11},{12,13},{... | collective-permute-start | bytes 6144008 | tf_op jit(solution)/shard_map/ppermute | solution.py:377
  16.2 1.3 collective-permute-start.1
  17.5 43.9 %project.1 = (f32[4,304,256]{2,1,0:T(8,128)}, f32[4,304,256]{2,1,0:T(8,128)}, f32[8,384,256]{2,1,0:T(8,128)}, f32[384,256]{1,0:T(8,128)}) custom-call(s32[1]{0:T(128)} %bitcast.me_ref, f32[4000,2048]{1,0:T(8,128)} %v_ref.5, f32[4000,256]{1,0:T(8,128)} %r_ref.5, f32[1,4000]{1,0:T(1,128)} %bitcast.52, f32[4000,128]{1,0:T(8,128)} %copy-done.4), custom_call_target="tpu_custom_call" | custom-call | flops 1024 | bytes 1024 | tf_op jit(solution)/shard_map/project/pallas_call | solution.py:132
  61.5 2.8 %collective-permute-done.1.refs_0_ = f32[4000,128]{1,0:T(8,128)} collective-permute-done((f32[4000,128]{1,0:T(8,128)S(1)}, f32[4000,128]{1,0:T(8,128)}, u32[]{:S(2)}, u32[]{:S(2)}) %collective-permute-start.1) | collective-permute-done | bytes 2048032 | tf_op jit(solution)/shard_map/ppermute | solution.py:377
  64.6 1.0 copy-done.5
  65.7 1.3 copy-done.10
  67.0 1.3 fusion.2
  68.2 1.6 collective-permute-start.3
  69.8 1.5 collective-permute-start.5
  71.8 1.3 collective-permute-start.10
  73.1 2.0 collective-permute-start.11
  75.1 3.5 %collective-permute-done.3 = f32[304,256]{1,0:T(8,128)S(1)} collective-permute-done((f32[304,256]{1,0:T(8,128)S(1)}, f32[304,256]{1,0:T(8,128)S(1)}, u32[]{:S(2)}, u32[]{:S(2)}) %collective-permute-start.3) | collective-permute-done | bytes 311328 | tf_op jit(solution)/shard_map/ppermute | solution.py:398
  78.5 6.9 %collective-permute-done.5 = f32[304,256]{1,0:T(8,128)S(1)} collective-permute-done((f32[304,256]{1,0:T(8,128)S(1)}, f32[304,256]{1,0:T(8,128)S(1)}, u32[]{:S(2)}, u32[]{:S(2)}) %collective-permute-start.5) | collective-permute-done | bytes 311328 | tf_op jit(solution)/shard_map/ppermute | solution.py:398
  85.4 1.4 collective-permute-done.4
  86.8 1.2 fusion.6
  89.0 1.5 collective-permute-start.6
  90.5 1.5 collective-permute-start.8
  92.0 5.9 %collective-permute-done.7 = f32[304,256]{1,0:T(8,128)S(1)} collective-permute-done((f32[304,256]{1,0:T(8,128)S(1)}, f32[304,256]{1,0:T(8,128)S(1)}, u32[]{:S(2)}, u32[]{:S(2)}) %collective-permute-start.7) | collective-permute-done | bytes 311328 | tf_op jit(solution)/shard_map/ppermute | solution.py:398
  97.9 1.3 collective-permute-done.6
  99.2 4.3 %collective-permute-done.8 = f32[304,256]{1,0:T(8,128)S(1)} collective-permute-done((f32[304,256]{1,0:T(8,128)S(1)}, f32[304,256]{1,0:T(8,128)S(1)}, u32[]{:S(2)}, u32[]{:S(2)}) %collective-permute-start.8) | collective-permute-done | bytes 311328 | tf_op jit(solution)/shard_map/ppermute | solution.py:398
  103.8 3.0 %collective-permute-done.9.odd_ref.refs_5_ = f32[4,304,256]{2,1,0:T(8,128)} collective-permute-done((f32[4,304,256]{2,1,0:T(8,128)S(1)}, f32[4,304,256]{2,1,0:T(8,128)}, u32[]{:S(2)}, u32[]{:S(2)}) %collective-permute-start.9) | collective-permute-done | bytes 1245216 | tf_op jit(solution)/shard_map/ppermute | solution.py:398
  106.8 12.5 %update.2 = (f32[4000,2048]{1,0:T(8,128)}, f32[8,128]{1,0:T(8,128)}) custom-call(s32[1]{0:T(128)} %bitcast.me_ref, f32[4000,2048]{1,0:T(8,128)} %v_ref.5, f32[4000,256]{1,0:T(8,128)} %r_ref.5, f32[4,304,256]{2,1,0:T(8,128)} %copy-done.2, f32[4,304,256]{2,1,0:T(8,128)} %collective-permute-done.9.odd_ref.refs_5_), custom_call_target="tpu_custom_call" | custom-call | flops 1024 | bytes 1024 | tf_op jit(solution)/shard_map/update/pallas_call | solution.py:173
  119.3 1.3 collective-permute-done.10.refs_0_
  120.6 1.4 copy-done.3
  122.0 1.0 collective-permute-start.14
  122.9 1.3 collective-permute-start.13
  124.8 20.6 %update.3 = (f32[4000,2048]{1,0:T(8,128)}, f32[8,128]{1,0:T(8,128)}) custom-call(s32[1]{0:T(128)} %bitcast.me_ref, f32[4000,2048]{1,0:T(8,128)} %v_ref.5, f32[4000,256]{1,0:T(8,128)} %r_ref.5, f32[4,304,256]{2,1,0:T(8,128)} %copy-done.2, f32[4,304,256]{2,1,0:T(8,128)} %collective-permute-done.9.odd_ref.refs_5_, ...), custom_call_target="tpu_custom_call", output_to_operand_aliasing={{0}: (6, {})} | custom-call | flops 1024 | bytes 1024 | tf_op jit(solution)/shard_map/update/pallas_call | solution.py:173
  145.4 23.3 %late.2 = (f32[4,256,256]{2,1,0:T(8,128)}, f32[4,256,256]{2,1,0:T(8,128)}) custom-call(s32[3]{0:T(128)} %pad_add_fusion.at_ref, f32[4000,2048]{1,0:T(8,128)} %get-tuple-element.16.u_ref, f32[8,128]{1,0:T(8,128)} %get-tuple-element.28.after_ref, f32[4000,128]{1,0:T(8,128)} %get-tuple-element.21.refs_1_.refs_0_, ...), custom_call_target="tpu_custom_call" | custom-call | flops 1024 | bytes 1024 | tf_op jit(solution)/shard_map/late/pallas_call | solution.py:241
  169.5 1.5 collective-permute-done.13.refs_2_
  171.0 18.9 %late.3 = (f32[4,128,256]{2,1,0:T(8,128)}, f32[4,128,256]{2,1,0:T(8,128)}) custom-call(s32[2]{0:T(128)} %pad_add_fusion.1.at_ref, f32[4000,2048]{1,0:T(8,128)} %get-tuple-element.16.u_ref, f32[384,256]{1,0:T(8,128)} %gate.9.after_ref.refs_0_, f32[4000,128]{1,0:T(8,128)} %get-tuple-element.24.refs_0_.refs_3_, f32[4000,128]{1,0:T(8,128)} %get-tuple-element.29.refs_4_.refs_1_, ...), custom_call_target="tpu_custom_call" | custom-call | flops 1024 | bytes 1024 | tf_op jit(solution)/shard_map/late/pallas_call | solution.py:241
  190.8 1.3 fusion.7
  192.2 1.9 own_columns.1.refs_1_.refs_0_
  194.1 5.5 %collective-permute-start.18 = (f32[128,256]{1,0:T(8,128)}, f32[128,256]{1,0:T(8,128)S(1)}, u32[]{:S(2)}, u32[]{:S(2)}) collective-permute-start(f32[128,256]{1,0:T(8,128)} %own_columns.1.refs_1_.refs_0_), channel_id=1, source_target_pairs={{0,3},{1,0},{2,1},{3,2},{4,7},{5,4},{6,5},{7,6},{8,11},{9,8},{10,9... | collective-permute-start | bytes 393224 | tf_op jit(solution)/shard_map/ppermute | solution.py:465
  199.6 1.2 collective-permute-start.17
  200.9 0.8 copy-done.7
  201.7 1.2 fusion.12
  202.8 0.8 pad_maximum_fusion.1.refs_1_.refs_0_
  203.6 2.0 collective-permute-start.16
  205.6 1.6 collective-permute-start.19
  207.2 1.5 collective-permute-start.20
  209.4 3.9 %collective-permute-done.17.refs_2_ = f32[128,256]{1,0:T(8,128)S(1)} collective-permute-done((f32[128,256]{1,0:T(8,128)}, f32[128,256]{1,0:T(8,128)S(1)}, u32[]{:S(2)}, u32[]{:S(2)}) %collective-permute-start.17) | collective-permute-done | bytes 131104 | tf_op jit(solution)/shard_map/ppermute | solution.py:465
  213.9 0.7 copy-done.18
  214.6 4.6 %base.1.base_ref = f32[512,256]{1,0:T(8,128)} custom-call(s32[5]{0:T(128)} %stack.54.at_ref, f32[384,256]{1,0:T(8,128)} %gate.11.ready_ref, f32[256,256]{1,0:T(8,128)} %copy-done.11, f32[128,256]{1,0:T(8,128)} %own_columns.1.refs_1_.refs_0_, f32[128,256]{1,0:T(8,128)} %copy-done.18, f32[128,256]{1,0:T(8,128)} %copy-done.17, f32[128,256]{1,0:T(8,128)} %copy-done.16, ...), custom_call_target="tpu_custom_call" | custom-call | flops 99999997952 | bytes 1024 | tf_op jit(solution)/shard_map/base/pallas_call | solution.py:315
  219.2 6.5 %collective-permute-done.20.refs_2_ = f32[384,256]{1,0:T(8,128)S(1)} collective-permute-done((f32[384,256]{1,0:T(8,128)S(1)}, f32[384,256]{1,0:T(8,128)S(1)}, u32[]{:S(2)}, u32[]{:S(2)}) %collective-permute-start.20) | collective-permute-done | bytes 393248 | tf_op jit(solution)/shard_map/ppermute | solution.py:398
  225.7 0.7 copy-done.14
  226.4 0.7 copy-done.15
  227.2 3.3 %last.1 = f32[256,512]{1,0:T(8,128)} custom-call(s32[5]{0:T(128)} %stack.54.at_ref, f32[512,256]{1,0:T(8,128)} %base.1.base_ref, f32[384,256]{1,0:T(8,128)} %pad_maximum_fusion.1.refs_1_.refs_0_, f32[384,256]{1,0:T(8,128)} %copy-done.13, f32[384,256]{1,0:T(8,128)} %copy-done.14, f32[384,256]{1,0:T(8,128)} %copy-done.15), custom_call_target="tpu_custom_call" | custom-call | flops 1024 | bytes 1024 | tf_op jit(solution)/shard_map/last/pallas_call | solution.py:344
  (67 shorter events, 5.7 us)
Async XLA Ops:
  7.2 80.8 %copy-start = (f32[256,256]{1,0:T(8,128)S(1)}, f32[256,256]{1,0:T(8,128)}, u32[]{:S(2)}) copy-start(f32[256,256]{1,0:T(8,128)} %param.6) | copy-start | bytes 786436
  7.2 162.3 %reduce-scatter.2.cloned.1.call-start = ((), (), s32[]{:S(2)}) async-start(), calls=%async_computation.1 | async-start | bytes 3538944 | tf_op jit(solution)/shard_map/reduce_scatter | solution.py:441
  10.0 7.6 %copy-start.4 = (f32[4000,128]{1,0:T(8,128)}, f32[4000,128]{1,0:T(8,128)S(1)}, u32[]{:S(2)}) copy-start(f32[4000,128]{1,0:T(8,128)S(1)} %slice_multiply_fusion.x_ref) | copy-start | bytes 6144004
  10.0 51.5 %collective-permute-start.2 = (f32[4000,128]{1,0:T(8,128)S(1)}, f32[4000,128]{1,0:T(8,128)}, u32[]{:S(2)}, u32[]{:S(2)}) collective-permute-start(f32[4000,128]{1,0:T(8,128)S(1)} %slice_multiply_fusion.x_ref), channel_id=1, source_target_pairs={{0,1},{1,2},{2,3},{4,5},{5,6},{6,7},{8,9},{9,10},{10,11},{12,13},{... | collective-permute-start | bytes 6144008 | tf_op jit(solution)/shard_map/ppermute | solution.py:377
  16.2 48.0 %collective-permute-start.1 = (f32[4000,128]{1,0:T(8,128)S(1)}, f32[4000,128]{1,0:T(8,128)}, u32[]{:S(2)}, u32[]{:S(2)}) collective-permute-start(f32[4000,128]{1,0:T(8,128)S(1)} %slice_multiply_fusion.x_ref), channel_id=1, source_target_pairs={{1,0},{2,1},{3,2},{5,4},{6,5},{7,6},{9,8},{10,9},{11,10},{13,12},{... | collective-permute-start | bytes 6144008 | tf_op jit(solution)/shard_map/ppermute | solution.py:377
  61.5 3.2 %collective-permute-start = (f32[4,304,256]{2,1,0:T(8,128)}, f32[4,304,256]{2,1,0:T(8,128)S(1)}, u32[]{:S(2)}, u32[]{:S(2)}) collective-permute-start(f32[4,304,256]{2,1,0:T(8,128)} %get-tuple-element.19), channel_id=1, source_target_pairs={{0,4},{4,0},{8,12},{12,8},{16,20},{20,16},{24,28},{28,24},{1,5},{5... | collective-permute-start | bytes 3735560 | tf_op jit(solution)/shard_map/ppermute | solution.py:398
  64.6 1.0 copy-start.5
  65.7 1.3 copy-start.10
  68.2 10.3 %collective-permute-start.3 = (f32[304,256]{1,0:T(8,128)S(1)}, f32[304,256]{1,0:T(8,128)S(1)}, u32[]{:S(2)}, u32[]{:S(2)}) collective-permute-start(f32[304,256]{1,0:T(8,128)S(1)} %get-tuple-element.34), channel_id=1, source_target_pairs={{0,8},{4,12},{8,0},{12,4},{16,24},{20,28},{24,16},{28,20},{1,9},{5... | collective-permute-start | bytes 933896 | tf_op jit(solution)/shard_map/ppermute | solution.py:398
  69.8 15.6 %collective-permute-start.5 = (f32[304,256]{1,0:T(8,128)S(1)}, f32[304,256]{1,0:T(8,128)S(1)}, u32[]{:S(2)}, u32[]{:S(2)}) collective-permute-start(f32[304,256]{1,0:T(8,128)S(1)} %get-tuple-element.35), channel_id=1, source_target_pairs={{0,24},{4,28},{8,16},{12,20},{16,8},{20,12},{24,0},{28,4},{1,25},{... | collective-permute-start | bytes 933896 | tf_op jit(solution)/shard_map/ppermute | solution.py:398
  71.3 15.5 %collective-permute-start.4 = (f32[304,256]{1,0:T(8,128)S(1)}, f32[304,256]{1,0:T(8,128)S(1)}, u32[]{:S(2)}, u32[]{:S(2)}) collective-permute-start(f32[304,256]{1,0:T(8,128)S(1)} %get-tuple-element.36), channel_id=1, source_target_pairs={{0,16},{4,20},{8,24},{12,28},{16,0},{20,4},{24,8},{28,12},{1,17},{... | collective-permute-start | bytes 933896 | tf_op jit(solution)/shard_map/ppermute | solution.py:398
  71.8 48.8 %collective-permute-start.10 = (f32[4000,128]{1,0:T(8,128)}, f32[4000,128]{1,0:T(8,128)S(1)}, u32[]{:S(2)}, u32[]{:S(2)}) collective-permute-start(f32[4000,128]{1,0:T(8,128)} %get-tuple-element.21.refs_1_.refs_0_), channel_id=1, source_target_pairs={{1,0},{2,1},{5,4},{6,5},{9,8},{10,9},{13,12},{14,13},{17,16},{18,1... | collective-permute-start | bytes 6144008 | tf_op jit(solution)/shard_map/ppermute | solution.py:377
  73.1 46.2 %collective-permute-start.11 = (f32[4000,128]{1,0:T(8,128)}, f32[4000,128]{1,0:T(8,128)}, u32[]{:S(2)}, u32[]{:S(2)}) collective-permute-start(f32[4000,128]{1,0:T(8,128)} %get-tuple-element.22.refs_1_.refs_2_), channel_id=1, source_target_pairs={{1,2},{2,3},{5,6},{6,7},{9,10},{10,11},{13,14},{14,15},{17,18},{18... | collective-permute-start | bytes 6144008 | tf_op jit(solution)/shard_map/ppermute | solution.py:377
  88.4 15.1 %copy-start.11 = (f32[256,256]{1,0:T(8,128)}, f32[256,256]{1,0:T(8,128)S(1)}, u32[]{:S(2)}) copy-start(f32[256,256]{1,0:T(8,128)S(1)} %convolution_bitcast_fusion.c_ref) | copy-start | bytes 786436
  88.5 9.5 %collective-permute-start.7 = (f32[304,256]{1,0:T(8,128)S(1)}, f32[304,256]{1,0:T(8,128)S(1)}, u32[]{:S(2)}, u32[]{:S(2)}) collective-permute-start(f32[304,256]{1,0:T(8,128)S(1)} %get-tuple-element.46), channel_id=1, source_target_pairs={{0,16},{4,20},{8,24},{12,28},{16,0},{20,4},{24,8},{28,12},{1,17},{... | collective-permute-start | bytes 933896 | tf_op jit(solution)/shard_map/ppermute | solution.py:398
  89.0 10.2 %collective-permute-start.6 = (f32[304,256]{1,0:T(8,128)S(1)}, f32[304,256]{1,0:T(8,128)S(1)}, u32[]{:S(2)}, u32[]{:S(2)}) collective-permute-start(f32[304,256]{1,0:T(8,128)S(1)} %get-tuple-element.46), channel_id=1, source_target_pairs={{0,8},{4,12},{8,0},{12,4},{16,24},{20,28},{24,16},{28,20},{1,9},{5... | collective-permute-start | bytes 933896 | tf_op jit(solution)/shard_map/ppermute | solution.py:398
  90.5 13.0 %collective-permute-start.8 = (f32[304,256]{1,0:T(8,128)S(1)}, f32[304,256]{1,0:T(8,128)S(1)}, u32[]{:S(2)}, u32[]{:S(2)}) collective-permute-start(f32[304,256]{1,0:T(8,128)S(1)} %get-tuple-element.46), channel_id=1, source_target_pairs={{0,24},{4,28},{8,16},{12,20},{16,8},{20,12},{24,0},{28,4},{1,25},{... | collective-permute-start | bytes 933896 | tf_op jit(solution)/shard_map/ppermute | solution.py:398
  103.7 3.2 %copy-start.2 = (f32[4,304,256]{2,1,0:T(8,128)}, f32[4,304,256]{2,1,0:T(8,128)S(1)}, u32[]{:S(2)}) copy-start(f32[4,304,256]{2,1,0:T(8,128)S(1)} %pad_maximum_fusion.even_ref.refs_4_) | copy-start | bytes 3735556
  103.7 3.1 %collective-permute-start.9 = (f32[4,304,256]{2,1,0:T(8,128)S(1)}, f32[4,304,256]{2,1,0:T(8,128)}, u32[]{:S(2)}, u32[]{:S(2)}) collective-permute-start(f32[4,304,256]{2,1,0:T(8,128)S(1)} %pad_maximum_fusion.even_ref.refs_4_), channel_id=1, source_target_pairs={{0,4},{4,0},{8,12},{12,8},{16,20},{20,16},{24,28},{28,24},{1,5},{5... | collective-permute-start | bytes 3735560 | tf_op jit(solution)/shard_map/ppermute | solution.py:398
  120.6 1.4 copy-start.3
  122.0 47.5 %collective-permute-start.14 = (f32[4000,128]{1,0:T(8,128)}, f32[4000,128]{1,0:T(8,128)S(1)}, u32[]{:S(2)}, u32[]{:S(2)}) collective-permute-start(f32[4000,128]{1,0:T(8,128)} %get-tuple-element.29.refs_4_.refs_1_), channel_id=1, source_target_pairs={{2,3},{6,7},{10,11},{14,15},{18,19},{22,23},{26,27},{30,31}} | collective-permute-start | bytes 6144008 | tf_op jit(solution)/shard_map/ppermute | solution.py:377
  122.9 48.1 %collective-permute-start.13 = (f32[4000,128]{1,0:T(8,128)}, f32[4000,128]{1,0:T(8,128)}, u32[]{:S(2)}, u32[]{:S(2)}) collective-permute-start(f32[4000,128]{1,0:T(8,128)} %get-tuple-element.24.refs_0_.refs_3_), channel_id=1, source_target_pairs={{1,0},{5,4},{9,8},{13,12},{17,16},{21,20},{25,24},{29,28}} | collective-permute-start | bytes 6144008 | tf_op jit(solution)/shard_map/ppermute | solution.py:377
  168.8 22.1 %collective-permute-start.12 = (f32[4,256,256]{2,1,0:T(8,128)}, f32[4,256,256]{2,1,0:T(8,128)}, u32[]{:S(2)}, u32[]{:S(2)}) collective-permute-start(f32[4,256,256]{2,1,0:T(8,128)} %get-tuple-element.31), channel_id=1, source_target_pairs={{0,4},{4,0},{8,12},{12,8},{16,20},{20,16},{24,28},{28,24},{1,5},{5... | collective-permute-start | bytes 3145736 | tf_op jit(solution)/shard_map/ppermute | solution.py:398
  169.5 21.4 %copy-start.6 = (f32[4,256,256]{2,1,0:T(8,128)S(1)}, f32[4,256,256]{2,1,0:T(8,128)}, u32[]{:S(2)}) copy-start(f32[4,256,256]{2,1,0:T(8,128)} %get-tuple-element.30.refs_1_) | copy-start | bytes 3145732
  169.5 1.5 copy-start.9
  189.9 10.9 %collective-permute-start.15 = (f32[4,128,256]{2,1,0:T(8,128)}, f32[4,128,256]{2,1,0:T(8,128)S(1)}, u32[]{:S(2)}, u32[]{:S(2)}) collective-permute-start(f32[4,128,256]{2,1,0:T(8,128)} %get-tuple-element.33), channel_id=1, source_target_pairs={{0,4},{4,0},{8,12},{12,8},{16,20},{20,16},{24,28},{28,24},{1,5},{5... | collective-permute-start | bytes 1572872 | tf_op jit(solution)/shard_map/ppermute | solution.py:398
  192.2 9.5 %copy-start.8 = (f32[4,128,256]{2,1,0:T(8,128)S(1)}, f32[4,128,256]{2,1,0:T(8,128)}, u32[]{:S(2)}) copy-start(f32[4,128,256]{2,1,0:T(8,128)} %get-tuple-element.32.after_ref) | copy-start | bytes 1572868
  194.1 9.5 %copy-start.12 = (f32[128,256]{1,0:T(8,128)S(1)}, f32[128,256]{1,0:T(8,128)}, u32[]{:S(2)}) copy-start(f32[128,256]{1,0:T(8,128)} %own_columns.1.refs_1_.refs_0_) | copy-start | bytes 393220
  194.1 14.7 %collective-permute-start.18 = (f32[128,256]{1,0:T(8,128)}, f32[128,256]{1,0:T(8,128)S(1)}, u32[]{:S(2)}, u32[]{:S(2)}) collective-permute-start(f32[128,256]{1,0:T(8,128)} %own_columns.1.refs_1_.refs_0_), channel_id=1, source_target_pairs={{0,3},{1,0},{2,1},{3,2},{4,7},{5,4},{6,5},{7,6},{8,11},{9,8},{10,9... | collective-permute-start | bytes 393224 | tf_op jit(solution)/shard_map/ppermute | solution.py:465
  199.6 13.6 %collective-permute-start.17 = (f32[128,256]{1,0:T(8,128)}, f32[128,256]{1,0:T(8,128)S(1)}, u32[]{:S(2)}, u32[]{:S(2)}) collective-permute-start(f32[128,256]{1,0:T(8,128)} %own_columns.1.refs_1_.refs_0_), channel_id=1, source_target_pairs={{0,2},{1,3},{2,0},{3,1},{4,6},{5,7},{6,4},{7,5},{8,10},{9,11},{10,... | collective-permute-start | bytes 393224 | tf_op jit(solution)/shard_map/ppermute | solution.py:465
  200.9 0.8 copy-start.7
  203.6 9.7 %collective-permute-start.16 = (f32[128,256]{1,0:T(8,128)S(1)}, f32[128,256]{1,0:T(8,128)S(1)}, u32[]{:S(2)}, u32[]{:S(2)}) collective-permute-start(f32[128,256]{1,0:T(8,128)S(1)} %copy-done.12), channel_id=1, source_target_pairs={{0,1},{1,2},{2,3},{3,0},{4,5},{5,6},{6,7},{7,4},{8,9},{9,10},{10,1... | collective-permute-start | bytes 393224 | tf_op jit(solution)/shard_map/ppermute | solution.py:465
  205.6 13.5 %collective-permute-start.19 = (f32[384,256]{1,0:T(8,128)S(1)}, f32[384,256]{1,0:T(8,128)S(1)}, u32[]{:S(2)}, u32[]{:S(2)}) collective-permute-start(f32[384,256]{1,0:T(8,128)S(1)} %pad_maximum_fusion.2), channel_id=1, source_target_pairs={{0,8},{4,12},{8,0},{12,4},{16,24},{20,28},{24,16},{28,20},{1,9},{5... | collective-permute-start | bytes 1179656 | tf_op jit(solution)/shard_map/ppermute | solution.py:398
  207.2 18.4 %collective-permute-start.20 = (f32[384,256]{1,0:T(8,128)S(1)}, f32[384,256]{1,0:T(8,128)S(1)}, u32[]{:S(2)}, u32[]{:S(2)}) collective-permute-start(f32[384,256]{1,0:T(8,128)S(1)} %pad_maximum_fusion.3), channel_id=1, source_target_pairs={{0,16},{4,20},{8,24},{12,28},{16,0},{20,4},{24,8},{28,12},{1,17},{... | collective-permute-start | bytes 1179656 | tf_op jit(solution)/shard_map/ppermute | solution.py:398
  208.8 4.5 %copy-start.16 = (f32[128,256]{1,0:T(8,128)}, f32[128,256]{1,0:T(8,128)S(1)}, u32[]{:S(2)}) copy-start(f32[128,256]{1,0:T(8,128)S(1)} %collective-permute-done.18.refs_3_) | copy-start | bytes 393220
  208.8 16.9 %collective-permute-start.21 = (f32[384,256]{1,0:T(8,128)S(1)}, f32[384,256]{1,0:T(8,128)S(1)}, u32[]{:S(2)}, u32[]{:S(2)}) collective-permute-start(f32[384,256]{1,0:T(8,128)S(1)} %pad_maximum_fusion.4), channel_id=1, source_target_pairs={{0,24},{4,28},{8,16},{12,20},{16,8},{20,12},{24,0},{28,4},{1,25},{... | collective-permute-start | bytes 1179656 | tf_op jit(solution)/shard_map/ppermute | solution.py:398
  213.3 0.6 copy-start.17
  213.9 0.7 copy-start.18
  214.6 15.9 %copy-start.1 = (f32[256,256]{1,0:T(8,128)S(1)}, f32[256,256]{1,0:T(8,128)}, u32[]{:S(2)}) copy-start(f32[256,256]{1,0:T(8,128)} %param.6) | copy-start | bytes 786436
  219.2 6.5 %copy-start.13 = (f32[384,256]{1,0:T(8,128)}, f32[384,256]{1,0:T(8,128)S(1)}, u32[]{:S(2)}) copy-start(f32[384,256]{1,0:T(8,128)S(1)} %collective-permute-done.19.refs_1_) | copy-start | bytes 1179652
  225.7 0.7 copy-start.14
  226.4 0.7 copy-start.15
Sparse Core Ops, SparseCore 0:
  103.9 47.7 reduce-scatter.1

commit v10 on v9

--- a/solution.py
+++ b/solution.py
@@ -199,7 +199,8 @@
 
 
 def late_kernel(per, counts, at_ref, u_ref, after_ref, *refs):
-    *refs, even_out, odd_out, both_ref, block_ref, sem_ref = refs
+    *refs, both_ref, block_ref, sem_ref = refs
+    outs = refs[sum(counts) :]
     j = pl.program_id(0)
     m = both_ref.shape[0] // 2
     each = block_ref.shape[2]
@@ -224,11 +225,14 @@
     value = stacked(both_ref[...], both_ref[:m], split(u_ref[...]))
     count = u_ref.shape[1] // per
     for g in range(count):
-        index = (j * count + g) ^ at_ref[0]
-        place(value[:, g * per : (g + 1) * per], index, even_out, odd_out, 0)
-
-
-def late(me, updated, slots, after, wide):
+        part = value[:, g * per : (g + 1) * per]
+        if len(outs) == 2:
+            place(part, (j * count + g) ^ at_ref[0], *outs, 0)
+        else:
+            outs[0][g] = part
+
+
+def late(me, updated, slots, after, wide, ordered):
     rows, columns = updated.shape
     per = columns // wide
     step = width(columns, wide)
@@ -237,21 +241,26 @@
     each = flat[0].shape[1]
     m = each * len(slots)
     at = jnp.stack([me[0]] + [which.astype(jnp.int32) for _, which in slots])
-    half = jax.ShapeDtypeStruct((wide // 2, m, per), F32)
+    if ordered:
+        shapes = [(wide, m, per)]
+        specs = [pl.BlockSpec((step // per, m, per), lambda j, *_: (j, 0, 0))]
+    else:
+        shapes = [(wide // 2, m, per)] * 2
+        specs = [whole(x) for x in shapes]
     return pl.pallas_call(
         functools.partial(late_kernel, per, counts),
         grid_spec=pltpu.PrefetchScalarGridSpec(
             num_scalar_prefetch=1,
             grid=(columns // step,),
             in_specs=[pl.BlockSpec((rows, step), lambda j, *_: (0, j))] + [ANY] * (1 + len(flat)),
-            out_specs=[whole(half.shape)] * 2,
+            out_specs=specs,
             scratch_shapes=[
                 pltpu.VMEM((2 * m, rows), BF16),
                 pltpu.VMEM((len(slots), rows, each), F32),
                 pltpu.SemaphoreType.DMA((len(slots),)),
             ],
         ),
-        out_shape=[half, half],
+        out_shape=[jax.ShapeDtypeStruct(x, F32) for x in shapes],
         compiler_params=params(),
         cost_estimate=SHORT,
         name="late",
@@ -323,24 +332,26 @@
         ),
         out_shape=jax.ShapeDtypeStruct((FB, per), F32),
         compiler_params=params(),
-        cost_estimate=LONG,
+        cost_estimate=SHORT,
         name="base",
     )(at, *operands)
 
 
-def last_kernel(each, at_ref, base_ref, *refs):
+def last_kernel(each, at_ref, base_ref, middle_ref, *refs):
     *refs, out_ref, total_ref = refs
     total_ref[...] = base_ref[...]
     total = functools.reduce(jnp.add, [ref[...] for ref in refs])
-    for slot in range(total.shape[0] // each):
+    middle = middle_ref[...]
+    pieces = [middle[k : k + each] for k in range(0, middle.shape[0], each)] + [total]
+    for slot, piece in enumerate(pieces):
         first = pl.multiple_of(at_ref[2 + slot] * each, each)
-        total_ref[pl.ds(first, each), :] += total[slot * each : (slot + 1) * each]
+        total_ref[pl.ds(first, each), :] += piece
     out_ref[...] = total_ref[...].T
 
 
-def last(at, held, terms, each):
+def last(at, held, middle, terms, each):
     per = held.shape[1]
-    operands = [held, *terms]
+    operands = [held, middle, *terms]
     return pl.pallas_call(
         functools.partial(last_kernel, each),
         grid_spec=pltpu.PrefetchScalarGridSpec(
@@ -398,13 +409,9 @@
     return lax.ppermute(x, "wide", [(i, i ^ distance) for i in range(wide)])
 
 
-def scatter_terms(halves, wide, after):
-    others = [swap(odd, wide, 1) for _, odd in halves]
-    others[-1:] = gate(others[-1:], after)
-    sums = [
-        [even[h] + other[h] for (even, _), other in zip(halves, others)] for h in range(wide // 2)
-    ]
-    sums = [x[0] if len(x) == 1 else jnp.concatenate(x, axis=0) for x in sums]
+def scatter_terms(even, odd, wide, after):
+    (other,) = gate([swap(odd, wide, 1)], after)
+    sums = [even[h] + other[h] for h in range(wide // 2)]
     return [sums[0]] + [swap(sums[h], wide, 2 * h) for h in range(1, wide // 2)]
 
 
@@ -440,7 +447,7 @@
         held = travel(came, held, n, 2, [small])
     ready = lax.psum_scatter(sums, "wide", scatter_dimension=0)
 
-    projected = functools.reduce(jnp.add, scatter_terms([(even, odd)], wide, came[(1, 0)]))
+    projected = functools.reduce(jnp.add, scatter_terms(even, odd, wide, came[(1, 0)]))
     highest = lax.Precision.HIGHEST
     coefficients = jnp.dot(triangle, projected[:nb], precision=highest)
     payload = coefficients
@@ -457,18 +464,19 @@
     )
 
     slots = [options(came, places, z) for places in table]
-    halves = [late(me, updated, slots[:-1], token, wide)]
-    (ready,) = gate([ready], halves[0][0])
-    halves.append(late(me, updated, slots[-1:], ready, wide))
-    mine = own_columns(me, c, halves[1][0], nb, each)
+    (middle,) = late(me, updated, slots[:-1], token, wide, True)
+    middle_sum = lax.psum_scatter(middle, "wide", scatter_dimension=0)
+    (ready,) = gate([ready], middle)
+    even, odd = late(me, updated, slots[-1:], ready, wide, False)
+    mine = own_columns(me, c, odd, nb, each)
     coef = [mine] + [
         lax.ppermute(mine, "narrow", [(p, (p + s) % n) for p in range(n)]) for s in range(1, n)
     ]
-    tail = scatter_terms(halves, wide, mine)
+    tail = scatter_terms(even, odd, wide, mine)
     (ready,) = gate([ready], tail[0])
     small = c if ride else [lax.psum(small, "wide")]
     base_block = base(at, ready, coefficients, coef, small, n, each, ride)
-    return (updated, last(at, base_block, tail, each))
+    return (updated, last(at, base_block, middle_sum, tail, each))
 
 
 def solution(mesh):

time: 238 us -> 269 us (1.13)
  waiting for transfers between devices: 42.6 us -> 80.6 us
  starting transfers between devices: 33.1 us -> 29.3 us
    ppermute x6, waiting for transfers between devices: 5.56 us -> 50 us  [travel(): held = [lax.ppermute(held[d], 'narrow', pairs[d]) for d in (0, 1)]]
    ppermute x13 -> x12, waiting for transfers between devices: 33.2 us -> 25.7 us  [swap(): return lax.ppermute(x, 'wide', [(i, i ^ distance) for i in range(wide)])]
    ppermute x3, starting transfers between devices: 8.8 us -> 5.27 us  [on_device(): lax.ppermute(mine, 'narrow', [(p, (p + s) % n) for p in range(n)])]
    unnamed x38 -> x34, local copies, waits for them, and re-layouts: 7.3 us -> 6.24 us
    ppermute x13 -> x12, starting transfers between devices: 11.2 us -> 10.7 us  [swap(): return lax.ppermute(x, 'wide', [(i, i ^ distance) for i in range(wide)])]
  transfers between devices with their start and end apart: 23 -> 23, of which waited for: 13 -> 12; matrix products, arithmetic and copies ran while one was open for 3% -> 2% of each run, Pallas kernels for 53% -> 47%
where the time goes in v10:
time: 269 us; the launch traced here: 268 us
  Pallas kernels  128 us (48%)
  waiting for transfers between devices  80.6 us (30%)
  starting transfers between devices  29.3 us (11%)
  between operations  14.3 us (5%)
  other arithmetic  8.23 us (3%)
  local copies, waits for them, and re-layouts  6.92 us (3%)
    ppermute x6, waiting for transfers between devices, travel(): held = [lax.ppermute(held[d], 'narrow', pairs[d]) for d in (0, 1)]  50 us
    pallas_call x1, Pallas kernels, project(): pl.pallas_call(functools.partial(project_kernel, per, wide), grid_spec=pl...  43.9 us
    pallas_call x2, Pallas kernels, late(): pl.pallas_call(functools.partial(late_kernel, per, counts), grid_spec=plt...  42.1 us
    pallas_call x2, Pallas kernels, update(): pl.pallas_call(update_kernel, grid_spec=pltpu.PrefetchScalarGridSpec(num_...  32.9 us
    ppermute x12, waiting for transfers between devices, swap(): return lax.ppermute(x, 'wide', [(i, i ^ distance) for i in range(wide)])  25.7 us
    ppermute x6, starting transfers between devices, travel(): held = [lax.ppermute(held[d], 'narrow', pairs[d]) for d in (0, 1)]  13 us
    ppermute x12, starting transfers between devices, swap(): return lax.ppermute(x, 'wide', [(i, i ^ distance) for i in range(wide)])  10.7 us
    unnamed x34, local copies, waits for them, and re-layouts  6.24 us
  transfers between devices with their start and end apart: 23, of which 12 were waited for; matrix products, arithmetic and copies ran while one was open for 2% of the time, Pallas kernels for 47%

profile of v10, /device:TPU:0, one launch (start us, length us, event | category | flops | bytes accessed | tf_op | source)
XLA Modules:
  0.0 268.1 jit_solution(5756082156181927383)
XLA Ops:
  7.2 2.7 %slice_multiply_fusion.x_ref = f32[4000,128]{1,0:T(8,128)S(1)} fusion(f32[4000,2048]{1,0:T(8,128)} %v_ref.5, f32[4000]{0:T(1024)} %param.7), kind=kLoop, calls=%fused_computation | loop fusion | flops 512000 | bytes 4112000 | tf_op jit(solution)/shard_map/mul | solution.py:438
  10.0 6.3 %collective-permute-start.2 = (f32[4000,128]{1,0:T(8,128)S(1)}, f32[4000,128]{1,0:T(8,128)}, u32[]{:S(2)}, u32[]{:S(2)}) collective-permute-start(f32[4000,128]{1,0:T(8,128)S(1)} %slice_multiply_fusion.x_ref), channel_id=1, source_target_pairs={{0,1},{1,2},{2,3},{4,5},{5,6},{6,7},{8,9},{9,10},{10,11},{12,13},{... | collective-permute-start | bytes 6144008 | tf_op jit(solution)/shard_map/ppermute | solution.py:388
  16.3 1.3 collective-permute-start.1
  17.6 43.9 %project.1 = (f32[4,304,256]{2,1,0:T(8,128)}, f32[4,304,256]{2,1,0:T(8,128)}, f32[8,384,256]{2,1,0:T(8,128)}, f32[384,256]{1,0:T(8,128)}) custom-call(s32[1]{0:T(128)} %bitcast.me_ref, f32[4000,2048]{1,0:T(8,128)} %v_ref.5, f32[4000,256]{1,0:T(8,128)} %r_ref.5, f32[1,4000]{1,0:T(1,128)} %bitcast.46, f32[4000,128]{1,0:T(8,128)} %copy-done.4), custom_call_target="tpu_custom_call" | custom-call | flops 1024 | bytes 1024 | tf_op jit(solution)/shard_map/project/pallas_call | solution.py:132
  61.6 2.8 %collective-permute-done.1.refs_0_ = f32[4000,128]{1,0:T(8,128)} collective-permute-done((f32[4000,128]{1,0:T(8,128)S(1)}, f32[4000,128]{1,0:T(8,128)}, u32[]{:S(2)}, u32[]{:S(2)}) %collective-permute-start.1) | collective-permute-done | bytes 2048032 | tf_op jit(solution)/shard_map/ppermute | solution.py:388
  64.7 1.0 copy-done.5
  65.8 1.3 copy-done.9
  67.1 1.3 fusion.2
  68.3 1.6 collective-permute-start.3
  69.9 1.5 collective-permute-start.5
  71.9 1.3 collective-permute-start.10
  73.2 2.0 collective-permute-start.11
  75.2 3.4 %collective-permute-done.3 = f32[304,256]{1,0:T(8,128)S(1)} collective-permute-done((f32[304,256]{1,0:T(8,128)S(1)}, f32[304,256]{1,0:T(8,128)S(1)}, u32[]{:S(2)}, u32[]{:S(2)}) %collective-permute-start.3) | collective-permute-done | bytes 311328 | tf_op jit(solution)/shard_map/ppermute | solution.py:409
  78.6 6.9 %collective-permute-done.5 = f32[304,256]{1,0:T(8,128)S(1)} collective-permute-done((f32[304,256]{1,0:T(8,128)S(1)}, f32[304,256]{1,0:T(8,128)S(1)}, u32[]{:S(2)}, u32[]{:S(2)}) %collective-permute-start.5) | collective-permute-done | bytes 311328 | tf_op jit(solution)/shard_map/ppermute | solution.py:409
  85.5 1.4 collective-permute-done.4
  86.9 1.1 fusion.6
  88.5 0.6 collective-permute-start.7
  89.0 1.5 collective-permute-start.6
  90.5 1.5 collective-permute-start.8
  92.0 5.9 %collective-permute-done.7 = f32[304,256]{1,0:T(8,128)S(1)} collective-permute-done((f32[304,256]{1,0:T(8,128)S(1)}, f32[304,256]{1,0:T(8,128)S(1)}, u32[]{:S(2)}, u32[]{:S(2)}) %collective-permute-start.7) | collective-permute-done | bytes 311328 | tf_op jit(solution)/shard_map/ppermute | solution.py:409
  97.9 1.3 collective-permute-done.6
  99.2 4.3 %collective-permute-done.8 = f32[304,256]{1,0:T(8,128)S(1)} collective-permute-done((f32[304,256]{1,0:T(8,128)S(1)}, f32[304,256]{1,0:T(8,128)S(1)}, u32[]{:S(2)}, u32[]{:S(2)}) %collective-permute-start.8) | collective-permute-done | bytes 311328 | tf_op jit(solution)/shard_map/ppermute | solution.py:409
  104.0 0.6 pad_add_fusion.at_ref
  104.6 2.1 collective-permute-done.9.odd_ref.refs_5_
  106.7 1.1 copy-done.3
  107.8 12.8 %update.2 = (f32[4000,2048]{1,0:T(8,128)}, f32[8,128]{1,0:T(8,128)}) custom-call(s32[1]{0:T(128)} %bitcast.me_ref, f32[4000,2048]{1,0:T(8,128)} %v_ref.5, f32[4000,256]{1,0:T(8,128)} %r_ref.5, f32[4,304,256]{2,1,0:T(8,128)} %copy-done.2, f32[4,304,256]{2,1,0:T(8,128)} %copy-done.3), custom_call_target="tpu_custom_call" | custom-call | flops 1024 | bytes 1024 | tf_op jit(solution)/shard_map/update/pallas_call | solution.py:173
  120.8 20.1 %update.3 = (f32[4000,2048]{1,0:T(8,128)}, f32[8,128]{1,0:T(8,128)}) custom-call(s32[1]{0:T(128)} %bitcast.me_ref, f32[4000,2048]{1,0:T(8,128)} %v_ref.5, f32[4000,256]{1,0:T(8,128)} %r_ref.5, f32[4,304,256]{2,1,0:T(8,128)} %copy-done.2, f32[4,304,256]{2,1,0:T(8,128)} %copy-done.3, ...), custom_call_target="tpu_custom_call", output_to_operand_aliasing={{0}: (6, {})} | custom-call | flops 1024 | bytes 1024 | tf_op jit(solution)/shard_map/update/pallas_call | solution.py:173
  140.9 23.2 %late.2.refs_1_ = f32[8,256,256]{2,1,0:T(8,128)} custom-call(s32[3]{0:T(128)} %pad_add_fusion.at_ref, f32[4000,2048]{1,0:T(8,128)} %get-tuple-element.14.u_ref, f32[8,128]{1,0:T(8,128)} %get-tuple-element.26.after_ref, f32[4000,128]{1,0:T(8,128)} %get-tuple-element.19.refs_1_.refs_0_, f32[4000,128]{1,0:T(8,128)} %get-tuple-element.20.refs_1_.refs_2_, ...), custom_call_target="tpu_custom_call" | custom-call | flops 1024 | bytes 1024 | tf_op jit(solution)/shard_map/late/pallas_call | solution.py:250
  164.1 0.8 collective-permute-start.13
  164.9 1.3 collective-permute-start.12
  166.2 0.6 pad_add_fusion.1.at_ref
  166.8 47.0 %collective-permute-done.12.refs_2_ = f32[4000,128]{1,0:T(8,128)} collective-permute-done((f32[4000,128]{1,0:T(8,128)}, f32[4000,128]{1,0:T(8,128)}, u32[]{:S(2)}, u32[]{:S(2)}) %collective-permute-start.12) | collective-permute-done | bytes 2048032 | tf_op jit(solution)/shard_map/ppermute | solution.py:388
  213.8 18.9 %late.3 = (f32[4,128,256]{2,1,0:T(8,128)}, f32[4,128,256]{2,1,0:T(8,128)}) custom-call(s32[2]{0:T(128)} %pad_add_fusion.1.at_ref, f32[4000,2048]{1,0:T(8,128)} %get-tuple-element.14.u_ref, f32[384,256]{1,0:T(8,128)} %gate.9.after_ref.refs_0_, f32[4000,128]{1,0:T(8,128)} %get-tuple-element.22.refs_0_.refs_3_, f32[4000,128]{1,0:T(8,128)} %get-tuple-element.27.refs_4_.refs_1_, ...), custom_call_target="tpu_custom_call" | custom-call | flops 1024 | bytes 1024 | tf_op jit(solution)/shard_map/late/pallas_call | solution.py:250
  232.8 1.9 own_columns.1.refs_1_.refs_0_
  234.7 4.7 %collective-permute-start.17 = (f32[128,256]{1,0:T(8,128)}, f32[128,256]{1,0:T(8,128)S(1)}, u32[]{:S(2)}, u32[]{:S(2)}) collective-permute-start(f32[128,256]{1,0:T(8,128)} %own_columns.1.refs_1_.refs_0_), channel_id=1, source_target_pairs={{0,3},{1,0},{2,1},{3,2},{4,7},{5,4},{6,5},{7,6},{8,11},{9,8},{10,9... | collective-permute-start | bytes 393224 | tf_op jit(solution)/shard_map/ppermute | solution.py:473
  239.4 0.6 collective-permute-start.15
  239.9 0.8 copy-done.7
  240.7 1.8 fusion.8
  242.6 2.2 collective-permute-start.20
  244.8 0.8 collective-permute-start.19
  245.6 0.5 collective-permute-start.18
  246.1 0.7 stack.54.at_ref
  246.8 4.9 %collective-permute-done.16.refs_2_ = f32[128,256]{1,0:T(8,128)S(1)} collective-permute-done((f32[128,256]{1,0:T(8,128)}, f32[128,256]{1,0:T(8,128)S(1)}, u32[]{:S(2)}, u32[]{:S(2)}) %collective-permute-start.16) | collective-permute-done | bytes 131104 | tf_op jit(solution)/shard_map/ppermute | solution.py:473
  251.7 0.6 copy-done.12
  252.3 0.7 copy-done.13
  253.0 4.5 %base.1.base_ref = f32[512,256]{1,0:T(8,128)} custom-call(s32[5]{0:T(128)} %stack.54.at_ref, f32[384,256]{1,0:T(8,128)} %gate.11.ready_ref, f32[256,256]{1,0:T(8,128)} %copy-done.6, f32[128,256]{1,0:T(8,128)} %own_columns.1.refs_1_.refs_0_, f32[128,256]{1,0:T(8,128)} %copy-done.13, f32[128,256]{1,0:T(8,128)} %copy-done.12, f32[128,256]{1,0:T(8,128)} %copy-done.11, ...), custom_call_target="tpu_custom_call" | custom-call | flops 1024 | bytes 1024 | tf_op jit(solution)/shard_map/base/pallas_call | solution.py:324
  257.5 0.6 copy-done.14
  258.2 3.0 %last.1 = f32[256,512]{1,0:T(8,128)} custom-call(s32[5]{0:T(128)} %stack.54.at_ref, f32[512,256]{1,0:T(8,128)} %base.1.base_ref, f32[256,256]{1,0:T(8,128)} %bitcast.45, f32[128,256]{1,0:T(8,128)} %get-tuple-element.36.refs_1_.refs_0_, f32[128,256]{1,0:T(8,128)} %copy-done.16, f32[128,256]{1,0:T(8,128)} %copy-done.15, f32[128,256]{1,0:T(8,128)} %copy-done.14), custom_call_target="tpu_custom_call" | custom-call | flops 1024 | bytes 1024 | tf_op jit(solution)/shard_map/last/pallas_call | solution.py:355
  (59 shorter events, 2.3 us)
Async XLA Ops:
  7.2 80.8 %copy-start = (f32[256,256]{1,0:T(8,128)S(1)}, f32[256,256]{1,0:T(8,128)}, u32[]{:S(2)}) copy-start(f32[256,256]{1,0:T(8,128)} %param.6) | copy-start | bytes 786436
  7.2 159.6 %reduce-scatter.3.cloned.1.call-start = ((), (), s32[]{:S(2)}) async-start(), calls=%async_computation.2 | async-start | bytes 3538944 | tf_op jit(solution)/shard_map/reduce_scatter | solution.py:448
  10.0 7.6 %copy-start.4 = (f32[4000,128]{1,0:T(8,128)}, f32[4000,128]{1,0:T(8,128)S(1)}, u32[]{:S(2)}) copy-start(f32[4000,128]{1,0:T(8,128)S(1)} %slice_multiply_fusion.x_ref) | copy-start | bytes 6144004
  10.0 51.6 %collective-permute-start.2 = (f32[4000,128]{1,0:T(8,128)S(1)}, f32[4000,128]{1,0:T(8,128)}, u32[]{:S(2)}, u32[]{:S(2)}) collective-permute-start(f32[4000,128]{1,0:T(8,128)S(1)} %slice_multiply_fusion.x_ref), channel_id=1, source_target_pairs={{0,1},{1,2},{2,3},{4,5},{5,6},{6,7},{8,9},{9,10},{10,11},{12,13},{... | collective-permute-start | bytes 6144008 | tf_op jit(solution)/shard_map/ppermute | solution.py:388
  16.3 48.0 %collective-permute-start.1 = (f32[4000,128]{1,0:T(8,128)S(1)}, f32[4000,128]{1,0:T(8,128)}, u32[]{:S(2)}, u32[]{:S(2)}) collective-permute-start(f32[4000,128]{1,0:T(8,128)S(1)} %slice_multiply_fusion.x_ref), channel_id=1, source_target_pairs={{1,0},{2,1},{3,2},{5,4},{6,5},{7,6},{9,8},{10,9},{11,10},{13,12},{... | collective-permute-start | bytes 6144008 | tf_op jit(solution)/shard_map/ppermute | solution.py:388
  61.6 3.2 %collective-permute-start = (f32[4,304,256]{2,1,0:T(8,128)}, f32[4,304,256]{2,1,0:T(8,128)S(1)}, u32[]{:S(2)}, u32[]{:S(2)}) collective-permute-start(f32[4,304,256]{2,1,0:T(8,128)} %get-tuple-element.17), channel_id=1, source_target_pairs={{0,4},{4,0},{8,12},{12,8},{16,20},{20,16},{24,28},{28,24},{1,5},{5... | collective-permute-start | bytes 3735560 | tf_op jit(solution)/shard_map/ppermute | solution.py:409
  64.7 1.0 copy-start.5
  65.8 1.3 copy-start.9
  68.3 10.3 %collective-permute-start.3 = (f32[304,256]{1,0:T(8,128)S(1)}, f32[304,256]{1,0:T(8,128)S(1)}, u32[]{:S(2)}, u32[]{:S(2)}) collective-permute-start(f32[304,256]{1,0:T(8,128)S(1)} %get-tuple-element.30), channel_id=1, source_target_pairs={{0,8},{4,12},{8,0},{12,4},{16,24},{20,28},{24,16},{28,20},{1,9},{5... | collective-permute-start | bytes 933896 | tf_op jit(solution)/shard_map/ppermute | solution.py:409
  69.9 15.6 %collective-permute-start.5 = (f32[304,256]{1,0:T(8,128)S(1)}, f32[304,256]{1,0:T(8,128)S(1)}, u32[]{:S(2)}, u32[]{:S(2)}) collective-permute-start(f32[304,256]{1,0:T(8,128)S(1)} %get-tuple-element.31), channel_id=1, source_target_pairs={{0,24},{4,28},{8,16},{12,20},{16,8},{20,12},{24,0},{28,4},{1,25},{... | collective-permute-start | bytes 933896 | tf_op jit(solution)/shard_map/ppermute | solution.py:409
  71.4 15.5 %collective-permute-start.4 = (f32[304,256]{1,0:T(8,128)S(1)}, f32[304,256]{1,0:T(8,128)S(1)}, u32[]{:S(2)}, u32[]{:S(2)}) collective-permute-start(f32[304,256]{1,0:T(8,128)S(1)} %get-tuple-element.32), channel_id=1, source_target_pairs={{0,16},{4,20},{8,24},{12,28},{16,0},{20,4},{24,8},{28,12},{1,17},{... | collective-permute-start | bytes 933896 | tf_op jit(solution)/shard_map/ppermute | solution.py:409
  71.9 48.9 %collective-permute-start.10 = (f32[4000,128]{1,0:T(8,128)}, f32[4000,128]{1,0:T(8,128)}, u32[]{:S(2)}, u32[]{:S(2)}) collective-permute-start(f32[4000,128]{1,0:T(8,128)} %get-tuple-element.19.refs_1_.refs_0_), channel_id=1, source_target_pairs={{1,0},{2,1},{5,4},{6,5},{9,8},{10,9},{13,12},{14,13},{17,16},{18,1... | collective-permute-start | bytes 6144008 | tf_op jit(solution)/shard_map/ppermute | solution.py:388
  73.2 47.4 %collective-permute-start.11 = (f32[4000,128]{1,0:T(8,128)}, f32[4000,128]{1,0:T(8,128)}, u32[]{:S(2)}, u32[]{:S(2)}) collective-permute-start(f32[4000,128]{1,0:T(8,128)} %get-tuple-element.20.refs_1_.refs_2_), channel_id=1, source_target_pairs={{1,2},{2,3},{5,6},{6,7},{9,10},{10,11},{13,14},{14,15},{17,18},{18... | collective-permute-start | bytes 6144008 | tf_op jit(solution)/shard_map/ppermute | solution.py:388
  88.4 15.1 %copy-start.6 = (f32[256,256]{1,0:T(8,128)}, f32[256,256]{1,0:T(8,128)S(1)}, u32[]{:S(2)}) copy-start(f32[256,256]{1,0:T(8,128)S(1)} %convolution_bitcast_fusion.c_ref) | copy-start | bytes 786436
  88.5 9.5 %collective-permute-start.7 = (f32[304,256]{1,0:T(8,128)S(1)}, f32[304,256]{1,0:T(8,128)S(1)}, u32[]{:S(2)}, u32[]{:S(2)}) collective-permute-start(f32[304,256]{1,0:T(8,128)S(1)} %get-tuple-element.38), channel_id=1, source_target_pairs={{0,16},{4,20},{8,24},{12,28},{16,0},{20,4},{24,8},{28,12},{1,17},{... | collective-permute-start | bytes 933896 | tf_op jit(solution)/shard_map/ppermute | solution.py:409
  89.0 10.2 %collective-permute-start.6 = (f32[304,256]{1,0:T(8,128)S(1)}, f32[304,256]{1,0:T(8,128)S(1)}, u32[]{:S(2)}, u32[]{:S(2)}) collective-permute-start(f32[304,256]{1,0:T(8,128)S(1)} %get-tuple-element.38), channel_id=1, source_target_pairs={{0,8},{4,12},{8,0},{12,4},{16,24},{20,28},{24,16},{28,20},{1,9},{5... | collective-permute-start | bytes 933896 | tf_op jit(solution)/shard_map/ppermute | solution.py:409
  90.5 13.0 %collective-permute-start.8 = (f32[304,256]{1,0:T(8,128)S(1)}, f32[304,256]{1,0:T(8,128)S(1)}, u32[]{:S(2)}, u32[]{:S(2)}) collective-permute-start(f32[304,256]{1,0:T(8,128)S(1)} %get-tuple-element.38), channel_id=1, source_target_pairs={{0,24},{4,28},{8,16},{12,20},{16,8},{20,12},{24,0},{28,4},{1,25},{... | collective-permute-start | bytes 933896 | tf_op jit(solution)/shard_map/ppermute | solution.py:409
  103.7 3.0 %copy-start.2 = (f32[4,304,256]{2,1,0:T(8,128)}, f32[4,304,256]{2,1,0:T(8,128)S(1)}, u32[]{:S(2)}) copy-start(f32[4,304,256]{2,1,0:T(8,128)S(1)} %pad_maximum_fusion.even_ref.refs_4_) | copy-start | bytes 3735556
  103.7 3.0 %collective-permute-start.9 = (f32[4,304,256]{2,1,0:T(8,128)S(1)}, f32[4,304,256]{2,1,0:T(8,128)S(1)}, u32[]{:S(2)}, u32[]{:S(2)}) collective-permute-start(f32[4,304,256]{2,1,0:T(8,128)S(1)} %pad_maximum_fusion.even_ref.refs_4_), channel_id=1, source_target_pairs={{0,4},{4,0},{8,12},{12,8},{16,20},{20,16},{24,28},{28,24},{1,5},{5... | collective-permute-start | bytes 3735560 | tf_op jit(solution)/shard_map/ppermute | solution.py:409
  103.8 153.7 %reduce-scatter.5.cloned.1.call-start = ((), (), s32[]{:S(2)}) async-start(), calls=%async_computation.3 | async-start | bytes 2359296 | tf_op jit(solution)/shard_map/reduce_scatter | solution.py:468
  106.7 1.1 copy-start.3
  164.1 2.7 %collective-permute-start.13 = (f32[4000,128]{1,0:T(8,128)}, f32[4000,128]{1,0:T(8,128)S(1)}, u32[]{:S(2)}, u32[]{:S(2)}) collective-permute-start(f32[4000,128]{1,0:T(8,128)} %get-tuple-element.27.refs_4_.refs_1_), channel_id=1, source_target_pairs={{2,3},{6,7},{10,11},{14,15},{18,19},{22,23},{26,27},{30,31}} | collective-permute-start | bytes 6144008 | tf_op jit(solution)/shard_map/ppermute | solution.py:388
  164.9 48.9 %collective-permute-start.12 = (f32[4000,128]{1,0:T(8,128)}, f32[4000,128]{1,0:T(8,128)}, u32[]{:S(2)}, u32[]{:S(2)}) collective-permute-start(f32[4000,128]{1,0:T(8,128)} %get-tuple-element.22.refs_0_.refs_3_), channel_id=1, source_target_pairs={{1,0},{5,4},{9,8},{13,12},{17,16},{21,20},{25,24},{29,28}} | collective-permute-start | bytes 6144008 | tf_op jit(solution)/shard_map/ppermute | solution.py:388
  166.8 47.0 %copy-start.8 = (f32[4000,128]{1,0:T(8,128)}, f32[4000,128]{1,0:T(8,128)S(1)}, u32[]{:S(2)}) copy-start(f32[4000,128]{1,0:T(8,128)S(1)} %collective-permute-done.13.refs_3_) | copy-start | bytes 6144004
  232.7 8.1 %copy-start.10 = (f32[4,128,256]{2,1,0:T(8,128)S(1)}, f32[4,128,256]{2,1,0:T(8,128)}, u32[]{:S(2)}) copy-start(f32[4,128,256]{2,1,0:T(8,128)} %get-tuple-element.28) | copy-start | bytes 1572868
  232.7 7.2 %collective-permute-start.14 = (f32[4,128,256]{2,1,0:T(8,128)}, f32[4,128,256]{2,1,0:T(8,128)S(1)}, u32[]{:S(2)}, u32[]{:S(2)}) collective-permute-start(f32[4,128,256]{2,1,0:T(8,128)} %get-tuple-element.29.after_ref), channel_id=1, source_target_pairs={{0,4},{4,0},{8,12},{12,8},{16,20},{20,16},{24,28},{28,24},{1,5},{5... | collective-permute-start | bytes 1572872 | tf_op jit(solution)/shard_map/ppermute | solution.py:409
  234.7 10.9 %collective-permute-start.17 = (f32[128,256]{1,0:T(8,128)}, f32[128,256]{1,0:T(8,128)S(1)}, u32[]{:S(2)}, u32[]{:S(2)}) collective-permute-start(f32[128,256]{1,0:T(8,128)} %own_columns.1.refs_1_.refs_0_), channel_id=1, source_target_pairs={{0,3},{1,0},{2,1},{3,2},{4,7},{5,4},{6,5},{7,6},{8,11},{9,8},{10,9... | collective-permute-start | bytes 393224 | tf_op jit(solution)/shard_map/ppermute | solution.py:473
  239.4 12.3 %collective-permute-start.16 = (f32[128,256]{1,0:T(8,128)}, f32[128,256]{1,0:T(8,128)S(1)}, u32[]{:S(2)}, u32[]{:S(2)}) collective-permute-start(f32[128,256]{1,0:T(8,128)} %own_columns.1.refs_1_.refs_0_), channel_id=1, source_target_pairs={{0,2},{1,3},{2,0},{3,1},{4,6},{5,7},{6,4},{7,5},{8,10},{9,11},{10,... | collective-permute-start | bytes 393224 | tf_op jit(solution)/shard_map/ppermute | solution.py:473
  239.4 12.3 %collective-permute-start.15 = (f32[128,256]{1,0:T(8,128)}, f32[128,256]{1,0:T(8,128)S(1)}, u32[]{:S(2)}, u32[]{:S(2)}) collective-permute-start(f32[128,256]{1,0:T(8,128)} %own_columns.1.refs_1_.refs_0_), channel_id=1, source_target_pairs={{0,1},{1,2},{2,3},{3,0},{4,5},{5,6},{6,7},{7,4},{8,9},{9,10},{10,1... | collective-permute-start | bytes 393224 | tf_op jit(solution)/shard_map/ppermute | solution.py:473
  239.9 0.8 copy-start.7
  242.6 14.8 %collective-permute-start.20 = (f32[128,256]{1,0:T(8,128)S(1)}, f32[128,256]{1,0:T(8,128)S(1)}, u32[]{:S(2)}, u32[]{:S(2)}) collective-permute-start(f32[128,256]{1,0:T(8,128)S(1)} %get-tuple-element.33), channel_id=1, source_target_pairs={{0,24},{4,28},{8,16},{12,20},{16,8},{20,12},{24,0},{28,4},{1,25},{... | collective-permute-start | bytes 393224 | tf_op jit(solution)/shard_map/ppermute | solution.py:409
  244.8 12.7 %collective-permute-start.19 = (f32[128,256]{1,0:T(8,128)S(1)}, f32[128,256]{1,0:T(8,128)S(1)}, u32[]{:S(2)}, u32[]{:S(2)}) collective-permute-start(f32[128,256]{1,0:T(8,128)S(1)} %get-tuple-element.34), channel_id=1, source_target_pairs={{0,16},{4,20},{8,24},{12,28},{16,0},{20,4},{24,8},{28,12},{1,17},{... | collective-permute-start | bytes 393224 | tf_op jit(solution)/shard_map/ppermute | solution.py:409
  245.6 6.1 %copy-start.11 = (f32[128,256]{1,0:T(8,128)}, f32[128,256]{1,0:T(8,128)S(1)}, u32[]{:S(2)}) copy-start(f32[128,256]{1,0:T(8,128)S(1)} %collective-permute-done.17.refs_3_) | copy-start | bytes 393220
  245.6 11.9 %collective-permute-start.18 = (f32[128,256]{1,0:T(8,128)S(1)}, f32[128,256]{1,0:T(8,128)S(1)}, u32[]{:S(2)}, u32[]{:S(2)}) collective-permute-start(f32[128,256]{1,0:T(8,128)S(1)} %get-tuple-element.35), channel_id=1, source_target_pairs={{0,8},{4,12},{8,0},{12,4},{16,24},{20,28},{24,16},{28,20},{1,9},{5... | collective-permute-start | bytes 393224 | tf_op jit(solution)/shard_map/ppermute | solution.py:409
  246.7 14.5 %copy-start.1 = (f32[256,256]{1,0:T(8,128)S(1)}, f32[256,256]{1,0:T(8,128)}, u32[]{:S(2)}) copy-start(f32[256,256]{1,0:T(8,128)} %param.6) | copy-start | bytes 786436
  251.7 0.6 copy-start.12
  252.3 0.7 copy-start.13
  257.4 0.6 copy-start.14
  257.4 0.7 copy-start.15
  257.5 0.7 copy-start.16
Sparse Core Ops, SparseCore 0:
  103.9 47.5 reduce-scatter.2
  164.2 45.4 reduce-scatter.4

commit v11 on v10

--- a/solution.py
+++ b/solution.py
@@ -262,7 +262,7 @@
         ),
         out_shape=[jax.ShapeDtypeStruct(x, F32) for x in shapes],
         compiler_params=params(),
-        cost_estimate=SHORT,
+        cost_estimate=SHORT if ordered else LONG,
         name="late",
     )(at, updated, after, *flat)
 

time: 269 us -> 229 us (0.85)
  waiting for transfers between devices: 80.6 us -> 36 us
  starting transfers between devices: 29.3 us -> 32.8 us
    ppermute x6, waiting for transfers between devices: 50 us -> 5.64 us  [travel(): held = [lax.ppermute(held[d], 'narrow', pairs[d]) for d in (0, 1)]]
    ppermute x3, starting transfers between devices: 5.27 us -> 8.97 us  [on_device(): lax.ppermute(mine, 'narrow', [(p, (p + s) % n) for p in range(n)])]
  transfers between devices with their start and end apart: 23 -> 23, of which waited for: 12 -> 12; matrix products, arithmetic and copies ran while one was open for 2% -> 2% of each run, Pallas kernels for 47% -> 55%
where the time goes in v11:
time: 229 us; the launch traced here: 228 us
  Pallas kernels  129 us (56%)
  waiting for transfers between devices  36 us (16%)
  starting transfers between devices  32.8 us (14%)
  between operations  14.4 us (6%)
  other arithmetic  8.31 us (4%)
  local copies, waits for them, and re-layouts  6.9 us (3%)
    pallas_call x1, Pallas kernels, project(): pl.pallas_call(functools.partial(project_kernel, per, wide), grid_spec=pl...  43.9 us
    pallas_call x2, Pallas kernels, late(): pl.pallas_call(functools.partial(late_kernel, per, counts), grid_spec=plt...  42.4 us
    pallas_call x2, Pallas kernels, update(): pl.pallas_call(update_kernel, grid_spec=pltpu.PrefetchScalarGridSpec(num_...  33.4 us
    ppermute x12, waiting for transfers between devices, swap(): return lax.ppermute(x, 'wide', [(i, i ^ distance) for i in range(wide)])  26.5 us
    ppermute x6, starting transfers between devices, travel(): held = [lax.ppermute(held[d], 'narrow', pairs[d]) for d in (0, 1)]  13 us
    ppermute x12, starting transfers between devices, swap(): return lax.ppermute(x, 'wide', [(i, i ^ distance) for i in range(wide)])  10.7 us
    ppermute x3, starting transfers between devices, on_device(): lax.ppermute(mine, 'narrow', [(p, (p + s) % n) for p in range(n)])  8.97 us
    unnamed x34, local copies, waits for them, and re-layouts  6.21 us
  transfers between devices with their start and end apart: 23, of which 12 were waited for; matrix products, arithmetic and copies ran while one was open for 2% of the time, Pallas kernels for 55%

profile of v11, /device:TPU:0, one launch (start us, length us, event | category | flops | bytes accessed | tf_op | source)
XLA Modules:
  0.0 227.9 jit_solution(665836879136497590)
XLA Ops:
  7.2 2.7 %slice_multiply_fusion.x_ref = f32[4000,128]{1,0:T(8,128)S(1)} fusion(f32[4000,2048]{1,0:T(8,128)} %v_ref.5, f32[4000]{0:T(1024)} %param.7), kind=kLoop, calls=%fused_computation | loop fusion | flops 512000 | bytes 4112000 | tf_op jit(solution)/shard_map/mul | solution.py:438
  10.0 6.2 %collective-permute-start.2 = (f32[4000,128]{1,0:T(8,128)S(1)}, f32[4000,128]{1,0:T(8,128)}, u32[]{:S(2)}, u32[]{:S(2)}) collective-permute-start(f32[4000,128]{1,0:T(8,128)S(1)} %slice_multiply_fusion.x_ref), channel_id=1, source_target_pairs={{0,1},{1,2},{2,3},{4,5},{5,6},{6,7},{8,9},{9,10},{10,11},{12,13},{... | collective-permute-start | bytes 6144008 | tf_op jit(solution)/shard_map/ppermute | solution.py:388
  16.2 1.3 collective-permute-start.1
  17.5 43.9 %project.1 = (f32[4,304,256]{2,1,0:T(8,128)}, f32[4,304,256]{2,1,0:T(8,128)}, f32[8,384,256]{2,1,0:T(8,128)}, f32[384,256]{1,0:T(8,128)}) custom-call(s32[1]{0:T(128)} %bitcast.me_ref, f32[4000,2048]{1,0:T(8,128)} %v_ref.5, f32[4000,256]{1,0:T(8,128)} %r_ref.5, f32[1,4000]{1,0:T(1,128)} %bitcast.46, f32[4000,128]{1,0:T(8,128)} %copy-done.4), custom_call_target="tpu_custom_call" | custom-call | flops 1024 | bytes 1024 | tf_op jit(solution)/shard_map/project/pallas_call | solution.py:132
  61.5 2.8 %collective-permute-done.1.refs_0_ = f32[4000,128]{1,0:T(8,128)} collective-permute-done((f32[4000,128]{1,0:T(8,128)S(1)}, f32[4000,128]{1,0:T(8,128)}, u32[]{:S(2)}, u32[]{:S(2)}) %collective-permute-start.1) | collective-permute-done | bytes 2048032 | tf_op jit(solution)/shard_map/ppermute | solution.py:388
  64.6 1.0 copy-done.5
  65.7 1.3 copy-done.8
  67.0 1.3 fusion.2
  68.2 1.6 collective-permute-start.3
  69.8 1.5 collective-permute-start.5
  71.3 0.5 collective-permute-start.4
  71.8 1.3 collective-permute-start.10
  73.1 2.0 collective-permute-start.11
  75.1 3.4 %collective-permute-done.3 = f32[304,256]{1,0:T(8,128)S(1)} collective-permute-done((f32[304,256]{1,0:T(8,128)S(1)}, f32[304,256]{1,0:T(8,128)S(1)}, u32[]{:S(2)}, u32[]{:S(2)}) %collective-permute-start.3) | collective-permute-done | bytes 311328 | tf_op jit(solution)/shard_map/ppermute | solution.py:409
  78.5 6.9 %collective-permute-done.5 = f32[304,256]{1,0:T(8,128)S(1)} collective-permute-done((f32[304,256]{1,0:T(8,128)S(1)}, f32[304,256]{1,0:T(8,128)S(1)}, u32[]{:S(2)}, u32[]{:S(2)}) %collective-permute-start.5) | collective-permute-done | bytes 311328 | tf_op jit(solution)/shard_map/ppermute | solution.py:409
  85.4 1.4 collective-permute-done.4
  86.8 1.1 fusion.6
  88.4 0.6 collective-permute-start.7
  88.9 1.5 collective-permute-start.6
  90.4 1.5 collective-permute-start.8
  91.9 5.9 %collective-permute-done.7 = f32[304,256]{1,0:T(8,128)S(1)} collective-permute-done((f32[304,256]{1,0:T(8,128)S(1)}, f32[304,256]{1,0:T(8,128)S(1)}, u32[]{:S(2)}, u32[]{:S(2)}) %collective-permute-start.7) | collective-permute-done | bytes 311328 | tf_op jit(solution)/shard_map/ppermute | solution.py:409
  97.8 1.3 collective-permute-done.6
  99.1 4.3 %collective-permute-done.8 = f32[304,256]{1,0:T(8,128)S(1)} collective-permute-done((f32[304,256]{1,0:T(8,128)S(1)}, f32[304,256]{1,0:T(8,128)S(1)}, u32[]{:S(2)}, u32[]{:S(2)}) %collective-permute-start.8) | collective-permute-done | bytes 311328 | tf_op jit(solution)/shard_map/ppermute | solution.py:409
  103.7 2.9 %collective-permute-done.9.odd_ref.refs_5_ = f32[4,304,256]{2,1,0:T(8,128)S(1)} collective-permute-done((f32[4,304,256]{2,1,0:T(8,128)S(1)}, f32[4,304,256]{2,1,0:T(8,128)S(1)}, u32[]{:S(2)}, u32[]{:S(2)}) %collective-permute-start.9) | collective-permute-done | bytes 1245216 | tf_op jit(solution)/shard_map/ppermute | solution.py:409
  106.6 1.1 copy-done.3
  107.6 12.8 %update.2 = (f32[4000,2048]{1,0:T(8,128)}, f32[8,128]{1,0:T(8,128)}) custom-call(s32[1]{0:T(128)} %bitcast.me_ref, f32[4000,2048]{1,0:T(8,128)} %v_ref.5, f32[4000,256]{1,0:T(8,128)} %r_ref.5, f32[4,304,256]{2,1,0:T(8,128)} %copy-done.2, f32[4,304,256]{2,1,0:T(8,128)} %copy-done.3), custom_call_target="tpu_custom_call" | custom-call | flops 1024 | bytes 1024 | tf_op jit(solution)/shard_map/update/pallas_call | solution.py:173
  120.7 1.0 collective-permute-start.13
  121.7 1.3 collective-permute-start.12
  123.0 0.6 pad_add_fusion.1.at_ref
  123.6 0.7 pad_add_fusion.at_ref
  124.2 20.6 %update.3 = (f32[4000,2048]{1,0:T(8,128)}, f32[8,128]{1,0:T(8,128)}) custom-call(s32[1]{0:T(128)} %bitcast.me_ref, f32[4000,2048]{1,0:T(8,128)} %v_ref.5, f32[4000,256]{1,0:T(8,128)} %r_ref.5, f32[4,304,256]{2,1,0:T(8,128)} %copy-done.2, f32[4,304,256]{2,1,0:T(8,128)} %copy-done.3, ...), custom_call_target="tpu_custom_call", output_to_operand_aliasing={{0}: (6, {})} | custom-call | flops 1024 | bytes 1024 | tf_op jit(solution)/shard_map/update/pallas_call | solution.py:173
  144.9 23.0 %late.2.refs_1_ = f32[8,256,256]{2,1,0:T(8,128)} custom-call(s32[3]{0:T(128)} %pad_add_fusion.at_ref, f32[4000,2048]{1,0:T(8,128)} %get-tuple-element.14.u_ref, f32[8,128]{1,0:T(8,128)} %get-tuple-element.26.after_ref, f32[4000,128]{1,0:T(8,128)} %get-tuple-element.19.refs_1_.refs_0_, f32[4000,128]{1,0:T(8,128)} %get-tuple-element.20.refs_1_.refs_2_, ...), custom_call_target="tpu_custom_call" | custom-call | flops 1024 | bytes 1024 | tf_op jit(solution)/shard_map/late/pallas_call | solution.py:250
  167.9 2.6 %collective-permute-done.12.refs_2_ = f32[4000,128]{1,0:T(8,128)} collective-permute-done((f32[4000,128]{1,0:T(8,128)}, f32[4000,128]{1,0:T(8,128)}, u32[]{:S(2)}, u32[]{:S(2)}) %collective-permute-start.12) | collective-permute-done | bytes 2048032 | tf_op jit(solution)/shard_map/ppermute | solution.py:388
  170.5 19.5 %late.3 = (f32[4,128,256]{2,1,0:T(8,128)}, f32[4,128,256]{2,1,0:T(8,128)}) custom-call(s32[2]{0:T(128)} %pad_add_fusion.1.at_ref, f32[4000,2048]{1,0:T(8,128)} %get-tuple-element.14.u_ref, f32[384,256]{1,0:T(8,128)} %gate.9.after_ref.refs_0_, f32[4000,128]{1,0:T(8,128)} %get-tuple-element.22.refs_0_.refs_3_, f32[4000,128]{1,0:T(8,128)} %get-tuple-element.27.refs_4_.refs_1_, ...), custom_call_target="tpu_custom_call" | custom-call | flops 99999997952 | bytes 1024 | tf_op jit(solution)/shard_map/late/pallas_call | solution.py:250
  190.1 1.9 own_columns.1.refs_1_.refs_0_
  192.0 5.3 %collective-permute-start.17 = (f32[128,256]{1,0:T(8,128)}, f32[128,256]{1,0:T(8,128)S(1)}, u32[]{:S(2)}, u32[]{:S(2)}) collective-permute-start(f32[128,256]{1,0:T(8,128)} %own_columns.1.refs_1_.refs_0_), channel_id=1, source_target_pairs={{0,3},{1,0},{2,1},{3,2},{4,7},{5,4},{6,5},{7,6},{8,11},{9,8},{10,9... | collective-permute-start | bytes 393224 | tf_op jit(solution)/shard_map/ppermute | solution.py:473
  197.2 1.7 collective-permute-start.16
  198.9 2.0 collective-permute-start.15
  200.9 0.8 copy-done.7
  201.7 1.8 fusion.8
  203.6 2.5 %collective-permute-start.20 = (f32[128,256]{1,0:T(8,128)S(1)}, f32[128,256]{1,0:T(8,128)S(1)}, u32[]{:S(2)}, u32[]{:S(2)}) collective-permute-start(f32[128,256]{1,0:T(8,128)S(1)} %get-tuple-element.33), channel_id=1, source_target_pairs={{0,24},{4,28},{8,16},{12,20},{16,8},{20,12},{24,0},{28,4},{1,25},{... | collective-permute-start | bytes 393224 | tf_op jit(solution)/shard_map/ppermute | solution.py:409
  207.1 0.7 stack.54.at_ref
  207.8 3.7 %collective-permute-done.16.refs_2_ = f32[128,256]{1,0:T(8,128)S(1)} collective-permute-done((f32[128,256]{1,0:T(8,128)}, f32[128,256]{1,0:T(8,128)S(1)}, u32[]{:S(2)}, u32[]{:S(2)}) %collective-permute-start.16) | collective-permute-done | bytes 131104 | tf_op jit(solution)/shard_map/ppermute | solution.py:473
  211.5 0.6 copy-done.11
  212.1 0.7 copy-done.12
  212.8 4.5 %base.1.base_ref = f32[512,256]{1,0:T(8,128)} custom-call(s32[5]{0:T(128)} %stack.54.at_ref, f32[384,256]{1,0:T(8,128)} %gate.11.ready_ref, f32[256,256]{1,0:T(8,128)} %copy-done.6, f32[128,256]{1,0:T(8,128)} %own_columns.1.refs_1_.refs_0_, f32[128,256]{1,0:T(8,128)} %copy-done.12, f32[128,256]{1,0:T(8,128)} %copy-done.11, f32[128,256]{1,0:T(8,128)} %copy-done.10, ...), custom_call_target="tpu_custom_call" | custom-call | flops 1024 | bytes 1024 | tf_op jit(solution)/shard_map/base/pallas_call | solution.py:324
  217.4 0.6 copy-done.13
  218.0 3.0 %last.1 = f32[256,512]{1,0:T(8,128)} custom-call(s32[5]{0:T(128)} %stack.54.at_ref, f32[512,256]{1,0:T(8,128)} %base.1.base_ref, f32[256,256]{1,0:T(8,128)} %bitcast.45, f32[128,256]{1,0:T(8,128)} %get-tuple-element.36.refs_1_.refs_0_, f32[128,256]{1,0:T(8,128)} %copy-done.15, f32[128,256]{1,0:T(8,128)} %copy-done.14, f32[128,256]{1,0:T(8,128)} %copy-done.13), custom_call_target="tpu_custom_call" | custom-call | flops 1024 | bytes 1024 | tf_op jit(solution)/shard_map/last/pallas_call | solution.py:355
  (59 shorter events, 2.7 us)
Async XLA Ops:
  7.2 80.7 %copy-start = (f32[256,256]{1,0:T(8,128)S(1)}, f32[256,256]{1,0:T(8,128)}, u32[]{:S(2)}) copy-start(f32[256,256]{1,0:T(8,128)} %param.6) | copy-start | bytes 786436
  7.2 160.7 %reduce-scatter.3.cloned.1.call-start = ((), (), s32[]{:S(2)}) async-start(), calls=%async_computation.2 | async-start | bytes 3538944 | tf_op jit(solution)/shard_map/reduce_scatter | solution.py:448
  10.0 7.5 %copy-start.4 = (f32[4000,128]{1,0:T(8,128)}, f32[4000,128]{1,0:T(8,128)S(1)}, u32[]{:S(2)}) copy-start(f32[4000,128]{1,0:T(8,128)S(1)} %slice_multiply_fusion.x_ref) | copy-start | bytes 6144004
  10.0 51.5 %collective-permute-start.2 = (f32[4000,128]{1,0:T(8,128)S(1)}, f32[4000,128]{1,0:T(8,128)}, u32[]{:S(2)}, u32[]{:S(2)}) collective-permute-start(f32[4000,128]{1,0:T(8,128)S(1)} %slice_multiply_fusion.x_ref), channel_id=1, source_target_pairs={{0,1},{1,2},{2,3},{4,5},{5,6},{6,7},{8,9},{9,10},{10,11},{12,13},{... | collective-permute-start | bytes 6144008 | tf_op jit(solution)/shard_map/ppermute | solution.py:388
  16.2 48.0 %collective-permute-start.1 = (f32[4000,128]{1,0:T(8,128)S(1)}, f32[4000,128]{1,0:T(8,128)}, u32[]{:S(2)}, u32[]{:S(2)}) collective-permute-start(f32[4000,128]{1,0:T(8,128)S(1)} %slice_multiply_fusion.x_ref), channel_id=1, source_target_pairs={{1,0},{2,1},{3,2},{5,4},{6,5},{7,6},{9,8},{10,9},{11,10},{13,12},{... | collective-permute-start | bytes 6144008 | tf_op jit(solution)/shard_map/ppermute | solution.py:388
  61.5 3.2 %collective-permute-start = (f32[4,304,256]{2,1,0:T(8,128)}, f32[4,304,256]{2,1,0:T(8,128)S(1)}, u32[]{:S(2)}, u32[]{:S(2)}) collective-permute-start(f32[4,304,256]{2,1,0:T(8,128)} %get-tuple-element.17), channel_id=1, source_target_pairs={{0,4},{4,0},{8,12},{12,8},{16,20},{20,16},{24,28},{28,24},{1,5},{5... | collective-permute-start | bytes 3735560 | tf_op jit(solution)/shard_map/ppermute | solution.py:409
  64.6 1.0 copy-start.5
  65.7 1.3 copy-start.8
  68.2 10.3 %collective-permute-start.3 = (f32[304,256]{1,0:T(8,128)S(1)}, f32[304,256]{1,0:T(8,128)S(1)}, u32[]{:S(2)}, u32[]{:S(2)}) collective-permute-start(f32[304,256]{1,0:T(8,128)S(1)} %get-tuple-element.30), channel_id=1, source_target_pairs={{0,8},{4,12},{8,0},{12,4},{16,24},{20,28},{24,16},{28,20},{1,9},{5... | collective-permute-start | bytes 933896 | tf_op jit(solution)/shard_map/ppermute | solution.py:409
  69.8 15.6 %collective-permute-start.5 = (f32[304,256]{1,0:T(8,128)S(1)}, f32[304,256]{1,0:T(8,128)S(1)}, u32[]{:S(2)}, u32[]{:S(2)}) collective-permute-start(f32[304,256]{1,0:T(8,128)S(1)} %get-tuple-element.31), channel_id=1, source_target_pairs={{0,24},{4,28},{8,16},{12,20},{16,8},{20,12},{24,0},{28,4},{1,25},{... | collective-permute-start | bytes 933896 | tf_op jit(solution)/shard_map/ppermute | solution.py:409
  71.3 15.5 %collective-permute-start.4 = (f32[304,256]{1,0:T(8,128)S(1)}, f32[304,256]{1,0:T(8,128)S(1)}, u32[]{:S(2)}, u32[]{:S(2)}) collective-permute-start(f32[304,256]{1,0:T(8,128)S(1)} %get-tuple-element.32), channel_id=1, source_target_pairs={{0,16},{4,20},{8,24},{12,28},{16,0},{20,4},{24,8},{28,12},{1,17},{... | collective-permute-start | bytes 933896 | tf_op jit(solution)/shard_map/ppermute | solution.py:409
  71.8 48.9 %collective-permute-start.10 = (f32[4000,128]{1,0:T(8,128)}, f32[4000,128]{1,0:T(8,128)}, u32[]{:S(2)}, u32[]{:S(2)}) collective-permute-start(f32[4000,128]{1,0:T(8,128)} %get-tuple-element.19.refs_1_.refs_0_), channel_id=1, source_target_pairs={{1,0},{2,1},{5,4},{6,5},{9,8},{10,9},{13,12},{14,13},{17,16},{18,1... | collective-permute-start | bytes 6144008 | tf_op jit(solution)/shard_map/ppermute | solution.py:388
  73.1 47.3 %collective-permute-start.11 = (f32[4000,128]{1,0:T(8,128)}, f32[4000,128]{1,0:T(8,128)}, u32[]{:S(2)}, u32[]{:S(2)}) collective-permute-start(f32[4000,128]{1,0:T(8,128)} %get-tuple-element.20.refs_1_.refs_2_), channel_id=1, source_target_pairs={{1,2},{2,3},{5,6},{6,7},{9,10},{10,11},{13,14},{14,15},{17,18},{18... | collective-permute-start | bytes 6144008 | tf_op jit(solution)/shard_map/ppermute | solution.py:388
  88.3 15.1 %copy-start.6 = (f32[256,256]{1,0:T(8,128)}, f32[256,256]{1,0:T(8,128)S(1)}, u32[]{:S(2)}) copy-start(f32[256,256]{1,0:T(8,128)S(1)} %convolution_bitcast_fusion.c_ref) | copy-start | bytes 786436
  88.4 9.5 %collective-permute-start.7 = (f32[304,256]{1,0:T(8,128)S(1)}, f32[304,256]{1,0:T(8,128)S(1)}, u32[]{:S(2)}, u32[]{:S(2)}) collective-permute-start(f32[304,256]{1,0:T(8,128)S(1)} %get-tuple-element.38), channel_id=1, source_target_pairs={{0,16},{4,20},{8,24},{12,28},{16,0},{20,4},{24,8},{28,12},{1,17},{... | collective-permute-start | bytes 933896 | tf_op jit(solution)/shard_map/ppermute | solution.py:409
  88.9 10.2 %collective-permute-start.6 = (f32[304,256]{1,0:T(8,128)S(1)}, f32[304,256]{1,0:T(8,128)S(1)}, u32[]{:S(2)}, u32[]{:S(2)}) collective-permute-start(f32[304,256]{1,0:T(8,128)S(1)} %get-tuple-element.38), channel_id=1, source_target_pairs={{0,8},{4,12},{8,0},{12,4},{16,24},{20,28},{24,16},{28,20},{1,9},{5... | collective-permute-start | bytes 933896 | tf_op jit(solution)/shard_map/ppermute | solution.py:409
  90.4 13.0 %collective-permute-start.8 = (f32[304,256]{1,0:T(8,128)S(1)}, f32[304,256]{1,0:T(8,128)S(1)}, u32[]{:S(2)}, u32[]{:S(2)}) collective-permute-start(f32[304,256]{1,0:T(8,128)S(1)} %get-tuple-element.38), channel_id=1, source_target_pairs={{0,24},{4,28},{8,16},{12,20},{16,8},{20,12},{24,0},{28,4},{1,25},{... | collective-permute-start | bytes 933896 | tf_op jit(solution)/shard_map/ppermute | solution.py:409
  103.5 3.0 %copy-start.2 = (f32[4,304,256]{2,1,0:T(8,128)}, f32[4,304,256]{2,1,0:T(8,128)S(1)}, u32[]{:S(2)}) copy-start(f32[4,304,256]{2,1,0:T(8,128)S(1)} %pad_maximum_fusion.even_ref.refs_4_) | copy-start | bytes 3735556
  103.6 3.0 %collective-permute-start.9 = (f32[4,304,256]{2,1,0:T(8,128)S(1)}, f32[4,304,256]{2,1,0:T(8,128)S(1)}, u32[]{:S(2)}, u32[]{:S(2)}) collective-permute-start(f32[4,304,256]{2,1,0:T(8,128)S(1)} %pad_maximum_fusion.even_ref.refs_4_), channel_id=1, source_target_pairs={{0,4},{4,0},{8,12},{12,8},{16,20},{20,16},{24,28},{28,24},{1,5},{5... | collective-permute-start | bytes 3735560 | tf_op jit(solution)/shard_map/ppermute | solution.py:409
  103.7 113.7 %reduce-scatter.5.cloned.1.call-start = ((), (), s32[]{:S(2)}) async-start(), calls=%async_computation.3 | async-start | bytes 2359296 | tf_op jit(solution)/shard_map/reduce_scatter | solution.py:468
  106.6 1.1 copy-start.3
  120.7 47.2 %collective-permute-start.13 = (f32[4000,128]{1,0:T(8,128)}, f32[4000,128]{1,0:T(8,128)S(1)}, u32[]{:S(2)}, u32[]{:S(2)}) collective-permute-start(f32[4000,128]{1,0:T(8,128)} %get-tuple-element.27.refs_4_.refs_1_), channel_id=1, source_target_pairs={{2,3},{6,7},{10,11},{14,15},{18,19},{22,23},{26,27},{30,31}} | collective-permute-start | bytes 6144008 | tf_op jit(solution)/shard_map/ppermute | solution.py:388
  121.7 48.9 %collective-permute-start.12 = (f32[4000,128]{1,0:T(8,128)}, f32[4000,128]{1,0:T(8,128)}, u32[]{:S(2)}, u32[]{:S(2)}) collective-permute-start(f32[4000,128]{1,0:T(8,128)} %get-tuple-element.22.refs_0_.refs_3_), channel_id=1, source_target_pairs={{1,0},{5,4},{9,8},{13,12},{17,16},{21,20},{25,24},{29,28}} | collective-permute-start | bytes 6144008 | tf_op jit(solution)/shard_map/ppermute | solution.py:388
  167.9 2.6 %copy-start.16 = (f32[4000,128]{1,0:T(8,128)}, f32[4000,128]{1,0:T(8,128)S(1)}, u32[]{:S(2)}) copy-start(f32[4000,128]{1,0:T(8,128)S(1)} %collective-permute-done.13.refs_3_) | copy-start | bytes 6144004
  190.0 11.7 %copy-start.9 = (f32[4,128,256]{2,1,0:T(8,128)S(1)}, f32[4,128,256]{2,1,0:T(8,128)}, u32[]{:S(2)}) copy-start(f32[4,128,256]{2,1,0:T(8,128)} %get-tuple-element.28) | copy-start | bytes 1572868
  190.0 10.9 %collective-permute-start.14 = (f32[4,128,256]{2,1,0:T(8,128)}, f32[4,128,256]{2,1,0:T(8,128)S(1)}, u32[]{:S(2)}, u32[]{:S(2)}) collective-permute-start(f32[4,128,256]{2,1,0:T(8,128)} %get-tuple-element.29.after_ref), channel_id=1, source_target_pairs={{0,4},{4,0},{8,12},{12,8},{16,20},{20,16},{24,28},{28,24},{1,5},{5... | collective-permute-start | bytes 1572872 | tf_op jit(solution)/shard_map/ppermute | solution.py:409
  192.0 14.6 %collective-permute-start.17 = (f32[128,256]{1,0:T(8,128)}, f32[128,256]{1,0:T(8,128)S(1)}, u32[]{:S(2)}, u32[]{:S(2)}) collective-permute-start(f32[128,256]{1,0:T(8,128)} %own_columns.1.refs_1_.refs_0_), channel_id=1, source_target_pairs={{0,3},{1,0},{2,1},{3,2},{4,7},{5,4},{6,5},{7,6},{8,11},{9,8},{10,9... | collective-permute-start | bytes 393224 | tf_op jit(solution)/shard_map/ppermute | solution.py:473
  197.2 14.2 %collective-permute-start.16 = (f32[128,256]{1,0:T(8,128)}, f32[128,256]{1,0:T(8,128)S(1)}, u32[]{:S(2)}, u32[]{:S(2)}) collective-permute-start(f32[128,256]{1,0:T(8,128)} %own_columns.1.refs_1_.refs_0_), channel_id=1, source_target_pairs={{0,2},{1,3},{2,0},{3,1},{4,6},{5,7},{6,4},{7,5},{8,10},{9,11},{10,... | collective-permute-start | bytes 393224 | tf_op jit(solution)/shard_map/ppermute | solution.py:473
  198.9 12.6 %collective-permute-start.15 = (f32[128,256]{1,0:T(8,128)}, f32[128,256]{1,0:T(8,128)S(1)}, u32[]{:S(2)}, u32[]{:S(2)}) collective-permute-start(f32[128,256]{1,0:T(8,128)} %own_columns.1.refs_1_.refs_0_), channel_id=1, source_target_pairs={{0,1},{1,2},{2,3},{3,0},{4,5},{5,6},{6,7},{7,4},{8,9},{9,10},{10,1... | collective-permute-start | bytes 393224 | tf_op jit(solution)/shard_map/ppermute | solution.py:473
  200.9 0.8 copy-start.7
  203.6 13.7 %collective-permute-start.20 = (f32[128,256]{1,0:T(8,128)S(1)}, f32[128,256]{1,0:T(8,128)S(1)}, u32[]{:S(2)}, u32[]{:S(2)}) collective-permute-start(f32[128,256]{1,0:T(8,128)S(1)} %get-tuple-element.33), channel_id=1, source_target_pairs={{0,24},{4,28},{8,16},{12,20},{16,8},{20,12},{24,0},{28,4},{1,25},{... | collective-permute-start | bytes 393224 | tf_op jit(solution)/shard_map/ppermute | solution.py:409
  206.1 11.2 %collective-permute-start.19 = (f32[128,256]{1,0:T(8,128)S(1)}, f32[128,256]{1,0:T(8,128)S(1)}, u32[]{:S(2)}, u32[]{:S(2)}) collective-permute-start(f32[128,256]{1,0:T(8,128)S(1)} %get-tuple-element.34), channel_id=1, source_target_pairs={{0,16},{4,20},{8,24},{12,28},{16,0},{20,4},{24,8},{28,12},{1,17},{... | collective-permute-start | bytes 393224 | tf_op jit(solution)/shard_map/ppermute | solution.py:409
  206.6 4.9 %copy-start.10 = (f32[128,256]{1,0:T(8,128)}, f32[128,256]{1,0:T(8,128)S(1)}, u32[]{:S(2)}) copy-start(f32[128,256]{1,0:T(8,128)S(1)} %collective-permute-done.17.refs_3_) | copy-start | bytes 393220
  206.6 10.7 %collective-permute-start.18 = (f32[128,256]{1,0:T(8,128)S(1)}, f32[128,256]{1,0:T(8,128)S(1)}, u32[]{:S(2)}, u32[]{:S(2)}) collective-permute-start(f32[128,256]{1,0:T(8,128)S(1)} %get-tuple-element.35), channel_id=1, source_target_pairs={{0,8},{4,12},{8,0},{12,4},{16,24},{20,28},{24,16},{28,20},{1,9},{5... | collective-permute-start | bytes 393224 | tf_op jit(solution)/shard_map/ppermute | solution.py:409
  207.7 13.3 %copy-start.1 = (f32[256,256]{1,0:T(8,128)S(1)}, f32[256,256]{1,0:T(8,128)}, u32[]{:S(2)}) copy-start(f32[256,256]{1,0:T(8,128)} %param.6) | copy-start | bytes 786436
  211.5 0.6 copy-start.11
  212.1 0.7 copy-start.12
  217.3 0.7 copy-start.13
  217.3 0.7 copy-start.14
  217.3 0.7 copy-start.15
Sparse Core Ops, SparseCore 0:
  103.8 47.7 reduce-scatter.2
  168.0 48.0 reduce-scatter.4

commit v12 on v11

--- a/solution.py
+++ b/solution.py
@@ -45,7 +45,8 @@
 
 
 def width(columns, wide):
-    return 256 if columns % 256 == 0 and 256 % (columns // wide) == 0 else columns // wide
+    fits = (x for x in (512, 256) if columns % x == 0 and x % (columns // wide) == 0)
+    return next(fits, columns // wide)
 
 
 def whole(shape):
@@ -409,10 +410,23 @@
     return lax.ppermute(x, "wide", [(i, i ^ distance) for i in range(wide)])
 
 
+def add_kernel(even_ref, other_ref, after_ref, *outs):
+    for h, out_ref in enumerate(outs):
+        out_ref[...] = even_ref[h] + other_ref[h]
+
+
 def scatter_terms(even, odd, wide, after):
-    (other,) = gate([swap(odd, wide, 1)], after)
-    sums = [even[h] + other[h] for h in range(wide // 2)]
-    return [sums[0]] + [swap(sums[h], wide, 2 * h) for h in range(1, wide // 2)]
+    count, *shape = even.shape
+    sums = pl.pallas_call(
+        add_kernel,
+        in_specs=[pl.BlockSpec(memory_space=pltpu.VMEM)] * 2 + [ANY],
+        out_specs=[pl.BlockSpec(memory_space=pltpu.VMEM)] * count,
+        out_shape=[jax.ShapeDtypeStruct(shape, F32)] * count,
+        compiler_params=pltpu.CompilerParams(vmem_limit_bytes=VMEM),
+        cost_estimate=SHORT,
+        name="add",
+    )(even, swap(odd, wide, 1), after)
+    return [sums[0]] + [swap(sums[h], wide, 2 * h) for h in range(1, count)]
 
 
 def collect(x, wide, after=()):

time: 229 us -> 229 us (level)
  Pallas kernels: 129 us -> 135 us
  other arithmetic: 8.31 us -> 5.19 us
    pallas_call x0 -> x2, Pallas kernels: none -> 4.78 us  [scatter_terms(): pl.pallas_call(add_kernel, in_specs=[pl.BlockSpec(memory_space=pltpu.VMEM...]
    add x2 -> x0, other arithmetic: 3.11 us -> none  [scatter_terms(): sums = [even[h] + other[h] for h in range(wide // 2)]]
    unnamed x34 -> x30, local copies, waits for them, and re-layouts: 6.21 us -> 4.91 us
  transfers between devices with their start and end apart: 23 -> 23, of which waited for: 12 -> 11; matrix products, arithmetic and copies ran while one was open for 2% -> 2% of each run, Pallas kernels for 55% -> 56%
where the time goes in v12:
time: 229 us; the launch traced here: 228 us
  Pallas kernels  135 us (59%)
  waiting for transfers between devices  35.9 us (16%)
  starting transfers between devices  32.3 us (14%)
  between operations  14.3 us (6%)
  local copies, waits for them, and re-layouts  5.52 us (2%)
  other arithmetic  5.19 us (2%)
    pallas_call x1, Pallas kernels, project(): pl.pallas_call(functools.partial(project_kernel, per, wide), grid_spec=pl...  44.4 us
    pallas_call x2, Pallas kernels, late(): pl.pallas_call(functools.partial(late_kernel, per, counts), grid_spec=plt...  42.8 us
    pallas_call x2, Pallas kernels, update(): pl.pallas_call(update_kernel, grid_spec=pltpu.PrefetchScalarGridSpec(num_...  33.4 us
    ppermute x12, waiting for transfers between devices, swap(): return lax.ppermute(x, 'wide', [(i, i ^ distance) for i in range(wide)])  26.9 us
    ppermute x6, starting transfers between devices, travel(): held = [lax.ppermute(held[d], 'narrow', pairs[d]) for d in (0, 1)]  12.9 us
    ppermute x12, starting transfers between devices, swap(): return lax.ppermute(x, 'wide', [(i, i ^ distance) for i in range(wide)])  10.7 us
    ppermute x3, starting transfers between devices, on_device(): lax.ppermute(mine, 'narrow', [(p, (p + s) % n) for p in range(n)])  8.54 us
    ppermute x6, waiting for transfers between devices, travel(): held = [lax.ppermute(held[d], 'narrow', pairs[d]) for d in (0, 1)]  5.01 us
  transfers between devices with their start and end apart: 23, of which 11 were waited for; matrix products, arithmetic and copies ran while one was open for 2% of the time, Pallas kernels for 56%

profile of v12, /device:TPU:0, one launch (start us, length us, event | category | flops | bytes accessed | tf_op | source)
XLA Modules:
  0.0 228.3 jit_solution(2724327406675596302)
XLA Ops:
  7.2 2.7 %slice_multiply_fusion.x_ref = f32[4000,128]{1,0:T(8,128)S(1)} fusion(f32[4000,2048]{1,0:T(8,128)} %v_ref.5, f32[4000]{0:T(1024)} %param.7), kind=kLoop, calls=%fused_computation | loop fusion | flops 512000 | bytes 4112000 | tf_op jit(solution)/shard_map/mul | solution.py:452
  10.0 6.3 %collective-permute-start.2 = (f32[4000,128]{1,0:T(8,128)S(1)}, f32[4000,128]{1,0:T(8,128)}, u32[]{:S(2)}, u32[]{:S(2)}) collective-permute-start(f32[4000,128]{1,0:T(8,128)S(1)} %slice_multiply_fusion.x_ref), channel_id=1, source_target_pairs={{0,1},{1,2},{2,3},{4,5},{5,6},{6,7},{8,9},{9,10},{10,11},{12,13},{... | collective-permute-start | bytes 6144008 | tf_op jit(solution)/shard_map/ppermute | solution.py:389
  16.3 1.3 collective-permute-start.1
  17.6 44.4 %project.1 = (f32[4,304,256]{2,1,0:T(8,128)}, f32[4,304,256]{2,1,0:T(8,128)}, f32[8,384,256]{2,1,0:T(8,128)}, f32[384,256]{1,0:T(8,128)}) custom-call(s32[1]{0:T(128)} %bitcast.me_ref, f32[4000,2048]{1,0:T(8,128)} %v_ref.5, f32[4000,256]{1,0:T(8,128)} %r_ref.5, f32[1,4000]{1,0:T(1,128)} %bitcast.24, f32[4000,128]{1,0:T(8,128)} %copy-done.4), custom_call_target="tpu_custom_call" | custom-call | flops 1024 | bytes 1024 | tf_op jit(solution)/shard_map/project/pallas_call | solution.py:133
  61.9 2.3 %collective-permute-done.1.refs_0_ = f32[4000,128]{1,0:T(8,128)} collective-permute-done((f32[4000,128]{1,0:T(8,128)S(1)}, f32[4000,128]{1,0:T(8,128)}, u32[]{:S(2)}, u32[]{:S(2)}) %collective-permute-start.1) | collective-permute-done | bytes 2048032 | tf_op jit(solution)/shard_map/ppermute | solution.py:389
  64.3 0.8 collective-permute-done.other_ref
  65.1 1.0 copy-done.6
  66.1 2.7 %add.29 = (f32[304,256]{1,0:T(8,128)}, f32[304,256]{1,0:T(8,128)}, f32[304,256]{1,0:T(8,128)}, f32[304,256]{1,0:T(8,128)}) custom-call(f32[4,304,256]{2,1,0:T(8,128)} %get-tuple-element.24.even_ref, f32[4,304,256]{2,1,0:T(8,128)} %copy-done.6, f32[4000,128]{1,0:T(8,128)} %get-tuple-element.27.after_ref.refs_0_), custom_call_target="tpu_custom_call" | custom-call | flops 1024 | bytes 1024 | tf_op jit(solution)/shard_map/add/pallas_call | solution.py:420
  68.8 1.5 collective-permute-start.3
  70.3 1.5 collective-permute-start.4
  71.8 0.5 collective-permute-start.5
  72.3 1.3 collective-permute-start.10
  73.6 2.0 collective-permute-start.11
  75.6 3.7 %collective-permute-done.3 = f32[304,256]{1,0:T(8,128)S(1)} collective-permute-done((f32[304,256]{1,0:T(8,128)}, f32[304,256]{1,0:T(8,128)S(1)}, u32[]{:S(2)}, u32[]{:S(2)}) %collective-permute-start.3) | collective-permute-done | bytes 311328 | tf_op jit(solution)/shard_map/ppermute | solution.py:410
  79.3 7.1 %collective-permute-done.4 = f32[304,256]{1,0:T(8,128)S(1)} collective-permute-done((f32[304,256]{1,0:T(8,128)}, f32[304,256]{1,0:T(8,128)S(1)}, u32[]{:S(2)}, u32[]{:S(2)}) %collective-permute-start.4) | collective-permute-done | bytes 311328 | tf_op jit(solution)/shard_map/ppermute | solution.py:410
  86.3 1.1 add_add_fusion
  87.9 1.6 collective-permute-start.7
  89.4 0.5 collective-permute-start.6
  90.0 1.4 collective-permute-start.8
  91.4 5.9 %collective-permute-done.7 = f32[304,256]{1,0:T(8,128)S(1)} collective-permute-done((f32[304,256]{1,0:T(8,128)S(1)}, f32[304,256]{1,0:T(8,128)S(1)}, u32[]{:S(2)}, u32[]{:S(2)}) %collective-permute-start.7) | collective-permute-done | bytes 311328 | tf_op jit(solution)/shard_map/ppermute | solution.py:410
  97.3 2.4 %collective-permute-done.6 = f32[304,256]{1,0:T(8,128)S(1)} collective-permute-done((f32[304,256]{1,0:T(8,128)S(1)}, f32[304,256]{1,0:T(8,128)S(1)}, u32[]{:S(2)}, u32[]{:S(2)}) %collective-permute-start.6) | collective-permute-done | bytes 311328 | tf_op jit(solution)/shard_map/ppermute | solution.py:410
  99.7 4.4 %collective-permute-done.8 = f32[304,256]{1,0:T(8,128)S(1)} collective-permute-done((f32[304,256]{1,0:T(8,128)S(1)}, f32[304,256]{1,0:T(8,128)S(1)}, u32[]{:S(2)}, u32[]{:S(2)}) %collective-permute-start.8) | collective-permute-done | bytes 311328 | tf_op jit(solution)/shard_map/ppermute | solution.py:410
  104.6 2.7 %collective-permute-done.9.odd_ref.refs_5_ = f32[4,304,256]{2,1,0:T(8,128)S(1)} collective-permute-done((f32[4,304,256]{2,1,0:T(8,128)S(1)}, f32[4,304,256]{2,1,0:T(8,128)S(1)}, u32[]{:S(2)}, u32[]{:S(2)}) %collective-permute-start.9) | collective-permute-done | bytes 1245216 | tf_op jit(solution)/shard_map/ppermute | solution.py:410
  107.3 1.0 copy-done.3
  108.3 12.8 %update.2 = (f32[4000,2048]{1,0:T(8,128)}, f32[8,128]{1,0:T(8,128)}) custom-call(s32[1]{0:T(128)} %bitcast.me_ref, f32[4000,2048]{1,0:T(8,128)} %v_ref.5, f32[4000,256]{1,0:T(8,128)} %r_ref.5, f32[4,304,256]{2,1,0:T(8,128)} %copy-done.2, f32[4,304,256]{2,1,0:T(8,128)} %copy-done.3), custom_call_target="tpu_custom_call" | custom-call | flops 1024 | bytes 1024 | tf_op jit(solution)/shard_map/update/pallas_call | solution.py:174
  121.2 0.8 collective-permute-start.13
  122.0 1.3 collective-permute-start.12
  123.3 0.6 pad_add_fusion.1.at_ref
  123.9 0.6 pad_add_fusion.at_ref
  124.6 20.6 %update.3 = (f32[4000,2048]{1,0:T(8,128)}, f32[8,128]{1,0:T(8,128)}) custom-call(s32[1]{0:T(128)} %bitcast.me_ref, f32[4000,2048]{1,0:T(8,128)} %v_ref.5, f32[4000,256]{1,0:T(8,128)} %r_ref.5, f32[4,304,256]{2,1,0:T(8,128)} %copy-done.2, f32[4,304,256]{2,1,0:T(8,128)} %copy-done.3, ...), custom_call_target="tpu_custom_call", output_to_operand_aliasing={{0}: (6, {})} | custom-call | flops 1024 | bytes 1024 | tf_op jit(solution)/shard_map/update/pallas_call | solution.py:174
  145.2 23.2 %late.2.refs_1_ = f32[8,256,256]{2,1,0:T(8,128)} custom-call(s32[3]{0:T(128)} %pad_add_fusion.at_ref, f32[4000,2048]{1,0:T(8,128)} %get-tuple-element.22.u_ref, f32[8,128]{1,0:T(8,128)} %get-tuple-element.38.after_ref, f32[4000,128]{1,0:T(8,128)} %get-tuple-element.27.after_ref.refs_0_, f32[4000,128]{1,0:T(8,128)} %get-tuple-element.32.refs_1_.refs_2_, ...), custom_call_target="tpu_custom_call" | custom-call | flops 1024 | bytes 1024 | tf_op jit(solution)/shard_map/late/pallas_call | solution.py:251
  168.5 2.6 %collective-permute-done.12.refs_2_ = f32[4000,128]{1,0:T(8,128)} collective-permute-done((f32[4000,128]{1,0:T(8,128)}, f32[4000,128]{1,0:T(8,128)}, u32[]{:S(2)}, u32[]{:S(2)}) %collective-permute-start.12) | collective-permute-done | bytes 2048032 | tf_op jit(solution)/shard_map/ppermute | solution.py:389
  171.1 19.5 %late.3 = (f32[4,128,256]{2,1,0:T(8,128)}, f32[4,128,256]{2,1,0:T(8,128)}) custom-call(s32[2]{0:T(128)} %pad_add_fusion.1.at_ref, f32[4000,2048]{1,0:T(8,128)} %get-tuple-element.22.u_ref, f32[384,256]{1,0:T(8,128)} %gate.6.after_ref.refs_0_, f32[4000,128]{1,0:T(8,128)} %get-tuple-element.34.refs_0_.refs_3_, f32[4000,128]{1,0:T(8,128)} %get-tuple-element.39.refs_4_.refs_1_, ...), custom_call_target="tpu_custom_call" | custom-call | flops 99999997952 | bytes 1024 | tf_op jit(solution)/shard_map/late/pallas_call | solution.py:251
  190.7 1.8 own_columns.1.after_ref.refs_0_
  192.5 5.2 %collective-permute-start.17 = (f32[128,256]{1,0:T(8,128)}, f32[128,256]{1,0:T(8,128)S(1)}, u32[]{:S(2)}, u32[]{:S(2)}) collective-permute-start(f32[128,256]{1,0:T(8,128)} %own_columns.1.after_ref.refs_0_), channel_id=1, source_target_pairs={{0,3},{1,0},{2,1},{3,2},{4,7},{5,4},{6,5},{7,6},{8,11},{9,8},{10,9... | collective-permute-start | bytes 393224 | tf_op jit(solution)/shard_map/ppermute | solution.py:487
  197.7 1.3 collective-permute-start.16
  199.0 2.0 collective-permute-start.15
  201.0 0.8 copy-done.7
  201.8 2.0 add.30
  203.9 1.5 collective-permute-start.18
  205.4 1.5 collective-permute-start.19
  207.4 0.6 stack.54.at_ref
  208.0 3.9 %collective-permute-done.16.refs_2_ = f32[128,256]{1,0:T(8,128)S(1)} collective-permute-done((f32[128,256]{1,0:T(8,128)}, f32[128,256]{1,0:T(8,128)S(1)}, u32[]{:S(2)}, u32[]{:S(2)}) %collective-permute-start.16) | collective-permute-done | bytes 131104 | tf_op jit(solution)/shard_map/ppermute | solution.py:487
  211.9 0.6 copy-done.9
  212.5 0.7 copy-done.10
  213.2 4.5 %base.1.base_ref = f32[512,256]{1,0:T(8,128)} custom-call(s32[5]{0:T(128)} %stack.54.at_ref, f32[384,256]{1,0:T(8,128)} %gate.7.ready_ref, f32[256,256]{1,0:T(8,128)} %copy-done.5, f32[128,256]{1,0:T(8,128)} %own_columns.1.after_ref.refs_0_, f32[128,256]{1,0:T(8,128)} %copy-done.10, f32[128,256]{1,0:T(8,128)} %copy-done.9, f32[128,256]{1,0:T(8,128)} %copy-done.8, ...), custom_call_target="tpu_custom_call" | custom-call | flops 1024 | bytes 1024 | tf_op jit(solution)/shard_map/base/pallas_call | solution.py:325
  217.7 0.6 copy-done.11
  218.4 3.0 %last.1 = f32[256,512]{1,0:T(8,128)} custom-call(s32[5]{0:T(128)} %stack.54.at_ref, f32[512,256]{1,0:T(8,128)} %base.1.base_ref, f32[256,256]{1,0:T(8,128)} %bitcast.23, f32[128,256]{1,0:T(8,128)} %get-tuple-element.42.refs_1_.refs_0_, f32[128,256]{1,0:T(8,128)} %copy-done.11, f32[128,256]{1,0:T(8,128)} %copy-done.12, f32[128,256]{1,0:T(8,128)} %copy-done.13), custom_call_target="tpu_custom_call" | custom-call | flops 1024 | bytes 1024 | tf_op jit(solution)/shard_map/last/pallas_call | solution.py:356
  (53 shorter events, 1.8 us)
Async XLA Ops:
  7.2 80.2 %copy-start = (f32[256,256]{1,0:T(8,128)S(1)}, f32[256,256]{1,0:T(8,128)}, u32[]{:S(2)}) copy-start(f32[256,256]{1,0:T(8,128)} %param.6) | copy-start | bytes 786436
  7.2 161.3 %reduce-scatter.3.cloned.1.call-start = ((), (), s32[]{:S(2)}) async-start(), calls=%async_computation.2 | async-start | bytes 3538944 | tf_op jit(solution)/shard_map/reduce_scatter | solution.py:462
  10.0 7.6 %copy-start.4 = (f32[4000,128]{1,0:T(8,128)}, f32[4000,128]{1,0:T(8,128)S(1)}, u32[]{:S(2)}) copy-start(f32[4000,128]{1,0:T(8,128)S(1)} %slice_multiply_fusion.x_ref) | copy-start | bytes 6144004
  10.0 51.9 %collective-permute-start.2 = (f32[4000,128]{1,0:T(8,128)S(1)}, f32[4000,128]{1,0:T(8,128)}, u32[]{:S(2)}, u32[]{:S(2)}) collective-permute-start(f32[4000,128]{1,0:T(8,128)S(1)} %slice_multiply_fusion.x_ref), channel_id=1, source_target_pairs={{0,1},{1,2},{2,3},{4,5},{5,6},{6,7},{8,9},{9,10},{10,11},{12,13},{... | collective-permute-start | bytes 6144008 | tf_op jit(solution)/shard_map/ppermute | solution.py:389
  16.3 48.0 %collective-permute-start.1 = (f32[4000,128]{1,0:T(8,128)S(1)}, f32[4000,128]{1,0:T(8,128)}, u32[]{:S(2)}, u32[]{:S(2)}) collective-permute-start(f32[4000,128]{1,0:T(8,128)S(1)} %slice_multiply_fusion.x_ref), channel_id=1, source_target_pairs={{1,0},{2,1},{3,2},{5,4},{6,5},{7,6},{9,8},{10,9},{11,10},{13,12},{... | collective-permute-start | bytes 6144008 | tf_op jit(solution)/shard_map/ppermute | solution.py:389
  61.9 3.2 %collective-permute-start = (f32[4,304,256]{2,1,0:T(8,128)}, f32[4,304,256]{2,1,0:T(8,128)S(1)}, u32[]{:S(2)}, u32[]{:S(2)}) collective-permute-start(f32[4,304,256]{2,1,0:T(8,128)} %get-tuple-element.25), channel_id=1, source_target_pairs={{0,4},{4,0},{8,12},{12,8},{16,20},{20,16},{24,28},{28,24},{1,5},{5... | collective-permute-start | bytes 3735560 | tf_op jit(solution)/shard_map/ppermute | solution.py:410
  65.1 1.0 copy-start.6
  68.8 10.4 %collective-permute-start.3 = (f32[304,256]{1,0:T(8,128)}, f32[304,256]{1,0:T(8,128)S(1)}, u32[]{:S(2)}, u32[]{:S(2)}) collective-permute-start(f32[304,256]{1,0:T(8,128)} %get-tuple-element.29), channel_id=1, source_target_pairs={{0,8},{4,12},{8,0},{12,4},{16,24},{20,28},{24,16},{28,20},{1,9},{5... | collective-permute-start | bytes 933896 | tf_op jit(solution)/shard_map/ppermute | solution.py:410
  70.3 16.0 %collective-permute-start.4 = (f32[304,256]{1,0:T(8,128)}, f32[304,256]{1,0:T(8,128)S(1)}, u32[]{:S(2)}, u32[]{:S(2)}) collective-permute-start(f32[304,256]{1,0:T(8,128)} %get-tuple-element.30), channel_id=1, source_target_pairs={{0,16},{4,20},{8,24},{12,28},{16,0},{20,4},{24,8},{28,12},{1,17},{... | collective-permute-start | bytes 933896 | tf_op jit(solution)/shard_map/ppermute | solution.py:410
  71.8 14.5 %collective-permute-start.5 = (f32[304,256]{1,0:T(8,128)}, f32[304,256]{1,0:T(8,128)S(1)}, u32[]{:S(2)}, u32[]{:S(2)}) collective-permute-start(f32[304,256]{1,0:T(8,128)} %get-tuple-element.31), channel_id=1, source_target_pairs={{0,24},{4,28},{8,16},{12,20},{16,8},{20,12},{24,0},{28,4},{1,25},{... | collective-permute-start | bytes 933896 | tf_op jit(solution)/shard_map/ppermute | solution.py:410
  72.3 48.9 %collective-permute-start.10 = (f32[4000,128]{1,0:T(8,128)}, f32[4000,128]{1,0:T(8,128)}, u32[]{:S(2)}, u32[]{:S(2)}) collective-permute-start(f32[4000,128]{1,0:T(8,128)} %get-tuple-element.27.after_ref.refs_0_), channel_id=1, source_target_pairs={{1,0},{2,1},{5,4},{6,5},{9,8},{10,9},{13,12},{14,13},{17,16},{18,1... | collective-permute-start | bytes 6144008 | tf_op jit(solution)/shard_map/ppermute | solution.py:389
  73.6 47.5 %collective-permute-start.11 = (f32[4000,128]{1,0:T(8,128)}, f32[4000,128]{1,0:T(8,128)}, u32[]{:S(2)}, u32[]{:S(2)}) collective-permute-start(f32[4000,128]{1,0:T(8,128)} %get-tuple-element.32.refs_1_.refs_2_), channel_id=1, source_target_pairs={{1,2},{2,3},{5,6},{6,7},{9,10},{10,11},{13,14},{14,15},{17,18},{18... | collective-permute-start | bytes 6144008 | tf_op jit(solution)/shard_map/ppermute | solution.py:389
  87.8 16.4 %copy-start.5 = (f32[256,256]{1,0:T(8,128)}, f32[256,256]{1,0:T(8,128)S(1)}, u32[]{:S(2)}) copy-start(f32[256,256]{1,0:T(8,128)S(1)} %convolution_bitcast_fusion.c_ref) | copy-start | bytes 786436
  87.9 9.5 %collective-permute-start.7 = (f32[304,256]{1,0:T(8,128)S(1)}, f32[304,256]{1,0:T(8,128)S(1)}, u32[]{:S(2)}, u32[]{:S(2)}) collective-permute-start(f32[304,256]{1,0:T(8,128)S(1)} %get-tuple-element.47), channel_id=1, source_target_pairs={{0,16},{4,20},{8,24},{12,28},{16,0},{20,4},{24,8},{28,12},{1,17},{... | collective-permute-start | bytes 933896 | tf_op jit(solution)/shard_map/ppermute | solution.py:410
  89.4 10.3 %collective-permute-start.6 = (f32[304,256]{1,0:T(8,128)S(1)}, f32[304,256]{1,0:T(8,128)S(1)}, u32[]{:S(2)}, u32[]{:S(2)}) collective-permute-start(f32[304,256]{1,0:T(8,128)S(1)} %get-tuple-element.47), channel_id=1, source_target_pairs={{0,8},{4,12},{8,0},{12,4},{16,24},{20,28},{24,16},{28,20},{1,9},{5... | collective-permute-start | bytes 933896 | tf_op jit(solution)/shard_map/ppermute | solution.py:410
  90.0 14.2 %collective-permute-start.8 = (f32[304,256]{1,0:T(8,128)S(1)}, f32[304,256]{1,0:T(8,128)S(1)}, u32[]{:S(2)}, u32[]{:S(2)}) collective-permute-start(f32[304,256]{1,0:T(8,128)S(1)} %get-tuple-element.47), channel_id=1, source_target_pairs={{0,24},{4,28},{8,16},{12,20},{16,8},{20,12},{24,0},{28,4},{1,25},{... | collective-permute-start | bytes 933896 | tf_op jit(solution)/shard_map/ppermute | solution.py:410
  104.3 3.0 %copy-start.2 = (f32[4,304,256]{2,1,0:T(8,128)}, f32[4,304,256]{2,1,0:T(8,128)S(1)}, u32[]{:S(2)}) copy-start(f32[4,304,256]{2,1,0:T(8,128)S(1)} %pad_maximum_fusion.even_ref.refs_4_) | copy-start | bytes 3735556
  104.3 3.0 %collective-permute-start.9 = (f32[4,304,256]{2,1,0:T(8,128)S(1)}, f32[4,304,256]{2,1,0:T(8,128)S(1)}, u32[]{:S(2)}, u32[]{:S(2)}) collective-permute-start(f32[4,304,256]{2,1,0:T(8,128)S(1)} %pad_maximum_fusion.even_ref.refs_4_), channel_id=1, source_target_pairs={{0,4},{4,0},{8,12},{12,8},{16,20},{20,16},{24,28},{28,24},{1,5},{5... | collective-permute-start | bytes 3735560 | tf_op jit(solution)/shard_map/ppermute | solution.py:410
  104.4 113.3 %reduce-scatter.5.cloned.1.call-start = ((), (), s32[]{:S(2)}) async-start(), calls=%async_computation.3 | async-start | bytes 2359296 | tf_op jit(solution)/shard_map/reduce_scatter | solution.py:482
  107.3 1.0 copy-start.3
  121.2 47.3 %collective-permute-start.13 = (f32[4000,128]{1,0:T(8,128)}, f32[4000,128]{1,0:T(8,128)S(1)}, u32[]{:S(2)}, u32[]{:S(2)}) collective-permute-start(f32[4000,128]{1,0:T(8,128)} %get-tuple-element.39.refs_4_.refs_1_), channel_id=1, source_target_pairs={{2,3},{6,7},{10,11},{14,15},{18,19},{22,23},{26,27},{30,31}} | collective-permute-start | bytes 6144008 | tf_op jit(solution)/shard_map/ppermute | solution.py:389
  122.0 49.1 %collective-permute-start.12 = (f32[4000,128]{1,0:T(8,128)}, f32[4000,128]{1,0:T(8,128)}, u32[]{:S(2)}, u32[]{:S(2)}) collective-permute-start(f32[4000,128]{1,0:T(8,128)} %get-tuple-element.34.refs_0_.refs_3_), channel_id=1, source_target_pairs={{1,0},{5,4},{9,8},{13,12},{17,16},{21,20},{25,24},{29,28}} | collective-permute-start | bytes 6144008 | tf_op jit(solution)/shard_map/ppermute | solution.py:389
  168.5 2.6 %copy-start.14 = (f32[4000,128]{1,0:T(8,128)}, f32[4000,128]{1,0:T(8,128)S(1)}, u32[]{:S(2)}) copy-start(f32[4000,128]{1,0:T(8,128)S(1)} %collective-permute-done.13.refs_3_) | copy-start | bytes 6144004
  190.6 10.5 %collective-permute-start.14 = (f32[4,128,256]{2,1,0:T(8,128)}, f32[4,128,256]{2,1,0:T(8,128)S(1)}, u32[]{:S(2)}, u32[]{:S(2)}) collective-permute-start(f32[4,128,256]{2,1,0:T(8,128)} %get-tuple-element.41.after_ref), channel_id=1, source_target_pairs={{0,4},{4,0},{8,12},{12,8},{16,20},{20,16},{24,28},{28,24},{1,5},{5... | collective-permute-start | bytes 1572872 | tf_op jit(solution)/shard_map/ppermute | solution.py:410
  192.5 14.4 %collective-permute-start.17 = (f32[128,256]{1,0:T(8,128)}, f32[128,256]{1,0:T(8,128)S(1)}, u32[]{:S(2)}, u32[]{:S(2)}) collective-permute-start(f32[128,256]{1,0:T(8,128)} %own_columns.1.after_ref.refs_0_), channel_id=1, source_target_pairs={{0,3},{1,0},{2,1},{3,2},{4,7},{5,4},{6,5},{7,6},{8,11},{9,8},{10,9... | collective-permute-start | bytes 393224 | tf_op jit(solution)/shard_map/ppermute | solution.py:487
  197.7 14.1 %collective-permute-start.16 = (f32[128,256]{1,0:T(8,128)}, f32[128,256]{1,0:T(8,128)S(1)}, u32[]{:S(2)}, u32[]{:S(2)}) collective-permute-start(f32[128,256]{1,0:T(8,128)} %own_columns.1.after_ref.refs_0_), channel_id=1, source_target_pairs={{0,2},{1,3},{2,0},{3,1},{4,6},{5,7},{6,4},{7,5},{8,10},{9,11},{10,... | collective-permute-start | bytes 393224 | tf_op jit(solution)/shard_map/ppermute | solution.py:487
  199.0 12.8 %collective-permute-start.15 = (f32[128,256]{1,0:T(8,128)}, f32[128,256]{1,0:T(8,128)S(1)}, u32[]{:S(2)}, u32[]{:S(2)}) collective-permute-start(f32[128,256]{1,0:T(8,128)} %own_columns.1.after_ref.refs_0_), channel_id=1, source_target_pairs={{0,1},{1,2},{2,3},{3,0},{4,5},{5,6},{6,7},{7,4},{8,9},{9,10},{10,1... | collective-permute-start | bytes 393224 | tf_op jit(solution)/shard_map/ppermute | solution.py:487
  201.0 0.8 copy-start.7
  203.9 13.8 %collective-permute-start.18 = (f32[128,256]{1,0:T(8,128)}, f32[128,256]{1,0:T(8,128)S(1)}, u32[]{:S(2)}, u32[]{:S(2)}) collective-permute-start(f32[128,256]{1,0:T(8,128)} %get-tuple-element.43), channel_id=1, source_target_pairs={{0,8},{4,12},{8,0},{12,4},{16,24},{20,28},{24,16},{28,20},{1,9},{5... | collective-permute-start | bytes 393224 | tf_op jit(solution)/shard_map/ppermute | solution.py:410
  205.4 12.2 %collective-permute-start.19 = (f32[128,256]{1,0:T(8,128)}, f32[128,256]{1,0:T(8,128)S(1)}, u32[]{:S(2)}, u32[]{:S(2)}) collective-permute-start(f32[128,256]{1,0:T(8,128)} %get-tuple-element.44), channel_id=1, source_target_pairs={{0,16},{4,20},{8,24},{12,28},{16,0},{20,4},{24,8},{28,12},{1,17},{... | collective-permute-start | bytes 393224 | tf_op jit(solution)/shard_map/ppermute | solution.py:410
  206.9 5.0 %copy-start.8 = (f32[128,256]{1,0:T(8,128)}, f32[128,256]{1,0:T(8,128)S(1)}, u32[]{:S(2)}) copy-start(f32[128,256]{1,0:T(8,128)S(1)} %collective-permute-done.17.refs_3_) | copy-start | bytes 393220
  206.9 10.8 %collective-permute-start.20 = (f32[128,256]{1,0:T(8,128)}, f32[128,256]{1,0:T(8,128)S(1)}, u32[]{:S(2)}, u32[]{:S(2)}) collective-permute-start(f32[128,256]{1,0:T(8,128)} %get-tuple-element.45), channel_id=1, source_target_pairs={{0,24},{4,28},{8,16},{12,20},{16,8},{20,12},{24,0},{28,4},{1,25},{... | collective-permute-start | bytes 393224 | tf_op jit(solution)/shard_map/ppermute | solution.py:410
  208.0 13.5 %copy-start.1 = (f32[256,256]{1,0:T(8,128)S(1)}, f32[256,256]{1,0:T(8,128)}, u32[]{:S(2)}) copy-start(f32[256,256]{1,0:T(8,128)} %param.6) | copy-start | bytes 786436
  211.8 0.7 copy-start.9
  212.5 0.7 copy-start.10
  217.6 0.6 copy-start.11
  217.6 0.7 copy-start.12
  217.7 0.7 copy-start.13
Sparse Core Ops, SparseCore 0:
  104.5 47.7 reduce-scatter.2
  168.5 48.6 reduce-scatter.4

commit v13 on v11

--- a/solution.py
+++ b/solution.py
@@ -10,6 +10,7 @@
 FB = 512
 OFF = 256
 VMEM = 60 * 1024 * 1024
+LESS = 29 * 1024 * 1024
 
 F32 = jnp.float32
 BF16 = jnp.bfloat16
@@ -38,9 +39,9 @@
     return top[:m] + top[m:] + mul(high, rl)
 
 
-def params():
+def params(limit=VMEM):
     return pltpu.CompilerParams(
-        dimension_semantics=("arbitrary",), vmem_limit_bytes=VMEM
+        dimension_semantics=("arbitrary",), vmem_limit_bytes=limit
     )
 
 
@@ -67,6 +68,7 @@
         out_specs=[ANY] * count,
         out_shape=[jax.ShapeDtypeStruct(x.shape, x.dtype) for x in held],
         input_output_aliases={k: k for k in range(count)},
+        compiler_params=pltpu.CompilerParams(vmem_limit_bytes=2**20),
         cost_estimate=cost,
         name="gate",
     )(*held, *others)
@@ -192,7 +194,7 @@
             jax.ShapeDtypeStruct((8, 128), F32),
         ],
         input_output_aliases={len(operands) - 1: 0} if before else {},
-        compiler_params=params(),
+        compiler_params=params(LESS),
         cost_estimate=SHORT,
         name="update",
     )(*operands)
@@ -261,7 +263,7 @@
             ],
         ),
         out_shape=[jax.ShapeDtypeStruct(x, F32) for x in shapes],
-        compiler_params=params(),
+        compiler_params=params(LESS),
         cost_estimate=SHORT if ordered else LONG,
         name="late",
     )(at, updated, after, *flat)
@@ -455,20 +457,20 @@
         payload = jnp.concatenate([coefficients, projected[nb:]], axis=0)
     c = collect(payload, wide)
 
-    of = next(x for x in range(4, rows) if rows % (16 * x) == 0)
-    updated, token = update(me, vectors, reflectors, c, 0, of // 2, of, [], [])
+    of = next(x for x in range(10, rows) if rows % (16 * x) == 0)
+    updated, token = update(me, vectors, reflectors, c, 0, of * 2 // 5, of, [], [])
     for hops in range(3, n):
         held = travel(came, held, n, hops, [token])
     updated, token = update(
-        me, vectors, reflectors, c, of // 2, of - of // 2, of, [came[(n - 2, 0)]], [updated]
+        me, vectors, reflectors, c, of * 2 // 5, of - of * 2 // 5, of, [came[(n - 2, 0)]], [updated]
     )
 
     slots = [options(came, places, z) for places in table]
     (middle,) = late(me, updated, slots[:-1], token, wide, True)
     middle_sum = lax.psum_scatter(middle, "wide", scatter_dimension=0)
-    (ready,) = gate([ready], middle)
+    mine = own_columns(me, c, middle, nb, each)
+    (ready,) = gate([ready], middle, mine)
     even, odd = late(me, updated, slots[-1:], ready, wide, False)
-    mine = own_columns(me, c, odd, nb, each)
     coef = [mine] + [
         lax.ppermute(mine, "narrow", [(p, (p + s) % n) for p in range(n)]) for s in range(1, n)
     ]

time: 229 us -> 228 us (level)
  local copies, waits for them, and re-layouts: 6.9 us -> 14.1 us
  other arithmetic: 8.31 us -> 3.34 us
  waiting for transfers between devices: 36 us -> 33.2 us
  starting transfers between devices: 32.8 us -> 35.2 us
    unnamed x34 -> x48, local copies, waits for them, and re-layouts: 6.21 us -> 13.5 us
    add x2, other arithmetic: 3.11 us -> 0.2 us  [scatter_terms(): sums = [even[h] + other[h] for h in range(wide // 2)]]
    ppermute x6, waiting for transfers between devices: 5.64 us -> 2.9 us  [travel(): held = [lax.ppermute(held[d], 'narrow', pairs[d]) for d in (0, 1)]]
  transfers between devices with their start and end apart: 23 -> 23, of which waited for: 12 -> 9; matrix products, arithmetic and copies ran while one was open for 2% -> 1% of each run, Pallas kernels for 55% -> 54%
where the time goes in v13:
time: 228 us; the launch traced here: 227 us
  Pallas kernels  127 us (56%)
  starting transfers between devices  35.2 us (15%)
  waiting for transfers between devices  33.2 us (15%)
  between operations  14.4 us (6%)
  local copies, waits for them, and re-layouts  14.1 us (6%)
  other arithmetic  3.34 us (1%)
    pallas_call x1, Pallas kernels, project(): pl.pallas_call(functools.partial(project_kernel, per, wide), grid_spec=pl...  43.9 us
    pallas_call x2, Pallas kernels, late(): pl.pallas_call(functools.partial(late_kernel, per, counts), grid_spec=plt...  41.2 us
    pallas_call x2, Pallas kernels, update(): pl.pallas_call(update_kernel, grid_spec=pltpu.PrefetchScalarGridSpec(num_...  32.1 us
    ppermute x12, waiting for transfers between devices, swap(): return lax.ppermute(x, 'wide', [(i, i ^ distance) for i in range(wide)])  24.8 us
    ppermute x6, starting transfers between devices, travel(): held = [lax.ppermute(held[d], 'narrow', pairs[d]) for d in (0, 1)]  14.3 us
    unnamed x48, local copies, waits for them, and re-layouts  13.5 us
    ppermute x12, starting transfers between devices, swap(): return lax.ppermute(x, 'wide', [(i, i ^ distance) for i in range(wide)])  10.8 us
    ppermute x3, starting transfers between devices, on_device(): lax.ppermute(mine, 'narrow', [(p, (p + s) % n) for p in range(n)])  10 us
  transfers between devices with their start and end apart: 23, of which 9 were waited for; matrix products, arithmetic and copies ran while one was open for 1% of the time, Pallas kernels for 54%

profile of v13, /device:TPU:0, one launch (start us, length us, event | category | flops | bytes accessed | tf_op | source)
XLA Modules:
  0.0 227.3 jit_solution(9385289764284901411)
XLA Ops:
  7.2 2.7 %slice_multiply_fusion.x_ref = f32[4000,128]{1,0:T(8,128)S(1)} fusion(f32[4000,2048]{1,0:T(8,128)} %v_ref.5, f32[4000]{0:T(1024)} %param.7), kind=kLoop, calls=%fused_computation | loop fusion | flops 512000 | bytes 4112000 | tf_op jit(solution)/shard_map/mul | solution.py:440
  10.0 6.3 %collective-permute-start.2 = (f32[4000,128]{1,0:T(8,128)S(1)}, f32[4000,128]{1,0:T(8,128)}, u32[]{:S(2)}, u32[]{:S(2)}) collective-permute-start(f32[4000,128]{1,0:T(8,128)S(1)} %slice_multiply_fusion.x_ref), channel_id=1, source_target_pairs={{0,1},{1,2},{2,3},{4,5},{5,6},{6,7},{8,9},{9,10},{10,11},{12,13},{... | collective-permute-start | bytes 6144008 | tf_op jit(solution)/shard_map/ppermute | solution.py:390
  16.3 1.3 collective-permute-start.1
  17.6 43.9 %project.1 = (f32[4,304,256]{2,1,0:T(8,128)}, f32[4,304,256]{2,1,0:T(8,128)}, f32[8,384,256]{2,1,0:T(8,128)}, f32[384,256]{1,0:T(8,128)}) custom-call(s32[1]{0:T(128)} %bitcast.me_ref, f32[4000,2048]{1,0:T(8,128)} %v_ref.5, f32[4000,256]{1,0:T(8,128)} %r_ref.5, f32[1,4000]{1,0:T(1,128)} %bitcast.46, f32[4000,128]{1,0:T(8,128)} %copy-done.15), custom_call_target="tpu_custom_call" | custom-call | flops 1024 | bytes 1024 | tf_op jit(solution)/shard_map/project/pallas_call | solution.py:134
  61.5 2.8 %collective-permute-done.1.refs_0_ = f32[4000,128]{1,0:T(8,128)} collective-permute-done((f32[4000,128]{1,0:T(8,128)S(1)}, f32[4000,128]{1,0:T(8,128)}, u32[]{:S(2)}, u32[]{:S(2)}) %collective-permute-start.1) | collective-permute-done | bytes 2048032 | tf_op jit(solution)/shard_map/ppermute | solution.py:390
  64.3 1.0 copy-done.14
  65.3 1.3 copy-done.17
  66.7 1.6 collective-permute-start.3
  68.3 1.5 collective-permute-start.5
  69.8 0.5 collective-permute-start.4
  70.3 1.3 collective-permute-start.10
  71.6 2.0 collective-permute-start.11
  73.6 3.5 %collective-permute-done.3 = f32[304,256]{1,0:T(8,128)S(1)} collective-permute-done((f32[304,256]{1,0:T(8,128)S(1)}, f32[304,256]{1,0:T(8,128)S(1)}, u32[]{:S(2)}, u32[]{:S(2)}) %collective-permute-start.3) | collective-permute-done | bytes 311328 | tf_op jit(solution)/shard_map/ppermute | solution.py:411
  77.1 6.2 %collective-permute-done.5 = f32[304,256]{1,0:T(8,128)S(1)} collective-permute-done((f32[304,256]{1,0:T(8,128)S(1)}, f32[304,256]{1,0:T(8,128)S(1)}, u32[]{:S(2)}, u32[]{:S(2)}) %collective-permute-start.5) | collective-permute-done | bytes 311328 | tf_op jit(solution)/shard_map/ppermute | solution.py:411
  83.3 1.4 collective-permute-done.4
  85.3 0.6 collective-permute-start.7
  85.8 1.5 collective-permute-start.6
  87.3 1.5 collective-permute-start.8
  88.8 6.7 %collective-permute-done.7 = f32[304,256]{1,0:T(8,128)S(1)} collective-permute-done((f32[304,256]{1,0:T(8,128)S(1)}, f32[304,256]{1,0:T(8,128)S(1)}, u32[]{:S(2)}, u32[]{:S(2)}) %collective-permute-start.7) | collective-permute-done | bytes 311328 | tf_op jit(solution)/shard_map/ppermute | solution.py:411
  95.6 4.1 %collective-permute-done.8 = f32[304,256]{1,0:T(8,128)S(1)} collective-permute-done((f32[304,256]{1,0:T(8,128)S(1)}, f32[304,256]{1,0:T(8,128)S(1)}, u32[]{:S(2)}, u32[]{:S(2)}) %collective-permute-start.8) | collective-permute-done | bytes 311328 | tf_op jit(solution)/shard_map/ppermute | solution.py:411
  99.9 2.9 %collective-permute-done.9.odd_ref.refs_5_ = f32[4,304,256]{2,1,0:T(8,128)S(1)} collective-permute-done((f32[4,304,256]{2,1,0:T(8,128)S(1)}, f32[4,304,256]{2,1,0:T(8,128)S(1)}, u32[]{:S(2)}, u32[]{:S(2)}) %collective-permute-start.9) | collective-permute-done | bytes 1245216 | tf_op jit(solution)/shard_map/ppermute | solution.py:411
  102.8 2.2 copy-done.2
  104.9 13.5 %update.2 = (f32[4000,2048]{1,0:T(8,128)}, f32[8,128]{1,0:T(8,128)S(1)}) custom-call(s32[1]{0:T(128)} %bitcast.me_ref, f32[4000,2048]{1,0:T(8,128)} %v_ref.5, f32[4000,256]{1,0:T(8,128)S(1)} %copy-done.2, f32[4,304,256]{2,1,0:T(8,128)S(1)} %pad_maximum_fusion.even_ref.refs_4_, f32[4,304,256]{2,1,0:T(8,128)S(1)} %collective-permute-done.9.odd_ref.refs_5_), custom_call_target="tpu_custom_call" | custom-call | flops 1024 | bytes 1024 | tf_op jit(solution)/shard_map/update/pallas_call | solution.py:175
  118.5 2.0 collective-permute-start.13
  120.6 1.5 collective-permute-start.12
  122.2 2.7 %copy-done.3 = f32[4000,256]{1,0:T(8,128)S(1)} copy-done((f32[4000,256]{1,0:T(8,128)S(1)}, f32[4000,256]{1,0:T(8,128)}, u32[]{:S(2)}) %copy-start.3) | copy-done | bytes 4096024
  124.9 18.6 %update.3 = (f32[4000,2048]{1,0:T(8,128)}, f32[8,128]{1,0:T(8,128)S(1)}) custom-call(s32[1]{0:T(128)} %bitcast.me_ref, f32[4000,2048]{1,0:T(8,128)} %v_ref.5, f32[4000,256]{1,0:T(8,128)S(1)} %copy-done.3, f32[4,304,256]{2,1,0:T(8,128)S(1)} %pad_maximum_fusion.even_ref.refs_4_, ...), custom_call_target="tpu_custom_call", output_to_operand_aliasing={{0}: (6, {})} | custom-call | flops 1024 | bytes 1024 | tf_op jit(solution)/shard_map/update/pallas_call | solution.py:175
  143.5 22.9 %late.2.after_ref.refs_1_ = f32[8,256,256]{2,1,0:T(8,128)} custom-call(s32[3]{0:T(128)S(1)} %pad_add_fusion.at_ref, f32[4000,2048]{1,0:T(8,128)} %get-tuple-element.14.u_ref, f32[8,128]{1,0:T(8,128)S(1)} %get-tuple-element.26.after_ref, f32[4000,128]{1,0:T(8,128)} %get-tuple-element.19.refs_1_.refs_0_, f32[4000,128]{1,0:T(8,128)} %get-tuple-element.20.refs_1_.refs_2_, ...), custom_call_target="tpu_custom_call" | custom-call | flops 1024 | bytes 1024 | tf_op jit(solution)/shard_map/late/pallas_call | solution.py:252
  166.4 1.8 own_columns.1.refs_2_.refs_1_.refs_0_
  168.3 1.0 copy-done.6
  169.3 0.9 copy-done.11
  170.2 0.7 copy-done.7
  170.9 1.0 copy-done.8
  171.9 18.3 %late.3 = (f32[4,128,256]{2,1,0:T(8,128)S(1)}, f32[4,128,256]{2,1,0:T(8,128)S(1)}) custom-call(s32[2]{0:T(128)S(1)} %pad_add_fusion.1.at_ref, f32[4000,2048]{1,0:T(8,128)} %get-tuple-element.14.u_ref, f32[384,256]{1,0:T(8,128)S(1)} %copy-done.8, f32[4000,128]{1,0:T(8,128)} %get-tuple-element.22.refs_0_.refs_3_, ...), custom_call_target="tpu_custom_call" | custom-call | flops 99999997952 | bytes 1024 | tf_op jit(solution)/shard_map/late/pallas_call | solution.py:252
  190.3 5.2 %collective-permute-start.17 = (f32[128,256]{1,0:T(8,128)S(1)}, f32[128,256]{1,0:T(8,128)S(1)}, u32[]{:S(2)}, u32[]{:S(2)}) collective-permute-start(f32[128,256]{1,0:T(8,128)S(1)} %copy-done.12), channel_id=1, source_target_pairs={{0,3},{1,0},{2,1},{3,2},{4,7},{5,4},{6,5},{7,6},{8,11},{9,8},{10,9... | collective-permute-start | bytes 393224 | tf_op jit(solution)/shard_map/ppermute | solution.py:475
  195.5 2.9 %collective-permute-start.16 = (f32[128,256]{1,0:T(8,128)S(1)}, f32[128,256]{1,0:T(8,128)S(1)}, u32[]{:S(2)}, u32[]{:S(2)}) collective-permute-start(f32[128,256]{1,0:T(8,128)S(1)} %copy-done.12), channel_id=1, source_target_pairs={{0,2},{1,3},{2,0},{3,1},{4,6},{5,7},{6,4},{7,5},{8,10},{9,11},{10,... | collective-permute-start | bytes 393224 | tf_op jit(solution)/shard_map/ppermute | solution.py:475
  198.4 1.9 collective-permute-start.15
  200.4 2.6 %collective-permute-start.20 = (f32[128,256]{1,0:T(8,128)S(1)}, f32[128,256]{1,0:T(8,128)S(1)}, u32[]{:S(2)}, u32[]{:S(2)}) collective-permute-start(f32[128,256]{1,0:T(8,128)S(1)} %get-tuple-element.33), channel_id=1, source_target_pairs={{0,24},{4,28},{8,16},{12,20},{16,8},{20,12},{24,0},{28,4},{1,25},{... | collective-permute-start | bytes 393224 | tf_op jit(solution)/shard_map/ppermute | solution.py:411
  203.0 0.6 collective-permute-start.19
  203.6 0.4 collective-permute-start.18
  204.0 0.6 stack.54.at_ref
  204.6 0.7 copy-done.10
  205.4 5.5 %collective-permute-done.16.refs_2_ = f32[128,256]{1,0:T(8,128)S(1)} collective-permute-done((f32[128,256]{1,0:T(8,128)S(1)}, f32[128,256]{1,0:T(8,128)S(1)}, u32[]{:S(2)}, u32[]{:S(2)}) %collective-permute-start.16) | collective-permute-done | bytes 131104 | tf_op jit(solution)/shard_map/ppermute | solution.py:475
  210.9 0.7 copy-done.19
  211.5 0.7 copy-done.20
  212.2 4.5 %base.1.base_ref = f32[512,256]{1,0:T(8,128)} custom-call(s32[5]{0:T(128)} %stack.54.at_ref, f32[384,256]{1,0:T(8,128)} %copy-done.10, f32[256,256]{1,0:T(8,128)} %copy-done.16, f32[128,256]{1,0:T(8,128)} %own_columns.1.refs_2_.refs_1_.refs_0_, f32[128,256]{1,0:T(8,128)} %copy-done.20, f32[128,256]{1,0:T(8,128)} %copy-done.19, f32[128,256]{1,0:T(8,128)} %copy-done.18, ...), custom_call_target="tpu_custom_call" | custom-call | flops 1024 | bytes 1024 | tf_op jit(solution)/shard_map/base/pallas_call | solution.py:326
  216.7 0.6 copy-done.21
  217.4 3.0 %last.1 = f32[256,512]{1,0:T(8,128)} custom-call(s32[5]{0:T(128)} %stack.54.at_ref, f32[512,256]{1,0:T(8,128)} %base.1.base_ref, f32[256,256]{1,0:T(8,128)} %bitcast.45, f32[128,256]{1,0:T(8,128)} %copy-done.13, f32[128,256]{1,0:T(8,128)} %copy-done.23, f32[128,256]{1,0:T(8,128)} %copy-done.22, f32[128,256]{1,0:T(8,128)} %copy-done.21), custom_call_target="tpu_custom_call" | custom-call | flops 1024 | bytes 1024 | tf_op jit(solution)/shard_map/last/pallas_call | solution.py:357
  (73 shorter events, 1.6 us)
Async XLA Ops:
  7.2 77.6 %copy-start = (f32[256,256]{1,0:T(8,128)S(1)}, f32[256,256]{1,0:T(8,128)}, u32[]{:S(2)}) copy-start(f32[256,256]{1,0:T(8,128)} %param.6) | copy-start | bytes 786436
  7.2 161.1 %reduce-scatter.3.cloned.1.call-start = ((), (), s32[]{:S(2)}) async-start(), calls=%async_computation.2 | async-start | bytes 3538944 | tf_op jit(solution)/shard_map/reduce_scatter | solution.py:450
  10.0 7.6 %copy-start.15 = (f32[4000,128]{1,0:T(8,128)}, f32[4000,128]{1,0:T(8,128)S(1)}, u32[]{:S(2)}) copy-start(f32[4000,128]{1,0:T(8,128)S(1)} %slice_multiply_fusion.x_ref) | copy-start | bytes 6144004
  10.0 51.5 %collective-permute-start.2 = (f32[4000,128]{1,0:T(8,128)S(1)}, f32[4000,128]{1,0:T(8,128)}, u32[]{:S(2)}, u32[]{:S(2)}) collective-permute-start(f32[4000,128]{1,0:T(8,128)S(1)} %slice_multiply_fusion.x_ref), channel_id=1, source_target_pairs={{0,1},{1,2},{2,3},{4,5},{5,6},{6,7},{8,9},{9,10},{10,11},{12,13},{... | collective-permute-start | bytes 6144008 | tf_op jit(solution)/shard_map/ppermute | solution.py:390
  16.3 48.0 %collective-permute-start.1 = (f32[4000,128]{1,0:T(8,128)S(1)}, f32[4000,128]{1,0:T(8,128)}, u32[]{:S(2)}, u32[]{:S(2)}) collective-permute-start(f32[4000,128]{1,0:T(8,128)S(1)} %slice_multiply_fusion.x_ref), channel_id=1, source_target_pairs={{1,0},{2,1},{3,2},{5,4},{6,5},{7,6},{9,8},{10,9},{11,10},{13,12},{... | collective-permute-start | bytes 6144008 | tf_op jit(solution)/shard_map/ppermute | solution.py:390
  61.5 3.8 %collective-permute-start = (f32[4,304,256]{2,1,0:T(8,128)}, f32[4,304,256]{2,1,0:T(8,128)S(1)}, u32[]{:S(2)}, u32[]{:S(2)}) collective-permute-start(f32[4,304,256]{2,1,0:T(8,128)} %get-tuple-element.17), channel_id=1, source_target_pairs={{0,4},{4,0},{8,12},{12,8},{16,20},{20,16},{24,28},{28,24},{1,5},{5... | collective-permute-start | bytes 3735560 | tf_op jit(solution)/shard_map/ppermute | solution.py:411
  64.3 1.0 copy-start.14
  65.3 1.3 copy-start.17
  66.7 10.4 %collective-permute-start.3 = (f32[304,256]{1,0:T(8,128)S(1)}, f32[304,256]{1,0:T(8,128)S(1)}, u32[]{:S(2)}, u32[]{:S(2)}) collective-permute-start(f32[304,256]{1,0:T(8,128)S(1)} %get-tuple-element.30), channel_id=1, source_target_pairs={{0,8},{4,12},{8,0},{12,4},{16,24},{20,28},{24,16},{28,20},{1,9},{5... | collective-permute-start | bytes 933896 | tf_op jit(solution)/shard_map/ppermute | solution.py:411
  68.3 15.0 %collective-permute-start.5 = (f32[304,256]{1,0:T(8,128)S(1)}, f32[304,256]{1,0:T(8,128)S(1)}, u32[]{:S(2)}, u32[]{:S(2)}) collective-permute-start(f32[304,256]{1,0:T(8,128)S(1)} %get-tuple-element.31), channel_id=1, source_target_pairs={{0,24},{4,28},{8,16},{12,20},{16,8},{20,12},{24,0},{28,4},{1,25},{... | collective-permute-start | bytes 933896 | tf_op jit(solution)/shard_map/ppermute | solution.py:411
  69.8 14.9 %collective-permute-start.4 = (f32[304,256]{1,0:T(8,128)S(1)}, f32[304,256]{1,0:T(8,128)S(1)}, u32[]{:S(2)}, u32[]{:S(2)}) collective-permute-start(f32[304,256]{1,0:T(8,128)S(1)} %get-tuple-element.32), channel_id=1, source_target_pairs={{0,16},{4,20},{8,24},{12,28},{16,0},{20,4},{24,8},{28,12},{1,17},{... | collective-permute-start | bytes 933896 | tf_op jit(solution)/shard_map/ppermute | solution.py:411
  70.3 48.3 %collective-permute-start.10 = (f32[4000,128]{1,0:T(8,128)}, f32[4000,128]{1,0:T(8,128)}, u32[]{:S(2)}, u32[]{:S(2)}) collective-permute-start(f32[4000,128]{1,0:T(8,128)} %get-tuple-element.19.refs_1_.refs_0_), channel_id=1, source_target_pairs={{1,0},{2,1},{5,4},{6,5},{9,8},{10,9},{13,12},{14,13},{17,16},{18,1... | collective-permute-start | bytes 6144008 | tf_op jit(solution)/shard_map/ppermute | solution.py:390
  71.6 46.8 %collective-permute-start.11 = (f32[4000,128]{1,0:T(8,128)}, f32[4000,128]{1,0:T(8,128)}, u32[]{:S(2)}, u32[]{:S(2)}) collective-permute-start(f32[4000,128]{1,0:T(8,128)} %get-tuple-element.20.refs_1_.refs_2_), channel_id=1, source_target_pairs={{1,2},{2,3},{5,6},{6,7},{9,10},{10,11},{13,14},{14,15},{17,18},{18... | collective-permute-start | bytes 6144008 | tf_op jit(solution)/shard_map/ppermute | solution.py:390
  85.2 14.4 %copy-start.16 = (f32[256,256]{1,0:T(8,128)}, f32[256,256]{1,0:T(8,128)S(1)}, u32[]{:S(2)}) copy-start(f32[256,256]{1,0:T(8,128)S(1)} %convolution_bitcast_fusion.c_ref) | copy-start | bytes 786436
  85.3 10.3 %collective-permute-start.7 = (f32[304,256]{1,0:T(8,128)S(1)}, f32[304,256]{1,0:T(8,128)S(1)}, u32[]{:S(2)}, u32[]{:S(2)}) collective-permute-start(f32[304,256]{1,0:T(8,128)S(1)} %get-tuple-element.38), channel_id=1, source_target_pairs={{0,16},{4,20},{8,24},{12,28},{16,0},{20,4},{24,8},{28,12},{1,17},{... | collective-permute-start | bytes 933896 | tf_op jit(solution)/shard_map/ppermute | solution.py:411
  85.8 9.7 %collective-permute-start.6 = (f32[304,256]{1,0:T(8,128)S(1)}, f32[304,256]{1,0:T(8,128)S(1)}, u32[]{:S(2)}, u32[]{:S(2)}) collective-permute-start(f32[304,256]{1,0:T(8,128)S(1)} %get-tuple-element.38), channel_id=1, source_target_pairs={{0,8},{4,12},{8,0},{12,4},{16,24},{20,28},{24,16},{28,20},{1,9},{5... | collective-permute-start | bytes 933896 | tf_op jit(solution)/shard_map/ppermute | solution.py:411
  87.3 12.3 %collective-permute-start.8 = (f32[304,256]{1,0:T(8,128)S(1)}, f32[304,256]{1,0:T(8,128)S(1)}, u32[]{:S(2)}, u32[]{:S(2)}) collective-permute-start(f32[304,256]{1,0:T(8,128)S(1)} %get-tuple-element.38), channel_id=1, source_target_pairs={{0,24},{4,28},{8,16},{12,20},{16,8},{20,12},{24,0},{28,4},{1,25},{... | collective-permute-start | bytes 933896 | tf_op jit(solution)/shard_map/ppermute | solution.py:411
  99.7 22.5 %copy-start.4 = (f32[4,304,256]{2,1,0:T(8,128)}, f32[4,304,256]{2,1,0:T(8,128)S(1)}, u32[]{:S(2)}) copy-start(f32[4,304,256]{2,1,0:T(8,128)S(1)} %pad_maximum_fusion.even_ref.refs_4_) | copy-start | bytes 3735556
  99.7 3.0 %collective-permute-start.9 = (f32[4,304,256]{2,1,0:T(8,128)S(1)}, f32[4,304,256]{2,1,0:T(8,128)S(1)}, u32[]{:S(2)}, u32[]{:S(2)}) collective-permute-start(f32[4,304,256]{2,1,0:T(8,128)S(1)} %pad_maximum_fusion.even_ref.refs_4_), channel_id=1, source_target_pairs={{0,4},{4,0},{8,12},{12,8},{16,20},{20,16},{24,28},{28,24},{1,5},{5... | collective-permute-start | bytes 3735560 | tf_op jit(solution)/shard_map/ppermute | solution.py:411
  99.8 116.9 %reduce-scatter.5.cloned.1.call-start = ((), (), s32[]{:S(2)}) async-start(), calls=%async_computation.3 | async-start | bytes 2359296 | tf_op jit(solution)/shard_map/reduce_scatter | solution.py:470
  102.8 2.2 copy-start.2
  104.9 17.3 %copy-start.5 = (f32[4,304,256]{2,1,0:T(8,128)}, f32[4,304,256]{2,1,0:T(8,128)S(1)}, u32[]{:S(2)}) copy-start(f32[4,304,256]{2,1,0:T(8,128)S(1)} %collective-permute-done.9.odd_ref.refs_5_) | copy-start | bytes 3735556
  118.5 52.4 %collective-permute-start.13 = (f32[4000,128]{1,0:T(8,128)}, f32[4000,128]{1,0:T(8,128)}, u32[]{:S(2)}, u32[]{:S(2)}) collective-permute-start(f32[4000,128]{1,0:T(8,128)} %get-tuple-element.27.refs_4_.refs_1_), channel_id=1, source_target_pairs={{2,3},{6,7},{10,11},{14,15},{18,19},{22,23},{26,27},{30,31}} | collective-permute-start | bytes 6144008 | tf_op jit(solution)/shard_map/ppermute | solution.py:390
  120.6 50.3 %collective-permute-start.12 = (f32[4000,128]{1,0:T(8,128)}, f32[4000,128]{1,0:T(8,128)}, u32[]{:S(2)}, u32[]{:S(2)}) collective-permute-start(f32[4000,128]{1,0:T(8,128)} %get-tuple-element.22.refs_0_.refs_3_), channel_id=1, source_target_pairs={{1,0},{5,4},{9,8},{13,12},{17,16},{21,20},{25,24},{29,28}} | collective-permute-start | bytes 6144008 | tf_op jit(solution)/shard_map/ppermute | solution.py:390
  122.2 2.7 %copy-start.3 = (f32[4000,256]{1,0:T(8,128)S(1)}, f32[4000,256]{1,0:T(8,128)}, u32[]{:S(2)}) copy-start(f32[4000,256]{1,0:T(8,128)} %r_ref.5) | copy-start | bytes 12288004
  168.3 1.0 copy-start.6
  169.3 0.9 copy-start.11
  170.2 20.2 %copy-start.12 = (f32[128,256]{1,0:T(8,128)S(1)}, f32[128,256]{1,0:T(8,128)}, u32[]{:S(2)}) copy-start(f32[128,256]{1,0:T(8,128)} %own_columns.1.refs_2_.refs_1_.refs_0_) | copy-start | bytes 393220
  170.2 0.7 copy-start.7
  170.9 1.0 copy-start.8
  190.2 14.4 %copy-start.9 = (f32[384,256]{1,0:T(8,128)S(1)}, f32[384,256]{1,0:T(8,128)}, u32[]{:S(2)}) copy-start(f32[384,256]{1,0:T(8,128)} %copy-done.7) | copy-start | bytes 1179652
  190.2 10.1 %collective-permute-start.14 = (f32[4,128,256]{2,1,0:T(8,128)S(1)}, f32[4,128,256]{2,1,0:T(8,128)S(1)}, u32[]{:S(2)}, u32[]{:S(2)}) collective-permute-start(f32[4,128,256]{2,1,0:T(8,128)S(1)} %get-tuple-element.29), channel_id=1, source_target_pairs={{0,4},{4,0},{8,12},{12,8},{16,20},{20,16},{24,28},{28,24},{1,5},{5... | collective-permute-start | bytes 1572872 | tf_op jit(solution)/shard_map/ppermute | solution.py:411
  190.3 13.2 %collective-permute-start.17 = (f32[128,256]{1,0:T(8,128)S(1)}, f32[128,256]{1,0:T(8,128)S(1)}, u32[]{:S(2)}, u32[]{:S(2)}) collective-permute-start(f32[128,256]{1,0:T(8,128)S(1)} %copy-done.12), channel_id=1, source_target_pairs={{0,3},{1,0},{2,1},{3,2},{4,7},{5,4},{6,5},{7,6},{8,11},{9,8},{10,9... | collective-permute-start | bytes 393224 | tf_op jit(solution)/shard_map/ppermute | solution.py:475
  195.5 15.3 %collective-permute-start.16 = (f32[128,256]{1,0:T(8,128)S(1)}, f32[128,256]{1,0:T(8,128)S(1)}, u32[]{:S(2)}, u32[]{:S(2)}) collective-permute-start(f32[128,256]{1,0:T(8,128)S(1)} %copy-done.12), channel_id=1, source_target_pairs={{0,2},{1,3},{2,0},{3,1},{4,6},{5,7},{6,4},{7,5},{8,10},{9,11},{10,... | collective-permute-start | bytes 393224 | tf_op jit(solution)/shard_map/ppermute | solution.py:475
  198.4 12.4 %collective-permute-start.15 = (f32[128,256]{1,0:T(8,128)S(1)}, f32[128,256]{1,0:T(8,128)S(1)}, u32[]{:S(2)}, u32[]{:S(2)}) collective-permute-start(f32[128,256]{1,0:T(8,128)S(1)} %copy-done.12), channel_id=1, source_target_pairs={{0,1},{1,2},{2,3},{3,0},{4,5},{5,6},{6,7},{7,4},{8,9},{9,10},{10,1... | collective-permute-start | bytes 393224 | tf_op jit(solution)/shard_map/ppermute | solution.py:475
  200.4 16.2 %copy-start.13 = (f32[128,256]{1,0:T(8,128)}, f32[128,256]{1,0:T(8,128)S(1)}, u32[]{:S(2)}) copy-start(f32[128,256]{1,0:T(8,128)S(1)} %get-tuple-element.36.refs_1_.refs_0_) | copy-start | bytes 393220
  200.4 16.2 %collective-permute-start.20 = (f32[128,256]{1,0:T(8,128)S(1)}, f32[128,256]{1,0:T(8,128)S(1)}, u32[]{:S(2)}, u32[]{:S(2)}) collective-permute-start(f32[128,256]{1,0:T(8,128)S(1)} %get-tuple-element.33), channel_id=1, source_target_pairs={{0,24},{4,28},{8,16},{12,20},{16,8},{20,12},{24,0},{28,4},{1,25},{... | collective-permute-start | bytes 393224 | tf_op jit(solution)/shard_map/ppermute | solution.py:411
  203.0 13.7 %collective-permute-start.19 = (f32[128,256]{1,0:T(8,128)S(1)}, f32[128,256]{1,0:T(8,128)S(1)}, u32[]{:S(2)}, u32[]{:S(2)}) collective-permute-start(f32[128,256]{1,0:T(8,128)S(1)} %get-tuple-element.34), channel_id=1, source_target_pairs={{0,16},{4,20},{8,24},{12,28},{16,0},{20,4},{24,8},{28,12},{1,17},{... | collective-permute-start | bytes 393224 | tf_op jit(solution)/shard_map/ppermute | solution.py:411
  203.6 7.3 %copy-start.18 = (f32[128,256]{1,0:T(8,128)}, f32[128,256]{1,0:T(8,128)S(1)}, u32[]{:S(2)}) copy-start(f32[128,256]{1,0:T(8,128)S(1)} %collective-permute-done.17.refs_3_) | copy-start | bytes 393220
  203.6 13.1 %collective-permute-start.18 = (f32[128,256]{1,0:T(8,128)S(1)}, f32[128,256]{1,0:T(8,128)S(1)}, u32[]{:S(2)}, u32[]{:S(2)}) collective-permute-start(f32[128,256]{1,0:T(8,128)S(1)} %get-tuple-element.35), channel_id=1, source_target_pairs={{0,8},{4,12},{8,0},{12,4},{16,24},{20,28},{24,16},{28,20},{1,9},{5... | collective-permute-start | bytes 393224 | tf_op jit(solution)/shard_map/ppermute | solution.py:411
  204.6 15.8 %copy-start.1 = (f32[256,256]{1,0:T(8,128)S(1)}, f32[256,256]{1,0:T(8,128)}, u32[]{:S(2)}) copy-start(f32[256,256]{1,0:T(8,128)} %param.6) | copy-start | bytes 786436
  204.6 0.7 copy-start.10
  210.8 0.7 copy-start.19
  211.5 0.7 copy-start.20
  216.6 0.7 copy-start.21
  216.7 0.7 copy-start.22
  216.7 0.7 copy-start.23
Sparse Core Ops, SparseCore 0:
  100.0 48.4 reduce-scatter.2
  166.5 46.5 reduce-scatter.4

commit v14 on v13

--- a/solution.py
+++ b/solution.py
@@ -194,13 +194,14 @@
             jax.ShapeDtypeStruct((8, 128), F32),
         ],
         input_output_aliases={len(operands) - 1: 0} if before else {},
-        compiler_params=params(LESS),
+        compiler_params=params(),
         cost_estimate=SHORT,
         name="update",
     )(*operands)
 
 
-def late_kernel(per, counts, at_ref, u_ref, after_ref, *refs):
+def late_kernel(per, counts, n_after, at_ref, u_ref, *refs):
+    refs = refs[n_after:]
     *refs, both_ref, block_ref, sem_ref = refs
     outs = refs[sum(counts) :]
     j = pl.program_id(0)
@@ -250,11 +251,11 @@
         shapes = [(wide // 2, m, per)] * 2
         specs = [whole(x) for x in shapes]
     return pl.pallas_call(
-        functools.partial(late_kernel, per, counts),
+        functools.partial(late_kernel, per, counts, len(after)),
         grid_spec=pltpu.PrefetchScalarGridSpec(
             num_scalar_prefetch=1,
             grid=(columns // step,),
-            in_specs=[pl.BlockSpec((rows, step), lambda j, *_: (0, j))] + [ANY] * (1 + len(flat)),
+            in_specs=[pl.BlockSpec((rows, step), lambda j, *_: (0, j))] + [ANY] * (len(after) + len(flat)),
             out_specs=specs,
             scratch_shapes=[
                 pltpu.VMEM((2 * m, rows), BF16),
@@ -266,7 +267,7 @@
         compiler_params=params(LESS),
         cost_estimate=SHORT if ordered else LONG,
         name="late",
-    )(at, updated, after, *flat)
+    )(at, updated, *after, *flat)
 
 
 def own_kernel(me_ref, even_ref, odd_ref, after_ref, out_ref):
@@ -466,11 +467,10 @@
     )
 
     slots = [options(came, places, z) for places in table]
-    (middle,) = late(me, updated, slots[:-1], token, wide, True)
+    (middle,) = late(me, updated, slots[:-1], [token], wide, True)
     middle_sum = lax.psum_scatter(middle, "wide", scatter_dimension=0)
     mine = own_columns(me, c, middle, nb, each)
-    (ready,) = gate([ready], middle, mine)
-    even, odd = late(me, updated, slots[-1:], ready, wide, False)
+    even, odd = late(me, updated, slots[-1:], [ready, mine], wide, False)
     coef = [mine] + [
         lax.ppermute(mine, "narrow", [(p, (p + s) % n) for p in range(n)]) for s in range(1, n)
     ]

time: 228 us -> 228 us (level)
  local copies, waits for them, and re-layouts: 14.1 us -> 7.41 us
  waiting for transfers between devices: 33.2 us -> 38.8 us
    unnamed x48 -> x36, local copies, waits for them, and re-layouts: 13.5 us -> 6.73 us
    ppermute x6, waiting for transfers between devices: 2.9 us -> 5.97 us  [travel(): held = [lax.ppermute(held[d], 'narrow', pairs[d]) for d in (0, 1)]]
    reduce_scatter x1, waiting for transfers between devices: 0.02 us -> 2.72 us  [on_device(): middle_sum = lax.psum_scatter(middle, 'wide', scatter_dimension=0)]
  transfers between devices with their start and end apart: 23 -> 23, of which waited for: 9 -> 11; matrix products, arithmetic and copies ran while one was open for 1% -> 1% of each run, Pallas kernels for 54% -> 55%
where the time goes in v14:
time: 228 us; the launch traced here: 227 us
  Pallas kernels  129 us (57%)
  waiting for transfers between devices  38.8 us (17%)
  starting transfers between devices  33.4 us (15%)
  between operations  14.3 us (6%)
  local copies, waits for them, and re-layouts  7.41 us (3%)
  other arithmetic  4.28 us (2%)
    pallas_call x1, Pallas kernels, project(): pl.pallas_call(functools.partial(project_kernel, per, wide), grid_spec=pl...  43.9 us
    pallas_call x2, Pallas kernels, late(): pl.pallas_call(functools.partial(late_kernel, per, counts, len(after)), g...  41.2 us
    pallas_call x2, Pallas kernels, update(): pl.pallas_call(update_kernel, grid_spec=pltpu.PrefetchScalarGridSpec(num_...  34.1 us
    ppermute x12, waiting for transfers between devices, swap(): return lax.ppermute(x, 'wide', [(i, i ^ distance) for i in range(wide)])  24.4 us
    ppermute x6, starting transfers between devices, travel(): held = [lax.ppermute(held[d], 'narrow', pairs[d]) for d in (0, 1)]  13.1 us
    ppermute x12, starting transfers between devices, swap(): return lax.ppermute(x, 'wide', [(i, i ^ distance) for i in range(wide)])  10.8 us
    ppermute x3, starting transfers between devices, on_device(): lax.ppermute(mine, 'narrow', [(p, (p + s) % n) for p in range(n)])  9.39 us
    unnamed x36, local copies, waits for them, and re-layouts  6.73 us
  transfers between devices with their start and end apart: 23, of which 11 were waited for; matrix products, arithmetic and copies ran while one was open for 1% of the time, Pallas kernels for 55%

profile of v14, /device:TPU:0, one launch (start us, length us, event | category | flops | bytes accessed | tf_op | source)
XLA Modules:
  0.0 227.4 jit_solution(8791304100887099903)
XLA Ops:
  7.2 3.7 %slice_multiply_fusion.x_ref = f32[4000,128]{1,0:T(8,128)} fusion(f32[4000,2048]{1,0:T(8,128)} %v_ref.5, f32[4000]{0:T(1024)} %param.7), kind=kLoop, calls=%fused_computation | loop fusion | flops 512000 | bytes 4112000 | tf_op jit(solution)/shard_map/mul | solution.py:441
  10.9 5.0 %collective-permute-start.2 = (f32[4000,128]{1,0:T(8,128)}, f32[4000,128]{1,0:T(8,128)S(1)}, u32[]{:S(2)}, u32[]{:S(2)}) collective-permute-start(f32[4000,128]{1,0:T(8,128)} %slice_multiply_fusion.x_ref), channel_id=1, source_target_pairs={{0,1},{1,2},{2,3},{4,5},{5,6},{6,7},{8,9},{9,10},{10,11},{12,13},{... | collective-permute-start | bytes 6144008 | tf_op jit(solution)/shard_map/ppermute | solution.py:391
  16.0 1.3 collective-permute-start.1
  17.3 43.9 %project.1 = (f32[4,304,256]{2,1,0:T(8,128)}, f32[4,304,256]{2,1,0:T(8,128)}, f32[8,384,256]{2,1,0:T(8,128)}, f32[384,256]{1,0:T(8,128)}) custom-call(s32[1]{0:T(128)} %bitcast.me_ref, f32[4000,2048]{1,0:T(8,128)} %v_ref.5, f32[4000,256]{1,0:T(8,128)} %r_ref.5, f32[1,4000]{1,0:T(1,128)} %bitcast.47, f32[4000,128]{1,0:T(8,128)} %slice_multiply_fusion.x_ref), custom_call_target="tpu_custom_call" | custom-call | flops 1024 | bytes 1024 | tf_op jit(solution)/shard_map/project/pallas_call | solution.py:134
  61.2 3.0 %collective-permute-done.1.refs_0_ = f32[4000,128]{1,0:T(8,128)} collective-permute-done((f32[4000,128]{1,0:T(8,128)}, f32[4000,128]{1,0:T(8,128)}, u32[]{:S(2)}, u32[]{:S(2)}) %collective-permute-start.1) | collective-permute-done | bytes 2048032 | tf_op jit(solution)/shard_map/ppermute | solution.py:391
  64.2 1.0 copy-done.7
  65.2 1.3 copy-done.11
  66.6 1.6 collective-permute-start.3
  68.2 1.5 collective-permute-start.5
  69.7 0.5 collective-permute-start.4
  70.2 1.3 collective-permute-start.10
  71.5 2.0 collective-permute-start.11
  73.5 3.5 %collective-permute-done.3 = f32[304,256]{1,0:T(8,128)S(1)} collective-permute-done((f32[304,256]{1,0:T(8,128)S(1)}, f32[304,256]{1,0:T(8,128)S(1)}, u32[]{:S(2)}, u32[]{:S(2)}) %collective-permute-start.3) | collective-permute-done | bytes 311328 | tf_op jit(solution)/shard_map/ppermute | solution.py:412
  77.0 6.0 %collective-permute-done.5 = f32[304,256]{1,0:T(8,128)S(1)} collective-permute-done((f32[304,256]{1,0:T(8,128)S(1)}, f32[304,256]{1,0:T(8,128)S(1)}, u32[]{:S(2)}, u32[]{:S(2)}) %collective-permute-start.5) | collective-permute-done | bytes 311328 | tf_op jit(solution)/shard_map/ppermute | solution.py:412
  83.0 1.4 collective-permute-done.4
  84.5 0.4 convolution_bitcast_fusion.c_ref
  85.0 0.6 collective-permute-start.7
  85.5 1.5 collective-permute-start.6
  87.0 1.5 collective-permute-start.8
  88.5 6.7 %collective-permute-done.7 = f32[304,256]{1,0:T(8,128)S(1)} collective-permute-done((f32[304,256]{1,0:T(8,128)S(1)}, f32[304,256]{1,0:T(8,128)S(1)}, u32[]{:S(2)}, u32[]{:S(2)}) %collective-permute-start.7) | collective-permute-done | bytes 311328 | tf_op jit(solution)/shard_map/ppermute | solution.py:412
  95.3 3.9 %collective-permute-done.8 = f32[304,256]{1,0:T(8,128)S(1)} collective-permute-done((f32[304,256]{1,0:T(8,128)S(1)}, f32[304,256]{1,0:T(8,128)S(1)}, u32[]{:S(2)}, u32[]{:S(2)}) %collective-permute-start.8) | collective-permute-done | bytes 311328 | tf_op jit(solution)/shard_map/ppermute | solution.py:412
  99.4 3.0 %collective-permute-done.9.odd_ref.refs_5_ = f32[4,304,256]{2,1,0:T(8,128)} collective-permute-done((f32[4,304,256]{2,1,0:T(8,128)S(1)}, f32[4,304,256]{2,1,0:T(8,128)}, u32[]{:S(2)}, u32[]{:S(2)}) %collective-permute-start.9) | collective-permute-done | bytes 1245216 | tf_op jit(solution)/shard_map/ppermute | solution.py:412
  102.4 13.9 %update.2 = (f32[4000,2048]{1,0:T(8,128)}, f32[8,128]{1,0:T(8,128)}) custom-call(s32[1]{0:T(128)} %bitcast.me_ref, f32[4000,2048]{1,0:T(8,128)} %v_ref.5, f32[4000,256]{1,0:T(8,128)} %r_ref.5, f32[4,304,256]{2,1,0:T(8,128)} %copy-done.9, f32[4,304,256]{2,1,0:T(8,128)} %collective-permute-done.9.odd_ref.refs_5_), custom_call_target="tpu_custom_call" | custom-call | flops 1024 | bytes 1024 | tf_op jit(solution)/shard_map/update/pallas_call | solution.py:175
  116.3 1.9 collective-permute-done.10.refs_0_
  118.2 0.7 copy-done.8
  118.9 2.0 collective-permute-start.13
  120.9 1.5 collective-permute-start.12
  122.6 20.1 %update.3 = (f32[4000,2048]{1,0:T(8,128)}, f32[8,128]{1,0:T(8,128)}) custom-call(s32[1]{0:T(128)} %bitcast.me_ref, f32[4000,2048]{1,0:T(8,128)} %v_ref.5, f32[4000,256]{1,0:T(8,128)} %r_ref.5, f32[4,304,256]{2,1,0:T(8,128)} %copy-done.9, f32[4,304,256]{2,1,0:T(8,128)} %collective-permute-done.9.odd_ref.refs_5_, ...), custom_call_target="tpu_custom_call", output_to_operand_aliasing={{0}: (6, {})} | custom-call | flops 1024 | bytes 1024 | tf_op jit(solution)/shard_map/update/pallas_call | solution.py:175
  142.8 0.7 copy-done.6
  143.4 22.9 %late.2.after_ref = f32[8,256,256]{2,1,0:T(8,128)} custom-call(s32[3]{0:T(128)S(1)} %pad_add_fusion.1.at_ref, f32[4000,2048]{1,0:T(8,128)} %get-tuple-element.14.u_ref, f32[8,128]{1,0:T(8,128)S(1)} %copy-done.6, f32[4000,128]{1,0:T(8,128)} %get-tuple-element.19.refs_1_, f32[4000,128]{1,0:T(8,128)S(1)} %get-tuple-element.20.refs_2_.refs_3_, ...), custom_call_target="tpu_custom_call" | custom-call | flops 1024 | bytes 1024 | tf_op jit(solution)/shard_map/late/pallas_call | solution.py:253
  166.3 1.8 own_columns.1.refs_1_.refs_0_
  168.2 1.1 collective-permute-done.12.refs_4_
  169.2 1.0 copy-done.2
  170.2 18.4 %late.3 = (f32[4,128,256]{2,1,0:T(8,128)S(1)}, f32[4,128,256]{2,1,0:T(8,128)S(1)}) custom-call(s32[2]{0:T(128)S(1)} %pad_add_fusion.at_ref, f32[4000,2048]{1,0:T(8,128)} %get-tuple-element.14.u_ref, f32[384,256]{1,0:T(8,128)S(1)} %bitcast.41, f32[128,256]{1,0:T(8,128)} %own_columns.1.refs_1_.refs_0_, f32[4000,128]{1,0:T(8,128)} %get-tuple-element.22.refs_0_.refs_4_.refs_2_, ...), custom_call_target="tpu_custom_call" | custom-call | flops 99999997952 | bytes 1024 | tf_op jit(solution)/shard_map/late/pallas_call | solution.py:253
  188.7 4.4 %collective-permute-start.17 = (f32[128,256]{1,0:T(8,128)}, f32[128,256]{1,0:T(8,128)S(1)}, u32[]{:S(2)}, u32[]{:S(2)}) collective-permute-start(f32[128,256]{1,0:T(8,128)} %own_columns.1.refs_1_.refs_0_), channel_id=1, source_target_pairs={{0,3},{1,0},{2,1},{3,2},{4,7},{5,4},{6,5},{7,6},{8,11},{9,8},{10,9... | collective-permute-start | bytes 393224 | tf_op jit(solution)/shard_map/ppermute | solution.py:475
  193.1 3.1 %collective-permute-start.16 = (f32[128,256]{1,0:T(8,128)}, f32[128,256]{1,0:T(8,128)S(1)}, u32[]{:S(2)}, u32[]{:S(2)}) collective-permute-start(f32[128,256]{1,0:T(8,128)} %own_columns.1.refs_1_.refs_0_), channel_id=1, source_target_pairs={{0,2},{1,3},{2,0},{3,1},{4,6},{5,7},{6,4},{7,5},{8,10},{9,11},{10,... | collective-permute-start | bytes 393224 | tf_op jit(solution)/shard_map/ppermute | solution.py:475
  196.2 1.9 collective-permute-start.15
  198.2 2.4 %collective-permute-start.20 = (f32[128,256]{1,0:T(8,128)S(1)}, f32[128,256]{1,0:T(8,128)S(1)}, u32[]{:S(2)}, u32[]{:S(2)}) collective-permute-start(f32[128,256]{1,0:T(8,128)S(1)} %get-tuple-element.33), channel_id=1, source_target_pairs={{0,24},{4,28},{8,16},{12,20},{16,8},{20,12},{24,0},{28,4},{1,25},{... | collective-permute-start | bytes 393224 | tf_op jit(solution)/shard_map/ppermute | solution.py:412
  200.6 0.6 collective-permute-start.19
  201.2 0.5 collective-permute-start.18
  201.7 0.7 stack.54.at_ref
  202.4 0.7 copy-done.4
  203.2 5.6 %collective-permute-done.16.refs_2_ = f32[128,256]{1,0:T(8,128)S(1)} collective-permute-done((f32[128,256]{1,0:T(8,128)}, f32[128,256]{1,0:T(8,128)S(1)}, u32[]{:S(2)}, u32[]{:S(2)}) %collective-permute-start.16) | collective-permute-done | bytes 131104 | tf_op jit(solution)/shard_map/ppermute | solution.py:475
  208.8 0.6 copy-done.13
  209.5 0.6 copy-done.14
  210.1 4.6 %base.1.base_ref = f32[512,256]{1,0:T(8,128)} custom-call(s32[5]{0:T(128)} %stack.54.at_ref, f32[384,256]{1,0:T(8,128)} %copy-done.4, f32[256,256]{1,0:T(8,128)} %copy-done.10, f32[128,256]{1,0:T(8,128)} %own_columns.1.refs_1_.refs_0_, f32[128,256]{1,0:T(8,128)} %copy-done.14, f32[128,256]{1,0:T(8,128)} %copy-done.13, f32[128,256]{1,0:T(8,128)} %copy-done.12, ...), custom_call_target="tpu_custom_call" | custom-call | flops 1024 | bytes 1024 | tf_op jit(solution)/shard_map/base/pallas_call | solution.py:327
  214.8 2.7 %reduce-scatter.5.cloned.1.call-done = f32[1,256,256]{2,1,0:T(8,128)} async-done(((f32[8,256,256]{2,1,0:T(8,128)}), f32[1,256,256]{2,1,0:T(8,128)}) %reduce-scatter.5.cloned.1.call-update) | async-done | bytes 262160 | tf_op jit(solution)/shard_map/reduce_scatter | solution.py:471
  217.5 3.0 %last.1 = f32[256,512]{1,0:T(8,128)} custom-call(s32[5]{0:T(128)} %stack.54.at_ref, f32[512,256]{1,0:T(8,128)} %base.1.base_ref, f32[256,256]{1,0:T(8,128)} %bitcast.46, f32[128,256]{1,0:T(8,128)} %copy-done.5, f32[128,256]{1,0:T(8,128)} %copy-done.17, f32[128,256]{1,0:T(8,128)} %copy-done.16, f32[128,256]{1,0:T(8,128)} %copy-done.15), custom_call_target="tpu_custom_call" | custom-call | flops 1024 | bytes 1024 | tf_op jit(solution)/shard_map/last/pallas_call | solution.py:358
  (60 shorter events, 1.0 us)
Async XLA Ops:
  7.2 77.3 %copy-start = (f32[256,256]{1,0:T(8,128)S(1)}, f32[256,256]{1,0:T(8,128)}, u32[]{:S(2)}) copy-start(f32[256,256]{1,0:T(8,128)} %param.6) | copy-start | bytes 786436
  7.2 161.0 %reduce-scatter.3.cloned.1.call-start = ((), (), s32[]{:S(2)}) async-start(), calls=%async_computation.2 | async-start | bytes 3538944 | tf_op jit(solution)/shard_map/reduce_scatter | solution.py:451
  10.9 50.3 %collective-permute-start.2 = (f32[4000,128]{1,0:T(8,128)}, f32[4000,128]{1,0:T(8,128)S(1)}, u32[]{:S(2)}, u32[]{:S(2)}) collective-permute-start(f32[4000,128]{1,0:T(8,128)} %slice_multiply_fusion.x_ref), channel_id=1, source_target_pairs={{0,1},{1,2},{2,3},{4,5},{5,6},{6,7},{8,9},{9,10},{10,11},{12,13},{... | collective-permute-start | bytes 6144008 | tf_op jit(solution)/shard_map/ppermute | solution.py:391
  16.0 48.2 %collective-permute-start.1 = (f32[4000,128]{1,0:T(8,128)}, f32[4000,128]{1,0:T(8,128)}, u32[]{:S(2)}, u32[]{:S(2)}) collective-permute-start(f32[4000,128]{1,0:T(8,128)} %slice_multiply_fusion.x_ref), channel_id=1, source_target_pairs={{1,0},{2,1},{3,2},{5,4},{6,5},{7,6},{9,8},{10,9},{11,10},{13,12},{... | collective-permute-start | bytes 6144008 | tf_op jit(solution)/shard_map/ppermute | solution.py:391
  61.2 4.0 %collective-permute-start = (f32[4,304,256]{2,1,0:T(8,128)}, f32[4,304,256]{2,1,0:T(8,128)S(1)}, u32[]{:S(2)}, u32[]{:S(2)}) collective-permute-start(f32[4,304,256]{2,1,0:T(8,128)} %get-tuple-element.17), channel_id=1, source_target_pairs={{0,4},{4,0},{8,12},{12,8},{16,20},{20,16},{24,28},{28,24},{1,5},{5... | collective-permute-start | bytes 3735560 | tf_op jit(solution)/shard_map/ppermute | solution.py:412
  64.2 1.0 copy-start.7
  65.2 1.3 copy-start.11
  66.6 10.4 %collective-permute-start.3 = (f32[304,256]{1,0:T(8,128)S(1)}, f32[304,256]{1,0:T(8,128)S(1)}, u32[]{:S(2)}, u32[]{:S(2)}) collective-permute-start(f32[304,256]{1,0:T(8,128)S(1)} %get-tuple-element.30), channel_id=1, source_target_pairs={{0,8},{4,12},{8,0},{12,4},{16,24},{20,28},{24,16},{28,20},{1,9},{5... | collective-permute-start | bytes 933896 | tf_op jit(solution)/shard_map/ppermute | solution.py:412
  68.2 14.8 %collective-permute-start.5 = (f32[304,256]{1,0:T(8,128)S(1)}, f32[304,256]{1,0:T(8,128)S(1)}, u32[]{:S(2)}, u32[]{:S(2)}) collective-permute-start(f32[304,256]{1,0:T(8,128)S(1)} %get-tuple-element.31), channel_id=1, source_target_pairs={{0,24},{4,28},{8,16},{12,20},{16,8},{20,12},{24,0},{28,4},{1,25},{... | collective-permute-start | bytes 933896 | tf_op jit(solution)/shard_map/ppermute | solution.py:412
  69.7 14.7 %collective-permute-start.4 = (f32[304,256]{1,0:T(8,128)S(1)}, f32[304,256]{1,0:T(8,128)S(1)}, u32[]{:S(2)}, u32[]{:S(2)}) collective-permute-start(f32[304,256]{1,0:T(8,128)S(1)} %get-tuple-element.32), channel_id=1, source_target_pairs={{0,16},{4,20},{8,24},{12,28},{16,0},{20,4},{24,8},{28,12},{1,17},{... | collective-permute-start | bytes 933896 | tf_op jit(solution)/shard_map/ppermute | solution.py:412
  70.2 48.0 %collective-permute-start.10 = (f32[4000,128]{1,0:T(8,128)}, f32[4000,128]{1,0:T(8,128)}, u32[]{:S(2)}, u32[]{:S(2)}) collective-permute-start(f32[4000,128]{1,0:T(8,128)} %get-tuple-element.19.refs_1_), channel_id=1, source_target_pairs={{1,0},{2,1},{5,4},{6,5},{9,8},{10,9},{13,12},{14,13},{17,16},{18,1... | collective-permute-start | bytes 6144008 | tf_op jit(solution)/shard_map/ppermute | solution.py:391
  71.5 44.8 %collective-permute-start.11 = (f32[4000,128]{1,0:T(8,128)S(1)}, f32[4000,128]{1,0:T(8,128)}, u32[]{:S(2)}, u32[]{:S(2)}) collective-permute-start(f32[4000,128]{1,0:T(8,128)S(1)} %get-tuple-element.20.refs_2_.refs_3_), channel_id=1, source_target_pairs={{1,2},{2,3},{5,6},{6,7},{9,10},{10,11},{13,14},{14,15},{17,18},{18... | collective-permute-start | bytes 6144008 | tf_op jit(solution)/shard_map/ppermute | solution.py:391
  84.9 14.2 %copy-start.10 = (f32[256,256]{1,0:T(8,128)}, f32[256,256]{1,0:T(8,128)S(1)}, u32[]{:S(2)}) copy-start(f32[256,256]{1,0:T(8,128)S(1)} %convolution_bitcast_fusion.c_ref) | copy-start | bytes 786436
  85.0 10.3 %collective-permute-start.7 = (f32[304,256]{1,0:T(8,128)S(1)}, f32[304,256]{1,0:T(8,128)S(1)}, u32[]{:S(2)}, u32[]{:S(2)}) collective-permute-start(f32[304,256]{1,0:T(8,128)S(1)} %get-tuple-element.38), channel_id=1, source_target_pairs={{0,16},{4,20},{8,24},{12,28},{16,0},{20,4},{24,8},{28,12},{1,17},{... | collective-permute-start | bytes 933896 | tf_op jit(solution)/shard_map/ppermute | solution.py:412
  85.5 9.7 %collective-permute-start.6 = (f32[304,256]{1,0:T(8,128)S(1)}, f32[304,256]{1,0:T(8,128)S(1)}, u32[]{:S(2)}, u32[]{:S(2)}) collective-permute-start(f32[304,256]{1,0:T(8,128)S(1)} %get-tuple-element.38), channel_id=1, source_target_pairs={{0,8},{4,12},{8,0},{12,4},{16,24},{20,28},{24,16},{28,20},{1,9},{5... | collective-permute-start | bytes 933896 | tf_op jit(solution)/shard_map/ppermute | solution.py:412
  87.0 12.1 %collective-permute-start.8 = (f32[304,256]{1,0:T(8,128)S(1)}, f32[304,256]{1,0:T(8,128)S(1)}, u32[]{:S(2)}, u32[]{:S(2)}) collective-permute-start(f32[304,256]{1,0:T(8,128)S(1)} %get-tuple-element.38), channel_id=1, source_target_pairs={{0,24},{4,28},{8,16},{12,20},{16,8},{20,12},{24,0},{28,4},{1,25},{... | collective-permute-start | bytes 933896 | tf_op jit(solution)/shard_map/ppermute | solution.py:412
  99.2 3.2 %copy-start.9 = (f32[4,304,256]{2,1,0:T(8,128)}, f32[4,304,256]{2,1,0:T(8,128)S(1)}, u32[]{:S(2)}) copy-start(f32[4,304,256]{2,1,0:T(8,128)S(1)} %pad_maximum_fusion.even_ref.refs_4_) | copy-start | bytes 3735556
  99.3 3.1 %collective-permute-start.9 = (f32[4,304,256]{2,1,0:T(8,128)S(1)}, f32[4,304,256]{2,1,0:T(8,128)}, u32[]{:S(2)}, u32[]{:S(2)}) collective-permute-start(f32[4,304,256]{2,1,0:T(8,128)S(1)} %pad_maximum_fusion.even_ref.refs_4_), channel_id=1, source_target_pairs={{0,4},{4,0},{8,12},{12,8},{16,20},{20,16},{24,28},{28,24},{1,5},{5... | collective-permute-start | bytes 3735560 | tf_op jit(solution)/shard_map/ppermute | solution.py:412
  99.4 118.1 %reduce-scatter.5.cloned.1.call-start = ((), (), s32[]{:S(2)}) async-start(), calls=%async_computation.3 | async-start | bytes 2359296 | tf_op jit(solution)/shard_map/reduce_scatter | solution.py:471
  118.2 0.7 copy-start.8
  118.9 49.2 %collective-permute-start.13 = (f32[4000,128]{1,0:T(8,128)}, f32[4000,128]{1,0:T(8,128)}, u32[]{:S(2)}, u32[]{:S(2)}) collective-permute-start(f32[4000,128]{1,0:T(8,128)} %get-tuple-element.27.refs_5_.refs_3_), channel_id=1, source_target_pairs={{2,3},{6,7},{10,11},{14,15},{18,19},{22,23},{26,27},{30,31}} | collective-permute-start | bytes 6144008 | tf_op jit(solution)/shard_map/ppermute | solution.py:391
  120.9 48.3 %collective-permute-start.12 = (f32[4000,128]{1,0:T(8,128)}, f32[4000,128]{1,0:T(8,128)}, u32[]{:S(2)}, u32[]{:S(2)}) collective-permute-start(f32[4000,128]{1,0:T(8,128)} %get-tuple-element.22.refs_0_.refs_4_.refs_2_), channel_id=1, source_target_pairs={{1,0},{5,4},{9,8},{13,12},{17,16},{21,20},{25,24},{29,28}} | collective-permute-start | bytes 6144008 | tf_op jit(solution)/shard_map/ppermute | solution.py:391
  142.8 0.7 copy-start.6
  169.2 1.0 copy-start.2
  188.6 13.8 %copy-start.3 = (f32[1,384,256]{2,1,0:T(8,128)S(1)}, f32[1,384,256]{2,1,0:T(8,128)}, u32[]{:S(2)}) copy-start(f32[1,384,256]{2,1,0:T(8,128)} %reduce-scatter.3.cloned.1.call-done) | copy-start | bytes 1179652
  188.6 9.5 %collective-permute-start.14 = (f32[4,128,256]{2,1,0:T(8,128)S(1)}, f32[4,128,256]{2,1,0:T(8,128)S(1)}, u32[]{:S(2)}, u32[]{:S(2)}) collective-permute-start(f32[4,128,256]{2,1,0:T(8,128)S(1)} %get-tuple-element.29), channel_id=1, source_target_pairs={{0,4},{4,0},{8,12},{12,8},{16,20},{20,16},{24,28},{28,24},{1,5},{5... | collective-permute-start | bytes 1572872 | tf_op jit(solution)/shard_map/ppermute | solution.py:412
  188.7 12.5 %collective-permute-start.17 = (f32[128,256]{1,0:T(8,128)}, f32[128,256]{1,0:T(8,128)S(1)}, u32[]{:S(2)}, u32[]{:S(2)}) collective-permute-start(f32[128,256]{1,0:T(8,128)} %own_columns.1.refs_1_.refs_0_), channel_id=1, source_target_pairs={{0,3},{1,0},{2,1},{3,2},{4,7},{5,4},{6,5},{7,6},{8,11},{9,8},{10,9... | collective-permute-start | bytes 393224 | tf_op jit(solution)/shard_map/ppermute | solution.py:475
  193.1 15.7 %collective-permute-start.16 = (f32[128,256]{1,0:T(8,128)}, f32[128,256]{1,0:T(8,128)S(1)}, u32[]{:S(2)}, u32[]{:S(2)}) collective-permute-start(f32[128,256]{1,0:T(8,128)} %own_columns.1.refs_1_.refs_0_), channel_id=1, source_target_pairs={{0,2},{1,3},{2,0},{3,1},{4,6},{5,7},{6,4},{7,5},{8,10},{9,11},{10,... | collective-permute-start | bytes 393224 | tf_op jit(solution)/shard_map/ppermute | solution.py:475
  196.2 12.7 %collective-permute-start.15 = (f32[128,256]{1,0:T(8,128)}, f32[128,256]{1,0:T(8,128)S(1)}, u32[]{:S(2)}, u32[]{:S(2)}) collective-permute-start(f32[128,256]{1,0:T(8,128)} %own_columns.1.refs_1_.refs_0_), channel_id=1, source_target_pairs={{0,1},{1,2},{2,3},{3,0},{4,5},{5,6},{6,7},{7,4},{8,9},{9,10},{10,1... | collective-permute-start | bytes 393224 | tf_op jit(solution)/shard_map/ppermute | solution.py:475
  198.2 16.5 %copy-start.5 = (f32[128,256]{1,0:T(8,128)}, f32[128,256]{1,0:T(8,128)S(1)}, u32[]{:S(2)}) copy-start(f32[128,256]{1,0:T(8,128)S(1)} %get-tuple-element.36.refs_1_.refs_0_) | copy-start | bytes 393220
  198.2 16.5 %collective-permute-start.20 = (f32[128,256]{1,0:T(8,128)S(1)}, f32[128,256]{1,0:T(8,128)S(1)}, u32[]{:S(2)}, u32[]{:S(2)}) collective-permute-start(f32[128,256]{1,0:T(8,128)S(1)} %get-tuple-element.33), channel_id=1, source_target_pairs={{0,24},{4,28},{8,16},{12,20},{16,8},{20,12},{24,0},{28,4},{1,25},{... | collective-permute-start | bytes 393224 | tf_op jit(solution)/shard_map/ppermute | solution.py:412
  200.6 14.1 %collective-permute-start.19 = (f32[128,256]{1,0:T(8,128)S(1)}, f32[128,256]{1,0:T(8,128)S(1)}, u32[]{:S(2)}, u32[]{:S(2)}) collective-permute-start(f32[128,256]{1,0:T(8,128)S(1)} %get-tuple-element.34), channel_id=1, source_target_pairs={{0,16},{4,20},{8,24},{12,28},{16,0},{20,4},{24,8},{28,12},{1,17},{... | collective-permute-start | bytes 393224 | tf_op jit(solution)/shard_map/ppermute | solution.py:412
  201.2 7.6 %copy-start.12 = (f32[128,256]{1,0:T(8,128)}, f32[128,256]{1,0:T(8,128)S(1)}, u32[]{:S(2)}) copy-start(f32[128,256]{1,0:T(8,128)S(1)} %collective-permute-done.17.refs_3_) | copy-start | bytes 393220
  201.2 13.5 %collective-permute-start.18 = (f32[128,256]{1,0:T(8,128)S(1)}, f32[128,256]{1,0:T(8,128)S(1)}, u32[]{:S(2)}, u32[]{:S(2)}) collective-permute-start(f32[128,256]{1,0:T(8,128)S(1)} %get-tuple-element.35), channel_id=1, source_target_pairs={{0,8},{4,12},{8,0},{12,4},{16,24},{20,28},{24,16},{28,20},{1,9},{5... | collective-permute-start | bytes 393224 | tf_op jit(solution)/shard_map/ppermute | solution.py:412
  202.4 18.1 %copy-start.1 = (f32[256,256]{1,0:T(8,128)S(1)}, f32[256,256]{1,0:T(8,128)}, u32[]{:S(2)}) copy-start(f32[256,256]{1,0:T(8,128)} %param.6) | copy-start | bytes 786436
  202.4 0.7 copy-start.4
  208.8 0.6 copy-start.13
  209.5 0.6 copy-start.14
  214.7 2.8 %copy-start.15 = (f32[128,256]{1,0:T(8,128)}, f32[128,256]{1,0:T(8,128)S(1)}, u32[]{:S(2)}) copy-start(f32[128,256]{1,0:T(8,128)S(1)} %collective-permute-done.20.refs_3_) | copy-start | bytes 393220
  214.7 2.8 %copy-start.16 = (f32[128,256]{1,0:T(8,128)}, f32[128,256]{1,0:T(8,128)S(1)}, u32[]{:S(2)}) copy-start(f32[128,256]{1,0:T(8,128)S(1)} %collective-permute-done.19.refs_2_) | copy-start | bytes 393220
  214.7 2.7 %copy-start.17 = (f32[128,256]{1,0:T(8,128)}, f32[128,256]{1,0:T(8,128)S(1)}, u32[]{:S(2)}) copy-start(f32[128,256]{1,0:T(8,128)S(1)} %collective-permute-done.18.refs_1_) | copy-start | bytes 393220
Sparse Core Ops, SparseCore 0:
  99.5 49.7 reduce-scatter.2
  166.5 50.9 reduce-scatter.4
